TPU v7x, 32 devices: a whole 2x2x4 slice. The times are simulated.
32 devices in a mesh: dp: 8 (over y, x, core), fsdp: 4 (over z).
Axes of the slice: x: 2, y: 2, z: 4, core: 2. Of those that a mesh axis runs over, the one named last changes fastest.
Arguments:
- master: float32 [3, 1777664], P(None, ('dp', 'fsdp')), as said below
- first_moment: float32 [3, 1777664], P(None, ('dp', 'fsdp')), as said below
- second_moment: float32 [3, 1777664], P(None, ('dp', 'fsdp')), as said below
- patches_small: bfloat16 [128, 196, 768], P(('dp', 'fsdp')), may hold values from -6 to 6
- patches_large: bfloat16 [64, 576, 768], P(('dp', 'fsdp')), may hold values from -6 to 6
- labels_small: int32 [128], P(('dp', 'fsdp')), may hold values from 0 to 999
- labels_large: int32 [64], P(('dp', 'fsdp')), may hold values from 0 to 999
- counts: int32 [32, 2], P(('dp', 'fsdp')), may hold values from 0 to 4, as said below
- step: int32 [1], replicated, may hold values from 1 to 20
Outputs:
- loss: float32 [], replicated
- gradients: float32 [3, 1777664], P(None, ('dp', 'fsdp'))
- new_first: float32 [3, 1777664], P(None, ('dp', 'fsdp'))
- new_second: float32 [3, 1777664], P(None, ('dp', 'fsdp'))
- new_master: float32 [3, 1777664], P(None, ('dp', 'fsdp'))
- weight_norms: float32 [3, 16], replicated
- update_norms: float32 [3, 16], replicated
- trust_ratios: float32 [3, 16], replicated
Inputs may be any that keep to these rules, and one draw needn't show every extreme that they name: `master`: each row holds its segments in the order of the steps, zeros after the last one. `first_moment`: zeros after the last segment of each row. `second_moment`: positive on every segment entry, zeros after the last segment of each row. `counts`: column 0 lies in 1 to 4, column 1 in 0 to 2; the first device has all its slots live.
All inputs are finite; a program needn't handle non-finite values.
Results may differ from a plain program's by a relative error of at most 0.0095.
The roundings to bfloat16 on the way count: a program that leaves them out, or rounds other values in their place, can miss the bound.
Values may be sent and summed in bfloat16 or wider, within the bound.
No kernel may reach another device: no remote copies, remote signals or barrier semaphores. Data moves between devices by JAX's collectives and lax.ppermute only.
A program may use at most 256 MiB of HBM per device.

v0:
```python
from functools import partial

import jax
import jax.numpy as jnp
import numpy as np
from jax import lax
from jax.sharding import PartitionSpec as P

D = 384
HEADS = 8
FF = 1536
CLASSES = 1000
PATCH_IN = 768
GRID_SMALL = 14
GRID_LARGE = 24


highest = lax.Precision.HIGHEST
smooth = 0.1
beta_one = 0.9
beta_two = 0.999
adam_eps = 1e-06
decay_rate = 0.01
learn_rate = 0.3
norm_eps = 1e-06


def shapes_of():
    dim = D
    tail = [(dim,), (dim,), (dim, FF), (FF,), (FF, dim), (dim,), (dim,)]
    stem = [
        (PATCH_IN, dim),
        (dim,),
        (GRID_SMALL * GRID_SMALL, dim),
        (dim,),
        (dim,),
        (dim,),
        (dim, CLASSES),
        (CLASSES,),
    ]
    selfb = [
        (dim,),
        (dim,),
        (dim, 3 * dim),
        (2 * dim,),
        (HEADS, HEADS),
        (HEADS, HEADS),
        (dim, dim),
        (dim,),
        (dim,),
    ] + tail
    classb = [
        (dim,),
        (dim,),
        (dim, dim),
        (dim,),
        (dim, 2 * dim),
        (dim,),
        (dim, dim),
        (dim,),
        (dim,),
    ] + tail
    return [stem, selfb, classb]


def unpack(packed, shapes):
    pieces = []
    start = 0
    for shape in shapes:
        count = int(np.prod(shape))
        pieces.append(packed[start : start + count].reshape(shape))
        start += count
    return pieces


def segment_bounds():
    starts = np.zeros((3, 16), np.int32)
    ends = np.zeros((3, 16), np.int32)
    real = np.zeros((3, 16), np.float32)
    for group, shapes in enumerate(shapes_of()):
        offset = 0
        for number, shape in enumerate(shapes):
            count = int(np.prod(shape))
            starts[group, number] = offset
            ends[group, number] = offset + count
            real[group, number] = 1.0
            offset += count
    return (starts, ends, real)


def resize_matrix(small, large):
    rows = jnp.arange(large).astype(jnp.float32) * ((small - 1) / (large - 1))
    cols = jnp.arange(small).astype(jnp.float32)
    line = jnp.maximum(0.0, 1.0 - jnp.abs(rows[:, None] - cols[None, :]))
    return (line[:, None, :, None] * line[None, :, None, :]).reshape(large * large, small * small)


def widen(value):
    return value.astype(jnp.float32)


def normed(value, gain, shift):
    centred = value - jnp.mean(value, -1, keepdims=True)
    spread = jnp.mean(centred * centred, -1, keepdims=True)
    return centred * lax.rsqrt(spread + 1e-06) * gain + shift


def dense(left, right):
    return jnp.einsum("...i,ij->...j", left, right, preferred_element_type=jnp.float32)


def dense_back(left, right):
    return jnp.einsum("...j,ij->...i", left, right, preferred_element_type=jnp.float32)


def outer_sum(left, right):
    return jnp.einsum("...i,...j->ij", left, right, preferred_element_type=jnp.float32)


def row_sum(value):
    return jnp.sum(widen(value).reshape(-1, value.shape[-1]), 0)


def flatten(pieces, length):
    joined = jnp.concatenate([piece.reshape(-1) for piece in pieces])
    return jnp.pad(joined, (0, length - joined.shape[0]))


def mixing(scores, mix_pre, mix_post):
    mixed = jnp.einsum("gh,nhqk->ngqk", mix_pre, scores, precision=highest)
    probs = jax.nn.softmax(mixed, -1)
    return jnp.einsum("gh,nhqk->ngqk", mix_post, probs, precision=highest)


def head_loss(logits, labels, live, total):
    logp = jax.nn.log_softmax(logits, -1)
    picked = jnp.sum(
        jnp.where(jnp.arange(logits.shape[-1])[None, :] == labels[:, None], logp, 0.0), -1
    )
    each = -((1.0 - smooth) * picked + smooth * jnp.mean(logp, -1))
    return jnp.sum(live * each) / total


def feed_forward(mid, weights):
    norm_gain, norm_shift, w_upper, b_upper, w_lower, b_lower, scale_two = weights
    normed_mid = normed(mid, widen(norm_gain), widen(norm_shift)).astype(jnp.bfloat16)
    upper = dense(normed_mid, w_upper) + widen(b_upper)
    active = jax.nn.gelu(upper, approximate=False).astype(jnp.bfloat16)
    lower = dense(active, w_lower) + widen(b_lower)
    return (mid + widen(scale_two) * lower, (upper, active, lower))


def feed_back(d_out, mid, kept, weights):
    norm_gain, norm_shift, w_upper, b_upper, w_lower, b_lower, scale_two = weights
    upper, active, lower = kept
    d_scale_two = row_sum(d_out * lower)
    d_lower = (d_out * widen(scale_two)).astype(jnp.bfloat16)
    d_w_lower = outer_sum(active, d_lower)
    d_active = dense_back(d_lower, w_lower)
    gelu_out, gelu_back = jax.vjp(partial(jax.nn.gelu, approximate=False), upper)
    d_upper = gelu_back(d_active)[0].astype(jnp.bfloat16)
    normed_out, norm_back = jax.vjp(normed, mid, widen(norm_gain), widen(norm_shift))
    d_w_upper = outer_sum(normed_out.astype(jnp.bfloat16), d_upper)
    d_mid, d_gain, d_shift = norm_back(dense_back(d_upper, w_upper))
    return (
        d_out + d_mid,
        [d_gain, d_shift, d_w_upper, row_sum(d_upper), d_w_lower, row_sum(d_lower), d_scale_two],
    )


def self_forward(tokens, weights):
    gain, shift, w_qkv, b_qv, mix_pre, mix_post, w_out, b_out, scale_one = weights[:9]
    batch, length, dim = tokens.shape
    width = dim // HEADS
    scale = width ** (-0.5)
    normed_in = normed(tokens, widen(gain), widen(shift)).astype(jnp.bfloat16)
    bias = widen(jnp.concatenate([b_qv[:dim], jnp.zeros((dim,), jnp.bfloat16), b_qv[dim:]]))
    projected = (
        (dense(normed_in, w_qkv) + bias)
        .astype(jnp.bfloat16)
        .reshape(batch, length, 3, HEADS, width)
    )
    pre_wide, post_wide = (widen(mix_pre), widen(mix_post))

    def attend_image(item):
        query, keys, values = item
        scores = jnp.einsum("qhc,khc->hqk", query, keys, preferred_element_type=jnp.float32) * scale
        weighted = mixing(scores[None], pre_wide, post_wide)[0].astype(jnp.bfloat16)
        return (
            jnp.einsum("hqk,khc->qhc", weighted, values, preferred_element_type=jnp.float32)
            .reshape(length, dim)
            .astype(jnp.bfloat16)
        )

    attended = lax.map(attend_image, (projected[:, :, 0], projected[:, :, 1], projected[:, :, 2]))
    branch = dense(attended, w_out) + widen(b_out)
    mid = tokens + widen(scale_one) * branch
    out, kept = feed_forward(mid, weights[9:])
    return (out, (projected, attended, branch, mid, kept))


def self_backward(d_out, tokens, saved, weights):
    gain, shift, w_qkv, b_qv, mix_pre, mix_post, w_out, b_out, scale_one = weights[:9]
    projected, attended, branch, mid, kept = saved
    batch, length, dim = tokens.shape
    width = dim // HEADS
    scale = width ** (-0.5)
    d_mid, tail_grads = feed_back(d_out, mid, kept, weights[9:])
    d_scale_one = row_sum(d_mid * branch)
    d_branch = (d_mid * widen(scale_one)).astype(jnp.bfloat16)
    d_w_out = outer_sum(attended, d_branch)
    d_attended = (
        dense_back(d_branch, w_out).astype(jnp.bfloat16).reshape(batch, length, HEADS, width)
    )
    pre_wide, post_wide = (widen(mix_pre), widen(mix_post))

    def attend_back(item):
        query, keys, values, d_att = item
        scores = jnp.einsum("qhc,khc->hqk", query, keys, preferred_element_type=jnp.float32) * scale
        weighted_out, mix_back = jax.vjp(mixing, scores[None], pre_wide, post_wide)
        weighted = weighted_out[0].astype(jnp.bfloat16)
        d_weighted = jnp.einsum("qhc,khc->hqk", d_att, values, preferred_element_type=jnp.float32)
        d_values = jnp.einsum("hqk,qhc->khc", weighted, d_att, preferred_element_type=jnp.float32)
        d_scores, d_pre, d_post = mix_back(d_weighted[None])
        d_scores = d_scores[0].astype(jnp.bfloat16)
        d_query = (
            jnp.einsum("hqk,khc->qhc", d_scores, keys, preferred_element_type=jnp.float32) * scale
        )
        d_keys = (
            jnp.einsum("hqk,qhc->khc", d_scores, query, preferred_element_type=jnp.float32) * scale
        )
        joined = (
            jnp.stack([d_query, d_keys, d_values], 1).reshape(length, 3 * dim).astype(jnp.bfloat16)
        )
        return (joined, d_pre, d_post)

    d_projected, pre_each, post_each = lax.map(
        attend_back, (projected[:, :, 0], projected[:, :, 1], projected[:, :, 2], d_attended)
    )
    d_mix_pre = jnp.sum(pre_each, 0)
    d_mix_post = jnp.sum(post_each, 0)
    d_b_qv = jnp.concatenate(
        [row_sum(d_projected[..., :dim]), row_sum(d_projected[..., 2 * dim :])]
    )
    normed_out, norm_back = jax.vjp(normed, tokens, widen(gain), widen(shift))
    d_w_qkv = outer_sum(normed_out.astype(jnp.bfloat16), d_projected)
    d_tokens, d_gain, d_shift = norm_back(dense_back(d_projected, w_qkv))
    grads = [
        d_gain,
        d_shift,
        d_w_qkv,
        d_b_qv,
        d_mix_pre,
        d_mix_post,
        d_w_out,
        row_sum(d_branch),
        d_scale_one,
    ] + tail_grads
    return (d_mid + d_tokens, grads)


def class_forward(cls_tok, tokens, weights):
    gain, shift, w_query, b_query, w_kv, b_value, w_out, b_out, scale_one = weights[:9]
    batch, length, dim = tokens.shape
    width = dim // HEADS
    joined = jnp.concatenate([jnp.broadcast_to(widen(cls_tok), (batch, 1, dim)), tokens], 1)
    normed_all = normed(joined, widen(gain), widen(shift)).astype(jnp.bfloat16)
    query = (
        (dense(normed_all[:, 0], w_query) + widen(b_query))
        .astype(jnp.bfloat16)
        .reshape(batch, HEADS, width)
    )
    bias = widen(jnp.concatenate([jnp.zeros((dim,), jnp.bfloat16), b_value]))
    keyval = (
        (dense(normed_all, w_kv) + bias)
        .astype(jnp.bfloat16)
        .reshape(batch, length + 1, 2, HEADS, width)
    )
    scores = jnp.einsum(
        "nhc,nkhc->nhk", query, keyval[:, :, 0], preferred_element_type=jnp.float32
    ) * width ** (-0.5)
    probs = jax.nn.softmax(scores, -1).astype(jnp.bfloat16)
    attended = jnp.einsum(
        "nhk,nkhc->nhc", probs, keyval[:, :, 1], preferred_element_type=jnp.float32
    )
    attended = attended.reshape(batch, dim).astype(jnp.bfloat16)
    branch = dense(attended, w_out) + widen(b_out)
    mid = widen(cls_tok) + widen(scale_one) * branch
    out, kept = feed_forward(mid, weights[9:])
    return (out, (joined, query, keyval, attended, branch, mid, kept))


def class_backward(d_out, saved, weights):
    gain, shift, w_query, b_query, w_kv, b_value, w_out, b_out, scale_one = weights[:9]
    joined, query, keyval, attended, branch, mid, kept = saved
    batch, rows, dim = joined.shape
    width = dim // HEADS
    scale = width ** (-0.5)
    d_mid, tail_grads = feed_back(d_out, mid, kept, weights[9:])
    d_scale_one = row_sum(d_mid * branch)
    d_branch = (d_mid * widen(scale_one)).astype(jnp.bfloat16)
    d_w_out = outer_sum(attended, d_branch)
    d_attended = dense_back(d_branch, w_out).astype(jnp.bfloat16).reshape(batch, HEADS, width)
    keys, values = (keyval[:, :, 0], keyval[:, :, 1])
    scores = jnp.einsum("nhc,nkhc->nhk", query, keys, preferred_element_type=jnp.float32) * scale
    probs_out, soft_back = jax.vjp(partial(jax.nn.softmax, axis=-1), scores)
    probs = probs_out.astype(jnp.bfloat16)
    d_probs = jnp.einsum("nhc,nkhc->nhk", d_attended, values, preferred_element_type=jnp.float32)
    d_values = jnp.einsum("nhk,nhc->nkhc", probs, d_attended, preferred_element_type=jnp.float32)
    d_scores = soft_back(d_probs)[0].astype(jnp.bfloat16)
    d_query = (
        jnp.einsum("nhk,nkhc->nhc", d_scores, keys, preferred_element_type=jnp.float32) * scale
    )
    d_query = d_query.reshape(batch, dim).astype(jnp.bfloat16)
    d_keys = (
        jnp.einsum("nhk,nhc->nkhc", d_scores, query, preferred_element_type=jnp.float32) * scale
    )
    d_keyval = jnp.stack([d_keys, d_values], 2).reshape(batch, rows, 2 * dim).astype(jnp.bfloat16)
    normed_out, norm_back = jax.vjp(normed, joined, widen(gain), widen(shift))
    normed_all = normed_out.astype(jnp.bfloat16)
    d_w_query = outer_sum(normed_all[:, 0], d_query)
    d_w_kv = outer_sum(normed_all, d_keyval)
    d_normed = dense_back(d_keyval, w_kv)
    d_normed = d_normed.at[:, 0].add(dense_back(d_query, w_query))
    d_joined, d_gain, d_shift = norm_back(d_normed)
    d_cls = jnp.sum(d_mid + d_joined[:, 0], 0)
    grads = [
        d_gain,
        d_shift,
        d_w_query,
        row_sum(d_query),
        d_w_kv,
        row_sum(d_keyval[..., dim:]),
        d_w_out,
        row_sum(d_branch),
        d_scale_one,
    ] + tail_grads
    return (d_joined[:, 1:], d_cls, grads)


def head_forward(cls_out, stem, labels, live, total):
    final_out, final_back = jax.vjp(normed, cls_out, widen(stem[4]), widen(stem[5]))
    final = final_out.astype(jnp.bfloat16)
    logits = dense(final, stem[6]) + widen(stem[7])
    part_loss, loss_back = jax.vjp(lambda values: head_loss(values, labels, live, total), logits)
    d_logits = loss_back(jnp.ones((), jnp.float32))[0].astype(jnp.bfloat16)
    return (part_loss, (final, final_back, d_logits))


def add_lists(first, second):
    return [left + right for left, right in zip(first, second)]


def on_device(
    master,
    first_moment,
    second_moment,
    patches_small,
    patches_large,
    labels_small,
    labels_large,
    counts,
    step,
):
    groups = shapes_of()
    shard = master.shape[1]
    length = shard * lax.axis_size(("dp", "fsdp"))
    starts, ends, real = segment_bounds()
    position = lax.axis_index(("dp", "fsdp")) * shard + jnp.arange(shard, dtype=jnp.int32)
    member = (
        (position[None, :, None] >= starts[:, None, :])
        & (position[None, :, None] < ends[:, None, :])
    ).astype(jnp.float32)
    weight_part = jnp.einsum("gi,gis->gs", master * master, member, precision=highest)
    local_count = jnp.sum(counts).astype(jnp.float32)
    total, weight_sq = lax.psum((local_count, weight_part), ("dp", "fsdp"))
    copies = master.astype(jnp.bfloat16)
    front = [
        unpack(lax.all_gather(copies[index], ("dp", "fsdp"), axis=0, tiled=True), groups[index])
        for index in range(3)
    ]
    stem, selfw, classw = front
    resize = resize_matrix(GRID_SMALL, GRID_LARGE)
    pos_small = widen(stem[2])
    pos_large = jnp.dot(resize, pos_small, precision=highest)
    live_small = (jnp.arange(patches_small.shape[0]) < counts[0, 0]).astype(jnp.float32)
    live_large = (jnp.arange(patches_large.shape[0]) < counts[0, 1]).astype(jnp.float32)
    batches = [
        (patches_small, labels_small, live_small, pos_small),
        (patches_large, labels_large, live_large, pos_large),
    ]
    saved = []
    loss_local = jnp.zeros((), jnp.float32)
    for patches, labels, live, pos in batches:
        tokens = dense(patches, stem[0]) + widen(stem[1]) + pos
        mixed, self_saved = self_forward(tokens, selfw)
        cls_out, class_saved = class_forward(stem[3], mixed, classw)
        part_loss, head_saved = head_forward(cls_out, stem, labels, live, total)
        loss_local = loss_local + part_loss
        saved.append((tokens, self_saved, class_saved, head_saved))
    back = [
        unpack(lax.all_gather(copies[index], ("dp", "fsdp"), axis=0, tiled=True), groups[index])
        for index in (0, 2, 1)
    ]
    stem_back, class_back, self_back = back
    head_grads = None
    class_grads = None
    d_cls_tok = jnp.zeros((D,), jnp.float32)
    d_mixed_list = []
    for tokens, self_saved, class_saved, head_saved in saved:
        final, final_back, d_logits = head_saved
        d_cls_out, d_final_gain, d_final_shift = final_back(dense_back(d_logits, stem_back[6]))
        grads_now = [d_final_gain, d_final_shift, outer_sum(final, d_logits), row_sum(d_logits)]
        head_grads = grads_now if head_grads is None else add_lists(head_grads, grads_now)
        d_mixed, d_cls, grads_now = class_backward(d_cls_out, class_saved, class_back)
        class_grads = grads_now if class_grads is None else add_lists(class_grads, grads_now)
        d_cls_tok = d_cls_tok + d_cls
        d_mixed_list.append(d_mixed)

    def reduce_group(pieces):
        return lax.psum_scatter(
            flatten(pieces, length), ("dp", "fsdp"), scatter_dimension=0, tiled=True
        )

    grad_class = reduce_group(class_grads)
    self_grads = None
    d_tokens_list = []
    for (tokens, self_saved, class_saved, head_saved), d_mixed in zip(saved, d_mixed_list):
        d_tokens, grads_now = self_backward(d_mixed, tokens, self_saved, self_back)
        self_grads = grads_now if self_grads is None else add_lists(self_grads, grads_now)
        d_tokens_list.append(d_tokens)
    grad_self = reduce_group(self_grads)
    d_patch_w = jnp.zeros((PATCH_IN, D), jnp.float32)
    d_patch_b = jnp.zeros((D,), jnp.float32)
    for (patches, labels, live, pos), d_tokens in zip(batches, d_tokens_list):
        d_patch_w = d_patch_w + outer_sum(patches, d_tokens.astype(jnp.bfloat16))
        d_patch_b = d_patch_b + row_sum(d_tokens)
    d_pos = jnp.sum(d_tokens_list[0], 0) + jnp.dot(
        resize.T, jnp.sum(d_tokens_list[1], 0), precision=highest
    )
    stem_grads = [d_patch_w, d_patch_b, d_pos, d_cls_tok] + head_grads
    grad_stem = reduce_group(stem_grads)
    gradients = jnp.stack([grad_stem, grad_self, grad_class])
    new_first = beta_one * first_moment + (1.0 - beta_one) * gradients
    new_second = beta_two * second_moment + (1.0 - beta_two) * gradients * gradients
    count_f = step[0].astype(jnp.float32)
    update = (
        new_first
        / (1.0 - beta_one**count_f)
        / (jnp.sqrt(new_second / (1.0 - beta_two**count_f)) + adam_eps)
        + decay_rate * master
    )
    update_part = jnp.einsum("gi,gis->gs", update * update, member, precision=highest)
    update_sq, loss = lax.psum((update_part, loss_local), ("dp", "fsdp"))
    weight_norms = jnp.sqrt(weight_sq)
    update_norms = jnp.sqrt(update_sq)
    trust_ratios = jnp.where(real > 0, weight_norms / (update_norms + norm_eps), 1.0)
    per_entry = jnp.einsum("gis,gs->gi", member, trust_ratios, precision=highest)
    new_master = master - learn_rate * per_entry * update
    return (
        loss,
        gradients,
        new_first,
        new_second,
        new_master,
        weight_norms,
        update_norms,
        trust_ratios,
    )


def solution(mesh):
    return jax.shard_map(
        on_device,
        mesh=mesh,
        in_specs=(
            P(None, ("dp", "fsdp")),
            P(None, ("dp", "fsdp")),
            P(None, ("dp", "fsdp")),
            P(("dp", "fsdp"), None, None),
            P(("dp", "fsdp"), None, None),
            P(("dp", "fsdp")),
            P(("dp", "fsdp")),
            P(("dp", "fsdp"), None),
            P(),
        ),
        out_specs=(
            P(),
            P(None, ("dp", "fsdp")),
            P(None, ("dp", "fsdp")),
            P(None, ("dp", "fsdp")),
            P(None, ("dp", "fsdp")),
            P(),
            P(),
            P(),
        ),
        check_vma=False,
    )
```

profile of v0, /device:TPU:0, one launch (start us, length us, event | category | flops | bytes accessed | tf_op | source)
XLA Modules:
  0.0 1900.5 jit_solution(8734476410575818098)
XLA Ops:
  12.8 42.5 %psum.28 = f32[]{:T(128)} all-reduce(f32[]{:T(128)S(6)} %convert_element_type.633), channel_id=1, replica_groups=mesh['dp'=8,'fsdp'=4] {'dp','fsdp'}, use_global_device_ids=true, to_apply=%region_22.23 | all-reduce | flops 1 | bytes 8 | tf_op jit(solution)/shard_map/psum | solution.py:376
  63.2 23.9 %all-gather.11.cloned.1.call-done = bf16[1,1777664]{1,0:T(2,128)(2,1)} async-done(((bf16[1,55552]{1,0:T(2,128)(2,1)}), bf16[1,1777664]{1,0:T(2,128)(2,1)}) %all-gather.11.cloned.1.call-update) | async-done | bytes 3555344 | tf_op jit(solution)/shard_map/all_gather | solution.py:379
  88.1 73.7 %all-gather.7.cloned.1.call-done = bf16[1,1777664]{1,0:T(2,128)(2,1)} async-done(((bf16[1,55552]{1,0:T(2,128)(2,1)}), bf16[1,1777664]{1,0:T(2,128)(2,1)}) %all-gather.7.cloned.1.call-update) | async-done | bytes 3555344 | tf_op jit(solution)/shard_map/all_gather | solution.py:379
  163.8 5.9 slice_reduce_fusion.10
  170.6 10.8 slice_reduce_fusion.7
  182.6 54.0 %all-gather.9.cloned.1.call-done = bf16[1,1777664]{1,0:T(2,128)(2,1)} async-done(((bf16[1,55552]{1,0:T(2,128)(2,1)}), bf16[1,1777664]{1,0:T(2,128)(2,1)}) %all-gather.9.cloned.1.call-update) | async-done | bytes 3555344 | tf_op jit(solution)/shard_map/all_gather | solution.py:379
  236.6 8.3 slice_reduce_fusion.8
  245.8 15.8 slice_reduce_fusion.4
  263.5 27.8 %slice_reduce_fusion.2 = (bf16[589824]{0:T(1024)(128)(2,1)S(1)}, bf16[589824]{0:T(1024)(128)(2,1)}) fusion(bf16[1,1777664]{1,0:T(2,128)(2,1)} %all-gather.11.cloned.1.call-done), kind=kLoop, calls=%fused_computation.276 | loop fusion | bytes 4718592 | tf_op jit(solution)/shard_map/slice | solution.py:71
  312.2 32.9 %while.50 = (s32[]{:T(128)}, bf16[4,196,384]{1,2,0:T(8,128)(2,1)}, bf16[4,196,8,48]{1,3,2,0:T(8,128)(2,1)}, bf16[4,196,8,48]{1,3,2,0:T(8,128)(2,1)}, bf16[4,196,...) while((s32[]{:T(128)}, bf16[4,196,384]{1,2,0:T(8,128)(2,1)}, ...), condition=%wide.region_5.6_spmd, body=%wide.region_2.5_spmd.sunk | while | flops 120237376 | bytes 8496357 | solution.py:195
  351.9 12.5 multiply_convert_fusion.1
  370.9 14.8 slice_reduce_fusion.5
  389.1 12.1 slice_reduce_fusion.6
  403.4 27.7 %slice_reduce_fusion = (bf16[589824]{0:T(1024)(128)(2,1)}, bf16[589824]{0:T(1024)(128)(2,1)}) fusion(bf16[1,1777664]{1,0:T(2,128)(2,1)} %all-gather.9.cloned.1.call-done), kind=kLoop, calls=%fused_computation.274 | loop fusion | bytes 4718592 | tf_op jit(solution)/shard_map/slice | solution.py:71
  501.6 105.8 %while.52 = (s32[]{:T(128)}, bf16[4,196,1152]{1,2,0:T(8,128)(2,1)}, f32[4,8,8]{2,1,0:T(8,128)}, f32[4,8,8]{2,1,0:T(8,128)}, bf16[4,196,8,48]{1,3,2,0:T(8,128)(2,...) while((s32[]{:T(128)}, bf16[4,196,1152]{1,2,0:T(8,128)(2,1)}, ...), condition=%wide.region_59.60_spmd, body=%wide.region_55.59_spmd.sunk | while | flops 332434816 | bytes 29248168 | solution.py:237
  635.4 92.1 %while.51 = (s32[]{:T(128)}, bf16[2,576,384]{1,2,0:T(8,128)(2,1)}, bf16[2,576,8,48]{1,3,2,0:T(8,128)(2,1)}, bf16[2,576,8,48]{1,3,2,0:T(8,128)(2,1)}, bf16[2,576,...) while((s32[]{:T(128)}, bf16[2,576,384]{1,2,0:T(8,128)(2,1)}, ...), condition=%wide.region_28.29_spmd, body=%wide.region_25.28_spmd.sunk | while | flops 1038007296 | bytes 84981552 | solution.py:195
  639.3 18.9 bitcast_reduce_fusion.9
  661.8 13.1 convert_bitcast_fusion.6
  681.5 18.9 bitcast_reduce_fusion.9
  704.0 13.1 convert_bitcast_fusion.6
  737.5 17.4 multiply_convert_fusion
  827.0 7.1 convert_reduce_fusion
  847.3 370.9 %while.53 = (s32[]{:T(128)}, bf16[2,576,1152]{1,2,0:T(8,128)(2,1)}, f32[2,8,8]{2,1,0:T(8,128)S(1)}, f32[2,8,8]{2,1,0:T(8,128)S(1)}, bf16[2,576,8,48]{1,3,2,0:T(8...) while((s32[]{:T(128)}, bf16[2,576,1152]{1,2,0:T(8,128)(2,1)}, ...), condition=%wide.region_76.77_spmd, body=%wide.region_72.76_spmd.sunk | while | flops 2863669248 | bytes 410025536 | solution.py:237
  848.5 7.2 convolution_bitcast_fusion.17
  857.5 18.6 bitcast_reduce_fusion.11
  880.3 30.9 %fusion.660 = f32[2,8,8]{2,1,0:T(8,128)S(1)} fusion(f32[2,8,8]{2,1,0:T(8,128)S(1)} %get-tuple-element.998, s32[]{:T(128)S(6)} %copy.528, f32[8,576]{0,1:T(8,128)S(1)} %fusion.654, f32[8,576]{0,1:T(8,128)S(1)} %get-tuple-element.900, f32[576,576,8]{1,2,0:T(8,128)} %copy-done.1, f32[576,576,8]{1,0,2:T(8,128)} %convolution_bitcast_fusion.17), kind=kOutput, calls=%fused_computation.167.clone.1 | convolution fusion | flops 260112384 | bytes 21827588 | tf_op jit(solution)/shard_map/while/body/eval_jaxpr/transpose(jvp(gh,nhqk->ngqk))/dot_general | solution.py:132
  911.3 31.6 %fusion.656 = (f32[8,576]{0,1:T(8,128)S(1)}, f32[576,576,8]{1,2,0:T(8,128)}) fusion(f32[576,576,8]{1,2,0:T(8,128)} %copy-done.1, f32[8,576]{0,1:T(8,128)S(1)} %multiply_divide_fusion.7, f32[8,576]{0,1:T(8,128)S(1)} %get-tuple-element.900, f32[8,8]{1,0:T(8,128)S(1)} %get-tuple-element.1013, f32[576,576,8]{1,0,2:T(8,128)} %convolution_bitcast_fusion.17), kind=kOutput, calls=%fused_computation.127.clone.1 | convolution fusion | flops 265416192 | bytes 31906048 | tf_op jit(solution)/shard_map/while/body/eval_jaxpr/transpose(jvp(gh,nhqk->ngqk))/dot_general | solution.py:132
  943.0 18.5 convert_bitcast_fusion.8
  961.5 9.9 exponential_multiply_fusion.16
  971.4 30.1 %fusion.659 = f32[2,8,8]{2,1,0:T(8,128)S(1)} fusion(f32[2,8,8]{2,1,0:T(8,128)S(1)} %get-tuple-element.997, s32[]{:T(128)S(6)} %copy.528, f32[8,576,576]{2,1,0:T(8,128)} %copy-done.2, f32[576,576,8]{1,2,0:T(8,128)} %exponential_multiply_fusion.16), kind=kOutput, calls=%fused_computation.165.clone.2 | convolution fusion | flops 254803968 | bytes 21237764 | tf_op jit(solution)/shard_map/while/body/eval_jaxpr/transpose(jvp(gh,nhqk->ngqk))/dot_general | solution.py:130
  1001.5 13.6 convert_bitcast_fusion.7
  1029.7 7.2 convolution_bitcast_fusion.17
  1038.6 18.6 bitcast_reduce_fusion.11
  1061.5 30.9 %fusion.660 = f32[2,8,8]{2,1,0:T(8,128)S(1)} fusion(f32[2,8,8]{2,1,0:T(8,128)S(1)} %get-tuple-element.998, s32[]{:T(128)S(6)} %copy.528, f32[8,576]{0,1:T(8,128)S(1)} %fusion.654, f32[8,576]{0,1:T(8,128)S(1)} %get-tuple-element.900, f32[576,576,8]{1,2,0:T(8,128)} %copy-done.1, f32[576,576,8]{1,0,2:T(8,128)} %convolution_bitcast_fusion.17), kind=kOutput, calls=%fused_computation.167.clone.1 | convolution fusion | flops 260112384 | bytes 21827588 | tf_op jit(solution)/shard_map/while/body/eval_jaxpr/transpose(jvp(gh,nhqk->ngqk))/dot_general | solution.py:132
  1092.4 31.6 %fusion.656 = (f32[8,576]{0,1:T(8,128)S(1)}, f32[576,576,8]{1,2,0:T(8,128)}) fusion(f32[576,576,8]{1,2,0:T(8,128)} %copy-done.1, f32[8,576]{0,1:T(8,128)S(1)} %multiply_divide_fusion.7, f32[8,576]{0,1:T(8,128)S(1)} %get-tuple-element.900, f32[8,8]{1,0:T(8,128)S(1)} %get-tuple-element.1013, f32[576,576,8]{1,0,2:T(8,128)} %convolution_bitcast_fusion.17), kind=kOutput, calls=%fused_computation.127.clone.1 | convolution fusion | flops 265416192 | bytes 31906048 | tf_op jit(solution)/shard_map/while/body/eval_jaxpr/transpose(jvp(gh,nhqk->ngqk))/dot_general | solution.py:132
  1124.1 18.5 convert_bitcast_fusion.8
  1142.7 9.9 exponential_multiply_fusion.16
  1152.5 30.1 %fusion.659 = f32[2,8,8]{2,1,0:T(8,128)S(1)} fusion(f32[2,8,8]{2,1,0:T(8,128)S(1)} %get-tuple-element.997, s32[]{:T(128)S(6)} %copy.528, f32[8,576,576]{2,1,0:T(8,128)} %copy-done.2, f32[576,576,8]{1,2,0:T(8,128)} %exponential_multiply_fusion.16), kind=kOutput, calls=%fused_computation.165.clone.2 | convolution fusion | flops 254803968 | bytes 21237764 | tf_op jit(solution)/shard_map/while/body/eval_jaxpr/transpose(jvp(gh,nhqk->ngqk))/dot_general | solution.py:130
  1182.6 13.6 convert_bitcast_fusion.7
  1220.8 6.1 multiply_reduce_fusion.7
  1277.5 20.8 %dynamic-update-slice.10 = f32[1774848]{0:T(1024)} dynamic-update-slice(f32[1774848]{0:T(1024)} %constant_dynamic-update-slice_fusion.22, f32[294912]{0:T(1024)} %reshape.1005, s32[]{} %constant.536) | dynamic-update-slice | bytes 2359300
  1312.2 21.1 %dynamic-update-slice.19 = f32[1774848]{0:T(1024)} dynamic-update-slice(f32[1774848]{0:T(1024)} %add_dynamic-update-slice_fusion, f32[589824]{0:T(1024)} %reshape.1008, s32[]{} %constant.545) | dynamic-update-slice | bytes 4718596
  1335.9 6.2 pad.19
  1395.8 68.0 %concatenate.47 = f32[1774976]{0:T(1024)} concatenate(f32[384]{0:T(512)} %add.805, f32[384]{0:T(512)} %add.806, f32[442368]{0:T(1024)S(1)} %copy-done.53, f32[768]{0:T(1024)S(1)} %maximum_add_fusion, f32[64]{0:T(128)} %add.810, f32[64]{0:T(128)} %add.812, f32[147456]{0:T(1024)} %reshape.1001, f32[384]{0:T(512)} %add.814, f32[384]{0:T(512)S(1)} %add.815, f32[384]{0:T(512)} %add.816, ...), dimensions={0} | concatenate | bytes 14199808 | tf_op jit(solution)/shard_map/concatenate | solution.py:125
  1482.3 341.4 %all-reduce.11.cloned.1.call-done = (f32[1777664]{0:T(1024)}, f32[1777664]{0:T(1024)}, f32[1777664]{0:T(1024)}) async-done(((f32[1777664]{0:T(1024)}, f32[1777664]{0:T(1024)}, f32[1777664]{0:T(1024)}), (f32[1777664]{0:T(1024)}, f32[1777664]{0:T(1024)}, f32[1777664]{0:T(1024)})) %all-reduce.11.cloned.1.call-update) | async-done | bytes 21331984
  1832.1 7.3 fusion.223
  1839.4 7.6 fusion.224
  1847.0 38.7 %all-reduce.7 = (f32[]{:T(128)}, f32[3,16]{1,0:T(4,128)}, f32[3,16]{1,0:T(4,128)}) all-reduce(f32[]{:T(128)S(6)} %add.785, f32[3,16]{1,0:T(4,128)S(1)} %bitcast.858, f32[3,16]{1,0:T(4,128)S(1)} %bitcast.857), channel_id=1, replica_groups=mesh['dp'=8,'fsdp'=4] {'dp','fsdp'}, use_global_device_ids=true, to_apply=%region_44.45 | all-reduce | flops 97 | bytes 776 | tf_op jit(solution)/shard_map/psum | solution.py:454
  (1112 shorter events, 603.3 us)
Async XLA Ops:
  7.2 613.9 %copy-start = (bf16[2,576,768]{2,1,0:T(8,128)(2,1)S(1)}, bf16[2,576,768]{2,1,0:T(8,128)(2,1)}, u32[]{:S(2)}) copy-start(bf16[2,576,768]{2,1,0:T(8,128)(2,1)} %param.28) | copy-start | bytes 5308420
  7.2 79.9 %all-gather.11.cloned.1.call-start = ((), (), s32[]{:S(2)}) async-start(), calls=%async_computation.2 | async-start | bytes 7332864 | tf_op jit(solution)/shard_map/all_gather | solution.py:379
  10.0 151.8 %all-gather.7.cloned.1.call-start = ((), (), s32[]{:S(2)}) async-start(), calls=%async_computation | async-start | bytes 7332864 | tf_op jit(solution)/shard_map/all_gather | solution.py:379
  10.8 225.9 %all-gather.9.cloned.1.call-start = ((), (), s32[]{:S(2)}) async-start(), calls=%async_computation.1 | async-start | bytes 7332864 | tf_op jit(solution)/shard_map/all_gather | solution.py:379
  11.5 1812.2 %all-reduce.11.cloned.1.call-start = ((), (), s32[]{:S(2)}) async-start(), calls=%async_computation.3 | async-start | bytes 42663936
  63.1 391.9 %copy-start.259 = (f32[4]{0:T(128)}, f32[4]{0:T(128)S(1)}, u32[]{:S(2)}) copy-start(f32[4]{0:T(128)S(1)} %get-tuple-element.663) | copy-start | bytes 52
  63.2 391.9 %copy-start.260 = (f32[4]{0:T(128)}, f32[4]{0:T(128)S(1)}, u32[]{:S(2)}) copy-start(f32[4]{0:T(128)S(1)} %get-tuple-element.664) | copy-start | bytes 52
  169.8 329.1 %copy-start.44 = (bf16[384,384,1]{1,0,2:T(8,128)(2,1)}, bf16[384,384,1]{1,0,2:T(8,128)(2,1)S(1)}, u32[]{:S(2)}) copy-start(bf16[384,384,1]{1,0,2:T(8,128)(2,1)S(1)} %reshape.1113) | copy-start | bytes 884740
  293.4 159.6 %copy-start.128 = (f32[384]{0:T(512)}, f32[384]{0:T(512)S(1)}, u32[]{:S(2)}) copy-start(f32[384]{0:T(512)S(1)} %get-tuple-element.353) | copy-start | bytes 4612
  293.4 321.2 %copy-start.120 = (f32[384]{0:T(512)}, f32[384]{0:T(512)S(1)}, u32[]{:S(2)}) copy-start(f32[384]{0:T(512)S(1)} %get-tuple-element.350) | copy-start | bytes 4612
  293.4 321.2 %copy-start.155 = (f32[384]{0:T(512)}, f32[384]{0:T(512)S(1)}, u32[]{:S(2)}) copy-start(f32[384]{0:T(512)S(1)} %get-tuple-element.351) | copy-start | bytes 4612
  295.9 49.2 %copy-start.13 = (f32[4,196,384]{2,1,0:T(8,128)}, f32[4,196,384]{2,1,0:T(8,128)S(1)}, u32[]{:S(2)}) copy-start(f32[4,196,384]{2,1,0:T(8,128)S(1)} %get-tuple-element.620) | copy-start | bytes 3612676
  295.9 313.8 %copy-start.123 = (f32[4,196]{1,0:T(4,128)}, f32[4,196]{1,0:T(4,128)S(1)}, u32[]{:S(2)}) copy-start(f32[4,196]{1,0:T(4,128)S(1)} %broadcast_multiply_fusion.8) | copy-start | bytes 9412
  301.3 43.8 %copy-start.175 = (f32[384]{0:T(512)}, f32[384]{0:T(512)S(1)}, u32[]{:S(2)}) copy-start(f32[384]{0:T(512)S(1)} %get-tuple-element.370) | copy-start | bytes 4612
  301.3 63.1 %copy-start.219 = (f32[384]{0:T(512)}, f32[384]{0:T(512)S(1)}, u32[]{:S(2)}) copy-start(f32[384]{0:T(512)S(1)} %get-tuple-element.374) | copy-start | bytes 4612
  301.3 178.1 %copy-start.198 = (f32[384]{0:T(512)}, f32[384]{0:T(512)S(1)}, u32[]{:S(2)}) copy-start(f32[384]{0:T(512)S(1)} %get-tuple-element.367) | copy-start | bytes 4612
  301.3 189.7 %copy-start.132 = (f32[384]{0:T(512)}, f32[384]{0:T(512)S(1)}, u32[]{:S(2)}) copy-start(f32[384]{0:T(512)S(1)} %get-tuple-element.368) | copy-start | bytes 4612
  301.3 194.0 %copy-start.106 = (f32[384]{0:T(512)}, f32[384]{0:T(512)S(1)}, u32[]{:S(2)}) copy-start(f32[384]{0:T(512)S(1)} %get-tuple-element.369) | copy-start | bytes 4612
  301.3 195.7 %copy-start.152 = (f32[384]{0:T(512)}, f32[384]{0:T(512)S(1)}, u32[]{:S(2)}) copy-start(f32[384]{0:T(512)S(1)} %get-tuple-element.373) | copy-start | bytes 4612
  301.4 321.5 %copy-start.148 = (f32[384]{0:T(512)}, f32[384]{0:T(512)S(1)}, u32[]{:S(2)}) copy-start(f32[384]{0:T(512)S(1)} %get-tuple-element.372) | copy-start | bytes 4612
  349.2 134.2 %copy-start.143 = (f32[1536]{0:T(1024)}, f32[1536]{0:T(1024)S(1)}, u32[]{:S(2)}) copy-start(f32[1536]{0:T(1024)S(1)} %fusion.317) | copy-start | bytes 18436
  368.5 80.5 %copy-start.195 = (f32[384]{0:T(512)}, f32[384]{0:T(512)S(1)}, u32[]{:S(2)}) copy-start(f32[384]{0:T(512)S(1)} %get-tuple-element.357) | copy-start | bytes 4612
  368.5 84.5 %copy-start.194 = (f32[384]{0:T(512)}, f32[384]{0:T(512)S(1)}, u32[]{:S(2)}) copy-start(f32[384]{0:T(512)S(1)} %get-tuple-element.362) | copy-start | bytes 4612
  368.5 89.8 %copy-start.146 = (f32[384]{0:T(512)}, f32[384]{0:T(512)S(1)}, u32[]{:S(2)}) copy-start(f32[384]{0:T(512)S(1)} %get-tuple-element.354) | copy-start | bytes 4612
  368.5 92.9 %copy-start.130 = (f32[384]{0:T(512)}, f32[384]{0:T(512)S(1)}, u32[]{:S(2)}) copy-start(f32[384]{0:T(512)S(1)} %get-tuple-element.361) | copy-start | bytes 4612
  368.6 109.8 %copy-start.115 = (f32[384]{0:T(512)}, f32[384]{0:T(512)S(1)}, u32[]{:S(2)}) copy-start(f32[384]{0:T(512)S(1)} %get-tuple-element.360) | copy-start | bytes 4612
  368.6 247.8 %copy-start.125 = (f32[384]{0:T(512)}, f32[384]{0:T(512)S(1)}, u32[]{:S(2)}) copy-start(f32[384]{0:T(512)S(1)} %get-tuple-element.356) | copy-start | bytes 4612
  368.6 247.8 %copy-start.192 = (f32[384]{0:T(512)}, f32[384]{0:T(512)S(1)}, u32[]{:S(2)}) copy-start(f32[384]{0:T(512)S(1)} %get-tuple-element.355) | copy-start | bytes 4612
  370.9 68.6 %copy-start.265 = (f32[768]{0:T(1024)}, f32[768]{0:T(1024)S(1)}, u32[]{:S(2)}) copy-start(f32[768]{0:T(1024)S(1)} %pad_convert_fusion) | copy-start | bytes 9220
  501.6 108.1 %copy-start.14 = (f32[4,196,384]{2,1,0:T(8,128)S(1)}, f32[4,196,384]{2,1,0:T(8,128)}, u32[]{:S(2)}) copy-start(f32[4,196,384]{2,1,0:T(8,128)} %copy-done.13) | copy-start | bytes 3612676
  635.4 92.1 %copy-start.153 = (f32[384]{0:T(512)S(1)}, f32[384]{0:T(512)}, u32[]{:S(2)}) copy-start(f32[384]{0:T(512)} %copy-done.152) | copy-start | bytes 4612
  635.4 92.1 %copy-start.176 = (f32[384]{0:T(512)S(1)}, f32[384]{0:T(512)}, u32[]{:S(2)}) copy-start(f32[384]{0:T(512)} %copy-done.175) | copy-start | bytes 4612
  731.8 106.7 %copy-start.104 = (f32[2,576]{1,0:T(2,128)}, f32[2,576]{1,0:T(2,128)S(1)}, u32[]{:S(2)}) copy-start(f32[2,576]{1,0:T(2,128)S(1)} %broadcast_multiply_fusion.4) | copy-start | bytes 13828
  911.3 50.2 %slice-start = ((s8[11796480]{0:T(1024)(128)(4,1)}), s8[4194304]{0:T(1024)(128)(4,1)S(1)}, s32[]{:S(2)}) async-start(s8[11796480]{0:T(1024)(128)(4,1)} %bitcast.814), calls=%async_computation.4 | async-start | bytes 8388608 | tf_op jit(solution)/shard_map/while
  911.3 50.2 %slice-start.1 = ((s8[11796480]{0:T(1024)(128)(4,1)}), s8[3407872]{0:T(1024)(128)(4,1)S(1)}, s32[]{:S(2)}) async-start(s8[11796480]{0:T(1024)(128)(4,1)} %bitcast.814), calls=%async_computation.5 | async-start | bytes 6815744 | tf_op jit(solution)/shard_map/while
  1092.4 50.2 %slice-start = ((s8[11796480]{0:T(1024)(128)(4,1)}), s8[4194304]{0:T(1024)(128)(4,1)S(1)}, s32[]{:S(2)}) async-start(s8[11796480]{0:T(1024)(128)(4,1)} %bitcast.814), calls=%async_computation.4 | async-start | bytes 8388608 | tf_op jit(solution)/shard_map/while
  1092.4 50.2 %slice-start.1 = ((s8[11796480]{0:T(1024)(128)(4,1)}), s8[3407872]{0:T(1024)(128)(4,1)S(1)}, s32[]{:S(2)}) async-start(s8[11796480]{0:T(1024)(128)(4,1)} %bitcast.814), calls=%async_computation.5 | async-start | bytes 6815744 | tf_op jit(solution)/shard_map/while
  1270.9 27.5 %copy-start.226 = (f32[384]{0:T(512)S(1)}, f32[384]{0:T(512)}, u32[]{:S(2)}) copy-start(f32[384]{0:T(512)} %convert_reduce_fusion.7) | copy-start | bytes 4612
  1270.9 27.5 %copy-start.234 = (f32[384]{0:T(512)S(1)}, f32[384]{0:T(512)}, u32[]{:S(2)}) copy-start(f32[384]{0:T(512)} %convert_reduce_fusion.2) | copy-start | bytes 4612
  1276.2 25.6 %copy-start.248 = (f32[384]{0:T(512)S(1)}, f32[384]{0:T(512)}, u32[]{:S(2)}) copy-start(f32[384]{0:T(512)} %get-tuple-element.543) | copy-start | bytes 4612
  1276.2 26.9 %copy-start.215 = (f32[2,384]{1,0:T(2,128)S(1)}, f32[2,384]{1,0:T(2,128)}, u32[]{:S(2)}) copy-start(f32[2,384]{1,0:T(2,128)} %get-tuple-element.641) | copy-start | bytes 9220
  1276.2 26.9 %copy-start.216 = (f32[2,1,384]{2,1,0:T(1,128)S(1)}, f32[2,1,384]{2,1,0:T(1,128)}, u32[]{:S(2)}) copy-start(f32[2,1,384]{2,1,0:T(1,128)} %slice.480) | copy-start | bytes 9220
  1276.2 26.9 %copy-start.217 = (f32[2,384]{1,0:T(2,128)S(1)}, f32[2,384]{1,0:T(2,128)}, u32[]{:S(2)}) copy-start(f32[2,384]{1,0:T(2,128)} %get-tuple-element.545) | copy-start | bytes 9220
  1277.5 27.5 %copy-start.225 = (f32[384]{0:T(512)S(1)}, f32[384]{0:T(512)}, u32[]{:S(2)}) copy-start(f32[384]{0:T(512)} %get-tuple-element.417) | copy-start | bytes 4612
  1277.5 27.5 %copy-start.232 = (f32[384]{0:T(512)S(1)}, f32[384]{0:T(512)}, u32[]{:S(2)}) copy-start(f32[384]{0:T(512)} %get-tuple-element.427) | copy-start | bytes 4612
  1277.5 28.8 %copy-start.224 = (f32[384]{0:T(512)S(1)}, f32[384]{0:T(512)}, u32[]{:S(2)}) copy-start(f32[384]{0:T(512)} %get-tuple-element.426) | copy-start | bytes 4612
  1277.5 28.8 %copy-start.231 = (f32[384]{0:T(512)S(1)}, f32[384]{0:T(512)}, u32[]{:S(2)}) copy-start(f32[384]{0:T(512)} %get-tuple-element.432) | copy-start | bytes 4612
  1475.6 351.8 %copy-start.43 = (f32[3,55552]{1,0:T(4,128)S(1)}, f32[3,55552]{1,0:T(4,128)}, u32[]{:S(2)}) copy-start(f32[3,55552]{1,0:T(4,128)} %param.24) | copy-start | bytes 1999876
  (275 other events, 1265.9 us)
Sparse Core Ops, SparseCore 0:
  11.5 75.5 all-gather.10
  90.6 71.2 all-gather.6
  165.3 71.2 all-gather.8
  1475.7 347.9 all-reduce.10
where the time goes:
time: 1920 us; the launch traced here: 1900 us
  matrix products  703 us (37%)
  waiting for transfers between devices  494 us (26%)
  local copies, waits for them, and re-layouts  404 us (21%)
  other arithmetic  177 us (9%)
  blocking collectives  81.3 us (4%)
  between operations  22.2 us (1%)
    unnamed x5, waiting for transfers between devices  343 us
    dot_general x24, matrix products, mixing(): return jnp.einsum('gh,nhqk->ngqk', mix_post, probs, precision=highest)  227 us
    dot_general x24, matrix products, mixing(): mixed = jnp.einsum('gh,nhqk->ngqk', mix_pre, scores, precision=highest)  216 us
    all_gather x3, waiting for transfers between devices, on_device(): lax.all_gather(copies[index], ('dp', 'fsdp'), axis=0, tiled=True)  152 us
    slice x10, local copies, waits for them, and re-layouts, unpack(): pieces.append(packed[start:start + count].reshape(shape))  126 us
    unnamed x554, local copies, waits for them, and re-layouts  69.9 us
    concatenate x1, local copies, waits for them, and re-layouts, flatten(): joined = jnp.concatenate([piece.reshape(-1) for piece in pieces])  68 us
    dot_general x22, matrix products, outer_sum(): jnp.einsum('...i,...j->ij', left, right, preferred_element_type=jnp.float32)  54.2 us
  transfers between devices with their start and end apart: 4, of which 4 were waited for; matrix products, arithmetic and copies ran while one was open for 2% of the time, Pallas kernels for 0%

commit v1 on v0

v1 whole, which is shorter than its diff:
```python
import functools

import jax
import jax.numpy as jnp
import numpy as np
from jax import lax
from jax.experimental import pallas as pl
from jax.experimental.pallas import tpu as pltpu
from jax.sharding import PartitionSpec as P

D = 384
HEADS = 8
WIDTH = D // HEADS
FF = 1536
CLASSES = 1000
CLASS_PAD = 1024
PATCH_IN = 768
GRID_SMALL = 14
GRID_LARGE = 24
LANES = 128
SEGMENTS = 16

LOG2E = 1.4426950408889634
SCALE = WIDTH**-0.5
NEG = -1e30
smooth = 0.1
beta_one = 0.9
beta_two = 0.999
adam_eps = 1e-06
decay_rate = 0.01
learn_rate = 0.3
norm_eps = 1e-06

f32 = jnp.float32
bf16 = jnp.bfloat16
AXES = ("dp", "fsdp")
VMEM_BYTES = 60 << 20


def shapes_of():
    dim = D
    tail = [(dim,), (dim,), (dim, FF), (FF,), (FF, dim), (dim,), (dim,)]
    stem = [
        (PATCH_IN, dim),
        (dim,),
        (GRID_SMALL * GRID_SMALL, dim),
        (dim,),
        (dim,),
        (dim,),
        (dim, CLASSES),
        (CLASSES,),
    ]
    selfb = [
        (dim,),
        (dim,),
        (dim, 3 * dim),
        (2 * dim,),
        (HEADS, HEADS),
        (HEADS, HEADS),
        (dim, dim),
        (dim,),
        (dim,),
    ] + tail
    classb = [
        (dim,),
        (dim,),
        (dim, dim),
        (dim,),
        (dim, 2 * dim),
        (dim,),
        (dim, dim),
        (dim,),
        (dim,),
    ] + tail
    return [stem, selfb, classb]


def segment_bounds():
    starts = np.zeros((3, SEGMENTS), np.int32)
    ends = np.zeros((3, SEGMENTS), np.int32)
    real = np.zeros((3, SEGMENTS), np.float32)
    for group, shapes in enumerate(shapes_of()):
        offset = 0
        for number, shape in enumerate(shapes):
            count = int(np.prod(shape))
            starts[group, number] = offset
            ends[group, number] = offset + count
            real[group, number] = 1.0
            offset += count
    return starts, ends, real


STARTS, ENDS, REAL = segment_bounds()


def row_of(group, number):
    return int(STARTS[group, number]) // LANES


def rows_used(group):
    return -(-int(ENDS[group].max()) // LANES)


def resize_table():
    rows = np.arange(GRID_LARGE).astype(np.float32) * np.float32((GRID_SMALL - 1) / (GRID_LARGE - 1))
    cols = np.arange(GRID_SMALL).astype(np.float32)
    line = np.maximum(np.float32(0.0), np.float32(1.0) - np.abs(rows[:, None] - cols[None, :]))
    return (line[:, None, :, None] * line[None, :, None, :]).reshape(GRID_LARGE**2, GRID_SMALL**2)


def nn(a, b):
    return lax.dot_general(a, b, (((1,), (0,)), ((), ())), preferred_element_type=f32)


def nt(a, b):
    return lax.dot_general(a, b, (((1,), (1,)), ((), ())), preferred_element_type=f32)


def tn(a, b):
    return lax.dot_general(a, b, (((0,), (0,)), ((), ())), preferred_element_type=f32)


def colsum(value):
    return jnp.sum(value, 0, keepdims=True)


def split(value):
    high = value.astype(bf16)
    return high, (value - high.astype(f32)).astype(bf16)


def stats(value):
    centred = value - jnp.mean(value, -1, keepdims=True)
    inverse = lax.rsqrt(jnp.mean(centred * centred, -1, keepdims=True) + 1e-06)
    return centred * inverse, inverse


def norm_back(d_out, unit, inverse, gain):
    inner = d_out * gain
    first = jnp.mean(inner, -1, keepdims=True)
    second = jnp.mean(inner * unit, -1, keepdims=True)
    return inverse * (inner - first - unit * second)


def gelu_pair(upper):
    cdf = 0.5 * (1.0 + lax.erf(upper * (0.5**0.5)))
    density = jnp.exp(-0.5 * upper * upper) * 0.3989422804014327
    return upper * cdf, cdf + upper * density


def head_mask(rows):
    lane = lax.broadcasted_iota(jnp.int32, (rows, D), 1)
    row = lax.broadcasted_iota(jnp.int32, (rows, D), 0)
    return (lane // WIDTH) == lax.rem(row, HEADS)


VM = pl.BlockSpec(memory_space=pltpu.VMEM)
SM = pl.BlockSpec(memory_space=pltpu.SMEM)


def params(**kw):
    return pltpu.CompilerParams(vmem_limit_bytes=VMEM_BYTES, **kw)


def sds(shape, dtype):
    return jax.ShapeDtypeStruct(shape, dtype)


def log2(n):
    return n.bit_length() - 1


def exchange(value, bit, z_bits):
    if bit < z_bits:
        n = lax.axis_size("fsdp")
        return lax.ppermute(value, "fsdp", [(i, i ^ (1 << bit)) for i in range(n)])
    n = lax.axis_size("dp")
    return lax.ppermute(value, "dp", [(i, i ^ (1 << (bit - z_bits))) for i in range(n)])


def gather_pieces(state, order, z_bits):
    merged = False
    for bit in order:
        if bit >= z_bits and not merged:
            state = merge(state)
            merged = True
        state = state + [(exchange(a, bit, z_bits), [r | (1 << bit) for r in rel]) for a, rel in state]
        if bit < z_bits:
            state = merge(state)
            merged = True
    return state


def merge(state):
    if len(state) == 1:
        return state
    return [(jnp.concatenate([a for a, _ in state], 0), [r for _, rel in state for r in rel])]


def put_matrix(flat, row, out_ref, rows, cols):
    step = cols // LANES
    for j in range(step):
        out_ref[:, LANES * j : LANES * (j + 1)] = flat[pl.ds(row + j, rows, stride=step), :].astype(bf16)


def put_row(flat, row, out_ref, at, cols):
    for j in range(cols // LANES):
        out_ref[at : at + 1, LANES * j : LANES * (j + 1)] = flat[row + j : row + j + 1, :]


def fill_flat(me, piece_refs, rels, rows, flat):
    for ref, rel in zip(piece_refs, rels):
        for k, r in enumerate(rel):
            flat[pl.ds(rows * jnp.bitwise_xor(me, r), rows), :] = ref[k, 0:rows, :].astype(f32)


def unpack_stem_kernel(rels, rows, me_ref, resize_ref, *refs):
    n = len(rels)
    pieces, (patch_w, vec, pos_small, pos_large, head_w, head_b), (flat, tiles) = refs[:n], refs[n : n + 6], refs[n + 6 :]
    fill_flat(me_ref[0], pieces, rels, rows, flat)
    put_matrix(flat, row_of(0, 0), patch_w, PATCH_IN, D)
    vec[...] = jnp.zeros_like(vec)
    for at, number in enumerate((1, 3, 4, 5)):
        put_row(flat, row_of(0, number), vec, at, D)
    bias = vec[0:1, :]
    small = GRID_SMALL**2
    pos_small[...] = jnp.zeros_like(pos_small)
    for j in range(D // LANES):
        pos_small[0:small, LANES * j : LANES * (j + 1)] = flat[pl.ds(row_of(0, 2) + j, small, stride=D // LANES), :]
    pos_large[...] = (
        lax.dot_general(
            resize_ref[...], pos_small[...], (((1,), (0,)), ((), ())),
            preferred_element_type=f32, precision=lax.Precision.HIGHEST,
        )
        + bias
    )
    pos_small[...] += bias
    lane = lax.broadcasted_iota(jnp.int32, (24, LANES), 1)
    base = row_of(0, 6)
    for rho in range(16):
        first, shift = (CLASSES * rho) // LANES, (CLASSES * rho) % LANES
        parts = [flat[pl.ds(base + first + t, 24, stride=125), :] for t in range(9)]
        if shift:
            parts = [pltpu.roll(p, LANES - shift, 1) for p in parts]
        for t in range(8):
            value = jnp.where(lane < LANES - shift, parts[t], parts[t + 1]) if shift else parts[t]
            if t == 7:
                value = jnp.where(lane < CLASSES - 7 * LANES, value, 0.0)
            tiles[t, pl.ds(rho, 24, stride=16), :] = value
    for t in range(8):
        head_w[:, LANES * t : LANES * (t + 1)] = tiles[t].astype(bf16)
    put_row(flat, row_of(0, 7), head_b, 0, CLASS_PAD)


def unpack_stem(me, pieces, rels, rows, count, padded):
    resize = np.zeros((GRID_LARGE**2, padded), np.float32)
    resize[:, : GRID_SMALL**2] = resize_table()
    return pl.pallas_call(
        functools.partial(unpack_stem_kernel, rels, rows),
        out_shape=[
            sds((PATCH_IN, D), bf16),
            sds((8, D), f32),
            sds((padded, D), f32),
            sds((GRID_LARGE**2, D), f32),
            sds((D, CLASS_PAD), bf16),
            sds((1, CLASS_PAD), f32),
        ],
        in_specs=[SM] + [VM] * (1 + len(pieces)),
        out_specs=[VM] * 6,
        scratch_shapes=[pltpu.VMEM((count * rows, LANES), f32), pltpu.VMEM((8, D, LANES), f32)],
        compiler_params=params(),
        name="unpack_stem",
    )(me, jnp.asarray(resize), *pieces)


SG1, SB1, SBQ, SBV, SBO, SLS1, SG2, SB2, SC2, SLS2 = range(10)
CG1, CB1, CBQ, CBV, CBO, CLS1, CG2, CB2, CC2, CLS2 = range(10)


def unpack_self_kernel(rels, rows, me_ref, *refs):
    n = len(rels)
    pieces = refs[:n]
    wqkv, wo, w1, w2, vec, c1, pre_col, post_col, pre_row, post_row, flat = refs[n:]
    fill_flat(me_ref[0], pieces, rels, rows, flat)
    put_matrix(flat, row_of(1, 2), wqkv, D, 3 * D)
    put_matrix(flat, row_of(1, 6), wo, D, D)
    put_matrix(flat, row_of(1, 11), w1, D, FF)
    put_matrix(flat, row_of(1, 13), w2, FF, D)
    vec[...] = jnp.zeros_like(vec)
    bq = row_of(1, 3)
    for at, row in (
        (SG1, row_of(1, 0)), (SB1, row_of(1, 1)), (SBQ, bq), (SBV, bq + D // LANES), (SBO, row_of(1, 7)),
        (SLS1, row_of(1, 8)), (SG2, row_of(1, 9)), (SB2, row_of(1, 10)), (SC2, row_of(1, 14)), (SLS2, row_of(1, 15)),
    ):
        put_row(flat, row, vec, at, D)
    put_row(flat, row_of(1, 12), c1, 0, FF)
    mix = jnp.broadcast_to(flat[row_of(1, 4) : row_of(1, 4) + 1, :], (HEADS, LANES))
    lane = lax.broadcasted_iota(jnp.int32, (HEADS, LANES), 1)
    row = lax.broadcasted_iota(jnp.int32, (HEADS, LANES), 0)
    pick_pre = jnp.where((lane < 64) & (lane // HEADS == row), mix, 0.0)
    pick_post = jnp.where((lane >= 64) & (lane % HEADS == row), mix, 0.0)
    table_lane = lax.broadcasted_iota(jnp.int32, (LANES, D), 0)
    table_col = lax.broadcasted_iota(jnp.int32, (LANES, D), 1) // WIDTH
    spread_pre = jnp.where(table_lane % HEADS == table_col, 1.0, 0.0).astype(bf16)
    spread_post = jnp.where((table_lane - 64) // HEADS == table_col, 1.0, 0.0).astype(bf16)
    factor = SCALE * LOG2E
    pre_row[...] = nn(pick_pre.astype(bf16), spread_pre) * factor
    post_row[...] = nn(pick_post.astype(bf16), spread_post)
    pre_all = lax.dot_general(
        spread_pre, pick_pre.astype(bf16), (((0,), (1,)), ((), ())), preferred_element_type=f32
    )
    post_all = lax.dot_general(
        spread_post, pick_post.astype(bf16), (((0,), (1,)), ((), ())), preferred_element_type=f32
    )
    pre_col[...] = pre_all * factor
    post_col[...] = post_all


def unpack_self(me, pieces, rels, rows, count):
    return pl.pallas_call(
        functools.partial(unpack_self_kernel, rels, rows),
        out_shape=[
            sds((D, 3 * D), bf16),
            sds((D, D), bf16),
            sds((D, FF), bf16),
            sds((FF, D), bf16),
            sds((16, D), f32),
            sds((1, FF), f32),
            sds((D, HEADS), f32),
            sds((D, HEADS), f32),
            sds((HEADS, D), f32),
            sds((HEADS, D), f32),
        ],
        in_specs=[SM] + [VM] * len(pieces),
        out_specs=[VM] * 10,
        scratch_shapes=[pltpu.VMEM((count * rows, LANES), f32)],
        compiler_params=params(),
        name="unpack_self",
    )(me, *pieces)


def unpack_class_kernel(rels, rows, me_ref, *refs):
    n = len(rels)
    pieces = refs[:n]
    wq, wkv, wo, w1, w2, vec, c1, total, flat = refs[n:]
    fill_flat(me_ref[0], pieces, rels, rows, flat)
    put_matrix(flat, row_of(2, 2), wq, D, D)
    put_matrix(flat, row_of(2, 4), wkv, D, 2 * D)
    put_matrix(flat, row_of(2, 6), wo, D, D)
    put_matrix(flat, row_of(2, 11), w1, D, FF)
    put_matrix(flat, row_of(2, 13), w2, FF, D)
    vec[...] = jnp.zeros_like(vec)
    for at, number in (
        (CG1, 0), (CB1, 1), (CBQ, 3), (CBV, 5), (CBO, 7), (CLS1, 8), (CG2, 9), (CB2, 10), (CC2, 14), (CLS2, 15),
    ):
        put_row(flat, row_of(2, number), vec, at, D)
    put_row(flat, row_of(2, 12), c1, 0, FF)
    count = jnp.zeros((1, LANES), f32)
    for ref, rel in zip(pieces, rels):
        for k in range(len(rel)):
            count = count + ref[k].astype(f32)[rows : rows + 1, :]
    total[...] = count


def unpack_class(me, pieces, rels, rows, count):
    return pl.pallas_call(
        functools.partial(unpack_class_kernel, rels, rows),
        out_shape=[
            sds((D, D), bf16),
            sds((D, 2 * D), bf16),
            sds((D, D), bf16),
            sds((D, FF), bf16),
            sds((FF, D), bf16),
            sds((16, D), f32),
            sds((1, FF), f32),
            sds((1, LANES), f32),
        ],
        in_specs=[SM] + [VM] * len(pieces),
        out_specs=[VM] * 8,
        scratch_shapes=[pltpu.VMEM((count * rows, LANES), f32)],
        compiler_params=params(),
        name="unpack_class",
    )(me, *pieces)


CHUNK = 384


def attend(qkv, lse_at, att_put, valid, pre_col, post_col, scr):
    length = qkv.shape[0]
    q_t, kk, v_t, acc = scr
    q_t[...] = qkv[:, 0:D].astype(f32).T
    kk[:, 0:D] = qkv[:, D : 2 * D]
    kk[:, D:] = qkv[:, D : 2 * D]
    v_t[...] = qkv[:, 2 * D :].astype(f32).T.astype(bf16)
    acc[...] = jnp.zeros_like(acc)
    for g in range(HEADS):
        high, low = split(q_t[...] * pre_col[:, g : g + 1])
        mixed = nn(kk[...], jnp.concatenate([high, low], 0))
        if valid < length:
            mixed = jnp.where(lax.broadcasted_iota(jnp.int32, mixed.shape, 0) < valid, mixed, NEG)
        top = jnp.max(mixed, 0, keepdims=True)
        raw = jnp.exp2(mixed - top)
        weight = colsum(raw)
        lse_at[g : g + 1, :] = top + jnp.log2(weight)
        acc[...] += nn(v_t[...], raw.astype(bf16)) * post_col[:, g : g + 1] * (1.0 / weight)
    att_put(acc[...].T.astype(bf16))


def self_forward_body(tok, lengths, valid, wr, outs, scr):
    wqkv, wo, w1, w2, vec, c1, pre_col, post_col = wr
    qkv_o, lse_o, att_o, branch_o, mid_o, act_o, slope_o, lower_o, out_o = outs
    n, length = qkv_o.shape[0], qkv_o.shape[1]
    rows = n * length
    row = lambda at: vec[at : at + 1, :]
    unit, _ = stats(tok)
    a1 = (unit * row(SG1) + row(SB1)).astype(bf16)
    for part, at in ((0, SBQ), (1, None), (2, SBV)):
        value = nn(a1, wqkv[:, D * part : D * (part + 1)])
        if at is not None:
            value = value + row(at)
        qkv_o[:, :, D * part : D * (part + 1)] = value.astype(bf16).reshape(n, length, D)
    for i in range(n):

        def put(value, i=i):
            att_o[i] = value

        attend(qkv_o.at[i], lse_o.at[i], put, valid, pre_col, post_col, scr)
    att = att_o[...].reshape(rows, D)
    branch = nn(att, wo[...]) + row(SBO)
    branch_o[...] = branch.astype(bf16).reshape(n, length, D)
    mid = tok + row(SLS1) * branch
    mid_o[...] = mid.reshape(n, length, D)
    unit, _ = stats(mid)
    n2 = (unit * row(SG2) + row(SB2)).astype(bf16)
    lower = jnp.broadcast_to(row(SC2), (rows, D))
    for c in range(0, FF, CHUNK):
        upper = nn(n2, w1[:, c : c + CHUNK]) + c1[:, c : c + CHUNK]
        act, slope = gelu_pair(upper)
        act = act.astype(bf16)
        act_o[:, :, c : c + CHUNK] = act.reshape(n, length, CHUNK)
        slope_o[:, :, c : c + CHUNK] = slope.astype(bf16).reshape(n, length, CHUNK)
        lower = lower + nn(act, w2[c : c + CHUNK, :])
    lower_o[...] = lower.astype(bf16).reshape(n, length, D)
    out_o[...] = (mid + row(SLS2) * lower).reshape(n, length, D)


def self_forward_kernel(steps_small, valid, *refs):
    (ps, plg, patch_w, pos_small, pos_large), refs = refs[:5], refs[5:]
    wr, refs = refs[:8], refs[8:]
    out_small, out_large, scr = refs[:10], refs[10:20], refs[20:]
    tok_small, scr_small, scr_large = scr[0], scr[1:5], scr[5:9]
    step = pl.program_id(0)

    @pl.when(step < steps_small)
    def _():
        n, length = out_small[0].shape[0], out_small[0].shape[1]
        for i in range(n):
            tok_small[length * i : length * (i + 1), :] = pos_small[...]
            tok_small[length * i : length * i + valid, :] += nn(ps[i], patch_w[...])
        tok = tok_small[...]
        out_small[0][...] = tok.reshape(n, length, D)
        self_forward_body(tok, None, valid, wr, out_small[1:], scr_small)

    @pl.when(step >= steps_small)
    def _():
        n, length = out_large[0].shape[0], out_large[0].shape[1]
        tok = nn(plg[0], patch_w[...]) + pos_large[...]
        out_large[0][...] = tok.reshape(n, length, D)
        self_forward_body(tok, None, length, wr, out_large[1:], scr_large)


def const_spec(a):
    return pl.BlockSpec(a.shape, lambda i, nd=a.ndim: (0,) * nd, pipeline_mode=pl.Buffered(1))


def pair_of(n):
    return 2 if n % 2 == 0 else 1


def image_specs(pair, steps_small, buffers):
    small = lambda *tail: pl.BlockSpec(
        (pair,) + tail, lambda i: (jnp.minimum(i, steps_small - 1), 0, 0), pipeline_mode=pl.Buffered(buffers)
    )
    large = lambda *tail: pl.BlockSpec((1,) + tail, lambda i: (jnp.maximum(i - steps_small, 0), 0, 0))
    return small, large


SAVED = [(D, f32), (3 * D, bf16), None, (D, bf16), (D, bf16), (D, f32), (FF, bf16), (FF, bf16), (D, bf16), (D, f32)]


def self_forward(ps, plg, stem, selfw, padded):
    ns, valid, _ = ps.shape
    nl, large_len, _ = plg.shape
    pair = pair_of(ns)
    steps_small = ns // pair
    patch_w, _, pos_small, pos_large = stem[:4]
    small, large = image_specs(pair, steps_small, 2)
    shapes, specs = [], []
    for n, length, spec in ((ns, padded, small), (nl, large_len, large)):
        for entry in SAVED:
            tail = (HEADS, length) if entry is None else (length, entry[0])
            shapes.append(sds((n,) + tail, f32 if entry is None else entry[1]))
            specs.append(spec(*tail))
    weights = selfw[:8]
    scratch = [pltpu.VMEM((pair * padded, D), f32)]
    for length in (padded, large_len):
        scratch += [
            pltpu.VMEM((D, length), f32),
            pltpu.VMEM((length, 2 * D), bf16),
            pltpu.VMEM((D, length), bf16),
            pltpu.VMEM((D, length), f32),
        ]
    out = pl.pallas_call(
        functools.partial(self_forward_kernel, steps_small, valid),
        grid=(steps_small + nl,),
        out_shape=shapes,
        in_specs=[small(valid, PATCH_IN), large(large_len, PATCH_IN)]
        + [const_spec(a) for a in (patch_w, pos_small, pos_large, *weights)],
        out_specs=specs,
        scratch_shapes=scratch,
        compiler_params=params(),
        cost_estimate=pl.CostEstimate(flops=60_000_000_000, bytes_accessed=60_000_000, transcendentals=0),
        name="self_forward",
    )(ps, plg, patch_w, pos_small, pos_large, *weights)
    return out[:10], out[10:]


BATCH = 8


def class_kernel(
    ns, nl, valid, out_s, out_l, wq, wkv, wo, w1, w2, vec, c1, svec, head_w, head_b, labels, live,
    d_s, d_l, g_wq, g_wkv, g_wo, g_w1, g_w2, g_vec, g_c1, g_svec, g_head_w, g_head_b, loss_o,
    a_s, a_l, p_s, p_l, z_ref, y_ref, b_ref, ps_ref, pc_ref, da_ref,
):
    row = lambda at: vec[at : at + 1, :]
    mask8 = head_mask(HEADS)
    mask64 = head_mask(HEADS * BATCH)
    cls = svec[1:2, :]
    unit_cls, inv_cls = stats(cls)
    a_cls = (unit_cls * row(CG1) + row(CB1)).astype(bf16)
    a_cls_f = a_cls.astype(f32)
    query = (nn(a_cls, wq[...]) + row(CBQ)).astype(bf16).astype(f32)
    q_diag = jnp.where(mask8, query, 0.0).astype(bf16)
    u_nat = nt(q_diag, wkv[:, 0:D]) * SCALE
    u_hi, u_lo = split(u_nat * LOG2E)
    u16 = jnp.concatenate([u_hi, u_lo], 0)
    s_cls = jnp.sum(u_nat * LOG2E * a_cls_f, -1, keepdims=True)
    z_ref[...] = jnp.zeros_like(z_ref)
    ps_ref[...] = jnp.zeros_like(ps_ref)

    def forward(i, src, a_ref, p_ref, slot):
        unit, _ = stats(src[i])
        a = (unit * row(CG1) + row(CB1)).astype(bf16)
        a_ref[i] = a
        s16 = nt(u16, a)
        s = s16[0:HEADS] + s16[HEADS:]
        keep = valid if a.shape[0] != GRID_LARGE**2 else a.shape[0]
        if keep < a.shape[0]:
            s = jnp.where(lax.broadcasted_iota(jnp.int32, s.shape, 1) < keep, s, NEG)
        top = jnp.maximum(jnp.max(s, -1, keepdims=True), s_cls)
        e = jnp.exp2(s - top)
        e_cls = jnp.exp2(s_cls - top)
        inverse = 1.0 / (jnp.sum(e, -1, keepdims=True) + e_cls)
        p, p_cls = e * inverse, e_cls * inverse
        p_ref[i] = p
        low, low_cls = p.astype(bf16), p_cls.astype(bf16).astype(f32)
        z_ref[pl.ds(slot * HEADS, HEADS), :] = nn(low, a) + low_cls * a_cls_f
        ps_ref[pl.ds(slot * HEADS, HEADS), :] = jnp.sum(low.astype(f32), -1, keepdims=True) + low_cls
        pc_ref[pl.ds(slot * HEADS, HEADS), :] = p_cls

    for i in range(ns):
        forward(i, out_s, a_s, p_s, i)
    for i in range(nl):
        forward(i, out_l, a_l, p_l, ns + i)

    z_hi, z_lo = split(z_ref[...])
    o_all = nn(jnp.concatenate([z_hi, z_lo], 0), wkv[:, D:])
    o_all = o_all[0 : HEADS * BATCH] + o_all[HEADS * BATCH :] + ps_ref[...] * row(CBV)
    att = jnp.sum(jnp.where(mask64, o_all, 0.0).reshape(BATCH, HEADS, D), 1).astype(bf16)
    branch = nn(att, wo[...]) + row(CBO)
    mid = cls + row(CLS1) * branch
    unit_mid, inv_mid = stats(mid)
    n2 = (unit_mid * row(CG2) + row(CB2)).astype(bf16)
    upper = nn(n2, w1[...]) + c1[...]
    act, slope = gelu_pair(upper)
    act = act.astype(bf16)
    lower = nn(act, w2[...]) + row(CC2)
    c_tok = mid + row(CLS2) * lower
    unit_c, inv_c = stats(c_tok)
    final = (unit_c * svec[2:3, :] + svec[3:4, :]).astype(bf16)
    logits = nn(final, head_w[...]) + head_b[...]
    lane = lax.broadcasted_iota(jnp.int32, logits.shape, 1)
    inside = lane < CLASSES
    logits = jnp.where(inside, logits, NEG)
    shifted = logits - jnp.max(logits, -1, keepdims=True)
    raw = jnp.exp(shifted)
    weight = jnp.sum(raw, -1, keepdims=True)
    logp = shifted - jnp.log(weight)
    hit = lane == labels[...]
    picked = jnp.sum(jnp.where(hit, logp, 0.0), -1, keepdims=True)
    mean = jnp.sum(jnp.where(inside, logp, 0.0), -1, keepdims=True) * (1.0 / CLASSES)
    each = -((1.0 - smooth) * picked + smooth * mean)
    scaled = live[...]
    loss_o[...] = jnp.broadcast_to(colsum(scaled * each), loss_o.shape)
    target = jnp.where(hit, 1.0 - smooth, 0.0) + smooth / CLASSES
    d_logits = jnp.where(inside, scaled * (raw / weight - target), 0.0).astype(bf16)

    d_final = nt(d_logits, head_w[...])
    g_head_w[...] = tn(final, d_logits)
    g_head_b[...] = colsum(d_logits.astype(f32))
    g_svec[...] = jnp.zeros_like(g_svec)
    g_svec[2:3, :] = colsum(d_final * unit_c)
    g_svec[3:4, :] = colsum(d_final)
    d_c = norm_back(d_final, unit_c, inv_c, svec[2:3, :])
    g_vec[...] = jnp.zeros_like(g_vec)
    g_vec[CLS2 : CLS2 + 1, :] = colsum(d_c * lower)
    d_lower = (d_c * row(CLS2)).astype(bf16)
    g_vec[CC2 : CC2 + 1, :] = colsum(d_lower.astype(f32))
    g_w2[...] = tn(act, d_lower)
    d_upper = (slope * nt(d_lower, w2[...])).astype(bf16)
    g_c1[...] = colsum(d_upper.astype(f32))
    g_w1[...] = tn(n2, d_upper)
    d_n2 = nt(d_upper, w1[...])
    g_vec[CG2 : CG2 + 1, :] = colsum(d_n2 * unit_mid)
    g_vec[CB2 : CB2 + 1, :] = colsum(d_n2)
    d_mid = d_c + norm_back(d_n2, unit_mid, inv_mid, row(CG2))
    g_vec[CLS1 : CLS1 + 1, :] = colsum(d_mid * branch)
    d_branch = (d_mid * row(CLS1)).astype(bf16)
    g_vec[CBO : CBO + 1, :] = colsum(d_branch.astype(f32))
    g_wo[...] = tn(att, d_branch)
    d_att = nt(d_branch, wo[...]).astype(bf16).astype(f32)
    d_diag = jnp.where(mask64, jnp.broadcast_to(d_att[:, None, :], (BATCH, HEADS, D)).reshape(BATCH * HEADS, D), 0.0)
    g_vec[CBV : CBV + 1, :] = colsum(d_diag * ps_ref[...])
    shift = jnp.sum(d_diag * row(CBV), -1, keepdims=True)
    d_diag_low = d_diag.astype(bf16)
    y_ref[...] = nt(d_diag_low, wkv[:, D:])
    g_wkv[:, D:] = tn(jnp.concatenate([z_hi, z_lo], 0), jnp.concatenate([d_diag_low, d_diag_low], 0))
    z_ref[:, 0:1] = shift
    b_ref[...] = jnp.zeros_like(b_ref)
    da_ref[...] = jnp.zeros_like(da_ref)
    un_hi, un_lo = split(u_nat)

    def backward(i, src, a_ref, p_ref, d_ref, slot):
        unit, inverse = stats(src[i])
        a = a_ref[i]
        here = pl.ds(slot * HEADS, HEADS)
        y = y_ref[here, :]
        y_hi, y_lo = split(y)
        d16 = nt(jnp.concatenate([y_hi, y_lo], 0), a)
        offset = z_ref[here, 0:1]
        d_p = d16[0:HEADS] + d16[HEADS:] + offset
        d_p_cls = jnp.sum(y * a_cls_f, -1, keepdims=True) + offset
        p, p_cls = p_ref[i], pc_ref[here, :]
        delta = jnp.sum(p * d_p, -1, keepdims=True) + p_cls * d_p_cls
        d_score = (p * (d_p - delta)).astype(bf16)
        d_score_cls = (p_cls * (d_p_cls - delta)).astype(bf16).astype(f32)
        low = p.astype(bf16)
        b_ref[...] += nn(d_score, a) + d_score_cls * a_cls_f
        da_ref[...] += d_score_cls * u_nat + p_cls.astype(bf16).astype(f32) * y
        left = jnp.concatenate([d_score.astype(f32), d_score.astype(f32), low.astype(f32), low.astype(f32)], 0)
        d_a = tn(left.astype(bf16), jnp.concatenate([un_hi, un_lo, y_hi, y_lo], 0))
        g_vec[CG1 : CG1 + 1, :] += colsum(d_a * unit)
        g_vec[CB1 : CB1 + 1, :] += colsum(d_a)
        d_ref[i] = norm_back(d_a, unit, inverse, row(CG1))

    for i in range(ns):
        backward(i, out_s, a_s, p_s, d_s, i)
    for i in range(nl):
        backward(i, out_l, a_l, p_l, d_l, ns + i)

    b_hi, b_lo = split(b_ref[...])
    bw = nn(jnp.concatenate([b_hi, b_lo], 0), wkv[:, 0:D])
    bw = bw[0:HEADS] + bw[HEADS:]
    d_query = (colsum(jnp.where(mask8, bw, 0.0)) * SCALE).astype(bf16)
    g_vec[CBQ : CBQ + 1, :] = d_query.astype(f32)
    q_scaled = q_diag.astype(f32) * SCALE
    qs_hi, qs_lo = split(q_scaled)
    g_wkv[:, 0:D] = tn(
        jnp.concatenate([b_hi, b_hi, b_lo, b_lo], 0), jnp.concatenate([qs_hi, qs_lo, qs_hi, qs_lo], 0)
    )
    first = lax.broadcasted_iota(jnp.int32, (16, D), 0) == 0
    spread_a = jnp.where(first, jnp.broadcast_to(a_cls_f, (16, D)), 0.0).astype(bf16)
    spread_q = jnp.where(first, jnp.broadcast_to(d_query.astype(f32), (16, D)), 0.0).astype(bf16)
    g_wq[...] = tn(spread_a, spread_q)
    d_a_cls = colsum(da_ref[...]) + nt(d_query, wq[...])
    g_vec[CG1 : CG1 + 1, :] += d_a_cls * unit_cls
    g_vec[CB1 : CB1 + 1, :] += d_a_cls
    g_svec[1:2, :] = colsum(d_mid) + norm_back(d_a_cls, unit_cls, inv_cls, row(CG1))


def class_block(out_s, out_l, classw, stem, labels, live, valid):
    ns, padded, _ = out_s.shape
    nl, large_len, _ = out_l.shape
    wq, wkv, wo, w1, w2, vec, c1 = classw
    _, svec, _, _, head_w, head_b = stem
    args = (out_s, out_l, wq, wkv, wo, w1, w2, vec, c1, svec, head_w, head_b, labels, live)
    return pl.pallas_call(
        functools.partial(class_kernel, ns, nl, valid),
        out_shape=[
            sds((ns, padded, D), f32),
            sds((nl, large_len, D), f32),
            sds((D, D), f32),
            sds((D, 2 * D), f32),
            sds((D, D), f32),
            sds((D, FF), f32),
            sds((FF, D), f32),
            sds((16, D), f32),
            sds((1, FF), f32),
            sds((8, D), f32),
            sds((D, CLASS_PAD), f32),
            sds((1, CLASS_PAD), f32),
            sds((1, LANES), f32),
        ],
        in_specs=[VM] * len(args),
        out_specs=[VM] * 13,
        scratch_shapes=[
            pltpu.VMEM((ns, padded, D), bf16),
            pltpu.VMEM((nl, large_len, D), bf16),
            pltpu.VMEM((ns, HEADS, padded), f32),
            pltpu.VMEM((nl, HEADS, large_len), f32),
            pltpu.VMEM((BATCH * HEADS, D), f32),
            pltpu.VMEM((BATCH * HEADS, D), f32),
            pltpu.VMEM((HEADS, D), f32),
            pltpu.VMEM((BATCH * HEADS, 1), f32),
            pltpu.VMEM((BATCH * HEADS, 1), f32),
            pltpu.VMEM((HEADS, D), f32),
        ],
        compiler_params=params(),
        cost_estimate=pl.CostEstimate(flops=10_000_000_000, bytes_accessed=60_000_000, transcendentals=0),
        name="class_block",
    )(*args)


def attend_back(qkv, d_att, lse, d_qkv, valid, pre_col, post_col, pre_row, post_row, g_pre, g_post, scr):
    length = qkv.shape[0]
    q_t, kk, k_t, do_t, dq_t, d_k, d_v = scr
    q, k, v = qkv[:, 0:D], qkv[:, D : 2 * D], qkv[:, 2 * D :]
    q_t[...] = q.astype(f32).T
    kk[:, 0:D] = k
    kk[:, D:] = k
    k_t[...] = k.astype(f32).T.astype(bf16)
    do_t[...] = d_att.astype(f32).T
    dq_t[...] = jnp.zeros_like(dq_t)
    d_k[...] = jnp.zeros_like(d_k)
    d_v[...] = jnp.zeros_like(d_v)
    for g in range(HEADS):
        high, low = split(q_t[...] * pre_col[:, g : g + 1])
        mixed = nn(kk[...], jnp.concatenate([high, low], 0))
        d_p = nn(v, (do_t[...] * post_col[:, g : g + 1]).astype(bf16))
        p = jnp.exp2(mixed - lse[g : g + 1, :])
        if valid < length:
            p = jnp.where(lax.broadcasted_iota(jnp.int32, p.shape, 0) < valid, p, 0.0)
        delta = colsum(p * d_p)
        d_mixed = (p * (d_p - delta)).astype(bf16)
        r = nn(p.astype(bf16), d_att)
        t = nn(d_mixed, q)
        u = nn(k_t[...], d_mixed)
        d_v[...] += r * post_row[g : g + 1, :]
        d_k[...] += t * pre_row[g : g + 1, :]
        dq_t[...] += u * pre_col[:, g : g + 1]
        g_post[g : g + 1, :] += colsum(r * v.astype(f32))
        g_pre[g : g + 1, :] += colsum(t * k.astype(f32))
    inverse = 1.0 / LOG2E
    d_qkv[:, 0:D] = (dq_t[...].T * inverse).astype(bf16)
    d_qkv[:, D : 2 * D] = (d_k[...] * inverse).astype(bf16)
    d_qkv[:, 2 * D :] = d_v[...].astype(bf16)


def self_backward_body(d_out, saved, valid, wr, grads, d_qkv, scr):
    wqkv, wo, w1, w2, vec, c1, pre_col, post_col, pre_row, post_row = wr
    g_wqkv, g_wo, g_w1, g_w2, g_vec, g_c1, g_pre, g_post = grads
    tok_r, qkv_r, lse_r, att_r, branch_r, mid_r, act_r, slope_r, lower_r = saved
    n, length = qkv_r.shape[0], qkv_r.shape[1]
    rows = n * length
    row = lambda at: vec[at : at + 1, :]

    def add(at, value):
        g_vec[at : at + 1, :] += value

    flat = lambda ref: ref[...].reshape(rows, D)
    add(SLS2, colsum(d_out * flat(lower_r).astype(f32)))
    d_lower = (d_out * row(SLS2)).astype(bf16)
    add(SC2, colsum(d_lower.astype(f32)))
    unit, inverse = stats(flat(mid_r))
    n2 = (unit * row(SG2) + row(SB2)).astype(bf16)
    d_n2 = None
    for c in range(0, FF, CHUNK):
        d_act = nt(d_lower, w2[c : c + CHUNK, :])
        slope = slope_r[:, :, c : c + CHUNK].reshape(rows, CHUNK).astype(f32)
        d_upper = (d_act * slope).astype(bf16)
        g_w2[c : c + CHUNK, :] += tn(act_r[:, :, c : c + CHUNK].reshape(rows, CHUNK), d_lower)
        g_w1[:, c : c + CHUNK] += tn(n2, d_upper)
        g_c1[:, c : c + CHUNK] += colsum(d_upper.astype(f32))
        part = nt(d_upper, w1[:, c : c + CHUNK])
        d_n2 = part if d_n2 is None else d_n2 + part
    add(SG2, colsum(d_n2 * unit))
    add(SB2, colsum(d_n2))
    d_mid = d_out + norm_back(d_n2, unit, inverse, row(SG2))
    add(SLS1, colsum(d_mid * flat(branch_r).astype(f32)))
    d_branch = (d_mid * row(SLS1)).astype(bf16)
    add(SBO, colsum(d_branch.astype(f32)))
    g_wo[...] += tn(flat(att_r), d_branch)
    d_att = nt(d_branch, wo[...]).astype(bf16)
    for i in range(n):
        attend_back(
            qkv_r.at[i], d_att[length * i : length * (i + 1), :], lse_r.at[i], d_qkv.at[pl.ds(length * i, length)],
            valid, pre_col, post_col, pre_row, post_row, g_pre, g_post, scr,
        )
    add(SBQ, colsum(d_qkv[:, 0:D].astype(f32)))
    add(SBV, colsum(d_qkv[:, 2 * D :].astype(f32)))
    unit, inverse = stats(flat(tok_r))
    a1 = (unit * row(SG1) + row(SB1)).astype(bf16)
    d_a1 = None
    for part in range(3):
        here = slice(D * part, D * (part + 1))
        g_wqkv[:, here] += tn(a1, d_qkv[:, here])
        term = nt(d_qkv[:, here], wqkv[:, here])
        d_a1 = term if d_a1 is None else d_a1 + term
    add(SG1, colsum(d_a1 * unit))
    add(SB1, colsum(d_a1))
    return d_mid + norm_back(d_a1, unit, inverse, row(SG1))


def self_backward_kernel(steps_small, steps, valid, *refs):
    (ps, plg, resize), refs = refs[:3], refs[3:]
    small, large, refs = refs[:10], refs[10:20], refs[20:]
    wr, refs = refs[:10], refs[10:]
    grads, (g_patch_w, g_patch_b, g_pos), refs = refs[:8], refs[8:11], refs[11:]
    pos_large, dq_small, dq_large, scr = refs[0], refs[1], refs[2], refs[3:]
    scr_small, scr_large = scr[:7], scr[7:14]
    step = pl.program_id(0)

    @pl.when(step == 0)
    def _():
        for ref in (*grads, g_patch_w, g_patch_b, g_pos, pos_large):
            ref[...] = jnp.zeros_like(ref)

    @pl.when(step < steps_small)
    def _():
        n, length = small[0].shape[0], small[0].shape[1]
        d_out = small[9][...].reshape(n * length, D)
        d_tok = self_backward_body(d_out, small[:9], valid, wr, grads, dq_small, scr_small)
        g_patch_b[0:1, :] += colsum(d_tok)
        for i in range(n):
            mine = d_tok[length * i : length * (i + 1), :]
            g_pos[...] += mine[0:valid, :]
            g_patch_w[...] += tn(ps[i], mine[0:valid, :].astype(bf16))

    @pl.when(step >= steps_small)
    def _():
        length = large[0].shape[1]
        d_tok = self_backward_body(large[9][0], large[:9], length, wr, grads, dq_large, scr_large)
        g_patch_b[0:1, :] += colsum(d_tok)
        pos_large[...] += d_tok
        g_patch_w[...] += tn(plg[0], d_tok.astype(bf16))

    @pl.when(step == steps - 1)
    def _():
        g_pos[...] += lax.dot_general(
            resize[...], pos_large[...], (((1,), (0,)), ((), ())),
            preferred_element_type=f32, precision=lax.Precision.HIGHEST,
        )


def self_backward(ps, plg, saved_s, saved_l, d_s, d_l, selfw):
    ns, valid, _ = ps.shape
    nl, large_len, _ = plg.shape
    padded = d_s.shape[1]
    pair = pair_of(ns)
    steps_small = ns // pair
    small, large = image_specs(pair, steps_small, 1)
    resize = jnp.asarray(resize_table().T.copy())
    in_specs = [small(valid, PATCH_IN), large(large_len, PATCH_IN), const_spec(resize)]
    for length, spec in ((padded, small), (large_len, large)):
        for entry in SAVED[:9]:
            in_specs.append(spec(*((HEADS, length) if entry is None else (length, entry[0]))))
        in_specs.append(spec(length, D))
    in_specs += [const_spec(a) for a in selfw]
    shapes = [
        sds((D, 3 * D), f32),
        sds((D, D), f32),
        sds((D, FF), f32),
        sds((FF, D), f32),
        sds((16, D), f32),
        sds((1, FF), f32),
        sds((HEADS, D), f32),
        sds((HEADS, D), f32),
        sds((PATCH_IN, D), f32),
        sds((8, D), f32),
        sds((valid, D), f32),
    ]
    scratch = [
        pltpu.VMEM((large_len, D), f32),
        pltpu.VMEM((pair * padded, 3 * D), bf16),
        pltpu.VMEM((large_len, 3 * D), bf16),
    ]
    for length in (padded, large_len):
        scratch += [
            pltpu.VMEM((D, length), f32),
            pltpu.VMEM((length, 2 * D), bf16),
            pltpu.VMEM((D, length), bf16),
            pltpu.VMEM((D, length), f32),
            pltpu.VMEM((D, length), f32),
            pltpu.VMEM((length, D), f32),
            pltpu.VMEM((length, D), f32),
        ]
    return pl.pallas_call(
        functools.partial(self_backward_kernel, steps_small, steps_small + nl, valid),
        grid=(steps_small + nl,),
        out_shape=shapes,
        in_specs=in_specs,
        out_specs=[pl.BlockSpec(s.shape, lambda i: (0, 0), pipeline_mode=pl.Buffered(1)) for s in shapes],
        scratch_shapes=scratch,
        compiler_params=params(),
        cost_estimate=pl.CostEstimate(flops=120_000_000_000, bytes_accessed=60_000_000, transcendentals=0),
        name="self_backward",
    )(ps, plg, resize, *saved_s[:9], d_s, *saved_l[:9], d_l, *selfw)


def take_matrix(flat, row, src, rows, cols):
    step = cols // LANES
    for j in range(step):
        flat[pl.ds(row + j, rows, stride=step), :] = src[:, LANES * j : LANES * (j + 1)]


def take_row(flat, row, src, at, cols):
    for j in range(cols // LANES):
        flat[row + j : row + j + 1, :] = src[at : at + 1, LANES * j : LANES * (j + 1)]


def slots_of(order):
    rels = [0]
    for bit in reversed(order):
        rels = rels + [r | (1 << bit) for r in rels]
    return rels


def emit_slots(me, flat, rows, rels, keep_ref, send_ref):
    half = len(rels) // 2
    for k, r in enumerate(rels):
        value = flat[pl.ds(rows * jnp.bitwise_xor(me, r), rows), :]
        if k < half:
            keep_ref[k] = value
        else:
            send_ref[k - half] = value.astype(bf16)


def pack_class_kernel(rels, rows, me_ref, wq, wkv, wo, w1, w2, vec, c1, keep, send, flat):
    used = rows_used(2)
    flat[used:, :] = jnp.zeros((flat.shape[0] - used, LANES), f32)
    take_matrix(flat, row_of(2, 2), wq, D, D)
    take_matrix(flat, row_of(2, 4), wkv, D, 2 * D)
    take_matrix(flat, row_of(2, 6), wo, D, D)
    take_matrix(flat, row_of(2, 11), w1, D, FF)
    take_matrix(flat, row_of(2, 13), w2, FF, D)
    for at, number in (
        (CG1, 0), (CB1, 1), (CBQ, 3), (CBV, 5), (CBO, 7), (CLS1, 8), (CG2, 9), (CB2, 10), (CC2, 14), (CLS2, 15),
    ):
        take_row(flat, row_of(2, number), vec, at, D)
    take_row(flat, row_of(2, 12), c1, 0, FF)
    emit_slots(me_ref[0], flat, rows, rels, keep, send)


def pack_self_kernel(rels, rows, me_ref, wqkv, wo, w1, w2, vec, c1, pre, post, keep, send, flat):
    used = rows_used(1)
    flat[used:, :] = jnp.zeros((flat.shape[0] - used, LANES), f32)
    take_matrix(flat, row_of(1, 2), wqkv, D, 3 * D)
    take_matrix(flat, row_of(1, 6), wo, D, D)
    take_matrix(flat, row_of(1, 11), w1, D, FF)
    take_matrix(flat, row_of(1, 13), w2, FF, D)
    bq = row_of(1, 3)
    for at, row in (
        (SG1, row_of(1, 0)), (SB1, row_of(1, 1)), (SBQ, bq), (SBV, bq + D // LANES), (SBO, row_of(1, 7)),
        (SLS1, row_of(1, 8)), (SG2, row_of(1, 9)), (SB2, row_of(1, 10)), (SC2, row_of(1, 14)), (SLS2, row_of(1, 15)),
    ):
        take_row(flat, row, vec, at, D)
    take_row(flat, row_of(1, 12), c1, 0, FF)
    table_col = lax.broadcasted_iota(jnp.int32, (D, LANES), 0) // WIDTH
    table_lane = lax.broadcasted_iota(jnp.int32, (D, LANES), 1)
    lane = lax.broadcasted_iota(jnp.int32, (HEADS, LANES), 1)
    row = lax.broadcasted_iota(jnp.int32, (HEADS, LANES), 0)
    exact = lambda a, b: lax.dot_general(
        a, b, (((1,), (0,)), ((), ())), preferred_element_type=f32, precision=lax.Precision.HIGHEST
    )
    sum_pre = exact(pre[...], jnp.where(table_lane % HEADS == table_col, 1.0, 0.0))
    sum_post = exact(post[...], jnp.where((table_lane - 64) // HEADS == table_col, 1.0, 0.0))
    line = colsum(jnp.where((lane < 64) & (lane // HEADS == row), sum_pre * SCALE, 0.0))
    line = line + colsum(jnp.where((lane >= 64) & (lane % HEADS == row), sum_post, 0.0))
    flat[row_of(1, 4) : row_of(1, 4) + 1, :] = line
    emit_slots(me_ref[0], flat, rows, rels, keep, send)


def pack_stem_kernel(
    rels, rows, me_ref, patch_w, patch_b, pos, svec, head_w, head_b, keep, send, flat, tiles
):
    used = row_of(0, 6)
    flat[used:, :] = jnp.zeros((flat.shape[0] - used, LANES), f32)
    take_matrix(flat, row_of(0, 0), patch_w, PATCH_IN, D)
    take_row(flat, row_of(0, 1), patch_b, 0, D)
    take_matrix(flat, row_of(0, 2), pos, GRID_SMALL**2, D)
    for at, number in ((1, 3), (2, 4), (3, 5)):
        take_row(flat, row_of(0, number), svec, at, D)
    for t in range(8):
        tiles[t] = head_w[:, LANES * t : LANES * (t + 1)]
    lane = lax.broadcasted_iota(jnp.int32, (24, LANES), 1)
    base = row_of(0, 6)
    for rho in range(16):
        first, shift = (CLASSES * rho) // LANES, (CLASSES * rho) % LANES
        parts = [tiles[t, pl.ds(rho, 24, stride=16), :] for t in range(8)]
        if shift:
            parts = [pltpu.roll(p, shift, 1) for p in parts]
        for t in range(9 if shift + CLASSES > CLASS_PAD else 8):
            if shift:
                value = jnp.where(lane >= shift, parts[t] if t < 8 else 0.0, parts[t - 1] if t > 0 else 0.0)
            else:
                value = parts[t]
            here = pl.ds(base + first + t, 24, stride=125)
            flat[here, :] = flat[here, :] + value
    take_row(flat, row_of(0, 7), head_b, 0, CLASS_PAD)
    emit_slots(me_ref[0], flat, rows, rels, keep, send)


def pack(kernel, name, me, arrays, rels, rows, extra=()):
    half = len(rels) // 2
    return pl.pallas_call(
        functools.partial(kernel, rels, rows),
        out_shape=[sds((half, rows, LANES), f32), sds((half, rows, LANES), bf16)],
        in_specs=[SM] + [VM] * len(arrays),
        out_specs=[VM] * 2,
        scratch_shapes=[pltpu.VMEM((len(rels) * rows, LANES), f32), *extra],
        compiler_params=params(),
        name=name,
    )(me, *arrays)


def reduce_slots(keep, send, order, z_bits):
    for number, bit in enumerate(order):
        got = exchange(send, bit, z_bits)
        total = keep + got.astype(f32)
        if number == len(order) - 1:
            return total[0]
        half = total.shape[0] // 2
        keep, send = total[:half], total[half:].astype(bf16)


def bounds_of(group, number):
    return int(STARTS[group, number]), int(ENDS[group, number])


def segment_sums(square, position):
    lane = lax.broadcasted_iota(jnp.int32, (3, LANES), 1)
    group = lax.broadcasted_iota(jnp.int32, (3, 1), 0)
    out = jnp.zeros((3, LANES), f32)
    for s in range(SEGMENTS):
        low = pick(group, [int(STARTS[g, s]) for g in range(3)])
        high = pick(group, [int(ENDS[g, s]) for g in range(3)])
        value = jnp.sum(jnp.where((position >= low) & (position < high), square, 0.0), -1, keepdims=True)
        out = jnp.where(lane == s, value, out)
    return out


def pick(group, values):
    return jnp.where(group == 0, values[0], jnp.where(group == 1, values[1], values[2]))


def adam_kernel(rows, me_ref, rate_ref, master, first, second, g0, g1, g2, grad_o, first_o, second_o, update_o, sums_o):
    shard = rows * LANES
    for g, ref in enumerate((g0, g1, g2)):
        grad_o[g : g + 1, :] = ref[...].reshape(1, shard)
    grad = grad_o[...]
    weight = master[...]
    new_first = beta_one * first[...] + (1.0 - beta_one) * grad
    new_second = beta_two * second[...] + (1.0 - beta_two) * grad * grad
    first_o[...] = new_first
    second_o[...] = new_second
    correct_one, correct_two = rate_ref[0], rate_ref[1]
    update = new_first / correct_one / (jnp.sqrt(new_second / correct_two) + adam_eps) + decay_rate * weight
    update_o[...] = update
    position = me_ref[0] * shard + lax.broadcasted_iota(jnp.int32, (3, shard), 1)
    sums_o[0:3, :] = segment_sums(weight * weight, position)
    sums_o[3:6, :] = segment_sums(update * update, position)
    sums_o[6:8, :] = jnp.zeros((2, LANES), f32)


def adam(me, rates, master, first, second, grads, rows):
    shape = master.shape
    return pl.pallas_call(
        functools.partial(adam_kernel, rows),
        out_shape=[sds(shape, f32)] * 4 + [sds((8, LANES), f32)],
        in_specs=[SM, SM] + [VM] * 6,
        out_specs=[VM] * 5,
        compiler_params=params(),
        name="adam",
    )(me, rates, master, first, second, *grads)


def apply_kernel(me_ref, sums, master, update, new_o, norms_o):
    shard = master.shape[1]
    roots = jnp.sqrt(sums[...])
    weight_norms, update_norms = roots[0:3, :], roots[3:6, :]
    lane = lax.broadcasted_iota(jnp.int32, (3, LANES), 1)
    group3 = lax.broadcasted_iota(jnp.int32, (3, LANES), 0)
    used = pick(group3, [int(REAL[g].sum()) for g in range(3)])
    trust = jnp.where(lane < used, weight_norms / (update_norms + norm_eps), 1.0)
    norms_o[0] = weight_norms
    norms_o[1] = update_norms
    norms_o[2] = trust
    position = me_ref[0] * shard + lax.broadcasted_iota(jnp.int32, (3, shard), 1)
    group = lax.broadcasted_iota(jnp.int32, (3, 1), 0)
    ratio = jnp.broadcast_to(trust[:, 0:1], (3, shard))
    for s in range(1, SEGMENTS):
        low = pick(group, [int(STARTS[g, s]) if REAL[g, s] > 0 else 2**30 for g in range(3)])
        ratio = jnp.where(position >= low, trust[:, s : s + 1], ratio)
    new_o[...] = master[...] - learn_rate * ratio * update[...]


def apply_update(me, sums, master, update):
    return pl.pallas_call(
        apply_kernel,
        out_shape=[sds(master.shape, f32), sds((3, 3, LANES), f32)],
        in_specs=[SM] + [VM] * 3,
        out_specs=[VM] * 2,
        compiler_params=params(),
        name="apply_update",
    )(me, sums, master, update)


def round_kernel(rows, count_ref, master, stem, selfb, classb):
    for g, ref in enumerate((stem, selfb, classb)):
        ref[0, 0:rows, :] = master[g : g + 1, :].reshape(rows, LANES).astype(bf16)
    tail = classb.shape[1] - rows
    classb[0, rows:, :] = jnp.full((tail, LANES), count_ref[0], f32).astype(bf16)


def round_shards(count, master, rows, class_rows):
    return pl.pallas_call(
        functools.partial(round_kernel, rows),
        out_shape=[sds((1, rows, LANES), bf16), sds((1, rows, LANES), bf16), sds((1, class_rows, LANES), bf16)],
        in_specs=[SM, VM],
        out_specs=[VM] * 3,
        compiler_params=params(),
        name="round_shards",
    )(count, master)


def on_device(
    master,
    first_moment,
    second_moment,
    patches_small,
    patches_large,
    labels_small,
    labels_large,
    counts,
    step,
):
    rows = master.shape[1] // LANES
    n_dp, n_z = lax.axis_size("dp"), lax.axis_size("fsdp")
    z_bits, bits = log2(n_z), log2(n_dp) + log2(n_z)
    devices = n_dp * n_z
    top = bits - 1
    ns, valid, _ = patches_small.shape
    nl = patches_large.shape[0]
    padded = -(-valid // 16) * 16
    index = lax.axis_index(AXES).astype(jnp.int32)
    me = index.reshape(1)

    z_order = list(range(z_bits - 1, -1, -1))
    core = z_bits
    middle = list(range(core + 1, bits))
    stem_short = int(ENDS[0].max()) <= (devices // 2) * master.shape[1]

    local_count = jnp.sum(counts).astype(f32).reshape(1)
    class_rows = rows + 1
    stem_shard, self_shard, class_shard = round_shards(local_count, master, rows, class_rows)

    if stem_short:
        half = n_dp // 2
        got = lax.ppermute(stem_shard, "dp", [(i, i + half) for i in range(half)])
        stem_shard = jnp.where(lax.axis_index("dp") < half, stem_shard, got)
        stem_me = jnp.bitwise_and(me, devices // 2 - 1)
        stem_order = z_order + middle[:-1] + [core]
        stem_count = devices // 2
    else:
        stem_me, stem_order, stem_count = me, z_order + middle + [core], devices
    self_state = gather_pieces([(self_shard, [0])], z_order + middle + [core], z_bits)
    stem_state = gather_pieces([(stem_shard, [0])], stem_order, z_bits)
    class_shard, _ = lax.optimization_barrier((class_shard, self_state[len(self_state) // 2][0]))
    class_state = gather_pieces([(class_shard, [0])], z_order + middle[::-1] + [core], z_bits)

    arrays = lambda state: ([a for a, _ in state], [r for _, r in state])
    stem = unpack_stem(stem_me, *arrays(stem_state), rows, stem_count, padded)
    selfw = unpack_self(me, *arrays(self_state), rows, devices)
    saved_s, saved_l = self_forward(patches_small, patches_large, stem, selfw, padded)
    *classw, total = unpack_class(me, *arrays(class_state), rows, devices)

    live = jnp.concatenate([jnp.arange(ns) < counts[0, 0], jnp.arange(nl) < counts[0, 1]]).astype(f32)
    live = jnp.pad(live, (0, BATCH - ns - nl)).reshape(BATCH, 1) / total[0, 0]
    labels = jnp.pad(jnp.concatenate([labels_small, labels_large]), (0, BATCH - ns - nl)).reshape(BATCH, 1)
    d_s, d_l, *class_grads, g_svec, g_head_w, g_head_b, loss = class_block(
        saved_s[9], saved_l[9], classw, stem, labels, live, valid
    )

    order = [core] + middle[::-1] + z_order
    rels = slots_of(order)
    grad_class = reduce_slots(*pack(pack_class_kernel, "pack_class", me, class_grads, rels, rows), order, z_bits)

    *self_grads, g_patch_w, g_patch_b, g_pos = self_backward(
        patches_small, patches_large, saved_s, saved_l, d_s, d_l, selfw
    )
    stem_grads = (g_patch_w, g_patch_b, g_pos, g_svec, g_head_w, g_head_b)
    tiles = [pltpu.VMEM((8, D, LANES), f32)]
    if stem_short:
        stem_order = [core] + middle[:-1] + z_order
        keep, send = pack(pack_stem_kernel, "pack_stem", stem_me, stem_grads, slots_of(stem_order), rows, tiles)
        part = reduce_slots(keep, send, stem_order, z_bits)
        got = lax.ppermute(part.astype(bf16), "dp", [(i + half, i) for i in range(half)])
        grad_stem = jnp.where(lax.axis_index("dp") < half, part + got.astype(f32), 0.0)
    else:
        grad_stem = reduce_slots(*pack(pack_stem_kernel, "pack_stem", me, stem_grads, rels, rows, tiles), order, z_bits)
    grad_self = reduce_slots(*pack(pack_self_kernel, "pack_self", me, self_grads, rels, rows), order, z_bits)

    count_f = step[0].astype(f32)
    rates = jnp.stack([1.0 - beta_one**count_f, 1.0 - beta_two**count_f])
    gradients, new_first, new_second, update, sums = adam(
        me, rates, master, first_moment, second_moment, (grad_stem, grad_self, grad_class), rows
    )
    sums = jnp.concatenate([sums[:6], loss, sums[7:]], 0)
    for bit in range(bits):
        sums = sums + exchange(sums, bit, z_bits)
    new_master, norms = apply_update(me, sums, master, update)
    return (
        sums[6, 0],
        gradients,
        new_first,
        new_second,
        new_master,
        norms[0, :, :SEGMENTS],
        norms[1, :, :SEGMENTS],
        norms[2, :, :SEGMENTS],
    )


def solution(mesh):
    return jax.shard_map(
        on_device,
        mesh=mesh,
        in_specs=(
            P(None, AXES),
            P(None, AXES),
            P(None, AXES),
            P(AXES, None, None),
            P(AXES, None, None),
            P(AXES),
            P(AXES),
            P(AXES, None),
            P(),
        ),
        out_specs=(
            P(),
            P(None, AXES),
            P(None, AXES),
            P(None, AXES),
            P(None, AXES),
            P(),
            P(),
            P(),
        ),
        check_vma=False,
    )
```

time: 1920 us -> 573 us (0.30)
  matrix products: 703 us -> 0 us
  local copies, waits for them, and re-layouts: 404 us -> 15 us
  Pallas kernels: 0 us -> 368 us
  waiting for transfers between devices: 494 us -> 126 us
  other arithmetic: 177 us -> 11.9 us
  blocking collectives: 81.3 us -> 0 us
  starting transfers between devices: 0.16 us -> 43.4 us
    dot_general x167 -> x0, matrix products: 703 us -> none  [the longest x24 227 us: mixing(): return jnp.einsum('gh,nhqk->ngqk', mix_post, probs, precision=highest)]
    pallas_call x0 -> x12, Pallas kernels: none -> 368 us  [the longest x1 212 us: self_backward(): pl.pallas_call(functools.partial(self_backward_kernel, steps_small, steps...]
    unnamed x5 -> x0, waiting for transfers between devices: 343 us -> none
    all_gather x3 -> x0, waiting for transfers between devices: 152 us -> none  [on_device(): lax.all_gather(copies[index], ('dp', 'fsdp'), axis=0, tiled=True)]
    slice x17 -> x16, local copies, waits for them, and re-layouts: 129 us -> 2.57 us  [the longest x13 0.79 us: reduce_slots(): keep, send = (total[:half], total[half:].astype(bf16))]
    ppermute x0 -> x44, waiting for transfers between devices: none -> 126 us  [the longest x28 76.6 us: exchange(): lax.ppermute(value, 'dp', [(i, i ^ 1 << bit - z_bits) for i in range(n)])]
    psum x2 -> x0, blocking collectives: 81.3 us -> none  [the longest x1 42.5 us: on_device(): total, weight_sq = lax.psum((local_count, weight_part), ('dp', 'fsdp'))]
    reduce_sum x71 -> x1, other arithmetic: 70.9 us -> 1.3 us  [on_device(): local_count = jnp.sum(counts).astype(f32).reshape(1)]
  transfers between devices with their start and end apart: 4 -> 44, of which waited for: 4 -> 25; matrix products, arithmetic and copies ran while one was open for 2% -> 3% of each run, Pallas kernels for 0% -> 19%
where the time goes in v1:
time: 573 us; the launch traced here: 568 us
  Pallas kernels  368 us (64%)
  waiting for transfers between devices  126 us (22%)
  starting transfers between devices  43.4 us (8%)
  local copies, waits for them, and re-layouts  15 us (3%)
  other arithmetic  11.9 us (2%)
    pallas_call x1, Pallas kernels, self_backward(): pl.pallas_call(functools.partial(self_backward_kernel, steps_small, steps...  212 us
    pallas_call x1, Pallas kernels, self_forward(): pl.pallas_call(functools.partial(self_forward_kernel, steps_small, valid)...  83.8 us
    ppermute x28, waiting for transfers between devices, exchange(): lax.ppermute(value, 'dp', [(i, i ^ 1 << bit - z_bits) for i in range(n)])  76.6 us
    ppermute x14, waiting for transfers between devices, exchange(): return lax.ppermute(value, 'fsdp', [(i, i ^ 1 << bit) for i in range(n)])  49.3 us
    ppermute x14, starting transfers between devices, exchange(): return lax.ppermute(value, 'fsdp', [(i, i ^ 1 << bit) for i in range(n)])  20.6 us
    pallas_call x1, Pallas kernels, class_block(): pl.pallas_call(functools.partial(class_kernel, ns, nl, valid), out_shape=...  17.7 us
    pallas_call x3, Pallas kernels, pack(): pl.pallas_call(functools.partial(kernel, rels, rows), out_shape=[sds((hal...  17.7 us
    ppermute x28, starting transfers between devices, exchange(): lax.ppermute(value, 'dp', [(i, i ^ 1 << bit - z_bits) for i in range(n)])  17.6 us
  transfers between devices with their start and end apart: 44, of which 25 were waited for; matrix products, arithmetic and copies ran while one was open for 3% of the time, Pallas kernels for 19%

profile of v1, /device:TPU:0, one launch (start us, length us, event | category | flops | bytes accessed | tf_op | source)
XLA Modules:
  0.0 567.9 jit_solution(14801584445439479130)
XLA Ops:
  2.6 1.9 round_shards.1
  4.5 4.0 collective-permute-start.6
  8.5 3.4 collective-permute-start
  17.0 3.3 collective-permute-start.1
  20.4 4.0 collective-permute-done.7
  24.6 3.0 collective-permute-start.2
  29.1 1.9 collective-permute-start.15
  31.0 4.1 collective-permute-done.2
  38.2 5.6 collective-permute-done.16
  43.8 1.6 collective-permute-start.17
  50.8 16.1 %collective-permute-done.9.refs_2_ = bf16[4,434,128]{2,1,0:T(8,128)(2,1)} collective-permute-done((bf16[4,434,128]{2,1,0:T(8,128)(2,1)S(1)}, bf16[4,434,128]{2,1,0:T(8,128)(2,1)}, u32[]{:S(2)}, u32[]{:S(2)}) %collective-permute-start.9) | collective-permute-done | bytes 444448 | tf_op jit(solution)/shard_map/ppermute | solution.py:178
  67.4 6.7 %collective-permute-done.10.refs_3_ = bf16[4,434,128]{2,1,0:T(8,128)(2,1)} collective-permute-done((bf16[4,434,128]{2,1,0:T(8,128)(2,1)}, bf16[4,434,128]{2,1,0:T(8,128)(2,1)}, u32[]{:S(2)}, u32[]{:S(2)}) %collective-permute-start.10) | collective-permute-done | bytes 444448 | tf_op jit(solution)/shard_map/ppermute | solution.py:178
  74.1 2.4 collective-permute-start.18
  78.5 4.9 unpack_stem.1
  84.1 3.6 collective-permute-done.18.refs_2_
  87.7 4.9 unpack_self.1
  92.7 2.5 collective-permute-done.19.refs_3_
  95.2 83.8 %self_forward.1 = (f32[4,208,384]{2,1,0:T(8,128)}, bf16[4,208,1152]{2,1,0:T(8,128)(2,1)}, f32[4,8,208]{2,1,0:T(8,128)}, bf16[4,208,384]{2,1,0:T(8,128)(2,1)}, bf...) custom-call(bf16[4,196,768]{2,1,0:T(8,128)(2,1)} %copy.26.refs_0_, ...), custom_call_target="tpu_custom_call" | custom-call | flops 60000002048 | bytes 60000000 | tf_op jit(solution)/shard_map/self_forward/pallas_call | solution.py:514
  180.7 4.4 unpack_class.1
  186.4 17.7 %class_block.1 = (f32[4,208,384]{2,1,0:T(8,128)}, f32[2,576,384]{2,1,0:T(8,128)}, f32[384,384]{1,0:T(8,128)}, f32[384,768]{1,0:T(8,128)}, f32[384,384]{1,0:T(8,1...) custom-call(f32[4,208,384]{2,1,0:T(8,128)} %get-tuple-element.115.ou, ...), custom_call_target="tpu_custom_call" | custom-call | flops 10000000000 | bytes 60000000 | tf_op jit(solution)/shard_map/class_block/pallas_call | solution.py:699
  204.1 211.6 %self_backward.1 = (f32[384,1152]{1,0:T(8,128)}, f32[384,384]{1,0:T(8,128)}, f32[384,1536]{1,0:T(8,128)}, f32[1536,384]{1,0:T(8,128)}, f32[16,384]{1,0:T(8,128)}...) custom-call(bf16[4,196,768]{2,1,0:T(8,128)(2,1)} %copy.26.refs_0_, ...), custom_call_target="tpu_custom_call" | custom-call | flops 120000004096 | bytes 60000000 | tf_op jit(solution)/shard_map/self_backward/pallas_call | solution.py:909
  415.7 4.7 pack_stem.1
  420.4 2.2 copy.27
  423.1 6.4 %pack_class.1 = (f32[16,434,128]{2,1,0:T(8,128)}, bf16[16,434,128]{2,1,0:T(8,128)(2,1)}) custom-call(s32[1]{0:T(128)} %bitcast.me_ref, f32[384,384]{1,0:T(8,128)} %get-tuple-element.161.wq, f32[384,768]{1,0:T(8,128)} %get-tuple-element.162.wkv, f32[384,384]{1,0:T(8,128)} %get-tuple-element.163.wo, f32[384,1536]{1,0:T(8,128)} %get-tuple-element.164.w1, ...), custom_call_target="tpu_custom_call" | custom-call | tf_op jit(solution)/shard_map/pack_class/pallas_call | solution.py:1027
  429.5 1.7 copy.33
  431.3 6.6 %pack_self.1 = (f32[16,434,128]{2,1,0:T(8,128)}, bf16[16,434,128]{2,1,0:T(8,128)(2,1)}) custom-call(s32[1]{0:T(128)} %bitcast.me_ref, f32[384,1152]{1,0:T(8,128)} %get-tuple-element.151.wqkv, f32[384,384]{1,0:T(8,128)} %get-tuple-element.152.wo, f32[384,1536]{1,0:T(8,128)} %get-tuple-element.153.w1, f32[1536,384]{1,0:T(8,128)} %get-tuple-element.154.w2, ...), custom_call_target="tpu_custom_call" | custom-call | tf_op jit(solution)/shard_map/pack_self/pallas_call | solution.py:1027
  437.9 1.9 copy.29
  441.7 1.8 collective-permute-start.25
  444.3 9.9 %collective-permute-done.25 = bf16[4,434,128]{2,1,0:T(8,128)(2,1)S(1)} collective-permute-done((bf16[4,434,128]{2,1,0:T(8,128)(2,1)S(1)}, bf16[4,434,128]{2,1,0:T(8,128)(2,1)S(1)}, u32[]{:S(2)}, u32[]{:S(2)}) %collective-permute-start.25) | collective-permute-done | bytes 444448 | tf_op jit(solution)/shard_map/ppermute | solution.py:178
  454.3 1.7 collective-permute-start.26
  456.7 1.6 collective-permute-start.35
  460.3 6.5 %collective-permute-done.26 = bf16[2,434,128]{2,1,0:T(8,128)(2,1)S(1)} collective-permute-done((bf16[2,434,128]{2,1,0:T(8,128)(2,1)S(1)}, bf16[2,434,128]{2,1,0:T(8,128)(2,1)S(1)}, u32[]{:S(2)}, u32[]{:S(2)}) %collective-permute-start.26) | collective-permute-done | bytes 222240 | tf_op jit(solution)/shard_map/ppermute | solution.py:176
  467.5 4.2 collective-permute-done.27
  471.7 1.8 collective-permute-start.28
  473.5 6.0 %collective-permute-done.35 = bf16[8,434,128]{2,0,1:T(8,128)(2,1)S(1)} collective-permute-done((bf16[8,434,128]{2,0,1:T(8,128)(2,1)S(1)}, bf16[8,434,128]{2,0,1:T(8,128)(2,1)S(1)}, u32[]{:S(2)}, u32[]{:S(2)}) %collective-permute-start.35) | collective-permute-done | bytes 888864 | tf_op jit(solution)/shard_map/ppermute | solution.py:178
  480.1 17.6 %collective-permute-done.30 = bf16[8,434,128]{2,0,1:T(8,128)(2,1)S(1)} collective-permute-done((bf16[8,434,128]{2,0,1:T(8,128)(2,1)S(1)}, bf16[8,434,128]{2,0,1:T(8,128)(2,1)S(1)}, u32[]{:S(2)}, u32[]{:S(2)}) %collective-permute-start.30) | collective-permute-done | bytes 888864 | tf_op jit(solution)/shard_map/ppermute | solution.py:178
  499.8 2.2 collective-permute-start.37
  502.0 5.1 collective-permute-done.31
  508.6 8.0 %collective-permute-done.37 = bf16[2,434,128]{2,1,0:T(8,128)(2,1)S(1)} collective-permute-done((bf16[2,434,128]{2,1,0:T(8,128)(2,1)S(1)}, bf16[2,434,128]{2,1,0:T(8,128)(2,1)S(1)}, u32[]{:S(2)}, u32[]{:S(2)}) %collective-permute-start.37) | collective-permute-done | bytes 222240 | tf_op jit(solution)/shard_map/ppermute | solution.py:176
  516.8 4.0 collective-permute-done.32
  521.0 2.2 collective-permute-done.38
  523.9 1.8 collective-permute-done.33
  526.4 15.4 %adam.1 = (f32[3,55552]{1,0:T(4,128)}, f32[3,55552]{1,0:T(4,128)}, f32[3,55552]{1,0:T(4,128)}, f32[3,55552]{1,0:T(4,128)}, f32[8,128]{1,0:T(8,128)}) custom-call(s32[1]{0:T(128)} %bitcast.me_ref, f32[2]{0:T(128)} %pad_maximum_fusion.5.rate_ref, f32[3,55552]{1,0:T(4,128)} %master.5, f32[3,55552]{1,0:T(4,128)} %first.1, f32[3,55552]{1,0:T(4,128)} %second.1, ...), custom_call_target="tpu_custom_call" | custom-call | tf_op jit(solution)/shard_map/adam/pallas_call | solution.py:1089
  543.2 3.6 collective-permute-done.39
  548.1 3.9 collective-permute-done.40
  553.7 3.1 collective-permute-done.42
  556.8 3.6 collective-permute-done.43
  561.0 5.5 apply_update.1
  (159 shorter events, 40.3 us)
Async XLA Ops:
  4.5 9.8 %collective-permute-start.6 = (bf16[1,434,128]{2,1,0:T(8,128)(2,1)}, bf16[1,434,128]{2,1,0:T(8,128)(2,1)S(1)}, u32[]{:S(2)}, u32[]{:S(2)}) collective-permute-start(bf16[1,434,128]{2,1,0:T(8,128)(2,1)} %get-tuple-element.97), channel_id=1, source_target_pairs={{0,2},{1,3},{2,0},{3,1},{4,6},{5,7},{6,4},{7,5},{8,10},{9,11},{10,... | collective-permute-start | bytes 333320 | tf_op jit(solution)/shard_map/ppermute | solution.py:176
  8.5 7.6 %collective-permute-start = (bf16[1,434,128]{2,1,0:T(8,128)(2,1)}, bf16[1,434,128]{2,1,0:T(8,128)(2,1)S(1)}, u32[]{:S(2)}, u32[]{:S(2)}) collective-permute-start(bf16[1,434,128]{2,1,0:T(8,128)(2,1)} %get-tuple-element.93), channel_id=1, source_target_pairs={{0,16},{4,20},{8,24},{12,28},{1,17},{5,21},{9,25},{13,29},{2,18},{... | collective-permute-start | bytes 333320 | tf_op jit(solution)/shard_map/ppermute | solution.py:1181
  15.2 33.6 %copy-start.4 = (bf16[4,196,768]{2,0,1:T(4,128)(2,1)S(1)}, bf16[4,196,768]{2,0,1:T(4,128)(2,1)}, u32[]{:S(2)}) copy-start(bf16[4,196,768]{2,0,1:T(4,128)(2,1)} %param.14) | copy-start | bytes 3612676
  15.2 9.2 %collective-permute-start.7 = (bf16[2,434,128]{2,1,0:T(8,128)(2,1)S(1)}, bf16[2,434,128]{2,1,0:T(8,128)(2,1)S(1)}, u32[]{:S(2)}, u32[]{:S(2)}) collective-permute-start(bf16[2,434,128]{2,1,0:T(8,128)(2,1)S(1)} %pad_maximum_fusion.2), channel_id=1, source_target_pairs={{0,1},{1,0},{2,3},{3,2},{4,5},{5,4},{6,7},{7,6},{8,9},{9,8},{10,11... | collective-permute-start | bytes 666632 | tf_op jit(solution)/shard_map/ppermute | solution.py:176
  17.0 7.5 %collective-permute-start.1 = (bf16[1,434,128]{2,1,0:T(8,128)(2,1)S(1)}, bf16[1,434,128]{2,1,0:T(8,128)(2,1)S(1)}, u32[]{:S(2)}, u32[]{:S(2)}) collective-permute-start(bf16[1,434,128]{2,1,0:T(8,128)(2,1)S(1)} %broadcast_select_fusion), channel_id=1, source_target_pairs={{0,2},{1,3},{2,0},{3,1},{4,6},{5,7},{6,4},{7,5},{8,10},{9,11},{10,... | collective-permute-start | bytes 333320 | tf_op jit(solution)/shard_map/ppermute | solution.py:176
  24.4 4.6 collective-permute-start.11
  24.6 10.6 %collective-permute-start.2 = (bf16[2,434,128]{2,1,0:T(8,128)(2,1)S(1)}, bf16[2,434,128]{2,1,0:T(8,128)(2,1)S(1)}, u32[]{:S(2)}, u32[]{:S(2)}) collective-permute-start(bf16[2,434,128]{2,1,0:T(8,128)(2,1)S(1)} %pad_maximum_fusion.1), channel_id=1, source_target_pairs={{0,1},{1,0},{2,3},{3,2},{4,5},{5,4},{6,7},{7,6},{8,9},{9,8},{10,11... | collective-permute-start | bytes 666632 | tf_op jit(solution)/shard_map/ppermute | solution.py:176
  27.6 18.3 %collective-permute-start.8 = (bf16[4,434,128]{2,1,0:T(8,128)(2,1)S(1)}, bf16[4,434,128]{2,1,0:T(8,128)(2,1)}, u32[]{:S(2)}, u32[]{:S(2)}) collective-permute-start(bf16[4,434,128]{2,1,0:T(8,128)(2,1)S(1)} %constant_dynamic-update-slice_fusion.refs_0_), channel_id=1, source_target_pairs={{0,8},{4,12},{8,0},{12,4},{16,24},{20,28},{24,16},{28,20},{1,9},{5... | collective-permute-start | bytes 1333256 | tf_op jit(solution)/shard_map/ppermute | solution.py:178
  29.1 7.7 %collective-permute-start.15 = (bf16[1,435,128]{2,1,0:T(8,128)(2,1)S(1)}, bf16[1,435,128]{2,1,0:T(8,128)(2,1)S(1)}, u32[]{:S(2)}, u32[]{:S(2)}) collective-permute-start(bf16[1,435,128]{2,1,0:T(8,128)(2,1)S(1)} %copy-done.7), channel_id=1, source_target_pairs={{0,2},{1,3},{2,0},{3,1},{4,6},{5,7},{6,4},{7,5},{8,10},{9,11},{10,... | collective-permute-start | bytes 334088 | tf_op jit(solution)/shard_map/ppermute | solution.py:176
  35.3 41.3 %copy-start.18 = (s32[1,2]{1,0:T(1,128)S(1)}, s32[1,2]{1,0:T(1,128)}, u32[]{:S(2)}) copy-start(s32[1,2]{1,0:T(1,128)} %param.18) | copy-start | bytes 28
  35.3 13.5 %collective-permute-start.3 = (bf16[4,434,128]{2,1,0:T(8,128)(2,1)S(1)}, bf16[4,434,128]{2,1,0:T(8,128)(2,1)}, u32[]{:S(2)}, u32[]{:S(2)}) collective-permute-start(bf16[4,434,128]{2,1,0:T(8,128)(2,1)S(1)} %pad_maximum_fusion.refs_0_), channel_id=1, source_target_pairs={{0,8},{4,12},{8,0},{12,4},{16,24},{20,28},{24,16},{28,20},{1,9},{5... | collective-permute-start | bytes 1333256 | tf_op jit(solution)/shard_map/ppermute | solution.py:178
  36.8 6.9 %collective-permute-start.16 = (bf16[2,435,128]{2,1,0:T(8,128)(2,1)S(1)}, bf16[2,435,128]{2,1,0:T(8,128)(2,1)S(1)}, u32[]{:S(2)}, u32[]{:S(2)}) collective-permute-start(bf16[2,435,128]{2,1,0:T(8,128)(2,1)S(1)} %pad_maximum_fusion.3), channel_id=1, source_target_pairs={{0,1},{1,0},{2,3},{3,2},{4,5},{5,4},{6,7},{7,6},{8,9},{9,8},{10,11... | collective-permute-start | bytes 668168 | tf_op jit(solution)/shard_map/ppermute | solution.py:176
  43.8 39.7 %copy-start.6 = (bf16[4,435,128]{2,1,0:T(8,128)(2,1)}, bf16[4,435,128]{2,1,0:T(8,128)(2,1)S(1)}, u32[]{:S(2)}) copy-start(bf16[4,435,128]{2,1,0:T(8,128)(2,1)S(1)} %constant_dynamic-update-slice_fusion.3.refs_0_) | copy-start | bytes 1336324
  43.8 32.7 %collective-permute-start.17 = (bf16[4,435,128]{2,1,0:T(8,128)(2,1)S(1)}, bf16[4,435,128]{2,1,0:T(8,128)(2,1)S(1)}, u32[]{:S(2)}, u32[]{:S(2)}) collective-permute-start(bf16[4,435,128]{2,1,0:T(8,128)(2,1)S(1)} %constant_dynamic-update-slice_fusion.3.refs_0_), channel_id=1, source_target_pairs={{0,16},{4,20},{8,24},{12,28},{16,0},{20,4},{24,8},{28,12},{1,17},{... | collective-permute-start | bytes 1336328 | tf_op jit(solution)/shard_map/ppermute | solution.py:178
  45.3 21.5 %collective-permute-start.9 = (bf16[4,434,128]{2,1,0:T(8,128)(2,1)S(1)}, bf16[4,434,128]{2,1,0:T(8,128)(2,1)}, u32[]{:S(2)}, u32[]{:S(2)}) collective-permute-start(bf16[4,434,128]{2,1,0:T(8,128)(2,1)S(1)} %constant_dynamic-update-slice_fusion.refs_0_), channel_id=1, source_target_pairs={{0,16},{4,20},{8,24},{12,28},{16,0},{20,4},{24,8},{28,12},{1,17},{... | collective-permute-start | bytes 1333256 | tf_op jit(solution)/shard_map/ppermute | solution.py:178
  45.9 21.0 %collective-permute-start.4 = (bf16[4,434,128]{2,1,0:T(8,128)(2,1)S(1)}, bf16[4,434,128]{2,1,0:T(8,128)(2,1)}, u32[]{:S(2)}, u32[]{:S(2)}) collective-permute-start(bf16[4,434,128]{2,1,0:T(8,128)(2,1)S(1)} %pad_maximum_fusion.refs_0_), channel_id=1, source_target_pairs={{0,4},{4,0},{8,12},{12,8},{16,20},{20,16},{24,28},{28,24},{1,5},{5... | collective-permute-start | bytes 1333256 | tf_op jit(solution)/shard_map/ppermute | solution.py:178
  45.9 28.2 %collective-permute-start.10 = (bf16[4,434,128]{2,1,0:T(8,128)(2,1)}, bf16[4,434,128]{2,1,0:T(8,128)(2,1)}, u32[]{:S(2)}, u32[]{:S(2)}) collective-permute-start(bf16[4,434,128]{2,1,0:T(8,128)(2,1)} %collective-permute-done.8.refs_1_), channel_id=1, source_target_pairs={{0,16},{4,20},{8,24},{12,28},{16,0},{20,4},{24,8},{28,12},{1,17},{... | collective-permute-start | bytes 1333256 | tf_op jit(solution)/shard_map/ppermute | solution.py:178
  48.8 27.7 %collective-permute-start.5 = (bf16[4,434,128]{2,1,0:T(8,128)(2,1)}, bf16[4,434,128]{2,1,0:T(8,128)(2,1)}, u32[]{:S(2)}, u32[]{:S(2)}) collective-permute-start(bf16[4,434,128]{2,1,0:T(8,128)(2,1)} %collective-permute-done.3.refs_1_), channel_id=1, source_target_pairs={{0,4},{4,0},{8,12},{12,8},{16,20},{20,16},{24,28},{28,24},{1,5},{5... | collective-permute-start | bytes 1333256 | tf_op jit(solution)/shard_map/ppermute | solution.py:178
  66.9 16.6 %collective-permute-start.12 = (bf16[4,434,128]{2,1,0:T(8,128)(2,1)}, bf16[4,434,128]{2,1,0:T(8,128)(2,1)S(1)}, u32[]{:S(2)}, u32[]{:S(2)}) collective-permute-start(bf16[4,434,128]{2,1,0:T(8,128)(2,1)} %collective-permute-done.8.refs_1_), channel_id=1, source_target_pairs={{0,4},{4,0},{8,12},{12,8},{16,20},{20,16},{24,28},{28,24},{1,5},{5... | collective-permute-start | bytes 1333256 | tf_op jit(solution)/shard_map/ppermute | solution.py:178
  66.9 17.2 %collective-permute-start.13 = (bf16[4,434,128]{2,1,0:T(8,128)(2,1)}, bf16[4,434,128]{2,1,0:T(8,128)(2,1)S(1)}, u32[]{:S(2)}, u32[]{:S(2)}) collective-permute-start(bf16[4,434,128]{2,1,0:T(8,128)(2,1)} %collective-permute-done.9.refs_2_), channel_id=1, source_target_pairs={{0,4},{4,0},{8,12},{12,8},{16,20},{20,16},{24,28},{28,24},{1,5},{5... | collective-permute-start | bytes 1333256 | tf_op jit(solution)/shard_map/ppermute | solution.py:178
  74.1 13.7 %collective-permute-start.18 = (bf16[4,435,128]{2,1,0:T(8,128)(2,1)S(1)}, bf16[4,435,128]{2,1,0:T(8,128)(2,1)S(1)}, u32[]{:S(2)}, u32[]{:S(2)}) collective-permute-start(bf16[4,435,128]{2,1,0:T(8,128)(2,1)S(1)} %constant_dynamic-update-slice_fusion.3.refs_0_), channel_id=1, source_target_pairs={{0,8},{4,12},{8,0},{12,4},{16,24},{20,28},{24,16},{28,20},{1,9},{5... | collective-permute-start | bytes 1336328 | tf_op jit(solution)/shard_map/ppermute | solution.py:178
  76.5 11.3 %collective-permute-start.14 = (bf16[4,434,128]{2,1,0:T(8,128)(2,1)}, bf16[4,434,128]{2,1,0:T(8,128)(2,1)}, u32[]{:S(2)}, u32[]{:S(2)}) collective-permute-start(bf16[4,434,128]{2,1,0:T(8,128)(2,1)} %collective-permute-done.10.refs_3_), channel_id=1, source_target_pairs={{0,4},{4,0},{8,12},{12,8},{16,20},{20,16},{24,28},{28,24},{1,5},{5... | collective-permute-start | bytes 1333256 | tf_op jit(solution)/shard_map/ppermute | solution.py:178
  76.5 18.7 %collective-permute-start.19 = (bf16[4,435,128]{2,1,0:T(8,128)(2,1)S(1)}, bf16[4,435,128]{2,1,0:T(8,128)(2,1)S(1)}, u32[]{:S(2)}, u32[]{:S(2)}) collective-permute-start(bf16[4,435,128]{2,1,0:T(8,128)(2,1)S(1)} %collective-permute-done.17.refs_1_), channel_id=1, source_target_pairs={{0,8},{4,12},{8,0},{12,4},{16,24},{20,28},{24,16},{28,20},{1,9},{5... | collective-permute-start | bytes 1336328 | tf_op jit(solution)/shard_map/ppermute | solution.py:178
  83.5 95.5 %collective-permute-start.20 = (bf16[4,435,128]{2,1,0:T(8,128)(2,1)S(1)}, bf16[4,435,128]{2,1,0:T(8,128)(2,1)S(1)}, u32[]{:S(2)}, u32[]{:S(2)}) collective-permute-start(bf16[4,435,128]{2,1,0:T(8,128)(2,1)S(1)} %constant_dynamic-update-slice_fusion.3.refs_0_), channel_id=1, source_target_pairs={{0,4},{4,0},{8,12},{12,8},{16,20},{20,16},{24,28},{28,24},{1,5},{5... | collective-permute-start | bytes 1336328 | tf_op jit(solution)/shard_map/ppermute | solution.py:178
  84.0 94.9 %collective-permute-start.21 = (bf16[4,435,128]{2,1,0:T(8,128)(2,1)S(1)}, bf16[4,435,128]{2,1,0:T(8,128)(2,1)S(1)}, u32[]{:S(2)}, u32[]{:S(2)}) collective-permute-start(bf16[4,435,128]{2,1,0:T(8,128)(2,1)S(1)} %collective-permute-done.17.refs_1_), channel_id=1, source_target_pairs={{0,4},{4,0},{8,12},{12,8},{16,20},{20,16},{24,28},{28,24},{1,5},{5... | collective-permute-start | bytes 1336328 | tf_op jit(solution)/shard_map/ppermute | solution.py:178
  87.7 91.3 %collective-permute-start.22 = (bf16[4,435,128]{2,1,0:T(8,128)(2,1)S(1)}, bf16[4,435,128]{2,1,0:T(8,128)(2,1)}, u32[]{:S(2)}, u32[]{:S(2)}) collective-permute-start(bf16[4,435,128]{2,1,0:T(8,128)(2,1)S(1)} %collective-permute-done.18.refs_2_), channel_id=1, source_target_pairs={{0,4},{4,0},{8,12},{12,8},{16,20},{20,16},{24,28},{28,24},{1,5},{5... | collective-permute-start | bytes 1336328 | tf_op jit(solution)/shard_map/ppermute | solution.py:178
  95.2 83.8 %copy-start.11 = (bf16[4,435,128]{2,1,0:T(8,128)(2,1)}, bf16[4,435,128]{2,1,0:T(8,128)(2,1)S(1)}, u32[]{:S(2)}) copy-start(bf16[4,435,128]{2,1,0:T(8,128)(2,1)S(1)} %collective-permute-done.19.refs_3_) | copy-start | bytes 1336324
  95.2 83.8 %collective-permute-start.23 = (bf16[4,435,128]{2,1,0:T(8,128)(2,1)S(1)}, bf16[4,435,128]{2,1,0:T(8,128)(2,1)S(1)}, u32[]{:S(2)}, u32[]{:S(2)}) collective-permute-start(bf16[4,435,128]{2,1,0:T(8,128)(2,1)S(1)} %collective-permute-done.19.refs_3_), channel_id=1, source_target_pairs={{0,4},{4,0},{8,12},{12,8},{16,20},{20,16},{24,28},{28,24},{1,5},{5... | collective-permute-start | bytes 1336328 | tf_op jit(solution)/shard_map/ppermute | solution.py:178
  422.6 17.7 %collective-permute-start.24 = (bf16[8,434,128]{2,0,1:T(8,128)(2,1)}, bf16[8,434,128]{2,0,1:T(8,128)(2,1)}, u32[]{:S(2)}, u32[]{:S(2)}) collective-permute-start(bf16[8,434,128]{2,0,1:T(8,128)(2,1)} %copy.27), channel_id=1, source_target_pairs={{0,4},{4,0},{8,12},{12,8},{16,20},{20,16},{24,28},{28,24},{1,5},{5... | collective-permute-start | bytes 2666504 | tf_op jit(solution)/shard_map/ppermute | solution.py:178
  431.2 24.8 %collective-permute-start.34 = (bf16[16,434,128]{2,0,1:T(8,128)(2,1)S(1)}, bf16[16,434,128]{2,0,1:T(8,128)(2,1)S(1)}, u32[]{:S(2)}, u32[]{:S(2)}) collective-permute-start(bf16[16,434,128]{2,0,1:T(8,128)(2,1)S(1)} %copy.33), channel_id=1, source_target_pairs={{0,4},{4,0},{8,12},{12,8},{16,20},{20,16},{24,28},{28,24},{1,5},{5... | collective-permute-start | bytes 5333000 | tf_op jit(solution)/shard_map/ppermute | solution.py:178
  439.8 18.5 %collective-permute-start.29 = (bf16[16,434,128]{2,0,1:T(8,128)(2,1)S(1)}, bf16[16,434,128]{2,0,1:T(8,128)(2,1)S(1)}, u32[]{:S(2)}, u32[]{:S(2)}) collective-permute-start(bf16[16,434,128]{2,0,1:T(8,128)(2,1)S(1)} %copy.29), channel_id=1, source_target_pairs={{0,4},{4,0},{8,12},{12,8},{16,20},{20,16},{24,28},{28,24},{1,5},{5... | collective-permute-start | bytes 5333000 | tf_op jit(solution)/shard_map/ppermute | solution.py:178
  441.7 12.4 %collective-permute-start.25 = (bf16[4,434,128]{2,1,0:T(8,128)(2,1)S(1)}, bf16[4,434,128]{2,1,0:T(8,128)(2,1)S(1)}, u32[]{:S(2)}, u32[]{:S(2)}) collective-permute-start(bf16[4,434,128]{2,1,0:T(8,128)(2,1)S(1)} %slice.196), channel_id=1, source_target_pairs={{0,8},{4,12},{8,0},{12,4},{16,24},{20,28},{24,16},{28,20},{1,9},{5... | collective-permute-start | bytes 1333256 | tf_op jit(solution)/shard_map/ppermute | solution.py:178
  454.3 12.5 %collective-permute-start.26 = (bf16[2,434,128]{2,1,0:T(8,128)(2,1)S(1)}, bf16[2,434,128]{2,1,0:T(8,128)(2,1)S(1)}, u32[]{:S(2)}, u32[]{:S(2)}) collective-permute-start(bf16[2,434,128]{2,1,0:T(8,128)(2,1)S(1)} %slice.199), channel_id=1, source_target_pairs={{0,2},{1,3},{2,0},{3,1},{4,6},{5,7},{6,4},{7,5},{8,10},{9,11},{10,... | collective-permute-start | bytes 666632 | tf_op jit(solution)/shard_map/ppermute | solution.py:176
  456.7 22.7 %collective-permute-start.35 = (bf16[8,434,128]{2,0,1:T(8,128)(2,1)S(1)}, bf16[8,434,128]{2,0,1:T(8,128)(2,1)S(1)}, u32[]{:S(2)}, u32[]{:S(2)}) collective-permute-start(bf16[8,434,128]{2,0,1:T(8,128)(2,1)S(1)} %copy.35), channel_id=1, source_target_pairs={{0,16},{4,20},{8,24},{12,28},{16,0},{20,4},{24,8},{28,12},{1,17},{... | collective-permute-start | bytes 2666504 | tf_op jit(solution)/shard_map/ppermute | solution.py:178
  459.0 38.6 %collective-permute-start.30 = (bf16[8,434,128]{2,0,1:T(8,128)(2,1)S(1)}, bf16[8,434,128]{2,0,1:T(8,128)(2,1)S(1)}, u32[]{:S(2)}, u32[]{:S(2)}) collective-permute-start(bf16[8,434,128]{2,0,1:T(8,128)(2,1)S(1)} %copy.31), channel_id=1, source_target_pairs={{0,16},{4,20},{8,24},{12,28},{16,0},{20,4},{24,8},{28,12},{1,17},{... | collective-permute-start | bytes 2666504 | tf_op jit(solution)/shard_map/ppermute | solution.py:178
  466.9 4.8 collective-permute-start.27
  471.7 27.1 %collective-permute-start.28 = (bf16[434,128]{1,0:T(8,128)(2,1)S(1)}, bf16[434,128]{1,0:T(8,128)(2,1)S(1)}, u32[]{:S(2)}, u32[]{:S(2)}) collective-permute-start(bf16[434,128]{1,0:T(8,128)(2,1)S(1)} %fusion.3), channel_id=1, source_target_pairs={{16,0},{20,4},{24,8},{28,12},{17,1},{21,5},{25,9},{29,13},{18,2},{... | collective-permute-start | bytes 333320 | tf_op jit(solution)/shard_map/ppermute | solution.py:1219
  479.7 19.9 %collective-permute-start.36 = (bf16[4,434,128]{2,1,0:T(8,128)(2,1)S(1)}, bf16[4,434,128]{2,1,0:T(8,128)(2,1)S(1)}, u32[]{:S(2)}, u32[]{:S(2)}) collective-permute-start(bf16[4,434,128]{2,1,0:T(8,128)(2,1)S(1)} %slice.194), channel_id=1, source_target_pairs={{0,8},{4,12},{8,0},{12,4},{16,24},{20,28},{24,16},{28,20},{1,9},{5... | collective-permute-start | bytes 1333256 | tf_op jit(solution)/shard_map/ppermute | solution.py:178
  497.9 9.2 %collective-permute-start.31 = (bf16[4,434,128]{2,1,0:T(8,128)(2,1)S(1)}, bf16[4,434,128]{2,1,0:T(8,128)(2,1)S(1)}, u32[]{:S(2)}, u32[]{:S(2)}) collective-permute-start(bf16[4,434,128]{2,1,0:T(8,128)(2,1)S(1)} %slice.195), channel_id=1, source_target_pairs={{0,8},{4,12},{8,0},{12,4},{16,24},{20,28},{24,16},{28,20},{1,9},{5... | collective-permute-start | bytes 1333256 | tf_op jit(solution)/shard_map/ppermute | solution.py:178
  499.8 16.9 %collective-permute-start.37 = (bf16[2,434,128]{2,1,0:T(8,128)(2,1)S(1)}, bf16[2,434,128]{2,1,0:T(8,128)(2,1)S(1)}, u32[]{:S(2)}, u32[]{:S(2)}) collective-permute-start(bf16[2,434,128]{2,1,0:T(8,128)(2,1)S(1)} %slice.197), channel_id=1, source_target_pairs={{0,2},{1,3},{2,0},{3,1},{4,6},{5,7},{6,4},{7,5},{8,10},{9,11},{10,... | collective-permute-start | bytes 666632 | tf_op jit(solution)/shard_map/ppermute | solution.py:176
  507.2 13.6 %collective-permute-start.32 = (bf16[2,434,128]{2,1,0:T(8,128)(2,1)S(1)}, bf16[2,434,128]{2,1,0:T(8,128)(2,1)S(1)}, u32[]{:S(2)}, u32[]{:S(2)}) collective-permute-start(bf16[2,434,128]{2,1,0:T(8,128)(2,1)S(1)} %slice.198), channel_id=1, source_target_pairs={{0,2},{1,3},{2,0},{3,1},{4,6},{5,7},{6,4},{7,5},{8,10},{9,11},{10,... | collective-permute-start | bytes 666632 | tf_op jit(solution)/shard_map/ppermute | solution.py:176
  516.7 6.5 %collective-permute-start.38 = (bf16[1,434,128]{2,1,0:T(8,128)(2,1)S(1)}, bf16[1,434,128]{2,1,0:T(8,128)(2,1)S(1)}, u32[]{:S(2)}, u32[]{:S(2)}) collective-permute-start(bf16[1,434,128]{2,1,0:T(8,128)(2,1)S(1)} %slice.200), channel_id=1, source_target_pairs={{0,1},{1,0},{2,3},{3,2},{4,5},{5,4},{6,7},{7,6},{8,9},{9,8},{10,11... | collective-permute-start | bytes 333320 | tf_op jit(solution)/shard_map/ppermute | solution.py:176
  520.9 4.8 collective-permute-start.33
  543.2 3.6 collective-permute-start.39
  547.5 4.5 collective-permute-start.40
  552.0 1.2 collective-permute-start.41
  553.2 3.6 collective-permute-start.42
  556.8 3.6 collective-permute-start.43
  (18 other events, 182.7 us)

commit v2 on v1

v2 whole, which is shorter than its diff:
```python
import functools
import math

import jax
import jax.numpy as jnp
import numpy as np
from jax import lax
from jax.experimental import pallas as pl
from jax.experimental.pallas import tpu as pltpu
from jax.sharding import PartitionSpec as P

D = 384
HEADS = 8
WIDTH = D // HEADS
FF = 1536
CLASSES = 1000
CLASS_PAD = 1024
PATCH_IN = 768
GRID_SMALL = 14
GRID_LARGE = 24
LANES = 128
SEGMENTS = 16

LOG2E = 1.4426950408889634
SCALE = WIDTH**-0.5
NEG = -1e30
smooth = 0.1
beta_one = 0.9
beta_two = 0.999
adam_eps = 1e-06
decay_rate = 0.01
learn_rate = 0.3
norm_eps = 1e-06

f32 = jnp.float32
bf16 = jnp.bfloat16
AXES = ("dp", "fsdp")
VMEM_BYTES = 60 << 20


def shapes_of():
    dim = D
    tail = [(dim,), (dim,), (dim, FF), (FF,), (FF, dim), (dim,), (dim,)]
    stem = [
        (PATCH_IN, dim),
        (dim,),
        (GRID_SMALL * GRID_SMALL, dim),
        (dim,),
        (dim,),
        (dim,),
        (dim, CLASSES),
        (CLASSES,),
    ]
    selfb = [
        (dim,),
        (dim,),
        (dim, 3 * dim),
        (2 * dim,),
        (HEADS, HEADS),
        (HEADS, HEADS),
        (dim, dim),
        (dim,),
        (dim,),
    ] + tail
    classb = [
        (dim,),
        (dim,),
        (dim, dim),
        (dim,),
        (dim, 2 * dim),
        (dim,),
        (dim, dim),
        (dim,),
        (dim,),
    ] + tail
    return [stem, selfb, classb]


def segment_bounds():
    starts = np.zeros((3, SEGMENTS), np.int32)
    ends = np.zeros((3, SEGMENTS), np.int32)
    real = np.zeros((3, SEGMENTS), np.float32)
    for group, shapes in enumerate(shapes_of()):
        offset = 0
        for number, shape in enumerate(shapes):
            count = int(np.prod(shape))
            starts[group, number] = offset
            ends[group, number] = offset + count
            real[group, number] = 1.0
            offset += count
    return starts, ends, real


STARTS, ENDS, REAL = segment_bounds()


def row_of(group, number):
    return int(STARTS[group, number]) // LANES


def rows_used(group):
    return -(-int(ENDS[group].max()) // LANES)


def resize_table():
    rows = np.arange(GRID_LARGE).astype(np.float32) * np.float32((GRID_SMALL - 1) / (GRID_LARGE - 1))
    cols = np.arange(GRID_SMALL).astype(np.float32)
    line = np.maximum(np.float32(0.0), np.float32(1.0) - np.abs(rows[:, None] - cols[None, :]))
    return (line[:, None, :, None] * line[None, :, None, :]).reshape(GRID_LARGE**2, GRID_SMALL**2)


def nn(a, b):
    return lax.dot_general(a, b, (((1,), (0,)), ((), ())), preferred_element_type=f32)


def nt(a, b):
    return lax.dot_general(a, b, (((1,), (1,)), ((), ())), preferred_element_type=f32)


def tn(a, b):
    return lax.dot_general(a, b, (((0,), (0,)), ((), ())), preferred_element_type=f32)


def colsum(value):
    return jnp.sum(value, 0, keepdims=True)


def split(value):
    high = value.astype(bf16)
    return high, (value - high.astype(f32)).astype(bf16)


def stats(value):
    centred = value - jnp.mean(value, -1, keepdims=True)
    inverse = lax.rsqrt(jnp.mean(centred * centred, -1, keepdims=True) + 1e-06)
    return centred * inverse, inverse


def norm_back(d_out, unit, inverse, gain):
    inner = d_out * gain
    first = jnp.mean(inner, -1, keepdims=True)
    second = jnp.mean(inner * unit, -1, keepdims=True)
    return inverse * (inner - first - unit * second)


def gelu_pair(upper):
    cdf = 0.5 * (1.0 + lax.erf(upper * (0.5**0.5)))
    density = jnp.exp(-0.5 * upper * upper) * 0.3989422804014327
    return upper * cdf, cdf + upper * density


def head_mask(rows):
    lane = lax.broadcasted_iota(jnp.int32, (rows, D), 1)
    row = lax.broadcasted_iota(jnp.int32, (rows, D), 0)
    return (lane // WIDTH) == lax.rem(row, HEADS)


VM = pl.BlockSpec(memory_space=pltpu.VMEM)
SM = pl.BlockSpec(memory_space=pltpu.SMEM)


def params(**kw):
    return pltpu.CompilerParams(vmem_limit_bytes=VMEM_BYTES, **kw)


def sds(shape, dtype):
    return jax.ShapeDtypeStruct(shape, dtype)


def call(kernel, args, after, in_specs, **kw):
    n, m = len(args), len(after)

    def wrapped(*refs):
        kernel(*refs[:n], *refs[n + m :])

    specs = list(in_specs) + [pl.BlockSpec(memory_space=pl.ANY)] * m
    return pl.pallas_call(wrapped, in_specs=specs, compiler_params=params(), **kw)(*args, *after)


def log2(n):
    return n.bit_length() - 1


def exchange(value, bit, z_bits):
    if bit < z_bits:
        n = lax.axis_size("fsdp")
        return lax.ppermute(value, "fsdp", [(i, i ^ (1 << bit)) for i in range(n)])
    n = lax.axis_size("dp")
    return lax.ppermute(value, "dp", [(i, i ^ (1 << (bit - z_bits))) for i in range(n)])


def exchange_z(value, k):
    n = lax.axis_size("fsdp")
    return lax.ppermute(value, "fsdp", [(i, i ^ k) for i in range(n)])


def tied(values, after):
    if after is None:
        return values
    return lax.optimization_barrier((*values, after))[:-1]


def gather_z(value, rel, after=None):
    n = lax.axis_size("fsdp")
    got = tied([exchange_z(value, k) for k in range(1, n)], after)
    return [(jnp.concatenate([value, *got], 0), [r | k for k in range(n) for r in rel])]


def gather_bit(state, bit, z_bits, after=None):
    got = tied([exchange(a, bit, z_bits) for a, _ in state], after)
    return state + [(a, [r | (1 << bit) for r in rel]) for a, (_, rel) in zip(got, state)]


def put_matrix(flat, row, out_ref, rows, cols):
    step = cols // LANES
    for j in range(step):
        out_ref[:, LANES * j : LANES * (j + 1)] = flat[pl.ds(row + j, rows, stride=step), :].astype(bf16)


def put_row(flat, row, out_ref, at, cols):
    for j in range(cols // LANES):
        out_ref[at : at + 1, LANES * j : LANES * (j + 1)] = flat[row + j : row + j + 1, :]


def fill_flat(me, piece_refs, rels, rows, flat):
    for ref, rel in zip(piece_refs, rels):
        for k, r in enumerate(rel):
            flat[pl.ds(rows * jnp.bitwise_xor(me, r), rows), :] = ref[k, 0:rows, :].astype(f32)


def unpack_stem_kernel(rels, rows, me_ref, resize_ref, *refs):
    n = len(rels)
    pieces, (patch_w, vec, pos_small, pos_large, head_w, head_b), (flat, tiles) = refs[:n], refs[n : n + 6], refs[n + 6 :]
    fill_flat(me_ref[0], pieces, rels, rows, flat)
    put_matrix(flat, row_of(0, 0), patch_w, PATCH_IN, D)
    vec[...] = jnp.zeros_like(vec)
    for at, number in enumerate((1, 3, 4, 5)):
        put_row(flat, row_of(0, number), vec, at, D)
    bias = vec[0:1, :]
    small = GRID_SMALL**2
    pos_small[...] = jnp.zeros_like(pos_small)
    for j in range(D // LANES):
        pos_small[0:small, LANES * j : LANES * (j + 1)] = flat[pl.ds(row_of(0, 2) + j, small, stride=D // LANES), :]
    pos_large[...] = (
        lax.dot_general(
            resize_ref[...], pos_small[...], (((1,), (0,)), ((), ())),
            preferred_element_type=f32, precision=lax.Precision.HIGHEST,
        )
        + bias
    )
    pos_small[...] += bias
    lane = lax.broadcasted_iota(jnp.int32, (24, LANES), 1)
    base = row_of(0, 6)
    for rho in range(16):
        first, shift = (CLASSES * rho) // LANES, (CLASSES * rho) % LANES
        parts = [flat[pl.ds(base + first + t, 24, stride=125), :] for t in range(9)]
        if shift:
            parts = [pltpu.roll(p, LANES - shift, 1) for p in parts]
        for t in range(8):
            value = jnp.where(lane < LANES - shift, parts[t], parts[t + 1]) if shift else parts[t]
            if t == 7:
                value = jnp.where(lane < CLASSES - 7 * LANES, value, 0.0)
            tiles[t, pl.ds(rho, 24, stride=16), :] = value
    for t in range(8):
        head_w[:, LANES * t : LANES * (t + 1)] = tiles[t].astype(bf16)
    put_row(flat, row_of(0, 7), head_b, 0, CLASS_PAD)


def unpack_stem(me, pieces, rels, rows, count, padded):
    resize = np.zeros((GRID_LARGE**2, padded), np.float32)
    resize[:, : GRID_SMALL**2] = resize_table()
    return pl.pallas_call(
        functools.partial(unpack_stem_kernel, rels, rows),
        out_shape=[
            sds((PATCH_IN, D), bf16),
            sds((8, D), f32),
            sds((padded, D), f32),
            sds((GRID_LARGE**2, D), f32),
            sds((D, CLASS_PAD), bf16),
            sds((1, CLASS_PAD), f32),
        ],
        in_specs=[SM] + [VM] * (1 + len(pieces)),
        out_specs=[VM] * 6,
        scratch_shapes=[pltpu.VMEM((count * rows, LANES), f32), pltpu.VMEM((8, D, LANES), f32)],
        compiler_params=params(),
        name="unpack_stem",
    )(me, jnp.asarray(resize), *pieces)


SG1, SB1, SBQ, SBV, SBO, SLS1, SG2, SB2, SC2, SLS2 = range(10)
CG1, CB1, CBQ, CBV, CBO, CLS1, CG2, CB2, CC2, CLS2 = range(10)


def unpack_low_kernel(rels, rows, me_ref, *refs):
    n = len(rels)
    pieces = refs[:n]
    wqkv, vec, pre_col, post_col, pre_row, post_row, flat = refs[n:]
    fill_flat(me_ref[0], pieces, rels, rows, flat)
    put_matrix(flat, row_of(1, 2), wqkv, D, 3 * D)
    vec[...] = jnp.zeros_like(vec)
    bq = row_of(1, 3)
    for at, row in ((SG1, row_of(1, 0)), (SB1, row_of(1, 1)), (SBQ, bq), (SBV, bq + D // LANES)):
        put_row(flat, row, vec, at, D)
    mix = jnp.broadcast_to(flat[row_of(1, 4) : row_of(1, 4) + 1, :], (HEADS, LANES))
    lane = lax.broadcasted_iota(jnp.int32, (HEADS, LANES), 1)
    row = lax.broadcasted_iota(jnp.int32, (HEADS, LANES), 0)
    pick_pre = jnp.where((lane < 64) & (lane // HEADS == row), mix, 0.0).astype(bf16)
    pick_post = jnp.where((lane >= 64) & (lane % HEADS == row), mix, 0.0).astype(bf16)
    table_lane = lax.broadcasted_iota(jnp.int32, (LANES, D), 0)
    table_col = lax.broadcasted_iota(jnp.int32, (LANES, D), 1) // WIDTH
    spread_pre = jnp.where(table_lane % HEADS == table_col, 1.0, 0.0).astype(bf16)
    spread_post = jnp.where((table_lane - 64) // HEADS == table_col, 1.0, 0.0).astype(bf16)
    factor = SCALE * LOG2E
    pre_row[...] = nn(pick_pre, spread_pre) * factor
    post_row[...] = nn(pick_post, spread_post)
    column = lambda a, b: lax.dot_general(a, b, (((0,), (1,)), ((), ())), preferred_element_type=f32)
    pre_col[...] = column(spread_pre, pick_pre) * factor
    post_col[...] = column(spread_post, pick_post)


def unpack_low(me, pieces, rels, rows, count):
    return pl.pallas_call(
        functools.partial(unpack_low_kernel, rels, rows),
        out_shape=[
            sds((D, 3 * D), bf16),
            sds((16, D), f32),
            sds((D, HEADS), f32),
            sds((D, HEADS), f32),
            sds((HEADS, D), f32),
            sds((HEADS, D), f32),
        ],
        in_specs=[SM] + [VM] * len(pieces),
        out_specs=[VM] * 6,
        scratch_shapes=[pltpu.VMEM((count * rows, LANES), f32)],
        compiler_params=params(),
        name="unpack_low",
    )(me, *pieces)


def unpack_feed_kernel(rels, rows, me_ref, *refs):
    n = len(rels)
    pieces = refs[:n]
    wo, w1, w2, vec, c1, flat = refs[n:]
    fill_flat(me_ref[0], pieces, rels, rows, flat)
    put_matrix(flat, row_of(1, 6), wo, D, D)
    put_matrix(flat, row_of(1, 11), w1, D, FF)
    put_matrix(flat, row_of(1, 13), w2, FF, D)
    vec[...] = jnp.zeros_like(vec)
    for at, number in ((SBO, 7), (SLS1, 8), (SG2, 9), (SB2, 10), (SC2, 14), (SLS2, 15)):
        put_row(flat, row_of(1, number), vec, at, D)
    put_row(flat, row_of(1, 12), c1, 0, FF)


def unpack_feed(me, pieces, rels, rows, count):
    return pl.pallas_call(
        functools.partial(unpack_feed_kernel, rels, rows),
        out_shape=[
            sds((D, D), bf16),
            sds((D, FF), bf16),
            sds((FF, D), bf16),
            sds((16, D), f32),
            sds((1, FF), f32),
        ],
        in_specs=[SM] + [VM] * len(pieces),
        out_specs=[VM] * 5,
        scratch_shapes=[pltpu.VMEM((count * rows, LANES), f32)],
        compiler_params=params(),
        name="unpack_feed",
    )(me, *pieces)


def unpack_class_kernel(rels, rows, me_ref, *refs):
    n = len(rels)
    pieces = refs[:n]
    wq, wkv, wo, w1, w2, vec, c1, total, flat = refs[n:]
    fill_flat(me_ref[0], pieces, rels, rows, flat)
    put_matrix(flat, row_of(2, 2), wq, D, D)
    put_matrix(flat, row_of(2, 4), wkv, D, 2 * D)
    put_matrix(flat, row_of(2, 6), wo, D, D)
    put_matrix(flat, row_of(2, 11), w1, D, FF)
    put_matrix(flat, row_of(2, 13), w2, FF, D)
    vec[...] = jnp.zeros_like(vec)
    for at, number in (
        (CG1, 0), (CB1, 1), (CBQ, 3), (CBV, 5), (CBO, 7), (CLS1, 8), (CG2, 9), (CB2, 10), (CC2, 14), (CLS2, 15),
    ):
        put_row(flat, row_of(2, number), vec, at, D)
    put_row(flat, row_of(2, 12), c1, 0, FF)
    count = jnp.zeros((1, LANES), f32)
    for ref, rel in zip(pieces, rels):
        for k in range(len(rel)):
            count = count + ref[k].astype(f32)[rows : rows + 1, :]
    total[...] = count


def unpack_class(me, pieces, rels, rows, count):
    return pl.pallas_call(
        functools.partial(unpack_class_kernel, rels, rows),
        out_shape=[
            sds((D, D), bf16),
            sds((D, 2 * D), bf16),
            sds((D, D), bf16),
            sds((D, FF), bf16),
            sds((FF, D), bf16),
            sds((16, D), f32),
            sds((1, FF), f32),
            sds((1, LANES), f32),
        ],
        in_specs=[SM] + [VM] * len(pieces),
        out_specs=[VM] * 8,
        scratch_shapes=[pltpu.VMEM((count * rows, LANES), f32)],
        compiler_params=params(),
        name="unpack_class",
    )(me, *pieces)


def const_spec(a):
    return pl.BlockSpec(a.shape, lambda i, nd=len(a.shape): (0,) * nd, pipeline_mode=pl.Buffered(1))


def cost(flops, read):
    return pl.CostEstimate(flops=int(flops), bytes_accessed=int(read), transcendentals=0)


class Steps:
    def __init__(self, ns, nl, padded, large_len):
        self.count = math.gcd(ns, nl)
        self.small, self.large = ns // self.count, nl // self.count
        self.padded, self.large_len = padded, large_len
        self.split = self.small * padded
        self.rows = self.split + self.large * large_len
        self.grid = (self.count,)

    def specs(self, cols):
        index = lambda i: (i, 0, 0)
        return [
            pl.BlockSpec((self.small, self.padded, cols), index),
            pl.BlockSpec((self.large, self.large_len, cols), index),
        ]

    def shapes(self, cols, kind):
        n = self.count
        return [sds((n * self.small, self.padded, cols), kind), sds((n * self.large, self.large_len, cols), kind)]

    def join(self, pair):
        cols = pair[0].shape[-1]
        return jnp.concatenate([ref[...].reshape(-1, cols) for ref in pair], 0)

    def put(self, pair, value):
        cols = value.shape[-1]
        pair[0][...] = value[: self.split].reshape(self.small, self.padded, cols)
        pair[1][...] = value[self.split :].reshape(self.large, self.large_len, cols)


def embed_kernel(steps, valid, ps, plg, patch_w, pos_small, pos_large, wqkv, vec, *outs):
    tok_o, qkv_o, tokens = outs[:2], outs[2:4], outs[4]
    row = lambda at: vec[at : at + 1, :]
    for i in range(steps.small):
        base = steps.padded * i
        tokens[base : base + steps.padded, :] = pos_small[...]
        tokens[base : base + valid, :] += nn(ps[i], patch_w[...])
    for i in range(steps.large):
        base = steps.split + steps.large_len * i
        tokens[base : base + steps.large_len, :] = nn(plg[i], patch_w[...]) + pos_large[...]
    tok = tokens[...]
    steps.put(tok_o, tok)
    unit, _ = stats(tok)
    a1 = (unit * row(SG1) + row(SB1)).astype(bf16)
    bias = jnp.concatenate([row(SBQ), jnp.zeros((1, D), f32), row(SBV)], 1)
    steps.put(qkv_o, (nn(a1, wqkv[...]) + bias).astype(bf16))


def embed(ps, plg, patch_w, pos_small, pos_large, wqkv, vec, padded, after):
    ns, valid, _ = ps.shape
    nl, large_len, _ = plg.shape
    steps = Steps(ns, nl, padded, large_len)
    weights = (patch_w, pos_small, pos_large, wqkv, vec)
    index = lambda i: (i, 0, 0)
    out = call(
        functools.partial(embed_kernel, steps, valid),
        (ps, plg, *weights),
        after,
        grid=steps.grid,
        out_shape=steps.shapes(D, f32) + steps.shapes(3 * D, bf16),
        in_specs=[
            pl.BlockSpec((steps.small, valid, PATCH_IN), index),
            pl.BlockSpec((steps.large, large_len, PATCH_IN), index),
        ]
        + [const_spec(a) for a in weights],
        out_specs=steps.specs(D) + steps.specs(3 * D),
        scratch_shapes=[pltpu.VMEM((steps.rows, D), f32)],
        cost_estimate=cost(12e9, 20e6),
        name="embed",
    )
    return out[:2], out[2:]


def attend_kernel(valid, qkv_ref, pre_col, post_col, att_ref, lse_ref, q_t, kk, v_t, acc):
    per, length = qkv_ref.shape[0], qkv_ref.shape[1]
    for i in range(per):
        q_t[i] = qkv_ref[i, :, 0:D].astype(f32).T
        kk[i, :, 0:D] = qkv_ref[i, :, D : 2 * D]
        kk[i, :, D:] = qkv_ref[i, :, D : 2 * D]
        v_t[i] = qkv_ref[i, :, 2 * D :].astype(f32).T.astype(bf16)
    for g in range(HEADS):
        pre, post = pre_col[:, g : g + 1], post_col[:, g : g + 1]
        for i in range(per):
            high, low = split(q_t[i] * pre)
            mixed = nn(kk[i], jnp.concatenate([high, low], 0))
            if valid < length:
                mixed = jnp.where(lax.broadcasted_iota(jnp.int32, mixed.shape, 0) < valid, mixed, NEG)
            top = jnp.max(mixed, 0, keepdims=True)
            raw = jnp.exp2(mixed - top)
            weight = colsum(raw)
            lse_ref[i, g : g + 1, :] = top + jnp.log2(weight)
            part = nn(v_t[i], raw.astype(bf16)) * post * (1.0 / weight)
            acc[i] = part if g == 0 else acc[i] + part
    for i in range(per):
        att_ref[i] = acc[i].T.astype(bf16)


def attend(qkv, pre_col, post_col, valid, per, flops, after):
    n, length, _ = qkv.shape
    spec = lambda *tail: pl.BlockSpec((per,) + tail, lambda i: (i, 0, 0))
    return call(
        functools.partial(attend_kernel, valid),
        (qkv, pre_col, post_col),
        after,
        grid=(n // per,),
        out_shape=[sds((n, length, D), bf16), sds((n, HEADS, length), f32)],
        in_specs=[spec(length, 3 * D), const_spec(pre_col), const_spec(post_col)],
        out_specs=[spec(length, D), spec(HEADS, length)],
        scratch_shapes=[
            pltpu.VMEM((per, D, length), f32),
            pltpu.VMEM((per, length, 2 * D), bf16),
            pltpu.VMEM((per, D, length), bf16),
            pltpu.VMEM((per, D, length), f32),
        ],
        cost_estimate=cost(flops, 10e6),
        name="attend",
    )


def feed_kernel(steps, tok_s, tok_l, att_s, att_l, wo, w1, w2, vec, c1, *outs):
    branch_o, mid_o, act_o, slope_o, lower_o, out_o = [outs[2 * i : 2 * i + 2] for i in range(6)]
    row = lambda at: vec[at : at + 1, :]
    branch = nn(steps.join((att_s, att_l)), wo[...]) + row(SBO)
    steps.put(branch_o, branch.astype(bf16))
    mid = steps.join((tok_s, tok_l)) + row(SLS1) * branch
    steps.put(mid_o, mid)
    unit, _ = stats(mid)
    n2 = (unit * row(SG2) + row(SB2)).astype(bf16)
    act, slope = gelu_pair(nn(n2, w1[...]) + c1[...])
    act = act.astype(bf16)
    steps.put(act_o, act)
    steps.put(slope_o, slope.astype(bf16))
    lower = nn(act, w2[...]) + row(SC2)
    steps.put(lower_o, lower.astype(bf16))
    steps.put(out_o, mid + row(SLS2) * lower)


FEED_OUT = [(D, bf16), (D, f32), (FF, bf16), (FF, bf16), (D, bf16), (D, f32)]


def feed(tok, att, weights, after):
    (ns, padded, _), (nl, large_len, _) = tok[0].shape, tok[1].shape
    steps = Steps(ns, nl, padded, large_len)
    out = call(
        functools.partial(feed_kernel, steps),
        (*tok, *att, *weights),
        after,
        grid=steps.grid,
        out_shape=[shape for entry in FEED_OUT for shape in steps.shapes(*entry)],
        in_specs=steps.specs(D) * 2 + [const_spec(a) for a in weights],
        out_specs=[spec for cols, _ in FEED_OUT for spec in steps.specs(cols)],
        cost_estimate=cost(20e9, 30e6),
        name="feed",
    )
    return [out[2 * i : 2 * i + 2] for i in range(6)]


BATCH = 8


def class_kernel(
    ns, nl, valid, out_s, out_l, wq, wkv, wo, w1, w2, vec, c1, svec, head_w, head_b, total, counts, labels_s, labels_l,
    d_s, d_l, g_wq, g_wkv, g_wo, g_w1, g_w2, g_vec, g_c1, g_svec, g_head_w, g_head_b, loss_o,
    a_s, a_l, p_s, p_l, z_ref, y_ref, b_ref, ps_ref, pc_ref, da_ref,
):
    row = lambda at: vec[at : at + 1, :]
    mask8 = head_mask(HEADS)
    mask64 = head_mask(HEADS * BATCH)
    cls = svec[1:2, :]
    unit_cls, inv_cls = stats(cls)
    a_cls = (unit_cls * row(CG1) + row(CB1)).astype(bf16)
    a_cls_f = a_cls.astype(f32)
    query = (nn(a_cls, wq[...]) + row(CBQ)).astype(bf16).astype(f32)
    q_diag = jnp.where(mask8, query, 0.0).astype(bf16)
    u_nat = nt(q_diag, wkv[:, 0:D]) * SCALE
    u_hi, u_lo = split(u_nat * LOG2E)
    u16 = jnp.concatenate([u_hi, u_lo], 0)
    s_cls = jnp.sum(u_nat * LOG2E * a_cls_f, -1, keepdims=True)
    z_ref[...] = jnp.zeros_like(z_ref)
    ps_ref[...] = jnp.zeros_like(ps_ref)

    def forward(i, src, a_ref, p_ref, slot):
        unit, _ = stats(src[i])
        a = (unit * row(CG1) + row(CB1)).astype(bf16)
        a_ref[i] = a
        s16 = nt(u16, a)
        s = s16[0:HEADS] + s16[HEADS:]
        keep = valid if a.shape[0] != GRID_LARGE**2 else a.shape[0]
        if keep < a.shape[0]:
            s = jnp.where(lax.broadcasted_iota(jnp.int32, s.shape, 1) < keep, s, NEG)
        top = jnp.maximum(jnp.max(s, -1, keepdims=True), s_cls)
        e = jnp.exp2(s - top)
        e_cls = jnp.exp2(s_cls - top)
        inverse = 1.0 / (jnp.sum(e, -1, keepdims=True) + e_cls)
        p, p_cls = e * inverse, e_cls * inverse
        p_ref[i] = p
        low, low_cls = p.astype(bf16), p_cls.astype(bf16).astype(f32)
        z_ref[pl.ds(slot * HEADS, HEADS), :] = nn(low, a) + low_cls * a_cls_f
        ps_ref[pl.ds(slot * HEADS, HEADS), :] = jnp.sum(low.astype(f32), -1, keepdims=True) + low_cls
        pc_ref[pl.ds(slot * HEADS, HEADS), :] = p_cls

    for i in range(ns):
        forward(i, out_s, a_s, p_s, i)
    for i in range(nl):
        forward(i, out_l, a_l, p_l, ns + i)

    z_hi, z_lo = split(z_ref[...])
    o_all = nn(jnp.concatenate([z_hi, z_lo], 0), wkv[:, D:])
    o_all = o_all[0 : HEADS * BATCH] + o_all[HEADS * BATCH :] + ps_ref[...] * row(CBV)
    att = jnp.sum(jnp.where(mask64, o_all, 0.0).reshape(BATCH, HEADS, D), 1).astype(bf16)
    branch = nn(att, wo[...]) + row(CBO)
    mid = cls + row(CLS1) * branch
    unit_mid, inv_mid = stats(mid)
    n2 = (unit_mid * row(CG2) + row(CB2)).astype(bf16)
    upper = nn(n2, w1[...]) + c1[...]
    act, slope = gelu_pair(upper)
    act = act.astype(bf16)
    lower = nn(act, w2[...]) + row(CC2)
    c_tok = mid + row(CLS2) * lower
    unit_c, inv_c = stats(c_tok)
    final = (unit_c * svec[2:3, :] + svec[3:4, :]).astype(bf16)
    logits = nn(final, head_w[...]) + head_b[...]
    lane = lax.broadcasted_iota(jnp.int32, logits.shape, 1)
    inside = lane < CLASSES
    logits = jnp.where(inside, logits, NEG)
    shifted = logits - jnp.max(logits, -1, keepdims=True)
    raw = jnp.exp(shifted)
    weight = jnp.sum(raw, -1, keepdims=True)
    logp = shifted - jnp.log(weight)
    image = lax.broadcasted_iota(jnp.int32, (BATCH, 1), 0)
    label = jnp.zeros((BATCH, 1), jnp.int32)
    for i in range(ns):
        label = jnp.where(image == i, labels_s[i], label)
    for i in range(nl):
        label = jnp.where(image == ns + i, labels_l[i], label)
    alive = ((image < ns) & (image < counts[0, 0])) | ((image >= ns) & (image - ns < counts[0, 1]))
    hit = lane == label
    picked = jnp.sum(jnp.where(hit, logp, 0.0), -1, keepdims=True)
    mean = jnp.sum(jnp.where(inside, logp, 0.0), -1, keepdims=True) * (1.0 / CLASSES)
    each = -((1.0 - smooth) * picked + smooth * mean)
    scaled = jnp.where(alive, 1.0, 0.0) / total[0:1, 0:1]
    loss_o[...] = jnp.broadcast_to(colsum(scaled * each), loss_o.shape)
    target = jnp.where(hit, 1.0 - smooth, 0.0) + smooth / CLASSES
    d_logits = jnp.where(inside, scaled * (raw / weight - target), 0.0).astype(bf16)

    d_final = nt(d_logits, head_w[...])
    g_head_w[...] = tn(final, d_logits)
    g_head_b[...] = colsum(d_logits.astype(f32))
    g_svec[...] = jnp.zeros_like(g_svec)
    g_svec[2:3, :] = colsum(d_final * unit_c)
    g_svec[3:4, :] = colsum(d_final)
    d_c = norm_back(d_final, unit_c, inv_c, svec[2:3, :])
    g_vec[...] = jnp.zeros_like(g_vec)
    g_vec[CLS2 : CLS2 + 1, :] = colsum(d_c * lower)
    d_lower = (d_c * row(CLS2)).astype(bf16)
    g_vec[CC2 : CC2 + 1, :] = colsum(d_lower.astype(f32))
    g_w2[...] = tn(act, d_lower)
    d_upper = (slope * nt(d_lower, w2[...])).astype(bf16)
    g_c1[...] = colsum(d_upper.astype(f32))
    g_w1[...] = tn(n2, d_upper)
    d_n2 = nt(d_upper, w1[...])
    g_vec[CG2 : CG2 + 1, :] = colsum(d_n2 * unit_mid)
    g_vec[CB2 : CB2 + 1, :] = colsum(d_n2)
    d_mid = d_c + norm_back(d_n2, unit_mid, inv_mid, row(CG2))
    g_vec[CLS1 : CLS1 + 1, :] = colsum(d_mid * branch)
    d_branch = (d_mid * row(CLS1)).astype(bf16)
    g_vec[CBO : CBO + 1, :] = colsum(d_branch.astype(f32))
    g_wo[...] = tn(att, d_branch)
    d_att = nt(d_branch, wo[...]).astype(bf16).astype(f32)
    d_diag = jnp.where(mask64, jnp.broadcast_to(d_att[:, None, :], (BATCH, HEADS, D)).reshape(BATCH * HEADS, D), 0.0)
    g_vec[CBV : CBV + 1, :] = colsum(d_diag * ps_ref[...])
    shift = jnp.sum(d_diag * row(CBV), -1, keepdims=True)
    d_diag_low = d_diag.astype(bf16)
    y_ref[...] = nt(d_diag_low, wkv[:, D:])
    g_wkv[:, D:] = tn(jnp.concatenate([z_hi, z_lo], 0), jnp.concatenate([d_diag_low, d_diag_low], 0))
    z_ref[:, 0:1] = shift
    b_ref[...] = jnp.zeros_like(b_ref)
    da_ref[...] = jnp.zeros_like(da_ref)
    un_hi, un_lo = split(u_nat)

    def backward(i, src, a_ref, p_ref, d_ref, slot):
        unit, inverse = stats(src[i])
        a = a_ref[i]
        here = pl.ds(slot * HEADS, HEADS)
        y = y_ref[here, :]
        y_hi, y_lo = split(y)
        d16 = nt(jnp.concatenate([y_hi, y_lo], 0), a)
        offset = z_ref[here, 0:1]
        d_p = d16[0:HEADS] + d16[HEADS:] + offset
        d_p_cls = jnp.sum(y * a_cls_f, -1, keepdims=True) + offset
        p, p_cls = p_ref[i], pc_ref[here, :]
        delta = jnp.sum(p * d_p, -1, keepdims=True) + p_cls * d_p_cls
        d_score = (p * (d_p - delta)).astype(bf16)
        d_score_cls = (p_cls * (d_p_cls - delta)).astype(bf16).astype(f32)
        low = p.astype(bf16)
        b_ref[...] += nn(d_score, a) + d_score_cls * a_cls_f
        da_ref[...] += d_score_cls * u_nat + p_cls.astype(bf16).astype(f32) * y
        left = jnp.concatenate([d_score.astype(f32), d_score.astype(f32), low.astype(f32), low.astype(f32)], 0)
        d_a = tn(left.astype(bf16), jnp.concatenate([un_hi, un_lo, y_hi, y_lo], 0))
        g_vec[CG1 : CG1 + 1, :] += colsum(d_a * unit)
        g_vec[CB1 : CB1 + 1, :] += colsum(d_a)
        d_ref[i] = norm_back(d_a, unit, inverse, row(CG1))

    for i in range(ns):
        backward(i, out_s, a_s, p_s, d_s, i)
    for i in range(nl):
        backward(i, out_l, a_l, p_l, d_l, ns + i)

    b_hi, b_lo = split(b_ref[...])
    bw = nn(jnp.concatenate([b_hi, b_lo], 0), wkv[:, 0:D])
    bw = bw[0:HEADS] + bw[HEADS:]
    d_query = (colsum(jnp.where(mask8, bw, 0.0)) * SCALE).astype(bf16)
    g_vec[CBQ : CBQ + 1, :] = d_query.astype(f32)
    q_scaled = q_diag.astype(f32) * SCALE
    qs_hi, qs_lo = split(q_scaled)
    g_wkv[:, 0:D] = tn(
        jnp.concatenate([b_hi, b_hi, b_lo, b_lo], 0), jnp.concatenate([qs_hi, qs_lo, qs_hi, qs_lo], 0)
    )
    first = lax.broadcasted_iota(jnp.int32, (16, D), 0) == 0
    spread_a = jnp.where(first, jnp.broadcast_to(a_cls_f, (16, D)), 0.0).astype(bf16)
    spread_q = jnp.where(first, jnp.broadcast_to(d_query.astype(f32), (16, D)), 0.0).astype(bf16)
    g_wq[...] = tn(spread_a, spread_q)
    d_a_cls = colsum(da_ref[...]) + nt(d_query, wq[...])
    g_vec[CG1 : CG1 + 1, :] += d_a_cls * unit_cls
    g_vec[CB1 : CB1 + 1, :] += d_a_cls
    g_svec[1:2, :] = colsum(d_mid) + norm_back(d_a_cls, unit_cls, inv_cls, row(CG1))


def class_block(out_s, out_l, classw, stem, total, counts, labels_s, labels_l, valid):
    ns, padded, _ = out_s.shape
    nl, large_len, _ = out_l.shape
    wq, wkv, wo, w1, w2, vec, c1 = classw
    _, svec, _, _, head_w, head_b = stem
    args = (out_s, out_l, wq, wkv, wo, w1, w2, vec, c1, svec, head_w, head_b, total, counts, labels_s, labels_l)
    return pl.pallas_call(
        functools.partial(class_kernel, ns, nl, valid),
        out_shape=[
            sds((ns, padded, D), f32),
            sds((nl, large_len, D), f32),
            sds((D, D), f32),
            sds((D, 2 * D), f32),
            sds((D, D), f32),
            sds((D, FF), f32),
            sds((FF, D), f32),
            sds((16, D), f32),
            sds((1, FF), f32),
            sds((8, D), f32),
            sds((D, CLASS_PAD), f32),
            sds((1, CLASS_PAD), f32),
            sds((1, LANES), f32),
        ],
        in_specs=[VM] * (len(args) - 3) + [SM] * 3,
        out_specs=[VM] * 13,
        scratch_shapes=[
            pltpu.VMEM((ns, padded, D), bf16),
            pltpu.VMEM((nl, large_len, D), bf16),
            pltpu.VMEM((ns, HEADS, padded), f32),
            pltpu.VMEM((nl, HEADS, large_len), f32),
            pltpu.VMEM((BATCH * HEADS, D), f32),
            pltpu.VMEM((BATCH * HEADS, D), f32),
            pltpu.VMEM((HEADS, D), f32),
            pltpu.VMEM((BATCH * HEADS, 1), f32),
            pltpu.VMEM((BATCH * HEADS, 1), f32),
            pltpu.VMEM((HEADS, D), f32),
        ],
        compiler_params=params(),
        cost_estimate=pl.CostEstimate(flops=10_000_000_000, bytes_accessed=60_000_000, transcendentals=0),
        name="class_block",
    )(*args)


def feed_back_kernel(steps, *refs):
    ins, (wo, w1, w2, vec), refs = [refs[2 * i : 2 * i + 2] for i in range(7)], refs[14:18], refs[18:]
    d_mid_o, d_att_o, sums = refs[:2], refs[2:4], refs[4:]
    g_wo, g_w1, g_w2, g_vec, g_c1 = sums
    row = lambda at: vec[at : at + 1, :]

    @pl.when(pl.program_id(0) == 0)
    def _():
        for ref in sums:
            ref[...] = jnp.zeros_like(ref)

    def add(at, value):
        g_vec[at : at + 1, :] += value

    d_out_r, mid_r, act_r, slope_r, lower_r, branch_r, att_r = ins
    d_out = steps.join(d_out_r)
    add(SLS2, colsum(d_out * steps.join(lower_r).astype(f32)))
    d_lower = (d_out * row(SLS2)).astype(bf16)
    add(SC2, colsum(d_lower.astype(f32)))
    unit, inverse = stats(steps.join(mid_r))
    n2 = (unit * row(SG2) + row(SB2)).astype(bf16)
    g_w2[...] += tn(steps.join(act_r), d_lower)
    d_upper = (nt(d_lower, w2[...]) * steps.join(slope_r).astype(f32)).astype(bf16)
    g_w1[...] += tn(n2, d_upper)
    g_c1[...] += colsum(d_upper.astype(f32))
    d_n2 = nt(d_upper, w1[...])
    add(SG2, colsum(d_n2 * unit))
    add(SB2, colsum(d_n2))
    d_mid = d_out + norm_back(d_n2, unit, inverse, row(SG2))
    steps.put(d_mid_o, d_mid)
    add(SLS1, colsum(d_mid * steps.join(branch_r).astype(f32)))
    d_branch = (d_mid * row(SLS1)).astype(bf16)
    add(SBO, colsum(d_branch.astype(f32)))
    g_wo[...] += tn(steps.join(att_r), d_branch)
    steps.put(d_att_o, nt(d_branch, wo[...]).astype(bf16))


def sum_specs(shapes):
    return [pl.BlockSpec(s.shape, lambda i: (0, 0), pipeline_mode=pl.Buffered(1)) for s in shapes]


def feed_back(pairs, weights, after):
    (ns, padded, _), (nl, large_len, _) = pairs[0][0].shape, pairs[0][1].shape
    steps = Steps(ns, nl, padded, large_len)
    sums = [sds((D, D), f32), sds((D, FF), f32), sds((FF, D), f32), sds((16, D), f32), sds((1, FF), f32)]
    out = call(
        functools.partial(feed_back_kernel, steps),
        (*[a for pair in pairs for a in pair], *weights),
        after,
        grid=steps.grid,
        out_shape=steps.shapes(D, f32) + steps.shapes(D, bf16) + sums,
        in_specs=[spec for pair in pairs for spec in steps.specs(pair[0].shape[2])] + [const_spec(a) for a in weights],
        out_specs=steps.specs(D) * 2 + sum_specs(sums),
        cost_estimate=cost(35e9, 30e6),
        name="feed_back",
    )
    return out[:2], out[2:4], out[4:]


def attend_back_kernel(valid, qkv_ref, d_att_ref, lse_ref, pre_col, post_col, pre_row, post_row, d_qkv_ref, g_pre, g_post,
                       q_t, kk, k_t, do_t, dq_t, d_k, d_v):
    per, length = qkv_ref.shape[0], qkv_ref.shape[1]
    for i in range(per):
        q_t[i] = qkv_ref[i, :, 0:D].astype(f32).T
        kk[i, :, 0:D] = qkv_ref[i, :, D : 2 * D]
        kk[i, :, D:] = qkv_ref[i, :, D : 2 * D]
        k_t[i] = qkv_ref[i, :, D : 2 * D].astype(f32).T.astype(bf16)
        do_t[i] = d_att_ref[i].astype(f32).T

    @pl.when(pl.program_id(0) == 0)
    def _():
        g_pre[...] = jnp.zeros_like(g_pre)
        g_post[...] = jnp.zeros_like(g_post)

    for g in range(HEADS):
        pre, post = pre_col[:, g : g + 1], post_col[:, g : g + 1]
        for i in range(per):
            q, k, v = qkv_ref[i, :, 0:D], qkv_ref[i, :, D : 2 * D], qkv_ref[i, :, 2 * D :]
            high, low = split(q_t[i] * pre)
            mixed = nn(kk[i], jnp.concatenate([high, low], 0))
            d_p = nn(v, (do_t[i] * post).astype(bf16))
            p = jnp.exp2(mixed - lse_ref[i, g : g + 1, :])
            if valid < length:
                p = jnp.where(lax.broadcasted_iota(jnp.int32, p.shape, 0) < valid, p, 0.0)
            delta = colsum(p * d_p)
            d_mixed = (p * (d_p - delta)).astype(bf16)
            r = nn(p.astype(bf16), d_att_ref[i])
            t = nn(d_mixed, q)
            u = nn(k_t[i], d_mixed)
            d_v_part, d_k_part, d_q_part = r * post_row[g : g + 1, :], t * pre_row[g : g + 1, :], u * pre
            d_v[i] = d_v_part if g == 0 else d_v[i] + d_v_part
            d_k[i] = d_k_part if g == 0 else d_k[i] + d_k_part
            dq_t[i] = d_q_part if g == 0 else dq_t[i] + d_q_part
            g_post[g : g + 1, :] += colsum(r * v.astype(f32))
            g_pre[g : g + 1, :] += colsum(t * k.astype(f32))
    inverse = 1.0 / LOG2E
    for i in range(per):
        d_qkv_ref[i, :, 0:D] = (dq_t[i].T * inverse).astype(bf16)
        d_qkv_ref[i, :, D : 2 * D] = (d_k[i] * inverse).astype(bf16)
        d_qkv_ref[i, :, 2 * D :] = d_v[i].astype(bf16)


def attend_back(qkv, d_att, lse, mixes, valid, first, count, per, flops, after):
    length = qkv.shape[1]
    spec = lambda *tail: pl.BlockSpec((per,) + tail, lambda i: (i + first // per, 0, 0))
    sums = [sds((HEADS, D), f32)] * 2
    return call(
        functools.partial(attend_back_kernel, valid),
        (qkv, d_att, lse, *mixes),
        after,
        grid=(count // per,),
        out_shape=[sds((count, length, 3 * D), bf16)] + sums,
        in_specs=[spec(length, 3 * D), spec(length, D), spec(HEADS, length)] + [const_spec(a) for a in mixes],
        out_specs=[pl.BlockSpec((per, length, 3 * D), lambda i: (i, 0, 0))] + sum_specs(sums),
        scratch_shapes=[
            pltpu.VMEM((per, D, length), f32),
            pltpu.VMEM((per, length, 2 * D), bf16),
            pltpu.VMEM((per, D, length), bf16),
            pltpu.VMEM((per, D, length), f32),
            pltpu.VMEM((per, D, length), f32),
            pltpu.VMEM((per, length, D), f32),
            pltpu.VMEM((per, length, D), f32),
        ],
        cost_estimate=cost(flops, 10e6),
        name="attend_back",
    )


def embed_back_kernel(steps, valid, ps, plg, resize, *refs):
    tok_r, dq_s, d_mid_r, refs = refs[:2], refs[2], refs[3:5], refs[5:]
    dq_l, (wqkv, vec), refs = refs[: steps.large * steps.count], refs[steps.large * steps.count :][:2], refs[steps.large * steps.count + 2 :]
    g_wqkv, g_vec, g_patch_w, g_patch_b, g_pos, pos_large, d_qkv = refs
    row = lambda at: vec[at : at + 1, :]
    step = pl.program_id(0)

    @pl.when(step == 0)
    def _():
        for ref in refs[:-1]:
            ref[...] = jnp.zeros_like(ref)

    d_qkv[: steps.split, :] = dq_s[...].reshape(steps.split, 3 * D)
    for k in range(steps.count):

        @pl.when(step == k)
        def _(k=k):
            for i in range(steps.large):
                base = steps.split + steps.large_len * i
                d_qkv[base : base + steps.large_len, :] = dq_l[k * steps.large + i][0]

    def add(at, value):
        g_vec[at : at + 1, :] += value

    add(SBQ, colsum(d_qkv[:, 0:D].astype(f32)))
    add(SBV, colsum(d_qkv[:, 2 * D :].astype(f32)))
    unit, inverse = stats(steps.join(tok_r))
    a1 = (unit * row(SG1) + row(SB1)).astype(bf16)
    g_wqkv[...] += tn(a1, d_qkv[...])
    d_a1 = nt(d_qkv[...], wqkv[...])
    add(SG1, colsum(d_a1 * unit))
    add(SB1, colsum(d_a1))
    d_tok = steps.join(d_mid_r) + norm_back(d_a1, unit, inverse, row(SG1))
    g_patch_b[0:1, :] += colsum(d_tok)
    for i in range(steps.small):
        mine = d_tok[steps.padded * i : steps.padded * i + valid, :]
        g_pos[...] += mine
        g_patch_w[...] += tn(ps[i], mine.astype(bf16))
    for i in range(steps.large):
        base = steps.split + steps.large_len * i
        mine = d_tok[base : base + steps.large_len, :]
        pos_large[...] += mine
        g_patch_w[...] += tn(plg[i], mine.astype(bf16))

    @pl.when(step == steps.count - 1)
    def _():
        g_pos[...] += lax.dot_general(
            resize[...], pos_large[...], (((1,), (0,)), ((), ())),
            preferred_element_type=f32, precision=lax.Precision.HIGHEST,
        )


def embed_back(ps, plg, tok, dq_s, d_mid, dq_l, wqkv, vec, after):
    ns, valid, _ = ps.shape
    nl, large_len, _ = plg.shape
    steps = Steps(ns, nl, tok[0].shape[1], large_len)
    resize = jnp.asarray(resize_table().T.copy())
    sums = [
        sds((D, 3 * D), f32),
        sds((16, D), f32),
        sds((PATCH_IN, D), f32),
        sds((8, D), f32),
        sds((valid, D), f32),
    ]
    index = lambda i: (i, 0, 0)
    return call(
        functools.partial(embed_back_kernel, steps, valid),
        (ps, plg, resize, *tok, dq_s, *d_mid, *dq_l, wqkv, vec),
        after,
        grid=steps.grid,
        out_shape=sums,
        in_specs=[
            pl.BlockSpec((steps.small, valid, PATCH_IN), index),
            pl.BlockSpec((steps.large, large_len, PATCH_IN), index),
            const_spec(resize),
            *steps.specs(D),
            steps.specs(3 * D)[0],
            *steps.specs(D),
        ]
        + [const_spec(a) for a in dq_l]
        + [const_spec(wqkv), const_spec(vec)],
        out_specs=sum_specs(sums),
        scratch_shapes=[pltpu.VMEM((large_len, D), f32), pltpu.VMEM((steps.rows, 3 * D), bf16)],
        cost_estimate=cost(20e9, 30e6),
        name="embed_back",
    )


def take_matrix(flat, row, src, rows, cols):
    step = cols // LANES
    for j in range(step):
        flat[pl.ds(row + j, rows, stride=step), :] = src[0:rows, LANES * j : LANES * (j + 1)]


def take_row(flat, row, src, at, cols):
    for j in range(cols // LANES):
        flat[row + j : row + j + 1, :] = src[at : at + 1, LANES * j : LANES * (j + 1)]


def slots_of(order):
    rels = [0]
    for bit in reversed(order):
        rels = rels + [r | (1 << bit) for r in rels]
    return rels


def emit_slots(me, flat, rows, rels, keep_ref, send_ref, offset=0):
    half = len(rels) // 2
    for k, r in enumerate(rels):
        value = flat[pl.ds(offset + rows * jnp.bitwise_xor(me, r), keep_ref.shape[1]), :]
        if k < half:
            keep_ref[k] = value
        else:
            send_ref[k - half] = value.astype(bf16)


def pack_class_kernel(rels, rows, me_ref, wq, wkv, wo, w1, w2, vec, c1, keep, send, flat):
    used = rows_used(2)
    flat[used:, :] = jnp.zeros((flat.shape[0] - used, LANES), f32)
    take_matrix(flat, row_of(2, 2), wq, D, D)
    take_matrix(flat, row_of(2, 4), wkv, D, 2 * D)
    take_matrix(flat, row_of(2, 6), wo, D, D)
    take_matrix(flat, row_of(2, 11), w1, D, FF)
    take_matrix(flat, row_of(2, 13), w2, FF, D)
    for at, number in (
        (CG1, 0), (CB1, 1), (CBQ, 3), (CBV, 5), (CBO, 7), (CLS1, 8), (CG2, 9), (CB2, 10), (CC2, 14), (CLS2, 15),
    ):
        take_row(flat, row_of(2, number), vec, at, D)
    take_row(flat, row_of(2, 12), c1, 0, FF)
    emit_slots(me_ref[0], flat, rows, rels, keep, send)


def take_head(flat, base, head_w, head_b, tiles, groups):
    for t in range(8):
        tiles[t] = head_w[:, LANES * t : LANES * (t + 1)]
    lane = lax.broadcasted_iota(jnp.int32, (groups, LANES), 1)
    for rho in range(16):
        first, shift = (CLASSES * rho) // LANES, (CLASSES * rho) % LANES
        parts = [tiles[t, pl.ds(rho, groups, stride=16), :] for t in range(8)]
        if shift:
            parts = [pltpu.roll(p, shift, 1) for p in parts]
        for t in range(9 if shift + CLASSES > CLASS_PAD else 8):
            if shift:
                value = jnp.where(lane >= shift, parts[t] if t < 8 else 0.0, parts[t - 1] if t > 0 else 0.0)
            else:
                value = parts[t]
            here = pl.ds(base + first + t, groups, stride=125)
            flat[here, :] = flat[here, :] + value
    if head_b is not None:
        take_row(flat, base + row_of(0, 7) - row_of(0, 6), head_b, 0, CLASS_PAD)


HEAD_GROUPS = D // 16


def pack_feed_kernel(rels, rows, offset, quarter_rows, me_ref, wo, w1, w2, vec, c1, head_w, head_b, keep, send, flat, tiles):
    used, first = rows_used(1), row_of(1, 6)
    flat[0 : offset + first, :] = jnp.zeros((offset + first, LANES), f32)
    flat[offset + used :, :] = jnp.zeros((flat.shape[0] - used - offset, LANES), f32)
    take_head(flat, offset + row_of(0, 6) - quarter_rows, head_w, head_b, tiles, HEAD_GROUPS)
    boundary = quarter_rows - first
    flat[offset + first : offset + quarter_rows, :] = jnp.zeros((boundary, LANES), f32)
    take_matrix(flat, offset + first, wo, D, D)
    flat[offset + first : offset + quarter_rows, :] = jnp.zeros((boundary, LANES), f32)
    take_matrix(flat, offset + row_of(1, 11), w1, D, FF)
    take_matrix(flat, offset + row_of(1, 13), w2, FF, D)
    for at, number in ((SBO, 7), (SLS1, 8), (SG2, 9), (SB2, 10), (SC2, 14), (SLS2, 15)):
        take_row(flat, offset + row_of(1, number), vec, at, D)
    take_row(flat, offset + row_of(1, 12), c1, 0, FF)
    emit_slots(me_ref[0], flat, rows, rels, keep, send, offset)


def pack_late_kernel(
    rels, rows, quarter_rows, me_ref, wqkv, vec, pre, post, wo, patch_w, patch_b, pos, svec, head_w, keep, send, flat, tiles
):
    padded_rows = keep.shape[1] // 2
    for g in range(2):
        pack_late_group(g, quarter_rows, wqkv, vec, pre, post, wo, patch_w, patch_b, pos, svec, head_w, flat, tiles)
        here = pl.ds(g * padded_rows, padded_rows)
        emit_slots(me_ref[0], flat, rows, rels, keep.at[:, here], send.at[:, here])


def pack_late_group(g, quarter_rows, wqkv, vec, pre, post, wo, patch_w, patch_b, pos, svec, head_w, flat, tiles):
    if g == 0:
        first = row_of(0, 6)
        flat[first:, :] = jnp.zeros((flat.shape[0] - first, LANES), f32)
        take_matrix(flat, row_of(0, 0), patch_w, PATCH_IN, D)
        take_row(flat, row_of(0, 1), patch_b, 0, D)
        take_matrix(flat, row_of(0, 2), pos, GRID_SMALL**2, D)
        for at, number in ((1, 3), (2, 4), (3, 5)):
            take_row(flat, row_of(0, number), svec, at, D)
        take_head(flat, first, head_w, None, tiles, 8)
        return
    first = row_of(1, 6)
    take_matrix(flat, row_of(1, 2), wqkv, D, 3 * D)
    take_matrix(flat, first, wo, 24, D)
    bq = row_of(1, 3)
    for at, row in ((SG1, row_of(1, 0)), (SB1, row_of(1, 1)), (SBQ, bq), (SBV, bq + D // LANES)):
        take_row(flat, row, vec, at, D)
    table_col = lax.broadcasted_iota(jnp.int32, (D, LANES), 0) // WIDTH
    table_lane = lax.broadcasted_iota(jnp.int32, (D, LANES), 1)
    lane = lax.broadcasted_iota(jnp.int32, (HEADS, LANES), 1)
    row = lax.broadcasted_iota(jnp.int32, (HEADS, LANES), 0)
    exact = lambda a, b: lax.dot_general(
        a, b, (((1,), (0,)), ((), ())), preferred_element_type=f32, precision=lax.Precision.HIGHEST
    )
    sum_pre = exact(pre[...], jnp.where(table_lane % HEADS == table_col, 1.0, 0.0))
    sum_post = exact(post[...], jnp.where((table_lane - 64) // HEADS == table_col, 1.0, 0.0))
    line = colsum(jnp.where((lane < 64) & (lane // HEADS == row), sum_pre * SCALE, 0.0))
    line = line + colsum(jnp.where((lane >= 64) & (lane % HEADS == row), sum_post, 0.0))
    flat[row_of(1, 4) : row_of(1, 4) + 1, :] = line


def pack(kernel, name, me, arrays, rels, padded_rows, flat_rows, extra=()):
    half = len(rels) // 2
    return pl.pallas_call(
        kernel,
        out_shape=[sds((half, padded_rows, LANES), f32), sds((half, padded_rows, LANES), bf16)],
        in_specs=[SM] + [VM] * len(arrays),
        out_specs=[VM] * 2,
        scratch_shapes=[pltpu.VMEM((flat_rows, LANES), f32), *extra],
        compiler_params=params(),
        name=name,
    )(me, *arrays)


class Chain:
    def __init__(self, keep, send, order, z_bits, z_last=False):
        self.keep, self.send, self.order, self.z_bits, self.z_last = keep, send, list(order), z_bits, z_last
        self.total = None
        self.done = False

    def finish(self, total):
        self.total = self.send = total
        self.done = True

    def step(self, after=None):
        if self.order:
            (got,) = tied((exchange(self.send, self.order.pop(0), self.z_bits),), after)
            total = self.keep + got.astype(f32)
            if self.order:
                half = total.shape[0] // 2
                self.keep, self.send = total[:half], total[half:].astype(bf16)
            elif self.z_last:
                self.keep, self.send = total[0], total[1:].astype(bf16)
            else:
                self.finish(total[0])
        elif not self.done:
            got = [exchange_z(self.send[k - 1], k) for k in range(1, self.send.shape[0] + 1)]
            total = self.keep
            for part in tied(tuple(got), after):
                total = total + part.astype(f32)
            self.finish(total)


def bounds_table():
    table = np.zeros((8, LANES), np.int32)
    table[0:3, :SEGMENTS] = STARTS // 64
    table[3:6, :SEGMENTS] = -(-ENDS // 64)
    return table


def pick(group, values):
    return jnp.where(group == 0, values[0], jnp.where(group == 1, values[1], values[2]))


def segment_sums(square, group, first_row, bounds):
    rows = square.shape[0]
    lane = lax.broadcasted_iota(jnp.int32, (rows, LANES), 1)
    left = jnp.sum(jnp.where(lane < 64, square, 0.0), -1, keepdims=True)
    right = jnp.sum(jnp.where(lane < 64, 0.0, square), -1, keepdims=True)
    place = 2 * (first_row + lax.broadcasted_iota(jnp.int32, (rows, LANES), 0))
    low, high = bounds[group : group + 1, :], bounds[3 + group : 4 + group, :]
    one = jnp.where((place >= low) & (place < high), left, 0.0)
    two = jnp.where((place + 1 >= low) & (place + 1 < high), right, 0.0)
    return colsum(one + two)


def adam_kernel(rows, me_ref, step_ref, bounds, master, first, second, g0, g1, g2, grad_o, first_o, second_o, update_o, sums_o):
    shard = rows * LANES
    for g, ref in enumerate((g0, g1, g2)):
        grad_o[g : g + 1, :] = ref[0:rows, :].reshape(1, shard)
    grad = grad_o[...]
    weight = master[...]
    new_first = beta_one * first[...] + (1.0 - beta_one) * grad
    new_second = beta_two * second[...] + (1.0 - beta_two) * grad * grad
    first_o[...] = new_first
    second_o[...] = new_second
    power = jnp.full((1, LANES), step_ref[0], jnp.int32).astype(f32)
    scale_one = (1.0 / (1.0 - jnp.power(f32(beta_one), power)))[:, 0:1]
    scale_two = (1.0 / (1.0 - jnp.power(f32(beta_two), power)))[:, 0:1]
    update = new_first * scale_one / (jnp.sqrt(new_second * scale_two) + adam_eps) + decay_rate * weight
    update_o[...] = update
    sums_o[...] = jnp.zeros_like(sums_o)
    first_row = me_ref[0] * rows
    for g in range(3):
        part = update_o[g : g + 1, :].reshape(rows, LANES)
        sums_o[3 + g : 4 + g, :] = segment_sums(part * part, g, first_row, bounds)


def adam(me, step, master, first, second, grads, rows):
    shape = master.shape
    return pl.pallas_call(
        functools.partial(adam_kernel, rows),
        out_shape=[sds(shape, f32)] * 4 + [sds((8, LANES), f32)],
        in_specs=[SM, SM] + [VM] * 7,
        out_specs=[VM] * 5,
        compiler_params=params(),
        name="adam",
    )(me, step, jnp.asarray(bounds_table()), master, first, second, *grads)


def apply_kernel(me_ref, sums, master, update, new_o, weight_o, norm_o, trust_o):
    shard = master.shape[1]
    roots = jnp.sqrt(sums[...])
    weight_norms, update_norms = roots[0:3, :], roots[3:6, :]
    lane = lax.broadcasted_iota(jnp.int32, (3, LANES), 1)
    group3 = lax.broadcasted_iota(jnp.int32, (3, LANES), 0)
    used = pick(group3, [int(REAL[g].sum()) for g in range(3)])
    trust = jnp.where(lane < used, weight_norms / (update_norms + norm_eps), 1.0)
    weight_o[...] = weight_norms[:, 0:SEGMENTS]
    norm_o[...] = update_norms[:, 0:SEGMENTS]
    trust_o[...] = trust[:, 0:SEGMENTS]
    position = me_ref[0] * shard + lax.broadcasted_iota(jnp.int32, (3, shard), 1)
    group = lax.broadcasted_iota(jnp.int32, (3, 1), 0)
    ratio = jnp.broadcast_to(trust[:, 0:1], (3, shard))
    for s in range(1, SEGMENTS):
        low = pick(group, [int(STARTS[g, s]) if REAL[g, s] > 0 else 2**30 for g in range(3)])
        ratio = jnp.where(position >= low, trust[:, s : s + 1], ratio)
    new_o[...] = master[...] - learn_rate * ratio * update[...]


def apply_update(me, sums, master, update):
    return pl.pallas_call(
        apply_kernel,
        out_shape=[sds(master.shape, f32)] + [sds((3, SEGMENTS), f32)] * 3,
        in_specs=[SM] + [VM] * 3,
        out_specs=[VM] * 4,
        compiler_params=params(),
        name="apply_update",
    )(me, sums, master, update)


def round_kernel(rows, counts, master, stem, selfb, classb):
    for g, ref in enumerate((stem, selfb, classb)):
        ref[0, 0:rows, :] = master[g : g + 1, :].reshape(rows, LANES).astype(bf16)
        tail = ref.shape[1] - rows
        count = counts[0, 0] + counts[0, 1] if g == 2 else 0
        ref[0, rows:, :] = jnp.full((tail, LANES), count, jnp.int32).astype(f32).astype(bf16)


def round_shards(counts, master, rows, padded_rows):
    return pl.pallas_call(
        functools.partial(round_kernel, rows),
        out_shape=[sds((1, padded_rows, LANES), bf16)] * 3,
        in_specs=[SM, VM],
        out_specs=[VM] * 3,
        compiler_params=params(),
        name="round_shards",
    )(counts, master)


def weight_kernel(rows, me_ref, bounds, master, sums_o):
    sums_o[...] = jnp.zeros_like(sums_o)
    for g in range(3):
        part = master[g : g + 1, :].reshape(rows, LANES)
        sums_o[g : g + 1, :] = segment_sums(part * part, g, me_ref[0] * rows, bounds)


def weight_sums(me, master, rows):
    return pl.pallas_call(
        functools.partial(weight_kernel, rows),
        out_shape=sds((8, LANES), f32),
        in_specs=[SM, VM, VM],
        out_specs=VM,
        compiler_params=params(),
        name="weight_sums",
    )(me, jnp.asarray(bounds_table()), master)


def on_device(
    master,
    first_moment,
    second_moment,
    patches_small,
    patches_large,
    labels_small,
    labels_large,
    counts,
    step,
):
    rows = master.shape[1] // LANES
    padded_rows = -(-(rows + 1) // 8) * 8
    n_dp, n_z = lax.axis_size("dp"), lax.axis_size("fsdp")
    z_bits, bits = log2(n_z), log2(n_dp) + log2(n_z)
    devices = n_dp * n_z
    half, quarter = devices // 2, devices // 4
    assert row_of(0, 7) + CLASS_PAD // LANES <= half * rows
    assert row_of(1, 6) <= quarter * rows <= row_of(1, 6) + 64
    ns, valid, _ = patches_small.shape
    nl = patches_large.shape[0]
    padded = -(-valid // 16) * 16
    small_per = 2 if ns % 2 == 0 else 1
    me = lax.axis_index(AXES).astype(jnp.int32).reshape(1)
    me_half = jnp.bitwise_and(me, half - 1)
    me_quarter = jnp.bitwise_and(me, quarter - 1)
    dp = lax.axis_index("dp")
    n_quarter = n_dp // 4
    in_half, quarter_id = dp < n_dp // 2, dp // n_quarter

    core, second, top = z_bits, bits - 2, bits - 1
    inner = list(range(core + 1, second))
    arrays = lambda state: ([a for a, _ in state], [r for _, r in state])

    old_sums = weight_sums(me, master, rows)
    stem_shard, self_shard, class_shard = round_shards(counts, master, rows, padded_rows)
    up = n_dp // 2
    got = lax.ppermute(stem_shard, "dp", [(i, i + up) for i in range(up)])
    others = [lax.ppermute(self_shard, "dp", [(i, i ^ (a * n_quarter)) for i in range(n_dp)]) for a in (1, 2, 3)]
    stem_state = gather_z(jnp.where(in_half, stem_shard, got), [0])

    def of_quarter(b):
        value = self_shard
        for a in (1, 2, 3):
            value = jnp.where(quarter_id == (a ^ b), others[a - 1], value)
        return value

    first_state = gather_z(of_quarter(0), [0])
    rest = jnp.concatenate([of_quarter(b) for b in (1, 2, 3)], 0)
    for bit in inner:
        first_state = gather_bit(first_state, bit, z_bits)
    for bit in [*inner, second]:
        stem_state = gather_bit(stem_state, bit, z_bits)
    rest, class_shard, _ = lax.optimization_barrier((rest, class_shard, first_state[0][0]))
    first_state = gather_bit(first_state, core, z_bits)
    stem_state = gather_bit(stem_state, core, z_bits)
    class_all = lax.all_gather(class_shard[0], AXES, axis=0, tiled=False)

    patch_w, svec, pos_small, pos_large, head_w, head_b = stem = unpack_stem(
        me_half, *arrays(stem_state), rows, half, padded
    )
    wqkv, vec, pre_col, post_col, pre_row, post_row = unpack_low(me_quarter, *arrays(first_state), rows, quarter)
    tok, (qkv_s, qkv_l) = embed(
        patches_small, patches_large, patch_w, pos_small, pos_large, wqkv, vec, padded, [old_sums]
    )
    att_s, lse_s = attend(qkv_s, pre_col, post_col, valid, small_per, 20e9, [])
    rest_state = gather_z(rest, [quarter, 2 * quarter, 3 * quarter], att_s)
    rest_all = rest_state[0][0]
    for bit in [*inner, core]:
        rest_state = gather_bit(rest_state, bit, z_bits)
    att_l, lse_l = attend(qkv_l, pre_col, post_col, qkv_l.shape[1], 1, 30e9, [rest_all, att_s])
    wo, w1, w2, vec_feed, c1 = unpack_feed(me_quarter, *arrays(first_state + rest_state), rows, devices)
    att = (att_s, att_l)
    branch, mid, act, slope, lower, out = feed(tok, att, (wo, w1, w2, vec_feed, c1), [])
    *classw, total = unpack_class(jnp.zeros_like(me), [class_all], [list(range(devices))], rows, devices)

    d_out_s, d_out_l, *class_grads, g_svec, g_head_w, g_head_b, loss = class_block(
        *out, classw, stem, total, counts, labels_small, labels_large, valid
    )

    z_order = list(range(z_bits - 1, -1, -1))
    near_far = list(range(z_bits))
    class_order = [core, top, second] + inner + near_far
    feed_order = [core] + near_far + [top, second] + inner
    class_rels, feed_rels = slots_of(class_order), slots_of(feed_order)
    tail = 8 * (padded_rows // 8 - rows // 8)

    class_chain = Chain(
        *pack(
            functools.partial(pack_class_kernel, class_rels, rows), "pack_class", me, class_grads, class_rels,
            padded_rows, devices * rows + tail,
        ),
        class_order, z_bits,
    )
    d_mid, (d_att_s, d_att_l), (g_wo, g_w1, g_w2, g_vec_feed, g_c1) = feed_back(
        ((d_out_s, d_out_l), mid, act, slope, lower, branch, att), (wo, w1, w2, vec_feed), [class_chain.send]
    )
    class_chain.step(d_att_s)
    quarter_rows = quarter * rows
    offset = -(-max(0, quarter_rows - row_of(0, 6)) // 8) * 8
    tiles = [pltpu.VMEM((8, D, LANES), f32)]
    feed_chain = Chain(
        *pack(
            functools.partial(pack_feed_kernel, feed_rels, rows, offset, quarter_rows), "pack_feed", me,
            (g_wo, g_w1, g_w2, g_vec_feed, g_c1, g_head_w, g_head_b), feed_rels, padded_rows,
            offset + devices * rows + tail, tiles,
        ),
        feed_order, z_bits,
    )
    chains = (class_chain, feed_chain)
    mixes = (pre_col, post_col, pre_row, post_row)
    dq_s, pre_sum, post_sum = attend_back(
        qkv_s, d_att_s, lse_s, mixes, valid, 0, ns, small_per, 25e9, [chain.send for chain in chains]
    )
    part, dq_l = dq_s, []
    for i in range(nl):
        for chain in chains:
            chain.step(part)
        wait = [part] + [chain.send for chain in chains]
        part, pre_l, post_l = attend_back(qkv_l, d_att_l, lse_l, mixes, qkv_l.shape[1], i, 1, 1, 25e9, wait)
        dq_l.append(part)
        pre_sum, post_sum = pre_sum + pre_l, post_sum + post_l
    for chain in chains:
        chain.step(part)
    g_wqkv, g_vec, g_patch_w, g_patch_b, g_pos = embed_back(
        patches_small, patches_large, tok, dq_s, d_mid, dq_l, wqkv, vec,
        [chain.send for chain in chains],
    )
    for chain in chains:
        while not chain.done:
            chain.step(g_vec)

    late_rels = slots_of([core] + inner + z_order)
    late_chain = Chain(
        *pack(
            functools.partial(pack_late_kernel, late_rels, rows, quarter_rows), "pack_late", me_quarter,
            (g_wqkv, g_vec, pre_sum, post_sum, g_wo, g_patch_w, g_patch_b, g_pos, g_svec, g_head_w), late_rels,
            2 * padded_rows, row_of(0, 6) + 1024, tiles,
        ),
        [core] + inner, z_bits, True,
    )
    while not late_chain.done:
        late_chain.step()
    part = late_chain.total
    send = part.astype(bf16)
    for a in (1, 2, 3):
        got = lax.ppermute(send, "dp", [(i + a * n_quarter, i) for i in range(n_quarter)])
        part = part + got.astype(f32)
    head_part = lax.ppermute(feed_chain.total, "dp", [(i, i + n_quarter) for i in range(n_quarter)])
    first = quarter_id == 0
    grad_stem = jnp.where(first, part[:padded_rows], head_part)
    grad_self = jnp.where(first, part[padded_rows:], feed_chain.total)

    gradients, new_first, new_second, update, sums = adam(
        me, step, master, first_moment, second_moment, (grad_stem, grad_self, class_chain.total), rows
    )
    line = lax.broadcasted_iota(jnp.int32, (8, 1), 0)
    sums = sums + old_sums + jnp.where(line == 6, loss, 0.0)
    for bit in range(bits):
        sums = sums + exchange(sums, bit, z_bits)
    new_master, weight_norms, update_norms, trust_ratios = apply_update(me, sums, master, update)
    return sums[6, 0], gradients, new_first, new_second, new_master, weight_norms, update_norms, trust_ratios


def solution(mesh):
    return jax.shard_map(
        on_device,
        mesh=mesh,
        in_specs=(
            P(None, AXES),
            P(None, AXES),
            P(None, AXES),
            P(AXES, None, None),
            P(AXES, None, None),
            P(AXES),
            P(AXES),
            P(AXES, None),
            P(),
        ),
        out_specs=(
            P(),
            P(None, AXES),
            P(None, AXES),
            P(None, AXES),
            P(None, AXES),
            P(),
            P(),
            P(),
        ),
        check_vma=False,
    )
```

time: 573 us -> 414 us (0.72)
  Pallas kernels: 368 us -> 253 us
  waiting for transfers between devices: 126 us -> 54.4 us
  between operations: 3.46 us -> 15.4 us
  starting transfers between devices: 43.4 us -> 55.1 us
  other arithmetic: 11.9 us -> 18.7 us
    pallas_call x7 -> x16, Pallas kernels: 323 us -> 220 us  [the longest x9 187 us: call(): pl.pallas_call(wrapped, in_specs=specs, compiler_params=params(), **kw)]
    ppermute x28 -> x15, waiting for transfers between devices: 76.6 us -> 11.3 us  [exchange(): lax.ppermute(value, 'dp', [(i, i ^ 1 << bit - z_bits) for i in range(n)])]
    ppermute x14 -> x6, waiting for transfers between devices: 49.3 us -> 6.14 us  [exchange(): return lax.ppermute(value, 'fsdp', [(i, i ^ 1 << bit) for i in range(n)])]
    ppermute x2 -> x20, waiting for transfers between devices: 0.48 us -> 37 us  [the longest x12 29.3 us: exchange_z(): return lax.ppermute(value, 'fsdp', [(i, i ^ k) for i in range(n)])]
    ppermute x2 -> x20, starting transfers between devices: 5.17 us -> 31.6 us  [the longest x12 17.9 us: exchange_z(): return lax.ppermute(value, 'fsdp', [(i, i ^ k) for i in range(n)])]
    pallas_call x1, Pallas kernels: 15.4 us -> 4.36 us  [adam(): pl.pallas_call(functools.partial(adam_kernel, rows), out_shape=[sds(shape...]
    add x11, other arithmetic: 3.03 us -> 12.5 us  [the longest x8 10.9 us: step(): total = self.keep + got.astype(f32)]
    ppermute x28 -> x15, starting transfers between devices: 17.6 us -> 9.65 us  [exchange(): lax.ppermute(value, 'dp', [(i, i ^ 1 << bit - z_bits) for i in range(n)])]
  transfers between devices with their start and end apart: 44 -> 42, of which waited for: 25 -> 16; matrix products, arithmetic and copies ran while one was open for 3% -> 5% of each run, Pallas kernels for 19% -> 47%
where the time goes in v2:
time: 414 us; the launch traced here: 409 us
  Pallas kernels  253 us (61%)
  starting transfers between devices  55.1 us (13%)
  waiting for transfers between devices  54.4 us (13%)
  other arithmetic  18.7 us (5%)
  between operations  15.4 us (4%)
  local copies, waits for them, and re-layouts  13.2 us (3%)
    pallas_call x9, Pallas kernels, call(): pl.pallas_call(wrapped, in_specs=specs, compiler_params=params(), **kw)  187 us
    ppermute x12, waiting for transfers between devices, exchange_z(): return lax.ppermute(value, 'fsdp', [(i, i ^ k) for i in range(n)])  29.3 us
    pallas_call x3, Pallas kernels, pack(): pl.pallas_call(kernel, out_shape=[sds((half, padded_rows, LANES), f32), s...  18.5 us
    ppermute x12, starting transfers between devices, exchange_z(): return lax.ppermute(value, 'fsdp', [(i, i ^ k) for i in range(n)])  17.9 us
    pallas_call x1, Pallas kernels, class_block(): pl.pallas_call(functools.partial(class_kernel, ns, nl, valid), out_shape=...  17 us
    ppermute x6, starting transfers between devices, exchange(): return lax.ppermute(value, 'fsdp', [(i, i ^ 1 << bit) for i in range(n)])  13.8 us
    ppermute x15, waiting for transfers between devices, exchange(): lax.ppermute(value, 'dp', [(i, i ^ 1 << bit - z_bits) for i in range(n)])  11.3 us
    add x8, other arithmetic, step(): total = self.keep + got.astype(f32)  10.9 us
  transfers between devices with their start and end apart: 42, of which 16 were waited for; matrix products, arithmetic and copies ran while one was open for 5% of the time, Pallas kernels for 47%

profile of v2, /device:TPU:0, one launch (start us, length us, event | category | flops | bytes accessed | tf_op | source)
XLA Modules:
  0.0 409.3 jit_solution(7468011776542156649)
XLA Ops:
  7.2 1.9 round_shards.1
  9.1 4.9 %collective-permute-start = (bf16[1,440,128]{2,1,0:T(8,128)(2,1)}, bf16[1,440,128]{2,1,0:T(8,128)(2,1)S(1)}, u32[]{:S(2)}, u32[]{:S(2)}) collective-permute-start(bf16[1,440,128]{2,1,0:T(8,128)(2,1)} %get-tuple-element.122), channel_id=1, source_target_pairs={{0,16},{4,20},{8,24},{12,28},{1,17},{5,21},{9,25},{13,29},{2,18},{... | collective-permute-start | bytes 337928 | tf_op jit(solution)/shard_map/ppermute | solution.py:1340
  14.0 2.6 collective-permute-done
  19.2 2.6 collective-permute-start.2
  22.1 2.4 collective-permute-start.7
  25.6 4.4 %collective-permute-done.2 = bf16[1,440,128]{2,1,0:T(8,128)(2,1)S(1)} collective-permute-done((bf16[1,440,128]{2,1,0:T(8,128)(2,1)S(1)}, bf16[1,440,128]{2,1,0:T(8,128)(2,1)S(1)}, u32[]{:S(2)}, u32[]{:S(2)}) %collective-permute-start.2) | collective-permute-done | bytes 112672 | tf_op jit(solution)/shard_map/ppermute | solution.py:194
  32.6 1.8 collective-permute-start.10
  34.5 2.0 collective-permute-start.11
  38.0 6.2 %collective-permute-done.11 = bf16[1,440,128]{2,1,0:T(8,128)(2,1)S(1)} collective-permute-done((bf16[1,440,128]{2,1,0:T(8,128)(2,1)S(1)}, bf16[1,440,128]{2,1,0:T(8,128)(2,1)S(1)}, u32[]{:S(2)}, u32[]{:S(2)}) %collective-permute-start.11) | collective-permute-done | bytes 112672 | tf_op jit(solution)/shard_map/ppermute | solution.py:194
  45.0 2.3 weight_sums.1.refs_7_
  48.5 2.0 collective-permute-start.14
  51.4 1.7 collective-permute-start.16
  53.1 2.6 unpack_low.1
  55.7 4.9 %unpack_stem.1 = (bf16[768,384]{1,0:T(8,128)(2,1)}, f32[8,384]{1,0:T(8,128)}, f32[208,384]{1,0:T(8,128)}, f32[576,384]{1,0:T(8,128)}, bf16[384,1024]{1,0:T(8,128)(2,1)}, /*index=5*/f32[1,1024]{1,0:T(1,128)}) custom-call(s32[1]{0:T(128)S(6)} %and.15.me_ref, f32[576,208]{1,0:T(8,128)} %constant.47.clone.resize_ref, bf16[4,440,128]{2,1,0:T(8,128)(2,1)} %copy-done.8, ...), custom_call_target="tpu_custom_call" | custom-call | tf_op jit(solution)/shard_map/unpack_stem/pallas_call | solution.py:272
  60.7 9.0 %embed.1 = (f32[4,208,384]{2,1,0:T(8,128)}, f32[2,576,384]{2,1,0:T(8,128)}, bf16[4,208,1152]{2,1,0:T(8,128)(2,1)}, bf16[2,576,1152]{2,1,0:T(8,128)(2,1)}) custom-call(bf16[4,196,768]{2,1,0:T(8,128)(2,1)} %copy.24.refs_0_, bf16[2,576,768]{2,1,0:T(8,128)(2,1)} %refs_1_.3, bf16[768,384]{1,0:T(8,128)(2,1)} %get-tuple-element.123.refs_2_, ...), custom_call_target="tpu_custom_call" | custom-call | flops 12000000000 | bytes 20000000 | tf_op jit(solution)/shard_map/embed/pallas_call | solution.py:177
  69.6 16.5 %attend.2 = (bf16[4,208,384]{2,1,0:T(8,128)(2,1)}, f32[4,8,208]{2,1,0:T(8,128)}) custom-call(bf16[4,208,1152]{2,1,0:T(8,128)(2,1)} %get-tuple-element.131.refs_0_, f32[384,8]{1,0:T(8,128)} %get-tuple-element.132.refs_1_.refs_3_, f32[384,8]{1,0:T(8,128)} %get-tuple-element.133.refs_2_.refs_4_), custom_call_target="tpu_custom_call" | custom-call | flops 20000000000 | bytes 10000000 | tf_op jit(solution)/shard_map/attend/pallas_call | solution.py:177
  88.4 25.8 %attend.3 = (bf16[2,576,384]{2,1,0:T(8,128)(2,1)}, f32[2,8,576]{2,1,0:T(8,128)}) custom-call(bf16[2,576,1152]{2,1,0:T(8,128)(2,1)} %get-tuple-element.135.refs_0_, f32[384,8]{1,0:T(8,128)} %get-tuple-element.132.refs_1_.refs_3_, f32[384,8]{1,0:T(8,128)} %get-tuple-element.133.refs_2_.refs_4_, bf16[12,440,128]{2,1,0:T(8,128)(2,1)} %copy-done.7, ...), custom_call_target="tpu_custom_call" | custom-call | flops 30000001024 | bytes 10000000 | tf_op jit(solution)/shard_map/attend/pallas_call | solution.py:177
  115.3 4.3 %unpack_feed.1 = (bf16[384,384]{1,0:T(8,128)(2,1)}, bf16[384,1536]{1,0:T(8,128)(2,1)}, bf16[1536,384]{1,0:T(8,128)(2,1)}, f32[16,384]{1,0:T(8,128)}, f32[1,1536]{1,0:T(1,128)}) custom-call(s32[1]{0:T(128)S(6)} %and.14.me_ref, bf16[4,440,128]{2,1,0:T(8,128)(2,1)} %copy-done.6, bf16[4,440,128]{2,1,0:T(8,128)(2,1)} %copy-done.9, ...), custom_call_target="tpu_custom_call" | custom-call | tf_op jit(solution)/shard_map/unpack_feed/pallas_call | solution.py:355
  119.6 26.7 %feed.1 = (bf16[4,208,384]{2,1,0:T(8,128)(2,1)}, bf16[2,576,384]{2,1,0:T(8,128)(2,1)}, f32[4,208,384]{2,1,0:T(8,128)}, f32[2,576,384]{2,1,0:T(8,128)}, bf16[4,20...) custom-call(f32[4,208,384]{2,1,0:T(8,128)} %get-tuple-element.129.re, ...), custom_call_target="tpu_custom_call" | custom-call | flops 20000000000 | bytes 30000000 | tf_op jit(solution)/shard_map/feed/pallas_call | solution.py:177
  146.3 4.5 %unpack_class.1 = (bf16[384,384]{1,0:T(8,128)(2,1)}, bf16[384,768]{1,0:T(8,128)(2,1)}, bf16[384,384]{1,0:T(8,128)(2,1)}, bf16[384,1536]{1,0:T(8,128)(2,1)}, bf16...) custom-call(s32[1]{0:T(128)} %constant.43.clone.1.me_ref, ...), custom_call_target="tpu_custom_call" | custom-call | tf_op jit(solution)/shard_map/unpack_class/pallas_call | solution.py:396
  150.8 17.0 %class_block.1 = (f32[4,208,384]{2,1,0:T(8,128)}, f32[2,576,384]{2,1,0:T(8,128)}, f32[384,384]{1,0:T(8,128)}, f32[384,768]{1,0:T(8,128)}, f32[384,384]{1,0:T(8,1...) custom-call(f32[4,208,384]{2,1,0:T(8,128)} %get-tuple-element.147.ou, ...), custom_call_target="tpu_custom_call" | custom-call | flops 10000000000 | bytes 60000000 | tf_op jit(solution)/shard_map/class_block/pallas_call | solution.py:758
  167.8 6.4 %pack_class.1 = (f32[16,440,128]{2,1,0:T(8,128)}, bf16[16,440,128]{2,1,0:T(8,128)(2,1)}) custom-call(s32[1]{0:T(128)} %bitcast.me_ref, f32[384,384]{1,0:T(8,128)} %get-tuple-element.173.wq, f32[384,768]{1,0:T(8,128)} %get-tuple-element.174.wkv, f32[384,384]{1,0:T(8,128)} %get-tuple-element.175.wo, f32[384,1536]{1,0:T(8,128)} %get-tuple-element.176.w1, ...), custom_call_target="tpu_custom_call" | custom-call | tf_op jit(solution)/shard_map/pack_class/pallas_call | solution.py:1138
  174.1 24.3 %feed_back.1 = (f32[4,208,384]{2,1,0:T(8,128)}, f32[2,576,384]{2,1,0:T(8,128)}, bf16[4,208,384]{2,1,0:T(8,128)(2,1)}, bf16[2,576,384]{2,1,0:T(8,128)(2,1)}, f32[...) custom-call(f32[4,208,384]{2,1,0:T(8,128)} %get-tuple-element.161.refs, ...), custom_call_target="tpu_custom_call" | custom-call | flops 35000000512 | bytes 30000000 | tf_op jit(solution)/shard_map/feed_back/pallas_call | solution.py:177
  198.4 7.2 %pack_feed.1 = (f32[16,440,128]{2,1,0:T(8,128)}, bf16[16,440,128]{2,1,0:T(8,128)(2,1)}) custom-call(s32[1]{0:T(128)} %bitcast.me_ref, f32[384,384]{1,0:T(8,128)} %get-tuple-element.187.wo, f32[384,1536]{1,0:T(8,128)} %get-tuple-element.188.w1, f32[1536,384]{1,0:T(8,128)} %get-tuple-element.189.w2, f32[16,384]{1,0:T(8,128)} %get-tuple-element.190.vec, ...), custom_call_target="tpu_custom_call" | custom-call | tf_op jit(solution)/shard_map/pack_feed/pallas_call | solution.py:1138
  207.3 2.9 convert_add_fusion.1
  212.7 20.1 %attend_back.3 = (bf16[4,208,1152]{2,1,0:T(8,128)(2,1)}, f32[8,384]{1,0:T(8,128)}, f32[8,384]{1,0:T(8,128)}) custom-call(bf16[4,208,1152]{2,1,0:T(8,128)(2,1)} %get-tuple-element.131.refs_0_, bf16[4,208,384]{2,1,0:T(8,128)(2,1)} %get-tuple-element.181.refs_1_, f32[4,8,208]{2,1,0:T(8,128)} %get-tuple-element.182.refs_2_, ...), custom_call_target="tpu_custom_call" | custom-call | flops 24999999488 | bytes 10000000 | tf_op jit(solution)/shard_map/attend_back/pallas_call | solution.py:177
  232.8 2.9 convert_add_fusion
  240.6 23.2 %attend_back.4 = (bf16[1,576,1152]{2,1,0:T(8,128)(2,1)}, f32[8,384]{1,0:T(8,128)}, f32[8,384]{1,0:T(8,128)}) custom-call(bf16[2,576,1152]{2,1,0:T(8,128)(2,1)} %get-tuple-element.135.refs_0_, bf16[2,576,384]{2,1,0:T(8,128)(2,1)} %get-tuple-element.198.refs_1_, f32[2,8,576]{2,1,0:T(8,128)} %get-tuple-element.199.refs_2_, ...), custom_call_target="tpu_custom_call" | custom-call | flops 24999999488 | bytes 10000000 | tf_op jit(solution)/shard_map/attend_back/pallas_call | solution.py:177
  266.7 1.7 collective-permute-start.24
  270.2 23.6 %attend_back.5 = (bf16[1,576,1152]{2,1,0:T(8,128)(2,1)}, f32[8,384]{1,0:T(8,128)}, f32[8,384]{1,0:T(8,128)}) custom-call(bf16[2,576,1152]{2,1,0:T(8,128)(2,1)} %get-tuple-element.135.refs_0_, bf16[2,576,384]{2,1,0:T(8,128)(2,1)} %get-tuple-element.198.refs_1_, f32[2,8,576]{2,1,0:T(8,128)} %get-tuple-element.199.refs_2_, ...), custom_call_target="tpu_custom_call" | custom-call | flops 24999999488 | bytes 10000000 | tf_op jit(solution)/shard_map/attend_back/pallas_call | solution.py:177
  298.3 2.3 collective-permute-done.23
  301.3 17.5 %embed_back.1 = (f32[384,1152]{1,0:T(8,128)}, f32[16,384]{1,0:T(8,128)}, f32[768,384]{1,0:T(8,128)}, f32[8,384]{1,0:T(8,128)}, f32[196,384]{1,0:T(8,128)}) custom-call(bf16[4,196,768]{2,1,0:T(8,128)(2,1)} %copy.24.refs_0_, bf16[2,576,768]{2,1,0:T(8,128)(2,1)} %refs_1_.3, f32[196,576]{1,0:T(8,128)} %constant.48.clone.refs_2_, ...), custom_call_target="tpu_custom_call" | custom-call | flops 20000000000 | bytes 30000000 | tf_op jit(solution)/shard_map/embed_back/pallas_call | solution.py:177
  318.8 5.0 %pack_late.1 = (f32[4,880,128]{2,1,0:T(8,128)}, bf16[4,880,128]{2,1,0:T(8,128)(2,1)}) custom-call(s32[1]{0:T(128)S(6)} %and.14.me_ref, f32[384,1152]{1,0:T(8,128)} %get-tuple-element.209.wqkv, f32[16,384]{1,0:T(8,128)} %get-tuple-element.210.vec, f32[8,384]{1,0:T(8,128)} %get-tuple-element.248.pre, f32[8,384]{1,0:T(8,128)} %get-tuple-element.247.post, ...), custom_call_target="tpu_custom_call" | custom-call | tf_op jit(solution)/shard_map/pack_late/pallas_call | solution.py:1138
  324.4 2.0 collective-permute-done.25
  326.4 1.8 fusion.7
  330.5 2.2 collective-permute-start.28
  333.1 6.6 %collective-permute-done.26 = bf16[880,128]{1,0:T(8,128)(2,1)S(1)} collective-permute-done((bf16[880,128]{1,0:T(8,128)(2,1)S(1)}, bf16[880,128]{1,0:T(8,128)(2,1)S(1)}, u32[]{:S(2)}, u32[]{:S(2)}) %collective-permute-start.26) | collective-permute-done | bytes 225312 | tf_op jit(solution)/shard_map/ppermute | solution.py:194
  339.7 11.1 %collective-permute-done.27 = bf16[880,128]{1,0:T(8,128)(2,1)S(1)} collective-permute-done((bf16[880,128]{1,0:T(8,128)(2,1)S(1)}, bf16[880,128]{1,0:T(8,128)(2,1)S(1)}, u32[]{:S(2)}, u32[]{:S(2)}) %collective-permute-start.27) | collective-permute-done | bytes 225312 | tf_op jit(solution)/shard_map/ppermute | solution.py:194
  357.0 2.9 collective-permute-done.33
  360.0 2.5 collective-permute-done.30
  365.6 2.5 collective-permute-done.34
  368.9 4.4 %adam.1 = (f32[3,55552]{1,0:T(4,128)}, f32[3,55552]{1,0:T(4,128)}, f32[3,55552]{1,0:T(4,128)}, f32[3,55552]{1,0:T(4,128)}, f32[8,128]{1,0:T(8,128)}) custom-call(s32[1]{0:T(128)} %bitcast.me_ref, s32[1]{0:T(128)S(6)} %copy.28.step_ref, s32[8,128]{1,0:T(8,128)} %constant.46.clone.bounds, f32[3,55552]{1,0:T(4,128)} %master.7, f32[3,55552]{1,0:T(4,128)} %first.1, ...), custom_call_target="tpu_custom_call" | custom-call | tf_op jit(solution)/shard_map/adam/pallas_call | solution.py:1225
  374.0 7.2 %collective-permute-start.36 = (f32[8,128]{1,0:T(8,128)S(1)}, f32[8,128]{1,0:T(8,128)S(1)}, u32[]{:S(2)}, u32[]{:S(2)}) collective-permute-start(f32[8,128]{1,0:T(8,128)S(1)} %select_add_fusion), channel_id=1, source_target_pairs={{0,1},{1,0},{2,3},{3,2},{4,5},{5,4},{6,7},{7,6},{8,9},{9,8},{10,11... | collective-permute-start | bytes 12296 | tf_op jit(solution)/shard_map/ppermute | solution.py:187
  382.8 2.2 collective-permute-start.37
  385.0 2.3 collective-permute-done.37
  388.5 2.5 collective-permute-start.39
  392.5 3.6 collective-permute-done.40
  396.7 5.5 %apply_update.1 = (f32[3,55552]{1,0:T(4,128)}, f32[3,16]{1,0:T(4,128)}, f32[3,16]{1,0:T(4,128)}, f32[3,16]{1,0:T(4,128)}) custom-call(s32[1]{0:T(128)} %bitcast.me_ref, f32[8,128]{1,0:T(8,128)} %copy-done.19, f32[3,55552]{1,0:T(4,128)} %master.7, f32[3,55552]{1,0:T(4,128)} %get-tuple-element.231.update), custom_call_target="tpu_custom_call" | custom-call | tf_op jit(solution)/shard_map/apply_update/pallas_call | solution.py:1256
  (156 shorter events, 51.7 us)
Async XLA Ops:
  7.2 139.1 %all-gather.2.cloned.1.call-start = ((), (), s32[]{:S(2)}) async-start(), calls=%async_computation | async-start | bytes 3717120 | tf_op jit(solution)/shard_map/all_gather | solution.py:1359
  9.1 7.5 %collective-permute-start = (bf16[1,440,128]{2,1,0:T(8,128)(2,1)}, bf16[1,440,128]{2,1,0:T(8,128)(2,1)S(1)}, u32[]{:S(2)}, u32[]{:S(2)}) collective-permute-start(bf16[1,440,128]{2,1,0:T(8,128)(2,1)} %get-tuple-element.122), channel_id=1, source_target_pairs={{0,16},{4,20},{8,24},{12,28},{1,17},{5,21},{9,25},{13,29},{2,18},{... | collective-permute-start | bytes 337928 | tf_op jit(solution)/shard_map/ppermute | solution.py:1340
  17.6 7.4 %collective-permute-start.1 = (bf16[1,440,128]{2,1,0:T(8,128)(2,1)S(1)}, bf16[1,440,128]{2,1,0:T(8,128)(2,1)S(1)}, u32[]{:S(2)}, u32[]{:S(2)}) collective-permute-start(bf16[1,440,128]{2,1,0:T(8,128)(2,1)S(1)} %broadcast_select_fusion), channel_id=1, source_target_pairs={{0,1},{1,0},{2,3},{3,2},{4,5},{5,4},{6,7},{7,6},{8,9},{9,8},{10,11... | collective-permute-start | bytes 337928 | tf_op jit(solution)/shard_map/ppermute | solution.py:194
  19.2 10.7 %collective-permute-start.2 = (bf16[1,440,128]{2,1,0:T(8,128)(2,1)S(1)}, bf16[1,440,128]{2,1,0:T(8,128)(2,1)S(1)}, u32[]{:S(2)}, u32[]{:S(2)}) collective-permute-start(bf16[1,440,128]{2,1,0:T(8,128)(2,1)S(1)} %broadcast_select_fusion), channel_id=1, source_target_pairs={{0,2},{1,3},{2,0},{3,1},{4,6},{5,7},{6,4},{7,5},{8,10},{9,11},{10,... | collective-permute-start | bytes 337928 | tf_op jit(solution)/shard_map/ppermute | solution.py:194
  21.8 8.1 %collective-permute-start.3 = (bf16[1,440,128]{2,1,0:T(8,128)(2,1)S(1)}, bf16[1,440,128]{2,1,0:T(8,128)(2,1)S(1)}, u32[]{:S(2)}, u32[]{:S(2)}) collective-permute-start(bf16[1,440,128]{2,1,0:T(8,128)(2,1)S(1)} %broadcast_select_fusion), channel_id=1, source_target_pairs={{0,3},{1,2},{2,1},{3,0},{4,7},{5,6},{6,5},{7,4},{8,11},{9,10},{10,... | collective-permute-start | bytes 337928 | tf_op jit(solution)/shard_map/ppermute | solution.py:194
  22.1 9.5 %collective-permute-start.7 = (bf16[1,440,128]{2,1,0:T(8,128)(2,1)}, bf16[1,440,128]{2,1,0:T(8,128)(2,1)S(1)}, u32[]{:S(2)}, u32[]{:S(2)}) collective-permute-start(bf16[1,440,128]{2,1,0:T(8,128)(2,1)} %get-tuple-element.126), channel_id=1, source_target_pairs={{0,24},{4,28},{8,16},{12,20},{16,8},{20,12},{24,0},{28,4},{1,25},{... | collective-permute-start | bytes 337928 | tf_op jit(solution)/shard_map/ppermute | solution.py:1341
  24.5 7.1 %collective-permute-start.8 = (bf16[1,440,128]{2,1,0:T(8,128)(2,1)}, bf16[1,440,128]{2,1,0:T(8,128)(2,1)S(1)}, u32[]{:S(2)}, u32[]{:S(2)}) collective-permute-start(bf16[1,440,128]{2,1,0:T(8,128)(2,1)} %get-tuple-element.126), channel_id=1, source_target_pairs={{0,16},{4,20},{8,24},{12,28},{16,0},{20,4},{24,8},{28,12},{1,17},{... | collective-permute-start | bytes 337928 | tf_op jit(solution)/shard_map/ppermute | solution.py:1341
  25.0 22.3 %copy-start.12 = (bf16[4,196,768]{2,0,1:T(4,128)(2,1)S(1)}, bf16[4,196,768]{2,0,1:T(4,128)(2,1)}, u32[]{:S(2)}) copy-start(bf16[4,196,768]{2,0,1:T(4,128)(2,1)} %param.16) | copy-start | bytes 3612676
  25.0 6.6 %collective-permute-start.9 = (bf16[1,440,128]{2,1,0:T(8,128)(2,1)}, bf16[1,440,128]{2,1,0:T(8,128)(2,1)S(1)}, u32[]{:S(2)}, u32[]{:S(2)}) collective-permute-start(bf16[1,440,128]{2,1,0:T(8,128)(2,1)} %get-tuple-element.126), channel_id=1, source_target_pairs={{0,8},{4,12},{8,0},{12,4},{16,24},{20,28},{24,16},{28,20},{1,9},{5... | collective-permute-start | bytes 337928 | tf_op jit(solution)/shard_map/ppermute | solution.py:1341
  30.0 18.5 %copy-start.8 = (bf16[4,440,128]{2,1,0:T(8,128)(2,1)}, bf16[4,440,128]{2,1,0:T(8,128)(2,1)S(1)}, u32[]{:S(2)}) copy-start(bf16[4,440,128]{2,1,0:T(8,128)(2,1)S(1)} %pad_maximum_fusion.refs_0_) | copy-start | bytes 1351684
  30.0 14.9 %collective-permute-start.4 = (bf16[4,440,128]{2,1,0:T(8,128)(2,1)S(1)}, bf16[4,440,128]{2,1,0:T(8,128)(2,1)}, u32[]{:S(2)}, u32[]{:S(2)}) collective-permute-start(bf16[4,440,128]{2,1,0:T(8,128)(2,1)S(1)} %pad_maximum_fusion.refs_0_), channel_id=1, source_target_pairs={{0,8},{4,12},{8,0},{12,4},{16,24},{20,28},{24,16},{28,20},{1,9},{5... | collective-permute-start | bytes 1351688 | tf_op jit(solution)/shard_map/ppermute | solution.py:189
  32.6 5.4 %collective-permute-start.10 = (bf16[1,440,128]{2,1,0:T(8,128)(2,1)S(1)}, bf16[1,440,128]{2,1,0:T(8,128)(2,1)S(1)}, u32[]{:S(2)}, u32[]{:S(2)}) collective-permute-start(bf16[1,440,128]{2,1,0:T(8,128)(2,1)S(1)} %get-tuple-element.246), channel_id=1, source_target_pairs={{0,1},{1,0},{2,3},{3,2},{4,5},{5,4},{6,7},{7,6},{8,9},{9,8},{10,11... | collective-permute-start | bytes 337928 | tf_op jit(solution)/shard_map/ppermute | solution.py:194
  34.5 9.8 %collective-permute-start.11 = (bf16[1,440,128]{2,1,0:T(8,128)(2,1)S(1)}, bf16[1,440,128]{2,1,0:T(8,128)(2,1)S(1)}, u32[]{:S(2)}, u32[]{:S(2)}) collective-permute-start(bf16[1,440,128]{2,1,0:T(8,128)(2,1)S(1)} %get-tuple-element.246), channel_id=1, source_target_pairs={{0,2},{1,3},{2,0},{3,1},{4,6},{5,7},{6,4},{7,5},{8,10},{9,11},{10,... | collective-permute-start | bytes 337928 | tf_op jit(solution)/shard_map/ppermute | solution.py:194
  36.4 7.9 %collective-permute-start.12 = (bf16[1,440,128]{2,1,0:T(8,128)(2,1)S(1)}, bf16[1,440,128]{2,1,0:T(8,128)(2,1)S(1)}, u32[]{:S(2)}, u32[]{:S(2)}) collective-permute-start(bf16[1,440,128]{2,1,0:T(8,128)(2,1)S(1)} %get-tuple-element.246), channel_id=1, source_target_pairs={{0,3},{1,2},{2,1},{3,0},{4,7},{5,6},{6,5},{7,4},{8,11},{9,10},{10,... | collective-permute-start | bytes 337928 | tf_op jit(solution)/shard_map/ppermute | solution.py:194
  44.4 7.1 %collective-permute-start.13 = (bf16[4,440,128]{2,1,0:T(8,128)(2,1)S(1)}, bf16[4,440,128]{2,1,0:T(8,128)(2,1)S(1)}, u32[]{:S(2)}, u32[]{:S(2)}) collective-permute-start(bf16[4,440,128]{2,1,0:T(8,128)(2,1)S(1)} %pad_maximum_fusion.1.refs_0_), channel_id=1, source_target_pairs={{0,4},{4,0},{8,12},{12,8},{16,20},{20,16},{24,28},{28,24},{1,5},{5... | collective-permute-start | bytes 1351688 | tf_op jit(solution)/shard_map/ppermute | solution.py:189
  44.4 11.3 %collective-permute-start.5 = (bf16[4,440,128]{2,1,0:T(8,128)(2,1)S(1)}, bf16[4,440,128]{2,1,0:T(8,128)(2,1)}, u32[]{:S(2)}, u32[]{:S(2)}) collective-permute-start(bf16[4,440,128]{2,1,0:T(8,128)(2,1)S(1)} %pad_maximum_fusion.refs_0_), channel_id=1, source_target_pairs={{0,4},{4,0},{8,12},{12,8},{16,20},{20,16},{24,28},{28,24},{1,5},{5... | collective-permute-start | bytes 1351688 | tf_op jit(solution)/shard_map/ppermute | solution.py:189
  44.9 10.8 %collective-permute-start.6 = (bf16[4,440,128]{2,1,0:T(8,128)(2,1)}, bf16[4,440,128]{2,1,0:T(8,128)(2,1)}, u32[]{:S(2)}, u32[]{:S(2)}) collective-permute-start(bf16[4,440,128]{2,1,0:T(8,128)(2,1)} %collective-permute-done.4.refs_1_), channel_id=1, source_target_pairs={{0,4},{4,0},{8,12},{12,8},{16,20},{20,16},{24,28},{28,24},{1,5},{5... | collective-permute-start | bytes 1351688 | tf_op jit(solution)/shard_map/ppermute | solution.py:189
  48.5 37.6 %collective-permute-start.14 = (bf16[3,440,128]{2,1,0:T(8,128)(2,1)S(1)}, bf16[3,440,128]{2,1,0:T(8,128)(2,1)S(1)}, u32[]{:S(2)}, u32[]{:S(2)}) collective-permute-start(bf16[3,440,128]{2,1,0:T(8,128)(2,1)S(1)} %pad_maximum_fusion.2), channel_id=1, source_target_pairs={{0,1},{1,0},{2,3},{3,2},{4,5},{5,4},{6,7},{7,6},{8,9},{9,8},{10,11... | collective-permute-start | bytes 1013768 | tf_op jit(solution)/shard_map/ppermute | solution.py:194
  50.5 35.7 %collective-permute-start.15 = (bf16[3,440,128]{2,1,0:T(8,128)(2,1)S(1)}, bf16[3,440,128]{2,1,0:T(8,128)(2,1)}, u32[]{:S(2)}, u32[]{:S(2)}) collective-permute-start(bf16[3,440,128]{2,1,0:T(8,128)(2,1)S(1)} %pad_maximum_fusion.2), channel_id=1, source_target_pairs={{0,2},{1,3},{2,0},{3,1},{4,6},{5,7},{6,4},{7,5},{8,10},{9,11},{10,... | collective-permute-start | bytes 1013768 | tf_op jit(solution)/shard_map/ppermute | solution.py:194
  51.4 34.7 %collective-permute-start.16 = (bf16[3,440,128]{2,1,0:T(8,128)(2,1)S(1)}, bf16[3,440,128]{2,1,0:T(8,128)(2,1)S(1)}, u32[]{:S(2)}, u32[]{:S(2)}) collective-permute-start(bf16[3,440,128]{2,1,0:T(8,128)(2,1)S(1)} %pad_maximum_fusion.2), channel_id=1, source_target_pairs={{0,3},{1,2},{2,1},{3,0},{4,7},{5,6},{6,5},{7,4},{8,11},{9,10},{10,... | collective-permute-start | bytes 1013768 | tf_op jit(solution)/shard_map/ppermute | solution.py:194
  87.3 26.9 %collective-permute-start.17 = (bf16[12,440,128]{2,1,0:T(8,128)(2,1)S(1)}, bf16[12,440,128]{2,1,0:T(8,128)(2,1)S(1)}, u32[]{:S(2)}, u32[]{:S(2)}) collective-permute-start(bf16[12,440,128]{2,1,0:T(8,128)(2,1)S(1)} %constant_dynamic-update-slice_fusion.refs_3_.refs_2_), channel_id=1, source_target_pairs={{0,4},{4,0},{8,12},{12,8},{16,20},{20,16},{24,28},{28,24},{1,5},{5... | collective-permute-start | bytes 4055048 | tf_op jit(solution)/shard_map/ppermute | solution.py:189
  174.1 32.0 %collective-permute-start.18 = (bf16[16,440,128]{2,1,0:T(8,128)(2,1)}, bf16[16,440,128]{2,1,0:T(8,128)(2,1)S(1)}, u32[]{:S(2)}, u32[]{:S(2)}) collective-permute-start(bf16[16,440,128]{2,1,0:T(8,128)(2,1)} %get-tuple-element.180.refs_18_), channel_id=1, source_target_pairs={{0,4},{4,0},{8,12},{12,8},{16,20},{20,16},{24,28},{28,24},{1,5},{5... | collective-permute-start | bytes 5406728 | tf_op jit(solution)/shard_map/ppermute | solution.py:189
  205.6 27.1 %collective-permute-start.20 = (bf16[16,440,128]{2,1,0:T(8,128)(2,1)}, bf16[16,440,128]{2,1,0:T(8,128)(2,1)}, u32[]{:S(2)}, u32[]{:S(2)}) collective-permute-start(bf16[16,440,128]{2,1,0:T(8,128)(2,1)} %get-tuple-element.194.refs_8_), channel_id=1, source_target_pairs={{0,4},{4,0},{8,12},{12,8},{16,20},{20,16},{24,28},{28,24},{1,5},{5... | collective-permute-start | bytes 5406728 | tf_op jit(solution)/shard_map/ppermute | solution.py:189
  211.3 26.7 %collective-permute-start.19 = (bf16[8,440,128]{2,1,0:T(8,128)(2,1)}, bf16[8,440,128]{2,1,0:T(8,128)(2,1)}, u32[]{:S(2)}, u32[]{:S(2)}) collective-permute-start(bf16[8,440,128]{2,1,0:T(8,128)(2,1)} %slice.164.refs_7_), channel_id=1, source_target_pairs={{0,16},{4,20},{8,24},{12,28},{16,0},{20,4},{24,8},{28,12},{1,17},{... | collective-permute-start | bytes 2703368 | tf_op jit(solution)/shard_map/ppermute | solution.py:189
  236.8 27.1 %collective-permute-start.22 = (bf16[8,440,128]{2,1,0:T(8,128)(2,1)}, bf16[8,440,128]{2,1,0:T(8,128)(2,1)}, u32[]{:S(2)}, u32[]{:S(2)}) collective-permute-start(bf16[8,440,128]{2,1,0:T(8,128)(2,1)} %slice.163.refs_9_), channel_id=1, source_target_pairs={{0,1},{1,0},{2,3},{3,2},{4,5},{5,4},{6,7},{7,6},{8,9},{9,8},{10,11... | collective-permute-start | bytes 2703368 | tf_op jit(solution)/shard_map/ppermute | solution.py:187
  239.4 29.0 %collective-permute-start.21 = (bf16[4,440,128]{2,1,0:T(8,128)(2,1)S(1)}, bf16[4,440,128]{2,1,0:T(8,128)(2,1)}, u32[]{:S(2)}, u32[]{:S(2)}) collective-permute-start(bf16[4,440,128]{2,1,0:T(8,128)(2,1)S(1)} %slice.166.refs_8_), channel_id=1, source_target_pairs={{0,8},{4,12},{8,0},{12,4},{16,24},{20,28},{24,16},{28,20},{1,9},{5... | collective-permute-start | bytes 1351688 | tf_op jit(solution)/shard_map/ppermute | solution.py:189
  240.6 23.2 %copy-start.1 = (f32[16,440,128]{2,1,0:T(8,128)S(1)}, f32[16,440,128]{2,1,0:T(8,128)}, u32[]{:S(2)}) copy-start(f32[16,440,128]{2,1,0:T(8,128)} %copy-done) | copy-start | bytes 10813444
  266.7 28.4 %collective-permute-start.24 = (bf16[4,440,128]{2,1,0:T(8,128)(2,1)S(1)}, bf16[4,440,128]{2,1,0:T(8,128)(2,1)S(1)}, u32[]{:S(2)}, u32[]{:S(2)}) collective-permute-start(bf16[4,440,128]{2,1,0:T(8,128)(2,1)S(1)} %slice.165.refs_9_), channel_id=1, source_target_pairs={{0,2},{1,3},{2,0},{3,1},{4,6},{5,7},{6,4},{7,5},{8,10},{9,11},{10,... | collective-permute-start | bytes 1351688 | tf_op jit(solution)/shard_map/ppermute | solution.py:187
  270.2 23.6 %copy-start.17 = (bf16[2,440,128]{2,1,0:T(8,128)(2,1)S(1)}, bf16[2,440,128]{2,1,0:T(8,128)(2,1)}, u32[]{:S(2)}) copy-start(bf16[2,440,128]{2,1,0:T(8,128)(2,1)} %slice.168.refs_8_) | copy-start | bytes 675844
  270.2 25.6 %copy-start.3 = (f32[8,440,128]{2,1,0:T(8,128)S(1)}, f32[8,440,128]{2,1,0:T(8,128)}, u32[]{:S(2)}) copy-start(f32[8,440,128]{2,1,0:T(8,128)} %copy-done.2) | copy-start | bytes 5406724
  293.9 6.7 %collective-permute-start.23 = (bf16[2,440,128]{2,1,0:T(8,128)(2,1)S(1)}, bf16[2,440,128]{2,1,0:T(8,128)(2,1)S(1)}, u32[]{:S(2)}, u32[]{:S(2)}) collective-permute-start(bf16[2,440,128]{2,1,0:T(8,128)(2,1)S(1)} %copy-done.17), channel_id=1, source_target_pairs={{0,1},{1,0},{2,3},{3,2},{4,5},{5,4},{6,7},{7,6},{8,9},{9,8},{10,11... | collective-permute-start | bytes 675848 | tf_op jit(solution)/shard_map/ppermute | solution.py:187
  323.8 2.7 collective-permute-start.25
  323.8 9.3 %collective-permute-start.32 = (bf16[2,440,128]{2,1,0:T(8,128)(2,1)S(1)}, bf16[2,440,128]{2,1,0:T(8,128)(2,1)S(1)}, u32[]{:S(2)}, u32[]{:S(2)}) collective-permute-start(bf16[2,440,128]{2,1,0:T(8,128)(2,1)S(1)} %copy-done.16), channel_id=1, source_target_pairs={{0,16},{4,20},{8,24},{12,28},{16,0},{20,4},{24,8},{28,12},{1,17},{... | collective-permute-start | bytes 675848 | tf_op jit(solution)/shard_map/ppermute | solution.py:189
  326.4 6.3 %copy-start.18 = (bf16[1,440,128]{2,1,0:T(8,128)(2,1)S(1)}, bf16[1,440,128]{2,1,0:T(8,128)(2,1)}, u32[]{:S(2)}) copy-start(bf16[1,440,128]{2,1,0:T(8,128)(2,1)} %slice.170.refs_12_) | copy-start | bytes 337924
  328.3 11.4 %collective-permute-start.26 = (bf16[880,128]{1,0:T(8,128)(2,1)S(1)}, bf16[880,128]{1,0:T(8,128)(2,1)S(1)}, u32[]{:S(2)}, u32[]{:S(2)}) collective-permute-start(bf16[880,128]{1,0:T(8,128)(2,1)S(1)} %get-tuple-element.240), channel_id=1, source_target_pairs={{0,1},{1,0},{2,3},{3,2},{4,5},{5,4},{6,7},{7,6},{8,9},{9,8},{10,11... | collective-permute-start | bytes 675848 | tf_op jit(solution)/shard_map/ppermute | solution.py:194
  329.4 21.4 %collective-permute-start.27 = (bf16[880,128]{1,0:T(8,128)(2,1)S(1)}, bf16[880,128]{1,0:T(8,128)(2,1)S(1)}, u32[]{:S(2)}, u32[]{:S(2)}) collective-permute-start(bf16[880,128]{1,0:T(8,128)(2,1)S(1)} %get-tuple-element.242), channel_id=1, source_target_pairs={{0,2},{1,3},{2,0},{3,1},{4,6},{5,7},{6,4},{7,5},{8,10},{9,11},{10,... | collective-permute-start | bytes 675848 | tf_op jit(solution)/shard_map/ppermute | solution.py:194
  330.5 20.3 %collective-permute-start.28 = (bf16[880,128]{1,0:T(8,128)(2,1)S(1)}, bf16[880,128]{1,0:T(8,128)(2,1)S(1)}, u32[]{:S(2)}, u32[]{:S(2)}) collective-permute-start(bf16[880,128]{1,0:T(8,128)(2,1)S(1)} %get-tuple-element.241), channel_id=1, source_target_pairs={{0,3},{1,2},{2,1},{3,0},{4,7},{5,6},{6,5},{7,4},{8,11},{9,10},{10,... | collective-permute-start | bytes 675848 | tf_op jit(solution)/shard_map/ppermute | solution.py:194
  332.7 24.3 %collective-permute-start.35 = (bf16[1,440,128]{2,1,0:T(8,128)(2,1)S(1)}, bf16[1,440,128]{2,1,0:T(8,128)(2,1)S(1)}, u32[]{:S(2)}, u32[]{:S(2)}) collective-permute-start(bf16[1,440,128]{2,1,0:T(8,128)(2,1)S(1)} %copy-done.18), channel_id=1, source_target_pairs={{0,2},{1,3},{2,0},{3,1},{4,6},{5,7},{6,4},{7,5},{8,10},{9,11},{10,... | collective-permute-start | bytes 337928 | tf_op jit(solution)/shard_map/ppermute | solution.py:187
  350.9 9.1 %collective-permute-start.29 = (bf16[880,128]{1,0:T(8,128)(2,1)S(1)}, bf16[880,128]{1,0:T(8,128)(2,1)S(1)}, u32[]{:S(2)}, u32[]{:S(2)}) collective-permute-start(bf16[880,128]{1,0:T(8,128)(2,1)S(1)} %fusion.5), channel_id=1, source_target_pairs={{8,0},{12,4},{9,1},{13,5},{10,2},{14,6},{11,3},{15,7}} | collective-permute-start | bytes 675848 | tf_op jit(solution)/shard_map/ppermute | solution.py:1449
  352.2 10.3 %collective-permute-start.30 = (bf16[880,128]{1,0:T(8,128)(2,1)S(1)}, bf16[880,128]{1,0:T(8,128)(2,1)S(1)}, u32[]{:S(2)}, u32[]{:S(2)}) collective-permute-start(bf16[880,128]{1,0:T(8,128)(2,1)S(1)} %fusion.5), channel_id=1, source_target_pairs={{16,0},{20,4},{17,1},{21,5},{18,2},{22,6},{19,3},{23,7}} | collective-permute-start | bytes 675848 | tf_op jit(solution)/shard_map/ppermute | solution.py:1449
  353.5 9.0 %collective-permute-start.31 = (bf16[880,128]{1,0:T(8,128)(2,1)S(1)}, bf16[880,128]{1,0:T(8,128)(2,1)S(1)}, u32[]{:S(2)}, u32[]{:S(2)}) collective-permute-start(bf16[880,128]{1,0:T(8,128)(2,1)S(1)} %fusion.5), channel_id=1, source_target_pairs={{24,0},{28,4},{25,1},{29,5},{26,2},{30,6},{27,3},{31,7}} | collective-permute-start | bytes 675848 | tf_op jit(solution)/shard_map/ppermute | solution.py:1449
  354.8 5.1 %collective-permute-start.33 = (bf16[1,440,128]{2,1,0:T(8,128)(2,1)S(1)}, bf16[1,440,128]{2,1,0:T(8,128)(2,1)S(1)}, u32[]{:S(2)}, u32[]{:S(2)}) collective-permute-start(bf16[1,440,128]{2,1,0:T(8,128)(2,1)S(1)} %slice.169), channel_id=1, source_target_pairs={{0,8},{4,12},{8,0},{12,4},{16,24},{20,28},{24,16},{28,20},{1,9},{5... | collective-permute-start | bytes 337928 | tf_op jit(solution)/shard_map/ppermute | solution.py:189
  363.4 4.8 %collective-permute-start.34 = (f32[440,128]{1,0:T(8,128)S(1)}, f32[440,128]{1,0:T(8,128)S(1)}, u32[]{:S(2)}, u32[]{:S(2)}) collective-permute-start(f32[440,128]{1,0:T(8,128)S(1)} %get-tuple-element.237), channel_id=1, source_target_pairs={{0,8},{4,12},{1,9},{5,13},{2,10},{6,14},{3,11},{7,15}} | collective-permute-start | bytes 675848 | tf_op jit(solution)/shard_map/ppermute | solution.py:1451
  374.0 8.8 %collective-permute-start.36 = (f32[8,128]{1,0:T(8,128)S(1)}, f32[8,128]{1,0:T(8,128)S(1)}, u32[]{:S(2)}, u32[]{:S(2)}) collective-permute-start(f32[8,128]{1,0:T(8,128)S(1)} %select_add_fusion), channel_id=1, source_target_pairs={{0,1},{1,0},{2,3},{3,2},{4,5},{5,4},{6,7},{7,6},{8,9},{9,8},{10,11... | collective-permute-start | bytes 12296 | tf_op jit(solution)/shard_map/ppermute | solution.py:187
  382.8 4.5 %collective-permute-start.37 = (f32[8,128]{1,0:T(8,128)S(1)}, f32[8,128]{1,0:T(8,128)S(1)}, u32[]{:S(2)}, u32[]{:S(2)}) collective-permute-start(f32[8,128]{1,0:T(8,128)S(1)} %add.112), channel_id=1, source_target_pairs={{0,2},{1,3},{2,0},{3,1},{4,6},{5,7},{6,4},{7,5},{8,10},{9,11},{10,... | collective-permute-start | bytes 12296 | tf_op jit(solution)/shard_map/ppermute | solution.py:187
  387.3 1.2 collective-permute-start.38
  388.5 4.1 collective-permute-start.39
  392.5 3.6 collective-permute-start.40
  (22 other events, 62.6 us)
Sparse Core Ops, SparseCore 0:
  51.5 71.9 all-gather.1

commit v3 on v2

--- a/solution.py
+++ b/solution.py
@@ -225,7 +225,7 @@
 def fill_flat(me, piece_refs, rels, rows, flat):
     for ref, rel in zip(piece_refs, rels):
         for k, r in enumerate(rel):
-            flat[pl.ds(rows * jnp.bitwise_xor(me, r), rows), :] = ref[k, 0:rows, :].astype(f32)
+            flat[pl.ds(rows * jnp.bitwise_xor(me, r), rows), :] = ref[k].astype(f32)[0:rows]
 
 
 def unpack_stem_kernel(rels, rows, me_ref, resize_ref, *refs):
@@ -262,7 +262,7 @@
                 value = jnp.where(lane < CLASSES - 7 * LANES, value, 0.0)
             tiles[t, pl.ds(rho, 24, stride=16), :] = value
     for t in range(8):
-        head_w[:, LANES * t : LANES * (t + 1)] = tiles[t].astype(bf16)
+        head_w[:, LANES * t : LANES * (t + 1)] = tiles[t, 0:D, :].astype(bf16)
     put_row(flat, row_of(0, 7), head_b, 0, CLASS_PAD)
 
 
@@ -281,7 +281,7 @@
         ],
         in_specs=[SM] + [VM] * (1 + len(pieces)),
         out_specs=[VM] * 6,
-        scratch_shapes=[pltpu.VMEM((count * rows, LANES), f32), pltpu.VMEM((8, D, LANES), f32)],
+        scratch_shapes=[pltpu.VMEM((count * rows, LANES), f32), pltpu.VMEM((8, D + 16, LANES), f32)],
         compiler_params=params(),
         name="unpack_stem",
     )(me, jnp.asarray(resize), *pieces)
@@ -390,27 +390,6 @@
         for k in range(len(rel)):
             count = count + ref[k].astype(f32)[rows : rows + 1, :]
     total[...] = count
-
-
-def unpack_class(me, pieces, rels, rows, count):
-    return pl.pallas_call(
-        functools.partial(unpack_class_kernel, rels, rows),
-        out_shape=[
-            sds((D, D), bf16),
-            sds((D, 2 * D), bf16),
-            sds((D, D), bf16),
-            sds((D, FF), bf16),
-            sds((FF, D), bf16),
-            sds((16, D), f32),
-            sds((1, FF), f32),
-            sds((1, LANES), f32),
-        ],
-        in_specs=[SM] + [VM] * len(pieces),
-        out_specs=[VM] * 8,
-        scratch_shapes=[pltpu.VMEM((count * rows, LANES), f32)],
-        compiler_params=params(),
-        name="unpack_class",
-    )(me, *pieces)
 
 
 def const_spec(a):
@@ -749,32 +728,50 @@
     g_svec[1:2, :] = colsum(d_mid) + norm_back(d_a_cls, unit_cls, inv_cls, row(CG1))
 
 
-def class_block(out_s, out_l, classw, stem, total, counts, labels_s, labels_l, valid):
-    ns, padded, _ = out_s.shape
-    nl, large_len, _ = out_l.shape
-    wq, wkv, wo, w1, w2, vec, c1 = classw
+CLASS_WEIGHTS = [(D, D), (D, 2 * D), (D, D), (D, FF), (FF, D)]
+
+
+def class_step_kernel(ns, nl, valid, unpack_rels, pack_rels, rows, n, me_ref, from_ref, counts, labels_s, labels_l, *refs):
+    pieces, (out_s, out_l, svec, head_w, head_b), refs = refs[:n], refs[n : n + 5], refs[n + 5 :]
+    (d_s, d_l, g_svec, g_head_w, g_head_b, loss, keep, send), refs = refs[:8], refs[8:]
+    weights, total, grads, flat, work = refs[:7], refs[7], refs[8:15], refs[15], refs[16:]
+    unpack_class_kernel(unpack_rels, rows, from_ref, *pieces, *weights, total, flat)
+    class_kernel(
+        ns, nl, valid, out_s, out_l, *weights, svec, head_w, head_b, total, counts, labels_s, labels_l,
+        d_s, d_l, *grads, g_svec, g_head_w, g_head_b, loss, *work,
+    )
+    pack_class_kernel(pack_rels, rows, me_ref, *grads, keep, send, flat)
+
+
+def class_step(me, unpack_me, pieces, unpack_rels, pack_rels, out, stem, counts, labels_s, labels_l, valid, rows, padded_rows):
+    (ns, padded, _), (nl, large_len, _) = out[0].shape, out[1].shape
     _, svec, _, _, head_w, head_b = stem
-    args = (out_s, out_l, wq, wkv, wo, w1, w2, vec, c1, svec, head_w, head_b, total, counts, labels_s, labels_l)
+    args = (me, unpack_me, counts, labels_s, labels_l, *pieces, *out, svec, head_w, head_b)
+    half = len(pack_rels) // 2
+    vectors = [pltpu.VMEM((16, D), f32), pltpu.VMEM((1, FF), f32)]
     return pl.pallas_call(
-        functools.partial(class_kernel, ns, nl, valid),
+        functools.partial(
+            class_step_kernel, ns, nl, valid, unpack_rels, pack_rels, rows, len(pieces)
+        ),
         out_shape=[
             sds((ns, padded, D), f32),
             sds((nl, large_len, D), f32),
-            sds((D, D), f32),
-            sds((D, 2 * D), f32),
-            sds((D, D), f32),
-            sds((D, FF), f32),
-            sds((FF, D), f32),
-            sds((16, D), f32),
-            sds((1, FF), f32),
             sds((8, D), f32),
             sds((D, CLASS_PAD), f32),
             sds((1, CLASS_PAD), f32),
             sds((1, LANES), f32),
+            sds((half, padded_rows, LANES), f32),
+            sds((half, padded_rows, LANES), bf16),
         ],
-        in_specs=[VM] * (len(args) - 3) + [SM] * 3,
-        out_specs=[VM] * 13,
-        scratch_shapes=[
+        in_specs=[SM] * 5 + [VM] * (len(args) - 5),
+        out_specs=[VM] * 8,
+        scratch_shapes=[pltpu.VMEM(shape, bf16) for shape in CLASS_WEIGHTS]
+        + vectors
+        + [pltpu.VMEM((1, LANES), f32)]
+        + [pltpu.VMEM(shape, f32) for shape in CLASS_WEIGHTS]
+        + vectors
+        + [
+            pltpu.VMEM((len(pack_rels) * rows + padded_rows - rows + 8, LANES), f32),
             pltpu.VMEM((ns, padded, D), bf16),
             pltpu.VMEM((nl, large_len, D), bf16),
             pltpu.VMEM((ns, HEADS, padded), f32),
@@ -787,8 +784,8 @@
             pltpu.VMEM((HEADS, D), f32),
         ],
         compiler_params=params(),
-        cost_estimate=pl.CostEstimate(flops=10_000_000_000, bytes_accessed=60_000_000, transcendentals=0),
-        name="class_block",
+        cost_estimate=cost(25e9, 40e6),
+        name="class_step",
     )(*args)
 
 
@@ -920,16 +917,18 @@
     )
 
 
-def embed_back_kernel(steps, valid, ps, plg, resize, *refs):
+def embed_back_kernel(steps, valid, late, me_ref, ps, plg, resize, *refs):
     tok_r, dq_s, d_mid_r, refs = refs[:2], refs[2], refs[3:5], refs[5:]
-    dq_l, (wqkv, vec), refs = refs[: steps.large * steps.count], refs[steps.large * steps.count :][:2], refs[steps.large * steps.count + 2 :]
-    g_wqkv, g_vec, g_patch_w, g_patch_b, g_pos, pos_large, d_qkv = refs
+    n = steps.large * steps.count
+    dq_l, (wqkv, vec, pre, post, g_wo, g_svec, g_head_w), refs = refs[:n], refs[n : n + 7], refs[n + 7 :]
+    (keep, send), sums, (d_qkv, flat, tiles) = refs[:2], refs[2:8], refs[8:]
+    g_wqkv, g_vec, g_patch_w, g_patch_b, g_pos, pos_large = sums
     row = lambda at: vec[at : at + 1, :]
     step = pl.program_id(0)
 
     @pl.when(step == 0)
     def _():
-        for ref in refs[:-1]:
+        for ref in sums:
             ref[...] = jnp.zeros_like(ref)
 
     d_qkv[: steps.split, :] = dq_s[...].reshape(steps.split, 3 * D)
@@ -970,9 +969,13 @@
             resize[...], pos_large[...], (((1,), (0,)), ((), ())),
             preferred_element_type=f32, precision=lax.Precision.HIGHEST,
         )
-
-
-def embed_back(ps, plg, tok, dq_s, d_mid, dq_l, wqkv, vec, after):
+        pack_late_kernel(
+            *late, me_ref, g_wqkv, g_vec, pre, post, g_wo, g_patch_w, g_patch_b, g_pos, g_svec, g_head_w,
+            keep, send, flat, tiles,
+        )
+
+
+def embed_back(me, ps, plg, tok, dq_s, d_mid, dq_l, wqkv, vec, others, late, padded_rows, after):
     ns, valid, _ = ps.shape
     nl, large_len, _ = plg.shape
     steps = Steps(ns, nl, tok[0].shape[1], large_len)
@@ -985,13 +988,16 @@
         sds((valid, D), f32),
     ]
     index = lambda i: (i, 0, 0)
+    half = len(late[0]) // 2
+    outs = [sds((half, 2 * padded_rows, LANES), f32), sds((half, 2 * padded_rows, LANES), bf16)]
     return call(
-        functools.partial(embed_back_kernel, steps, valid),
-        (ps, plg, resize, *tok, dq_s, *d_mid, *dq_l, wqkv, vec),
+        functools.partial(embed_back_kernel, steps, valid, late),
+        (me, ps, plg, resize, *tok, dq_s, *d_mid, *dq_l, wqkv, vec, *others),
         after,
         grid=steps.grid,
-        out_shape=sums,
+        out_shape=outs,
         in_specs=[
+            SM,
             pl.BlockSpec((steps.small, valid, PATCH_IN), index),
             pl.BlockSpec((steps.large, large_len, PATCH_IN), index),
             const_spec(resize),
@@ -999,10 +1005,15 @@
             steps.specs(3 * D)[0],
             *steps.specs(D),
         ]
-        + [const_spec(a) for a in dq_l]
-        + [const_spec(wqkv), const_spec(vec)],
-        out_specs=sum_specs(sums),
-        scratch_shapes=[pltpu.VMEM((large_len, D), f32), pltpu.VMEM((steps.rows, 3 * D), bf16)],
+        + [const_spec(a) for a in (*dq_l, wqkv, vec, *others)],
+        out_specs=[const_spec(a) for a in outs],
+        scratch_shapes=[pltpu.VMEM(a.shape, f32) for a in sums]
+        + [
+            pltpu.VMEM((large_len, D), f32),
+            pltpu.VMEM((steps.rows, 3 * D), bf16),
+            pltpu.VMEM((row_of(0, 6) + 1280, LANES), f32),
+            pltpu.VMEM((8, D + 16, LANES), f32),
+        ],
         cost_estimate=cost(20e9, 30e6),
         name="embed_back",
     )
@@ -1054,7 +1065,7 @@
 
 def take_head(flat, base, head_w, head_b, tiles, groups):
     for t in range(8):
-        tiles[t] = head_w[:, LANES * t : LANES * (t + 1)]
+        tiles[t, 0:D, :] = head_w[:, LANES * t : LANES * (t + 1)]
     lane = lax.broadcasted_iota(jnp.int32, (groups, LANES), 1)
     for rho in range(16):
         first, shift = (CLASSES * rho) // LANES, (CLASSES * rho) % LANES
@@ -1232,7 +1243,7 @@
     )(me, step, jnp.asarray(bounds_table()), master, first, second, *grads)
 
 
-def apply_kernel(me_ref, sums, master, update, new_o, weight_o, norm_o, trust_o):
+def apply_kernel(me_ref, sums, bounds, master, update, new_o, weight_o, norm_o, trust_o):
     shard = master.shape[1]
     roots = jnp.sqrt(sums[...])
     weight_norms, update_norms = roots[0:3, :], roots[3:6, :]
@@ -1243,32 +1254,35 @@
     weight_o[...] = weight_norms[:, 0:SEGMENTS]
     norm_o[...] = update_norms[:, 0:SEGMENTS]
     trust_o[...] = trust[:, 0:SEGMENTS]
-    position = me_ref[0] * shard + lax.broadcasted_iota(jnp.int32, (3, shard), 1)
-    group = lax.broadcasted_iota(jnp.int32, (3, 1), 0)
-    ratio = jnp.broadcast_to(trust[:, 0:1], (3, shard))
-    for s in range(1, SEGMENTS):
-        low = pick(group, [int(STARTS[g, s]) if REAL[g, s] > 0 else 2**30 for g in range(3)])
-        ratio = jnp.where(position >= low, trust[:, s : s + 1], ratio)
-    new_o[...] = master[...] - learn_rate * ratio * update[...]
+    rows = shard // LANES
+    place = 2 * (me_ref[0] * rows + lax.broadcasted_iota(jnp.int32, (rows, LANES), 0))
+    lane = lax.broadcasted_iota(jnp.int32, (rows, LANES), 1)
+    for g in range(3):
+        low, high, mine = bounds[g : g + 1, :], bounds[3 + g : 4 + g, :], trust[g : g + 1, :]
+        left = jnp.sum(jnp.where((place >= low) & (place < high), mine, 0.0), -1, keepdims=True)
+        right = jnp.sum(jnp.where((place + 1 >= low) & (place + 1 < high), mine, 0.0), -1, keepdims=True)
+        ratio = jnp.where(lane < 64, left, right).reshape(1, shard)
+        new_o[g : g + 1, :] = master[g : g + 1, :] - learn_rate * ratio * update[g : g + 1, :]
 
 
 def apply_update(me, sums, master, update):
     return pl.pallas_call(
         apply_kernel,
         out_shape=[sds(master.shape, f32)] + [sds((3, SEGMENTS), f32)] * 3,
-        in_specs=[SM] + [VM] * 3,
+        in_specs=[SM] + [VM] * 4,
         out_specs=[VM] * 4,
         compiler_params=params(),
         name="apply_update",
-    )(me, sums, master, update)
-
-
-def round_kernel(rows, counts, master, stem, selfb, classb):
+    )(me, sums, jnp.asarray(bounds_table()), master, update)
+
+
+def round_kernel(rows, counts, master, stem, selfb, classb, lines):
+    tail = lines.shape[0] - rows
     for g, ref in enumerate((stem, selfb, classb)):
-        ref[0, 0:rows, :] = master[g : g + 1, :].reshape(rows, LANES).astype(bf16)
-        tail = ref.shape[1] - rows
+        lines[0:rows, :] = master[g : g + 1, :].reshape(rows, LANES)
         count = counts[0, 0] + counts[0, 1] if g == 2 else 0
-        ref[0, rows:, :] = jnp.full((tail, LANES), count, jnp.int32).astype(f32).astype(bf16)
+        lines[rows:, :] = jnp.full((tail, LANES), count, jnp.int32).astype(f32)
+        ref[0] = lines[...].astype(bf16)
 
 
 def round_shards(counts, master, rows, padded_rows):
@@ -1277,6 +1291,7 @@
         out_shape=[sds((1, padded_rows, LANES), bf16)] * 3,
         in_specs=[SM, VM],
         out_specs=[VM] * 3,
+        scratch_shapes=[pltpu.VMEM((padded_rows, LANES), f32)],
         compiler_params=params(),
         name="round_shards",
     )(counts, master)
@@ -1312,7 +1327,7 @@
     step,
 ):
     rows = master.shape[1] // LANES
-    padded_rows = -(-(rows + 1) // 8) * 8
+    padded_rows = -(-(rows + 1) // 16) * 16
     n_dp, n_z = lax.axis_size("dp"), lax.axis_size("fsdp")
     z_bits, bits = log2(n_z), log2(n_dp) + log2(n_z)
     devices = n_dp * n_z
@@ -1338,6 +1353,7 @@
     stem_shard, self_shard, class_shard = round_shards(counts, master, rows, padded_rows)
     up = n_dp // 2
     got = lax.ppermute(stem_shard, "dp", [(i, i + up) for i in range(up)])
+    (got,) = tied((got,), old_sums)
     others = [lax.ppermute(self_shard, "dp", [(i, i ^ (a * n_quarter)) for i in range(n_dp)]) for a in (1, 2, 3)]
     stem_state = gather_z(jnp.where(in_half, stem_shard, got), [0])
 
@@ -1363,7 +1379,7 @@
     )
     wqkv, vec, pre_col, post_col, pre_row, post_row = unpack_low(me_quarter, *arrays(first_state), rows, quarter)
     tok, (qkv_s, qkv_l) = embed(
-        patches_small, patches_large, patch_w, pos_small, pos_large, wqkv, vec, padded, [old_sums]
+        patches_small, patches_large, patch_w, pos_small, pos_large, wqkv, vec, padded, []
     )
     att_s, lse_s = attend(qkv_s, pre_col, post_col, valid, small_per, 20e9, [])
     rest_state = gather_z(rest, [quarter, 2 * quarter, 3 * quarter], att_s)
@@ -1374,33 +1390,25 @@
     wo, w1, w2, vec_feed, c1 = unpack_feed(me_quarter, *arrays(first_state + rest_state), rows, devices)
     att = (att_s, att_l)
     branch, mid, act, slope, lower, out = feed(tok, att, (wo, w1, w2, vec_feed, c1), [])
-    *classw, total = unpack_class(jnp.zeros_like(me), [class_all], [list(range(devices))], rows, devices)
-
-    d_out_s, d_out_l, *class_grads, g_svec, g_head_w, g_head_b, loss = class_block(
-        *out, classw, stem, total, counts, labels_small, labels_large, valid
-    )
-
     z_order = list(range(z_bits - 1, -1, -1))
     near_far = list(range(z_bits))
     class_order = [core, top, second] + inner + near_far
     feed_order = [core] + near_far + [top, second] + inner
     class_rels, feed_rels = slots_of(class_order), slots_of(feed_order)
-    tail = 8 * (padded_rows // 8 - rows // 8)
-
-    class_chain = Chain(
-        *pack(
-            functools.partial(pack_class_kernel, class_rels, rows), "pack_class", me, class_grads, class_rels,
-            padded_rows, devices * rows + tail,
-        ),
-        class_order, z_bits,
-    )
+    tail = padded_rows - rows + 8
+
+    d_out_s, d_out_l, g_svec, g_head_w, g_head_b, loss, keep, send = class_step(
+        me, jnp.zeros_like(me), [class_all], [list(range(devices))], class_rels, out, stem, counts, labels_small,
+        labels_large, valid, rows, padded_rows,
+    )
+    class_chain = Chain(keep, send, class_order, z_bits)
     d_mid, (d_att_s, d_att_l), (g_wo, g_w1, g_w2, g_vec_feed, g_c1) = feed_back(
         ((d_out_s, d_out_l), mid, act, slope, lower, branch, att), (wo, w1, w2, vec_feed), [class_chain.send]
     )
     class_chain.step(d_att_s)
     quarter_rows = quarter * rows
     offset = -(-max(0, quarter_rows - row_of(0, 6)) // 8) * 8
-    tiles = [pltpu.VMEM((8, D, LANES), f32)]
+    tiles = [pltpu.VMEM((8, D + 16, LANES), f32)]
     feed_chain = Chain(
         *pack(
             functools.partial(pack_feed_kernel, feed_rels, rows, offset, quarter_rows), "pack_feed", me,
@@ -1424,23 +1432,16 @@
         pre_sum, post_sum = pre_sum + pre_l, post_sum + post_l
     for chain in chains:
         chain.step(part)
-    g_wqkv, g_vec, g_patch_w, g_patch_b, g_pos = embed_back(
-        patches_small, patches_large, tok, dq_s, d_mid, dq_l, wqkv, vec,
+    late_rels = slots_of([core] + inner + z_order)
+    keep, send = embed_back(
+        me_quarter, patches_small, patches_large, tok, dq_s, d_mid, dq_l, wqkv, vec,
+        (pre_sum, post_sum, g_wo, g_svec, g_head_w), (late_rels, rows, quarter_rows), padded_rows,
         [chain.send for chain in chains],
     )
     for chain in chains:
         while not chain.done:
-            chain.step(g_vec)
-
-    late_rels = slots_of([core] + inner + z_order)
-    late_chain = Chain(
-        *pack(
-            functools.partial(pack_late_kernel, late_rels, rows, quarter_rows), "pack_late", me_quarter,
-            (g_wqkv, g_vec, pre_sum, post_sum, g_wo, g_patch_w, g_patch_b, g_pos, g_svec, g_head_w), late_rels,
-            2 * padded_rows, row_of(0, 6) + 1024, tiles,
-        ),
-        [core] + inner, z_bits, True,
-    )
+            chain.step(send)
+    late_chain = Chain(keep, send, [core] + inner, z_bits, True)
     while not late_chain.done:
         late_chain.step()
     part = late_chain.total

time: 414 us -> 397 us (0.959)
  Pallas kernels: 253 us -> 236 us
    pallas_call x3 -> x1, Pallas kernels: 18.5 us -> 7.1 us  [pack(): pl.pallas_call(kernel, out_shape=[sds((half, padded_rows, LANES), f32), s...]
    pallas_call x2 -> x1, Pallas kernels: 21.5 us -> 18 us  [class_step(): pl.pallas_call(functools.partial(class_step_kernel, ns, nl, valid, unpack...]
    unnamed x60 -> x62, local copies, waits for them, and re-layouts: 8.14 us -> 8.33 us
  transfers between devices with their start and end apart: 42 -> 42, of which waited for: 16 -> 16; matrix products, arithmetic and copies ran while one was open for 5% -> 6% of each run, Pallas kernels for 47% -> 48%
where the time goes in v3:
time: 397 us; the launch traced here: 392 us
  Pallas kernels  236 us (59%)
  starting transfers between devices  55.1 us (14%)
  waiting for transfers between devices  54.2 us (14%)
  other arithmetic  17.8 us (4%)
  between operations  15.4 us (4%)
  local copies, waits for them, and re-layouts  13.5 us (3%)
    pallas_call x9, Pallas kernels, call(): pl.pallas_call(wrapped, in_specs=specs, compiler_params=params(), **kw)  188 us
    ppermute x12, waiting for transfers between devices, exchange_z(): return lax.ppermute(value, 'fsdp', [(i, i ^ k) for i in range(n)])  30.2 us
    pallas_call x1, Pallas kernels, class_step(): pl.pallas_call(functools.partial(class_step_kernel, ns, nl, valid, unpack...  18 us
    ppermute x12, starting transfers between devices, exchange_z(): return lax.ppermute(value, 'fsdp', [(i, i ^ k) for i in range(n)])  17.9 us
    ppermute x6, starting transfers between devices, exchange(): return lax.ppermute(value, 'fsdp', [(i, i ^ 1 << bit) for i in range(n)])  13.7 us
    ppermute x15, waiting for transfers between devices, exchange(): lax.ppermute(value, 'dp', [(i, i ^ 1 << bit - z_bits) for i in range(n)])  11.1 us
    add x8, other arithmetic, step(): total = self.keep + got.astype(f32)  11 us
    ppermute x15, starting transfers between devices, exchange(): lax.ppermute(value, 'dp', [(i, i ^ 1 << bit - z_bits) for i in range(n)])  9.8 us
  transfers between devices with their start and end apart: 42, of which 16 were waited for; matrix products, arithmetic and copies ran while one was open for 6% of the time, Pallas kernels for 48%

profile of v3, /device:TPU:0, one launch (start us, length us, event | category | flops | bytes accessed | tf_op | source)
XLA Modules:
  0.0 392.0 jit_solution(2853749093409036162)
XLA Ops:
  7.2 1.9 round_shards.1
  9.2 5.0 %collective-permute-start = (bf16[1,448,128]{2,1,0:T(8,128)(2,1)}, bf16[1,448,128]{2,1,0:T(8,128)(2,1)S(1)}, u32[]{:S(2)}, u32[]{:S(2)}) collective-permute-start(bf16[1,448,128]{2,1,0:T(8,128)(2,1)} %get-tuple-element.103), channel_id=1, source_target_pairs={{0,16},{4,20},{8,24},{12,28},{1,17},{5,21},{9,25},{13,29},{2,18},{... | collective-permute-start | bytes 344072 | tf_op jit(solution)/shard_map/ppermute | solution.py:1355
  14.2 2.4 weight_sums.1
  17.8 1.6 collective-permute-start.1
  19.4 2.6 collective-permute-start.2
  22.2 2.4 collective-permute-start.7
  25.7 4.8 %collective-permute-done.2 = bf16[1,448,128]{2,1,0:T(8,128)(2,1)S(1)} collective-permute-done((bf16[1,448,128]{2,1,0:T(8,128)(2,1)S(1)}, bf16[1,448,128]{2,1,0:T(8,128)(2,1)S(1)}, u32[]{:S(2)}, u32[]{:S(2)}) %collective-permute-start.2) | collective-permute-done | bytes 114720 | tf_op jit(solution)/shard_map/ppermute | solution.py:194
  30.6 1.6 collective-permute-start.4
  32.3 1.9 collective-permute-start.10
  34.1 1.5 collective-permute-start.11
  37.8 6.3 %collective-permute-done.11 = bf16[1,448,128]{2,1,0:T(8,128)(2,1)S(1)} collective-permute-done((bf16[1,448,128]{2,1,0:T(8,128)(2,1)S(1)}, bf16[1,448,128]{2,1,0:T(8,128)(2,1)S(1)}, u32[]{:S(2)}, u32[]{:S(2)}) %collective-permute-start.11) | collective-permute-done | bytes 114720 | tf_op jit(solution)/shard_map/ppermute | solution.py:194
  46.1 1.9 collective-permute-start.14
  49.0 1.7 collective-permute-start.16
  50.7 2.6 unpack_low.1
  53.3 4.9 %unpack_stem.1 = (bf16[768,384]{1,0:T(8,128)(2,1)}, f32[8,384]{1,0:T(8,128)}, f32[208,384]{1,0:T(8,128)}, f32[576,384]{1,0:T(8,128)}, bf16[384,1024]{1,0:T(8,128)(2,1)}, /*index=5*/f32[1,1024]{1,0:T(1,128)}) custom-call(s32[1]{0:T(128)S(6)} %and.15.me_ref, f32[576,208]{1,0:T(8,128)} %constant.47.clone.resize_ref, bf16[4,448,128]{2,1,0:T(8,128)(2,1)} %copy-done.8, ...), custom_call_target="tpu_custom_call" | custom-call | tf_op jit(solution)/shard_map/unpack_stem/pallas_call | solution.py:272
  58.2 8.9 %embed.1 = (f32[4,208,384]{2,1,0:T(8,128)}, f32[2,576,384]{2,1,0:T(8,128)}, bf16[4,208,1152]{2,1,0:T(8,128)(2,1)}, bf16[2,576,1152]{2,1,0:T(8,128)(2,1)}) custom-call(bf16[4,196,768]{2,1,0:T(8,128)(2,1)} %copy.25.refs_0_.refs_1_, bf16[2,576,768]{2,1,0:T(8,128)(2,1)} %refs_2_.1, bf16[768,384]{1,0:T(8,128)(2,1)} %get-tuple-element.105.refs_2_, ...), custom_call_target="tpu_custom_call" | custom-call | flops 12000000000 | bytes 20000000 | tf_op jit(solution)/shard_map/embed/pallas_call | solution.py:177
  67.2 16.5 %attend.2 = (bf16[4,208,384]{2,1,0:T(8,128)(2,1)}, f32[4,8,208]{2,1,0:T(8,128)}) custom-call(bf16[4,208,1152]{2,1,0:T(8,128)(2,1)} %get-tuple-element.113.refs_0_, f32[384,8]{1,0:T(8,128)} %get-tuple-element.116.refs_1_.refs_3_, f32[384,8]{1,0:T(8,128)} %get-tuple-element.117.refs_2_.refs_4_), custom_call_target="tpu_custom_call" | custom-call | flops 20000000000 | bytes 10000000 | tf_op jit(solution)/shard_map/attend/pallas_call | solution.py:177
  86.9 25.8 %attend.3 = (bf16[2,576,384]{2,1,0:T(8,128)(2,1)}, f32[2,8,576]{2,1,0:T(8,128)}) custom-call(bf16[2,576,1152]{2,1,0:T(8,128)(2,1)} %get-tuple-element.119.refs_0_, f32[384,8]{1,0:T(8,128)} %get-tuple-element.116.refs_1_.refs_3_, f32[384,8]{1,0:T(8,128)} %get-tuple-element.117.refs_2_.refs_4_, bf16[12,448,128]{2,1,0:T(8,128)(2,1)} %copy-done.7, ...), custom_call_target="tpu_custom_call" | custom-call | flops 30000001024 | bytes 10000000 | tf_op jit(solution)/shard_map/attend/pallas_call | solution.py:177
  113.8 4.3 %unpack_feed.1 = (bf16[384,384]{1,0:T(8,128)(2,1)}, bf16[384,1536]{1,0:T(8,128)(2,1)}, bf16[1536,384]{1,0:T(8,128)(2,1)}, f32[16,384]{1,0:T(8,128)}, f32[1,1536]{1,0:T(1,128)}) custom-call(s32[1]{0:T(128)S(6)} %and.14.me_ref.refs_0_, bf16[4,448,128]{2,1,0:T(8,128)(2,1)} %copy-done.6, bf16[4,448,128]{2,1,0:T(8,128)(2,1)} %copy-done.9, ...), custom_call_target="tpu_custom_call" | custom-call | tf_op jit(solution)/shard_map/unpack_feed/pallas_call | solution.py:355
  118.1 26.2 %feed.1 = (bf16[4,208,384]{2,1,0:T(8,128)(2,1)}, bf16[2,576,384]{2,1,0:T(8,128)(2,1)}, f32[4,208,384]{2,1,0:T(8,128)}, f32[2,576,384]{2,1,0:T(8,128)}, bf16[4,20...) custom-call(f32[4,208,384]{2,1,0:T(8,128)} %get-tuple-element.111.re, ...), custom_call_target="tpu_custom_call" | custom-call | flops 20000000000 | bytes 30000000 | tf_op jit(solution)/shard_map/feed/pallas_call | solution.py:177
  144.3 18.0 %class_step.1 = (f32[4,208,384]{2,1,0:T(8,128)}, f32[2,576,384]{2,1,0:T(8,128)}, f32[8,384]{1,0:T(8,128)}, f32[384,1024]{1,0:T(8,128)}, f32[1,1024]{1,0:T(1,128)...) custom-call(s32[1]{0:T(128)} %bitcast.me_ref, s32[1]{0:T(128)} %constant.43.clone.1.from_ref, ...), custom_call_target="tpu_custom_call" | custom-call | flops 24999999488 | bytes 40000000 | tf_op jit(solution)/shard_map/class_step/pallas_call | solution.py:752
  162.3 24.3 %feed_back.1 = (f32[4,208,384]{2,1,0:T(8,128)}, f32[2,576,384]{2,1,0:T(8,128)}, bf16[4,208,384]{2,1,0:T(8,128)(2,1)}, bf16[2,576,384]{2,1,0:T(8,128)(2,1)}, f32[...) custom-call(f32[4,208,384]{2,1,0:T(8,128)} %get-tuple-element.135.refs, ...), custom_call_target="tpu_custom_call" | custom-call | flops 35000000512 | bytes 30000000 | tf_op jit(solution)/shard_map/feed_back/pallas_call | solution.py:177
  186.7 7.1 %pack_feed.1 = (f32[16,448,128]{2,1,0:T(8,128)}, bf16[16,448,128]{2,1,0:T(8,128)(2,1)}) custom-call(s32[1]{0:T(128)} %bitcast.me_ref, f32[384,384]{1,0:T(8,128)} %get-tuple-element.154.wo.refs_15_, f32[384,1536]{1,0:T(8,128)} %get-tuple-element.155.w1, f32[1536,384]{1,0:T(8,128)} %get-tuple-element.156.w2, f32[16,384]{1,0:T(8,128)} %get-tuple-element.157.vec, ...), custom_call_target="tpu_custom_call" | custom-call | tf_op jit(solution)/shard_map/pack_feed/pallas_call | solution.py:1149
  195.5 3.0 convert_add_fusion.1
  200.6 20.1 %attend_back.3 = (bf16[4,208,1152]{2,1,0:T(8,128)(2,1)}, f32[8,384]{1,0:T(8,128)}, f32[8,384]{1,0:T(8,128)}) custom-call(bf16[4,208,1152]{2,1,0:T(8,128)(2,1)} %get-tuple-element.113.refs_0_, bf16[4,208,384]{2,1,0:T(8,128)(2,1)} %get-tuple-element.148.refs_1_, f32[4,8,208]{2,1,0:T(8,128)} %get-tuple-element.149.refs_2_, ...), custom_call_target="tpu_custom_call" | custom-call | flops 24999999488 | bytes 10000000 | tf_op jit(solution)/shard_map/attend_back/pallas_call | solution.py:177
  220.7 3.0 convert_add_fusion
  228.8 23.3 %attend_back.4 = (bf16[1,576,1152]{2,1,0:T(8,128)(2,1)}, f32[8,384]{1,0:T(8,128)}, f32[8,384]{1,0:T(8,128)}) custom-call(bf16[2,576,1152]{2,1,0:T(8,128)(2,1)} %get-tuple-element.119.refs_0_, bf16[2,576,384]{2,1,0:T(8,128)(2,1)} %get-tuple-element.165.refs_1_, f32[2,8,576]{2,1,0:T(8,128)} %get-tuple-element.166.refs_2_, ...), custom_call_target="tpu_custom_call" | custom-call | flops 24999999488 | bytes 10000000 | tf_op jit(solution)/shard_map/attend_back/pallas_call | solution.py:177
  254.8 1.9 collective-permute-start.24
  258.6 23.7 %attend_back.5 = (bf16[1,576,1152]{2,1,0:T(8,128)(2,1)}, f32[8,384]{1,0:T(8,128)}, f32[8,384]{1,0:T(8,128)}) custom-call(bf16[2,576,1152]{2,1,0:T(8,128)(2,1)} %get-tuple-element.119.refs_0_, bf16[2,576,384]{2,1,0:T(8,128)(2,1)} %get-tuple-element.165.refs_1_, f32[2,8,576]{2,1,0:T(8,128)} %get-tuple-element.166.refs_2_, ...), custom_call_target="tpu_custom_call" | custom-call | flops 24999999488 | bytes 10000000 | tf_op jit(solution)/shard_map/attend_back/pallas_call | solution.py:177
  285.8 3.4 collective-permute-done.23
  289.8 18.8 %embed_back.1 = (f32[4,896,128]{2,1,0:T(8,128)}, bf16[4,896,128]{2,1,0:T(8,128)(2,1)}) custom-call(s32[1]{0:T(128)S(6)} %and.14.me_ref.refs_0_, bf16[4,196,768]{2,1,0:T(8,128)(2,1)} %copy.25.refs_0_.refs_1_, bf16[2,576,768]{2,1,0:T(8,128)(2,1)} %refs_2_.1, f32[196,576]{1,0:T(8,128)} %constant.48.clone.refs_3_, ...), custom_call_target="tpu_custom_call" | custom-call | flops 20000000000 | bytes 30000000 | tf_op jit(solution)/shard_map/embed_back/pallas_call | solution.py:177
  309.7 1.7 collective-permute-done.25
  311.4 1.8 fusion.7
  315.3 2.3 collective-permute-start.28
  317.8 7.0 %collective-permute-done.26 = bf16[896,128]{1,0:T(8,128)(2,1)S(1)} collective-permute-done((bf16[896,128]{1,0:T(8,128)(2,1)S(1)}, bf16[896,128]{1,0:T(8,128)(2,1)S(1)}, u32[]{:S(2)}, u32[]{:S(2)}) %collective-permute-start.26) | collective-permute-done | bytes 229408 | tf_op jit(solution)/shard_map/ppermute | solution.py:194
  324.8 11.0 %collective-permute-done.27 = bf16[896,128]{1,0:T(8,128)(2,1)S(1)} collective-permute-done((bf16[896,128]{1,0:T(8,128)(2,1)S(1)}, bf16[896,128]{1,0:T(8,128)(2,1)S(1)}, u32[]{:S(2)}, u32[]{:S(2)}) %collective-permute-start.27) | collective-permute-done | bytes 229408 | tf_op jit(solution)/shard_map/ppermute | solution.py:194
  342.1 3.0 collective-permute-done.33
  345.1 2.5 collective-permute-done.30
  350.6 2.8 collective-permute-done.34
  354.1 4.4 %adam.1 = (f32[3,55552]{1,0:T(4,128)}, f32[3,55552]{1,0:T(4,128)}, f32[3,55552]{1,0:T(4,128)}, f32[3,55552]{1,0:T(4,128)}, f32[8,128]{1,0:T(8,128)}) custom-call(s32[1]{0:T(128)} %bitcast.me_ref, s32[1]{0:T(128)S(6)} %copy.29.step_ref, s32[8,128]{1,0:T(8,128)} %constant.46.clone.bounds, f32[3,55552]{1,0:T(4,128)} %master.7, f32[3,55552]{1,0:T(4,128)} %first.1, ...), custom_call_target="tpu_custom_call" | custom-call | tf_op jit(solution)/shard_map/adam/pallas_call | solution.py:1236
  359.2 7.4 %collective-permute-start.36 = (f32[8,128]{1,0:T(8,128)S(1)}, f32[8,128]{1,0:T(8,128)S(1)}, u32[]{:S(2)}, u32[]{:S(2)}) collective-permute-start(f32[8,128]{1,0:T(8,128)S(1)} %select_add_fusion), channel_id=1, source_target_pairs={{0,1},{1,0},{2,3},{3,2},{4,5},{5,4},{6,7},{7,6},{8,9},{9,8},{10,11... | collective-permute-start | bytes 12296 | tf_op jit(solution)/shard_map/ppermute | solution.py:187
  366.6 1.6 collective-permute-done.36
  368.2 2.2 collective-permute-start.37
  370.4 2.3 collective-permute-done.37
  373.9 2.5 collective-permute-start.39
  376.4 1.6 collective-permute-done.39
  377.9 3.6 collective-permute-done.40
  382.1 2.8 apply_update.1
  (155 shorter events, 44.8 us)
Async XLA Ops:
  7.2 137.1 %all-gather.2.cloned.1.call-start = ((), (), s32[]{:S(2)}) async-start(), calls=%async_computation | async-start | bytes 3784704 | tf_op jit(solution)/shard_map/all_gather | solution.py:1375
  9.1 23.1 %copy-start.18 = (bf16[1,448,128]{2,1,0:T(8,128)(2,1)S(1)}, bf16[1,448,128]{2,1,0:T(8,128)(2,1)}, u32[]{:S(2)}) copy-start(bf16[1,448,128]{2,1,0:T(8,128)(2,1)} %get-tuple-element.108) | copy-start | bytes 344068
  9.2 7.7 %collective-permute-start = (bf16[1,448,128]{2,1,0:T(8,128)(2,1)}, bf16[1,448,128]{2,1,0:T(8,128)(2,1)S(1)}, u32[]{:S(2)}, u32[]{:S(2)}) collective-permute-start(bf16[1,448,128]{2,1,0:T(8,128)(2,1)} %get-tuple-element.103), channel_id=1, source_target_pairs={{0,16},{4,20},{8,24},{12,28},{1,17},{5,21},{9,25},{13,29},{2,18},{... | collective-permute-start | bytes 344072 | tf_op jit(solution)/shard_map/ppermute | solution.py:1355
  14.2 30.7 %copy-start.12 = (bf16[4,196,768]{2,0,1:T(4,128)(2,1)S(1)}, bf16[4,196,768]{2,0,1:T(4,128)(2,1)}, u32[]{:S(2)}) copy-start(bf16[4,196,768]{2,0,1:T(4,128)(2,1)} %param.17) | copy-start | bytes 3612676
  17.8 7.4 %collective-permute-start.1 = (bf16[1,448,128]{2,1,0:T(8,128)(2,1)S(1)}, bf16[1,448,128]{2,1,0:T(8,128)(2,1)S(1)}, u32[]{:S(2)}, u32[]{:S(2)}) collective-permute-start(bf16[1,448,128]{2,1,0:T(8,128)(2,1)S(1)} %broadcast_select_fusion), channel_id=1, source_target_pairs={{0,1},{1,0},{2,3},{3,2},{4,5},{5,4},{6,7},{7,6},{8,9},{9,8},{10,11... | collective-permute-start | bytes 344072 | tf_op jit(solution)/shard_map/ppermute | solution.py:194
  19.4 11.1 %collective-permute-start.2 = (bf16[1,448,128]{2,1,0:T(8,128)(2,1)S(1)}, bf16[1,448,128]{2,1,0:T(8,128)(2,1)S(1)}, u32[]{:S(2)}, u32[]{:S(2)}) collective-permute-start(bf16[1,448,128]{2,1,0:T(8,128)(2,1)S(1)} %broadcast_select_fusion), channel_id=1, source_target_pairs={{0,2},{1,3},{2,0},{3,1},{4,6},{5,7},{6,4},{7,5},{8,10},{9,11},{10,... | collective-permute-start | bytes 344072 | tf_op jit(solution)/shard_map/ppermute | solution.py:194
  22.0 8.6 %collective-permute-start.3 = (bf16[1,448,128]{2,1,0:T(8,128)(2,1)S(1)}, bf16[1,448,128]{2,1,0:T(8,128)(2,1)S(1)}, u32[]{:S(2)}, u32[]{:S(2)}) collective-permute-start(bf16[1,448,128]{2,1,0:T(8,128)(2,1)S(1)} %broadcast_select_fusion), channel_id=1, source_target_pairs={{0,3},{1,2},{2,1},{3,0},{4,7},{5,6},{6,5},{7,4},{8,11},{9,10},{10,... | collective-permute-start | bytes 344072 | tf_op jit(solution)/shard_map/ppermute | solution.py:194
  22.2 10.0 %collective-permute-start.7 = (bf16[1,448,128]{2,1,0:T(8,128)(2,1)}, bf16[1,448,128]{2,1,0:T(8,128)(2,1)S(1)}, u32[]{:S(2)}, u32[]{:S(2)}) collective-permute-start(bf16[1,448,128]{2,1,0:T(8,128)(2,1)} %get-tuple-element.108), channel_id=1, source_target_pairs={{0,24},{4,28},{8,16},{12,20},{16,8},{20,12},{24,0},{28,4},{1,25},{... | collective-permute-start | bytes 344072 | tf_op jit(solution)/shard_map/ppermute | solution.py:1357
  24.6 7.6 %collective-permute-start.8 = (bf16[1,448,128]{2,1,0:T(8,128)(2,1)}, bf16[1,448,128]{2,1,0:T(8,128)(2,1)S(1)}, u32[]{:S(2)}, u32[]{:S(2)}) collective-permute-start(bf16[1,448,128]{2,1,0:T(8,128)(2,1)} %get-tuple-element.108), channel_id=1, source_target_pairs={{0,16},{4,20},{8,24},{12,28},{16,0},{20,4},{24,8},{28,12},{1,17},{... | collective-permute-start | bytes 344072 | tf_op jit(solution)/shard_map/ppermute | solution.py:1357
  25.2 7.0 %collective-permute-start.9 = (bf16[1,448,128]{2,1,0:T(8,128)(2,1)}, bf16[1,448,128]{2,1,0:T(8,128)(2,1)S(1)}, u32[]{:S(2)}, u32[]{:S(2)}) collective-permute-start(bf16[1,448,128]{2,1,0:T(8,128)(2,1)} %get-tuple-element.108), channel_id=1, source_target_pairs={{0,8},{4,12},{8,0},{12,4},{16,24},{20,28},{24,16},{28,20},{1,9},{5... | collective-permute-start | bytes 344072 | tf_op jit(solution)/shard_map/ppermute | solution.py:1357
  30.6 14.2 %collective-permute-start.4 = (bf16[4,448,128]{2,1,0:T(8,128)(2,1)S(1)}, bf16[4,448,128]{2,1,0:T(8,128)(2,1)S(1)}, u32[]{:S(2)}, u32[]{:S(2)}) collective-permute-start(bf16[4,448,128]{2,1,0:T(8,128)(2,1)S(1)} %pad_maximum_fusion.refs_0_), channel_id=1, source_target_pairs={{0,8},{4,12},{8,0},{12,4},{16,24},{20,28},{24,16},{28,20},{1,9},{5... | collective-permute-start | bytes 1376264 | tf_op jit(solution)/shard_map/ppermute | solution.py:189
  32.3 5.5 %collective-permute-start.10 = (bf16[1,448,128]{2,1,0:T(8,128)(2,1)S(1)}, bf16[1,448,128]{2,1,0:T(8,128)(2,1)S(1)}, u32[]{:S(2)}, u32[]{:S(2)}) collective-permute-start(bf16[1,448,128]{2,1,0:T(8,128)(2,1)S(1)} %get-tuple-element.208), channel_id=1, source_target_pairs={{0,1},{1,0},{2,3},{3,2},{4,5},{5,4},{6,7},{7,6},{8,9},{9,8},{10,11... | collective-permute-start | bytes 344072 | tf_op jit(solution)/shard_map/ppermute | solution.py:194
  34.1 10.0 %collective-permute-start.11 = (bf16[1,448,128]{2,1,0:T(8,128)(2,1)S(1)}, bf16[1,448,128]{2,1,0:T(8,128)(2,1)S(1)}, u32[]{:S(2)}, u32[]{:S(2)}) collective-permute-start(bf16[1,448,128]{2,1,0:T(8,128)(2,1)S(1)} %get-tuple-element.208), channel_id=1, source_target_pairs={{0,2},{1,3},{2,0},{3,1},{4,6},{5,7},{6,4},{7,5},{8,10},{9,11},{10,... | collective-permute-start | bytes 344072 | tf_op jit(solution)/shard_map/ppermute | solution.py:194
  35.6 8.5 %collective-permute-start.12 = (bf16[1,448,128]{2,1,0:T(8,128)(2,1)S(1)}, bf16[1,448,128]{2,1,0:T(8,128)(2,1)S(1)}, u32[]{:S(2)}, u32[]{:S(2)}) collective-permute-start(bf16[1,448,128]{2,1,0:T(8,128)(2,1)S(1)} %get-tuple-element.208), channel_id=1, source_target_pairs={{0,3},{1,2},{2,1},{3,0},{4,7},{5,6},{6,5},{7,4},{8,11},{9,10},{10,... | collective-permute-start | bytes 344072 | tf_op jit(solution)/shard_map/ppermute | solution.py:194
  44.2 4.8 %collective-permute-start.13 = (bf16[4,448,128]{2,1,0:T(8,128)(2,1)S(1)}, bf16[4,448,128]{2,1,0:T(8,128)(2,1)S(1)}, u32[]{:S(2)}, u32[]{:S(2)}) collective-permute-start(bf16[4,448,128]{2,1,0:T(8,128)(2,1)S(1)} %pad_maximum_fusion.1.refs_0_), channel_id=1, source_target_pairs={{0,4},{4,0},{8,12},{12,8},{16,20},{20,16},{24,28},{28,24},{1,5},{5... | collective-permute-start | bytes 1376264 | tf_op jit(solution)/shard_map/ppermute | solution.py:189
  44.3 9.0 %collective-permute-start.5 = (bf16[4,448,128]{2,1,0:T(8,128)(2,1)S(1)}, bf16[4,448,128]{2,1,0:T(8,128)(2,1)}, u32[]{:S(2)}, u32[]{:S(2)}) collective-permute-start(bf16[4,448,128]{2,1,0:T(8,128)(2,1)S(1)} %pad_maximum_fusion.refs_0_), channel_id=1, source_target_pairs={{0,4},{4,0},{8,12},{12,8},{16,20},{20,16},{24,28},{28,24},{1,5},{5... | collective-permute-start | bytes 1376264 | tf_op jit(solution)/shard_map/ppermute | solution.py:189
  44.8 8.5 %collective-permute-start.6 = (bf16[4,448,128]{2,1,0:T(8,128)(2,1)S(1)}, bf16[4,448,128]{2,1,0:T(8,128)(2,1)}, u32[]{:S(2)}, u32[]{:S(2)}) collective-permute-start(bf16[4,448,128]{2,1,0:T(8,128)(2,1)S(1)} %collective-permute-done.4.refs_1_), channel_id=1, source_target_pairs={{0,4},{4,0},{8,12},{12,8},{16,20},{20,16},{24,28},{28,24},{1,5},{5... | collective-permute-start | bytes 1376264 | tf_op jit(solution)/shard_map/ppermute | solution.py:189
  46.1 37.6 %collective-permute-start.14 = (bf16[3,448,128]{2,1,0:T(8,128)(2,1)S(1)}, bf16[3,448,128]{2,1,0:T(8,128)(2,1)}, u32[]{:S(2)}, u32[]{:S(2)}) collective-permute-start(bf16[3,448,128]{2,1,0:T(8,128)(2,1)S(1)} %pad_maximum_fusion.2), channel_id=1, source_target_pairs={{0,1},{1,0},{2,3},{3,2},{4,5},{5,4},{6,7},{7,6},{8,9},{9,8},{10,11... | collective-permute-start | bytes 1032200 | tf_op jit(solution)/shard_map/ppermute | solution.py:194
  48.0 35.7 %collective-permute-start.15 = (bf16[3,448,128]{2,1,0:T(8,128)(2,1)S(1)}, bf16[3,448,128]{2,1,0:T(8,128)(2,1)}, u32[]{:S(2)}, u32[]{:S(2)}) collective-permute-start(bf16[3,448,128]{2,1,0:T(8,128)(2,1)S(1)} %pad_maximum_fusion.2), channel_id=1, source_target_pairs={{0,2},{1,3},{2,0},{3,1},{4,6},{5,7},{6,4},{7,5},{8,10},{9,11},{10,... | collective-permute-start | bytes 1032200 | tf_op jit(solution)/shard_map/ppermute | solution.py:194
  49.0 34.7 %collective-permute-start.16 = (bf16[3,448,128]{2,1,0:T(8,128)(2,1)S(1)}, bf16[3,448,128]{2,1,0:T(8,128)(2,1)S(1)}, u32[]{:S(2)}, u32[]{:S(2)}) collective-permute-start(bf16[3,448,128]{2,1,0:T(8,128)(2,1)S(1)} %pad_maximum_fusion.2), channel_id=1, source_target_pairs={{0,3},{1,2},{2,1},{3,0},{4,7},{5,6},{6,5},{7,4},{8,11},{9,10},{10,... | collective-permute-start | bytes 1032200 | tf_op jit(solution)/shard_map/ppermute | solution.py:194
  85.8 26.9 %collective-permute-start.17 = (bf16[12,448,128]{2,1,0:T(8,128)(2,1)S(1)}, bf16[12,448,128]{2,1,0:T(8,128)(2,1)S(1)}, u32[]{:S(2)}, u32[]{:S(2)}) collective-permute-start(bf16[12,448,128]{2,1,0:T(8,128)(2,1)S(1)} %constant_dynamic-update-slice_fusion.refs_3_.refs_2_), channel_id=1, source_target_pairs={{0,4},{4,0},{8,12},{12,8},{16,20},{20,16},{24,28},{28,24},{1,5},{5... | collective-permute-start | bytes 4128776 | tf_op jit(solution)/shard_map/ppermute | solution.py:189
  162.3 31.9 %collective-permute-start.18 = (bf16[16,448,128]{2,1,0:T(8,128)(2,1)}, bf16[16,448,128]{2,1,0:T(8,128)(2,1)S(1)}, u32[]{:S(2)}, u32[]{:S(2)}) collective-permute-start(bf16[16,448,128]{2,1,0:T(8,128)(2,1)} %get-tuple-element.147.refs_18_), channel_id=1, source_target_pairs={{0,4},{4,0},{8,12},{12,8},{16,20},{20,16},{24,28},{28,24},{1,5},{5... | collective-permute-start | bytes 5505032 | tf_op jit(solution)/shard_map/ppermute | solution.py:189
  193.8 27.0 %collective-permute-start.20 = (bf16[16,448,128]{2,1,0:T(8,128)(2,1)}, bf16[16,448,128]{2,1,0:T(8,128)(2,1)}, u32[]{:S(2)}, u32[]{:S(2)}) collective-permute-start(bf16[16,448,128]{2,1,0:T(8,128)(2,1)} %get-tuple-element.161.refs_8_), channel_id=1, source_target_pairs={{0,4},{4,0},{8,12},{12,8},{16,20},{20,16},{24,28},{28,24},{1,5},{5... | collective-permute-start | bytes 5505032 | tf_op jit(solution)/shard_map/ppermute | solution.py:189
  199.5 26.5 %collective-permute-start.19 = (bf16[8,448,128]{2,1,0:T(8,128)(2,1)}, bf16[8,448,128]{2,1,0:T(8,128)(2,1)}, u32[]{:S(2)}, u32[]{:S(2)}) collective-permute-start(bf16[8,448,128]{2,1,0:T(8,128)(2,1)} %slice.164.refs_7_), channel_id=1, source_target_pairs={{0,16},{4,20},{8,24},{12,28},{16,0},{20,4},{24,8},{28,12},{1,17},{... | collective-permute-start | bytes 2752520 | tf_op jit(solution)/shard_map/ppermute | solution.py:189
  225.0 27.1 %collective-permute-start.22 = (bf16[8,448,128]{2,1,0:T(8,128)(2,1)}, bf16[8,448,128]{2,1,0:T(8,128)(2,1)}, u32[]{:S(2)}, u32[]{:S(2)}) collective-permute-start(bf16[8,448,128]{2,1,0:T(8,128)(2,1)} %slice.163.refs_9_), channel_id=1, source_target_pairs={{0,1},{1,0},{2,3},{3,2},{4,5},{5,4},{6,7},{7,6},{8,9},{9,8},{10,11... | collective-permute-start | bytes 2752520 | tf_op jit(solution)/shard_map/ppermute | solution.py:187
  227.5 29.3 %collective-permute-start.21 = (bf16[4,448,128]{2,1,0:T(8,128)(2,1)S(1)}, bf16[4,448,128]{2,1,0:T(8,128)(2,1)}, u32[]{:S(2)}, u32[]{:S(2)}) collective-permute-start(bf16[4,448,128]{2,1,0:T(8,128)(2,1)S(1)} %slice.166.refs_8_), channel_id=1, source_target_pairs={{0,8},{4,12},{8,0},{12,4},{16,24},{20,28},{24,16},{28,20},{1,9},{5... | collective-permute-start | bytes 1376264 | tf_op jit(solution)/shard_map/ppermute | solution.py:189
  228.8 23.3 %copy-start.1 = (f32[16,448,128]{2,1,0:T(8,128)S(1)}, f32[16,448,128]{2,1,0:T(8,128)}, u32[]{:S(2)}) copy-start(f32[16,448,128]{2,1,0:T(8,128)} %copy-done) | copy-start | bytes 11010052
  254.8 28.4 %collective-permute-start.24 = (bf16[4,448,128]{2,1,0:T(8,128)(2,1)S(1)}, bf16[4,448,128]{2,1,0:T(8,128)(2,1)}, u32[]{:S(2)}, u32[]{:S(2)}) collective-permute-start(bf16[4,448,128]{2,1,0:T(8,128)(2,1)S(1)} %slice.165.refs_9_), channel_id=1, source_target_pairs={{0,2},{1,3},{2,0},{3,1},{4,6},{5,7},{6,4},{7,5},{8,10},{9,11},{10,... | collective-permute-start | bytes 1376264 | tf_op jit(solution)/shard_map/ppermute | solution.py:187
  258.6 23.7 %copy-start.17 = (bf16[2,448,128]{2,1,0:T(8,128)(2,1)S(1)}, bf16[2,448,128]{2,1,0:T(8,128)(2,1)}, u32[]{:S(2)}) copy-start(bf16[2,448,128]{2,1,0:T(8,128)(2,1)} %slice.168.refs_8_) | copy-start | bytes 688132
  258.6 24.7 %copy-start.3 = (f32[8,448,128]{2,1,0:T(8,128)S(1)}, f32[8,448,128]{2,1,0:T(8,128)}, u32[]{:S(2)}) copy-start(f32[8,448,128]{2,1,0:T(8,128)} %copy-done.2) | copy-start | bytes 5505028
  282.3 6.8 %collective-permute-start.23 = (bf16[2,448,128]{2,1,0:T(8,128)(2,1)S(1)}, bf16[2,448,128]{2,1,0:T(8,128)(2,1)S(1)}, u32[]{:S(2)}, u32[]{:S(2)}) collective-permute-start(bf16[2,448,128]{2,1,0:T(8,128)(2,1)S(1)} %copy-done.17), channel_id=1, source_target_pairs={{0,1},{1,0},{2,3},{3,2},{4,5},{5,4},{6,7},{7,6},{8,9},{9,8},{10,11... | collective-permute-start | bytes 688136 | tf_op jit(solution)/shard_map/ppermute | solution.py:187
  289.8 18.9 %copy-start.16 = (bf16[2,448,128]{2,1,0:T(8,128)(2,1)S(1)}, bf16[2,448,128]{2,1,0:T(8,128)(2,1)}, u32[]{:S(2)}) copy-start(bf16[2,448,128]{2,1,0:T(8,128)(2,1)} %slice.167.refs_19_) | copy-start | bytes 688132
  308.6 2.7 collective-permute-start.25
  308.7 9.1 %collective-permute-start.32 = (bf16[2,448,128]{2,1,0:T(8,128)(2,1)S(1)}, bf16[2,448,128]{2,1,0:T(8,128)(2,1)S(1)}, u32[]{:S(2)}, u32[]{:S(2)}) collective-permute-start(bf16[2,448,128]{2,1,0:T(8,128)(2,1)S(1)} %copy-done.16), channel_id=1, source_target_pairs={{0,16},{4,20},{8,24},{12,28},{16,0},{20,4},{24,8},{28,12},{1,17},{... | collective-permute-start | bytes 688136 | tf_op jit(solution)/shard_map/ppermute | solution.py:189
  313.2 11.6 %collective-permute-start.26 = (bf16[896,128]{1,0:T(8,128)(2,1)S(1)}, bf16[896,128]{1,0:T(8,128)(2,1)S(1)}, u32[]{:S(2)}, u32[]{:S(2)}) collective-permute-start(bf16[896,128]{1,0:T(8,128)(2,1)S(1)} %get-tuple-element.202), channel_id=1, source_target_pairs={{0,1},{1,0},{2,3},{3,2},{4,5},{5,4},{6,7},{7,6},{8,9},{9,8},{10,11... | collective-permute-start | bytes 688136 | tf_op jit(solution)/shard_map/ppermute | solution.py:194
  314.1 21.7 %collective-permute-start.27 = (bf16[896,128]{1,0:T(8,128)(2,1)S(1)}, bf16[896,128]{1,0:T(8,128)(2,1)S(1)}, u32[]{:S(2)}, u32[]{:S(2)}) collective-permute-start(bf16[896,128]{1,0:T(8,128)(2,1)S(1)} %get-tuple-element.204), channel_id=1, source_target_pairs={{0,2},{1,3},{2,0},{3,1},{4,6},{5,7},{6,4},{7,5},{8,10},{9,11},{10,... | collective-permute-start | bytes 688136 | tf_op jit(solution)/shard_map/ppermute | solution.py:194
  315.3 20.5 %collective-permute-start.28 = (bf16[896,128]{1,0:T(8,128)(2,1)S(1)}, bf16[896,128]{1,0:T(8,128)(2,1)S(1)}, u32[]{:S(2)}, u32[]{:S(2)}) collective-permute-start(bf16[896,128]{1,0:T(8,128)(2,1)S(1)} %get-tuple-element.203), channel_id=1, source_target_pairs={{0,3},{1,2},{2,1},{3,0},{4,7},{5,6},{6,5},{7,4},{8,11},{9,10},{10,... | collective-permute-start | bytes 688136 | tf_op jit(solution)/shard_map/ppermute | solution.py:194
  317.6 24.5 %collective-permute-start.35 = (bf16[1,448,128]{2,1,0:T(8,128)(2,1)S(1)}, bf16[1,448,128]{2,1,0:T(8,128)(2,1)S(1)}, u32[]{:S(2)}, u32[]{:S(2)}) collective-permute-start(bf16[1,448,128]{2,1,0:T(8,128)(2,1)S(1)} %copy-done.19), channel_id=1, source_target_pairs={{0,2},{1,3},{2,0},{3,1},{4,6},{5,7},{6,4},{7,5},{8,10},{9,11},{10,... | collective-permute-start | bytes 344072 | tf_op jit(solution)/shard_map/ppermute | solution.py:187
  335.9 9.1 %collective-permute-start.29 = (bf16[896,128]{1,0:T(8,128)(2,1)S(1)}, bf16[896,128]{1,0:T(8,128)(2,1)S(1)}, u32[]{:S(2)}, u32[]{:S(2)}) collective-permute-start(bf16[896,128]{1,0:T(8,128)(2,1)S(1)} %fusion.5), channel_id=1, source_target_pairs={{8,0},{12,4},{9,1},{13,5},{10,2},{14,6},{11,3},{15,7}} | collective-permute-start | bytes 688136 | tf_op jit(solution)/shard_map/ppermute | solution.py:1450
  337.2 10.4 %collective-permute-start.30 = (bf16[896,128]{1,0:T(8,128)(2,1)S(1)}, bf16[896,128]{1,0:T(8,128)(2,1)S(1)}, u32[]{:S(2)}, u32[]{:S(2)}) collective-permute-start(bf16[896,128]{1,0:T(8,128)(2,1)S(1)} %fusion.5), channel_id=1, source_target_pairs={{16,0},{20,4},{17,1},{21,5},{18,2},{22,6},{19,3},{23,7}} | collective-permute-start | bytes 688136 | tf_op jit(solution)/shard_map/ppermute | solution.py:1450
  338.5 9.1 %collective-permute-start.31 = (bf16[896,128]{1,0:T(8,128)(2,1)S(1)}, bf16[896,128]{1,0:T(8,128)(2,1)S(1)}, u32[]{:S(2)}, u32[]{:S(2)}) collective-permute-start(bf16[896,128]{1,0:T(8,128)(2,1)S(1)} %fusion.5), channel_id=1, source_target_pairs={{24,0},{28,4},{25,1},{29,5},{26,2},{30,6},{27,3},{31,7}} | collective-permute-start | bytes 688136 | tf_op jit(solution)/shard_map/ppermute | solution.py:1450
  339.9 5.2 %collective-permute-start.33 = (bf16[1,448,128]{2,1,0:T(8,128)(2,1)S(1)}, bf16[1,448,128]{2,1,0:T(8,128)(2,1)S(1)}, u32[]{:S(2)}, u32[]{:S(2)}) collective-permute-start(bf16[1,448,128]{2,1,0:T(8,128)(2,1)S(1)} %slice.169), channel_id=1, source_target_pairs={{0,8},{4,12},{8,0},{12,4},{16,24},{20,28},{24,16},{28,20},{1,9},{5... | collective-permute-start | bytes 344072 | tf_op jit(solution)/shard_map/ppermute | solution.py:189
  348.5 4.8 %collective-permute-start.34 = (f32[448,128]{1,0:T(8,128)S(1)}, f32[448,128]{1,0:T(8,128)S(1)}, u32[]{:S(2)}, u32[]{:S(2)}) collective-permute-start(f32[448,128]{1,0:T(8,128)S(1)} %get-tuple-element.199), channel_id=1, source_target_pairs={{0,8},{4,12},{1,9},{5,13},{2,10},{6,14},{3,11},{7,15}} | collective-permute-start | bytes 688136 | tf_op jit(solution)/shard_map/ppermute | solution.py:1452
  359.2 9.0 %collective-permute-start.36 = (f32[8,128]{1,0:T(8,128)S(1)}, f32[8,128]{1,0:T(8,128)S(1)}, u32[]{:S(2)}, u32[]{:S(2)}) collective-permute-start(f32[8,128]{1,0:T(8,128)S(1)} %select_add_fusion), channel_id=1, source_target_pairs={{0,1},{1,0},{2,3},{3,2},{4,5},{5,4},{6,7},{7,6},{8,9},{9,8},{10,11... | collective-permute-start | bytes 12296 | tf_op jit(solution)/shard_map/ppermute | solution.py:187
  368.2 4.5 %collective-permute-start.37 = (f32[8,128]{1,0:T(8,128)S(1)}, f32[8,128]{1,0:T(8,128)S(1)}, u32[]{:S(2)}, u32[]{:S(2)}) collective-permute-start(f32[8,128]{1,0:T(8,128)S(1)} %add.112), channel_id=1, source_target_pairs={{0,2},{1,3},{2,0},{3,1},{4,6},{5,7},{6,4},{7,5},{8,10},{9,11},{10,... | collective-permute-start | bytes 12296 | tf_op jit(solution)/shard_map/ppermute | solution.py:187
  372.7 1.2 collective-permute-start.38
  373.9 4.1 %collective-permute-start.39 = (f32[8,128]{1,0:T(8,128)S(1)}, f32[8,128]{1,0:T(8,128)S(1)}, u32[]{:S(2)}, u32[]{:S(2)}) collective-permute-start(f32[8,128]{1,0:T(8,128)S(1)} %add.114), channel_id=1, source_target_pairs={{0,8},{4,12},{8,0},{12,4},{16,24},{20,28},{24,16},{28,20},{1,9},{5... | collective-permute-start | bytes 12296 | tf_op jit(solution)/shard_map/ppermute | solution.py:189
  377.9 3.6 collective-permute-start.40
  (23 other events, 78.0 us)
Sparse Core Ops, SparseCore 0:
  49.1 72.0 all-gather.1

commit v4 on v3

--- a/solution.py
+++ b/solution.py
@@ -760,7 +760,7 @@
             sds((D, CLASS_PAD), f32),
             sds((1, CLASS_PAD), f32),
             sds((1, LANES), f32),
-            sds((half, padded_rows, LANES), f32),
+            sds((half, padded_rows, LANES), bf16),
             sds((half, padded_rows, LANES), bf16),
         ],
         in_specs=[SM] * 5 + [VM] * (len(args) - 5),
@@ -1042,7 +1042,7 @@
     for k, r in enumerate(rels):
         value = flat[pl.ds(offset + rows * jnp.bitwise_xor(me, r), keep_ref.shape[1]), :]
         if k < half:
-            keep_ref[k] = value
+            keep_ref[k] = value.astype(keep_ref.dtype)
         else:
             send_ref[k - half] = value.astype(bf16)
 
@@ -1148,7 +1148,7 @@
     half = len(rels) // 2
     return pl.pallas_call(
         kernel,
-        out_shape=[sds((half, padded_rows, LANES), f32), sds((half, padded_rows, LANES), bf16)],
+        out_shape=[sds((half, padded_rows, LANES), bf16)] * 2,
         in_specs=[SM] + [VM] * len(arrays),
         out_specs=[VM] * 2,
         scratch_shapes=[pltpu.VMEM((flat_rows, LANES), f32), *extra],
@@ -1170,14 +1170,13 @@
     def step(self, after=None):
         if self.order:
             (got,) = tied((exchange(self.send, self.order.pop(0), self.z_bits),), after)
-            total = self.keep + got.astype(f32)
-            if self.order:
-                half = total.shape[0] // 2
-                self.keep, self.send = total[:half], total[half:].astype(bf16)
-            elif self.z_last:
-                self.keep, self.send = total[0], total[1:].astype(bf16)
-            else:
-                self.finish(total[0])
+            half = got.shape[0] // 2 if self.order else 1
+            kept = self.keep[:half].astype(f32) + got[:half].astype(f32)
+            if half == got.shape[0]:
+                self.finish(kept[0])
+                return
+            passed = (self.keep[half:].astype(f32) + got[half:].astype(f32)).astype(bf16)
+            self.keep, self.send = (kept, passed) if self.order else (kept[0], passed)
         elif not self.done:
             got = [exchange_z(self.send[k - 1], k) for k in range(1, self.send.shape[0] + 1)]
             total = self.keep

time: 397 us -> 390 us (0.982)
  local copies, waits for them, and re-layouts: 13.5 us -> 5.43 us
    slice x8 -> x0, local copies, waits for them, and re-layouts: 4.53 us -> none  [step(): self.keep, self.send = (total[:half], total[half:].astype(bf16))]
    unnamed x62 -> x52, local copies, waits for them, and re-layouts: 8.33 us -> 4.82 us
    add x8 -> x6, other arithmetic: 11 us -> 12.6 us  [step(): kept = self.keep[:half].astype(f32) + got[:half].astype(f32)]
  transfers between devices with their start and end apart: 42 -> 42, of which waited for: 16 -> 16; matrix products, arithmetic and copies ran while one was open for 6% -> 4% of each run, Pallas kernels for 48% -> 49%
where the time goes in v4:
time: 390 us; the launch traced here: 385 us
  Pallas kernels  235 us (60%)
  starting transfers between devices  54.9 us (14%)
  waiting for transfers between devices  54.9 us (14%)
  other arithmetic  20 us (5%)
  between operations  15.3 us (4%)
  local copies, waits for them, and re-layouts  5.43 us (1%)
    pallas_call x9, Pallas kernels, call(): pl.pallas_call(wrapped, in_specs=specs, compiler_params=params(), **kw)  187 us
    ppermute x12, waiting for transfers between devices, exchange_z(): return lax.ppermute(value, 'fsdp', [(i, i ^ k) for i in range(n)])  30.2 us
    ppermute x12, starting transfers between devices, exchange_z(): return lax.ppermute(value, 'fsdp', [(i, i ^ k) for i in range(n)])  17.9 us
    pallas_call x1, Pallas kernels, class_step(): pl.pallas_call(functools.partial(class_step_kernel, ns, nl, valid, unpack...  17.4 us
    ppermute x6, starting transfers between devices, exchange(): return lax.ppermute(value, 'fsdp', [(i, i ^ 1 << bit) for i in range(n)])  13.7 us
    add x6, other arithmetic, step(): kept = self.keep[:half].astype(f32) + got[:half].astype(f32)  12.6 us
    ppermute x15, waiting for transfers between devices, exchange(): lax.ppermute(value, 'dp', [(i, i ^ 1 << bit - z_bits) for i in range(n)])  11.2 us
    ppermute x15, starting transfers between devices, exchange(): lax.ppermute(value, 'dp', [(i, i ^ 1 << bit - z_bits) for i in range(n)])  9.55 us
  transfers between devices with their start and end apart: 42, of which 16 were waited for; matrix products, arithmetic and copies ran while one was open for 4% of the time, Pallas kernels for 49%

profile of v4, /device:TPU:0, one launch (start us, length us, event | category | flops | bytes accessed | tf_op | source)
XLA Modules:
  0.0 385.4 jit_solution(697515118572711310)
XLA Ops:
  7.2 1.9 round_shards.1
  9.2 5.0 %collective-permute-start = (bf16[1,448,128]{2,1,0:T(8,128)(2,1)}, bf16[1,448,128]{2,1,0:T(8,128)(2,1)S(1)}, u32[]{:S(2)}, u32[]{:S(2)}) collective-permute-start(bf16[1,448,128]{2,1,0:T(8,128)(2,1)} %get-tuple-element.103), channel_id=1, source_target_pairs={{0,16},{4,20},{8,24},{12,28},{1,17},{5,21},{9,25},{13,29},{2,18},{... | collective-permute-start | bytes 344072 | tf_op jit(solution)/shard_map/ppermute | solution.py:1354
  14.2 2.4 weight_sums.1
  17.8 1.6 collective-permute-start.1
  19.4 2.6 collective-permute-start.2
  22.2 2.4 collective-permute-start.7
  25.7 4.8 %collective-permute-done.2 = bf16[1,448,128]{2,1,0:T(8,128)(2,1)S(1)} collective-permute-done((bf16[1,448,128]{2,1,0:T(8,128)(2,1)S(1)}, bf16[1,448,128]{2,1,0:T(8,128)(2,1)S(1)}, u32[]{:S(2)}, u32[]{:S(2)}) %collective-permute-start.2) | collective-permute-done | bytes 114720 | tf_op jit(solution)/shard_map/ppermute | solution.py:194
  32.3 1.9 collective-permute-start.10
  37.8 6.3 %collective-permute-done.11 = bf16[1,448,128]{2,1,0:T(8,128)(2,1)S(1)} collective-permute-done((bf16[1,448,128]{2,1,0:T(8,128)(2,1)S(1)}, bf16[1,448,128]{2,1,0:T(8,128)(2,1)S(1)}, u32[]{:S(2)}, u32[]{:S(2)}) %collective-permute-start.11) | collective-permute-done | bytes 114720 | tf_op jit(solution)/shard_map/ppermute | solution.py:194
  46.1 1.9 collective-permute-start.14
  49.0 1.7 collective-permute-start.16
  50.7 2.6 unpack_low.1
  53.3 4.9 %unpack_stem.1 = (bf16[768,384]{1,0:T(8,128)(2,1)}, f32[8,384]{1,0:T(8,128)}, f32[208,384]{1,0:T(8,128)}, f32[576,384]{1,0:T(8,128)}, bf16[384,1024]{1,0:T(8,128)(2,1)}, /*index=5*/f32[1,1024]{1,0:T(1,128)}) custom-call(s32[1]{0:T(128)S(6)} %and.15.me_ref, f32[576,208]{1,0:T(8,128)} %constant.47.clone.resize_ref, bf16[4,448,128]{2,1,0:T(8,128)(2,1)} %copy-done.6, ...), custom_call_target="tpu_custom_call" | custom-call | tf_op jit(solution)/shard_map/unpack_stem/pallas_call | solution.py:272
  58.2 8.9 %embed.1 = (f32[4,208,384]{2,1,0:T(8,128)}, f32[2,576,384]{2,1,0:T(8,128)}, bf16[4,208,1152]{2,1,0:T(8,128)(2,1)}, bf16[2,576,1152]{2,1,0:T(8,128)(2,1)}) custom-call(bf16[4,196,768]{2,1,0:T(8,128)(2,1)} %copy.25.refs_0_.refs_1_, bf16[2,576,768]{2,1,0:T(8,128)(2,1)} %refs_2_.1, bf16[768,384]{1,0:T(8,128)(2,1)} %get-tuple-element.105.refs_2_, ...), custom_call_target="tpu_custom_call" | custom-call | flops 12000000000 | bytes 20000000 | tf_op jit(solution)/shard_map/embed/pallas_call | solution.py:177
  67.1 16.5 %attend.2 = (bf16[4,208,384]{2,1,0:T(8,128)(2,1)}, f32[4,8,208]{2,1,0:T(8,128)}) custom-call(bf16[4,208,1152]{2,1,0:T(8,128)(2,1)} %get-tuple-element.113.refs_0_, f32[384,8]{1,0:T(8,128)} %get-tuple-element.116.refs_1_.refs_3_, f32[384,8]{1,0:T(8,128)} %get-tuple-element.117.refs_2_.refs_4_), custom_call_target="tpu_custom_call" | custom-call | flops 20000000000 | bytes 10000000 | tf_op jit(solution)/shard_map/attend/pallas_call | solution.py:177
  84.9 25.9 %attend.3 = (bf16[2,576,384]{2,1,0:T(8,128)(2,1)}, f32[2,8,576]{2,1,0:T(8,128)}) custom-call(bf16[2,576,1152]{2,1,0:T(8,128)(2,1)} %get-tuple-element.119.refs_0_, f32[384,8]{1,0:T(8,128)} %get-tuple-element.116.refs_1_.refs_3_, f32[384,8]{1,0:T(8,128)} %get-tuple-element.117.refs_2_.refs_4_, bf16[12,448,128]{2,1,0:T(8,128)(2,1)} %copy-done.3, ...), custom_call_target="tpu_custom_call" | custom-call | flops 30000001024 | bytes 10000000 | tf_op jit(solution)/shard_map/attend/pallas_call | solution.py:177
  112.0 4.3 %unpack_feed.1 = (bf16[384,384]{1,0:T(8,128)(2,1)}, bf16[384,1536]{1,0:T(8,128)(2,1)}, bf16[1536,384]{1,0:T(8,128)(2,1)}, f32[16,384]{1,0:T(8,128)}, f32[1,1536]{1,0:T(1,128)}) custom-call(s32[1]{0:T(128)S(6)} %and.14.me_ref.refs_0_, bf16[4,448,128]{2,1,0:T(8,128)(2,1)} %copy-done, bf16[4,448,128]{2,1,0:T(8,128)(2,1)} %copy-done.7, ...), custom_call_target="tpu_custom_call" | custom-call | tf_op jit(solution)/shard_map/unpack_feed/pallas_call | solution.py:355
  116.3 26.1 %feed.1 = (bf16[4,208,384]{2,1,0:T(8,128)(2,1)}, bf16[2,576,384]{2,1,0:T(8,128)(2,1)}, f32[4,208,384]{2,1,0:T(8,128)}, f32[2,576,384]{2,1,0:T(8,128)}, bf16[4,20...) custom-call(f32[4,208,384]{2,1,0:T(8,128)} %get-tuple-element.111.re, ...), custom_call_target="tpu_custom_call" | custom-call | flops 20000000000 | bytes 30000000 | tf_op jit(solution)/shard_map/feed/pallas_call | solution.py:177
  142.4 17.4 %class_step.1 = (f32[4,208,384]{2,1,0:T(8,128)}, f32[2,576,384]{2,1,0:T(8,128)}, f32[8,384]{1,0:T(8,128)}, f32[384,1024]{1,0:T(8,128)}, f32[1,1024]{1,0:T(1,128)...) custom-call(s32[1]{0:T(128)} %bitcast.me_ref, s32[1]{0:T(128)} %constant.43.clone.1.from_ref, ...), custom_call_target="tpu_custom_call" | custom-call | flops 24999999488 | bytes 40000000 | tf_op jit(solution)/shard_map/class_step/pallas_call | solution.py:752
  159.9 24.5 %feed_back.1 = (f32[4,208,384]{2,1,0:T(8,128)}, f32[2,576,384]{2,1,0:T(8,128)}, bf16[4,208,384]{2,1,0:T(8,128)(2,1)}, bf16[2,576,384]{2,1,0:T(8,128)(2,1)}, f32[...) custom-call(f32[4,208,384]{2,1,0:T(8,128)} %get-tuple-element.135.refs, ...), custom_call_target="tpu_custom_call" | custom-call | flops 35000000512 | bytes 30000000 | tf_op jit(solution)/shard_map/feed_back/pallas_call | solution.py:177
  184.3 6.6 %pack_feed.1 = (bf16[16,448,128]{2,1,0:T(8,128)(2,1)}, bf16[16,448,128]{2,1,0:T(8,128)(2,1)}) custom-call(s32[1]{0:T(128)} %bitcast.me_ref, f32[384,384]{1,0:T(8,128)} %get-tuple-element.154.wo.refs_15_, f32[384,1536]{1,0:T(8,128)} %get-tuple-element.155.w1, f32[1536,384]{1,0:T(8,128)} %get-tuple-element.156.w2, f32[16,384]{1,0:T(8,128)} %get-tuple-element.157.vec, ...), custom_call_target="tpu_custom_call" | custom-call | tf_op jit(solution)/shard_map/pack_feed/pallas_call | solution.py:1149
  192.7 2.8 convert_add_fusion.1
  196.4 20.1 %attend_back.3 = (bf16[4,208,1152]{2,1,0:T(8,128)(2,1)}, f32[8,384]{1,0:T(8,128)}, f32[8,384]{1,0:T(8,128)}) custom-call(bf16[4,208,1152]{2,1,0:T(8,128)(2,1)} %get-tuple-element.113.refs_0_, bf16[4,208,384]{2,1,0:T(8,128)(2,1)} %get-tuple-element.148.refs_1_, f32[4,8,208]{2,1,0:T(8,128)} %get-tuple-element.149.refs_2_, ...), custom_call_target="tpu_custom_call" | custom-call | flops 24999999488 | bytes 10000000 | tf_op jit(solution)/shard_map/attend_back/pallas_call | solution.py:177
  216.6 3.4 convert_add_fusion
  221.0 2.4 slice_add_fusion.2
  224.3 23.1 %attend_back.4 = (bf16[1,576,1152]{2,1,0:T(8,128)(2,1)}, f32[8,384]{1,0:T(8,128)}, f32[8,384]{1,0:T(8,128)}) custom-call(bf16[2,576,1152]{2,1,0:T(8,128)(2,1)} %get-tuple-element.119.refs_0_, bf16[2,576,384]{2,1,0:T(8,128)(2,1)} %get-tuple-element.165.refs_1_, f32[2,8,576]{2,1,0:T(8,128)} %get-tuple-element.166.refs_2_, ...), custom_call_target="tpu_custom_call" | custom-call | flops 24999999488 | bytes 10000000 | tf_op jit(solution)/shard_map/attend_back/pallas_call | solution.py:177
  248.8 1.8 collective-permute-start.24
  250.6 1.8 slice_add_fusion.6
  252.4 23.6 %attend_back.5 = (bf16[1,576,1152]{2,1,0:T(8,128)(2,1)}, f32[8,384]{1,0:T(8,128)}, f32[8,384]{1,0:T(8,128)}) custom-call(bf16[2,576,1152]{2,1,0:T(8,128)(2,1)} %get-tuple-element.119.refs_0_, bf16[2,576,384]{2,1,0:T(8,128)(2,1)} %get-tuple-element.165.refs_1_, f32[2,8,576]{2,1,0:T(8,128)} %get-tuple-element.166.refs_2_, ...), custom_call_target="tpu_custom_call" | custom-call | flops 24999999488 | bytes 10000000 | tf_op jit(solution)/shard_map/attend_back/pallas_call | solution.py:177
  278.5 4.1 %collective-permute-done.23 = bf16[2,448,128]{2,1,0:T(8,128)(2,1)S(1)} collective-permute-done((bf16[2,448,128]{2,1,0:T(8,128)(2,1)S(1)}, bf16[2,448,128]{2,1,0:T(8,128)(2,1)S(1)}, u32[]{:S(2)}, u32[]{:S(2)}) %collective-permute-start.23) | collective-permute-done | bytes 229408 | tf_op jit(solution)/shard_map/ppermute | solution.py:187
  283.2 18.8 %embed_back.1 = (f32[4,896,128]{2,1,0:T(8,128)}, bf16[4,896,128]{2,1,0:T(8,128)(2,1)}) custom-call(s32[1]{0:T(128)S(6)} %and.14.me_ref.refs_0_, bf16[4,196,768]{2,1,0:T(8,128)(2,1)} %copy.25.refs_0_.refs_1_, bf16[2,576,768]{2,1,0:T(8,128)(2,1)} %refs_2_.1, f32[196,576]{1,0:T(8,128)} %constant.48.clone.refs_3_, ...), custom_call_target="tpu_custom_call" | custom-call | flops 20000000000 | bytes 30000000 | tf_op jit(solution)/shard_map/embed_back/pallas_call | solution.py:177
  303.0 1.8 collective-permute-done.25
  304.7 1.6 add_convert_fusion.2
  308.6 2.3 collective-permute-start.28
  311.2 6.9 %collective-permute-done.26 = bf16[896,128]{1,0:T(8,128)(2,1)S(1)} collective-permute-done((bf16[896,128]{1,0:T(8,128)(2,1)S(1)}, bf16[896,128]{1,0:T(8,128)(2,1)S(1)}, u32[]{:S(2)}, u32[]{:S(2)}) %collective-permute-start.26) | collective-permute-done | bytes 229408 | tf_op jit(solution)/shard_map/ppermute | solution.py:194
  318.1 11.0 %collective-permute-done.27 = bf16[896,128]{1,0:T(8,128)(2,1)S(1)} collective-permute-done((bf16[896,128]{1,0:T(8,128)(2,1)S(1)}, bf16[896,128]{1,0:T(8,128)(2,1)S(1)}, u32[]{:S(2)}, u32[]{:S(2)}) %collective-permute-start.27) | collective-permute-done | bytes 229408 | tf_op jit(solution)/shard_map/ppermute | solution.py:194
  335.4 3.0 collective-permute-done.33
  338.4 2.5 collective-permute-done.30
  343.9 2.8 collective-permute-done.34
  347.5 4.4 %adam.1 = (f32[3,55552]{1,0:T(4,128)}, f32[3,55552]{1,0:T(4,128)}, f32[3,55552]{1,0:T(4,128)}, f32[3,55552]{1,0:T(4,128)}, f32[8,128]{1,0:T(8,128)}) custom-call(s32[1]{0:T(128)} %bitcast.me_ref, s32[1]{0:T(128)S(6)} %copy.29.step_ref, s32[8,128]{1,0:T(8,128)} %constant.46.clone.bounds, f32[3,55552]{1,0:T(4,128)} %master.7, f32[3,55552]{1,0:T(4,128)} %first.1, ...), custom_call_target="tpu_custom_call" | custom-call | tf_op jit(solution)/shard_map/adam/pallas_call | solution.py:1235
  352.6 7.4 %collective-permute-start.36 = (f32[8,128]{1,0:T(8,128)S(1)}, f32[8,128]{1,0:T(8,128)S(1)}, u32[]{:S(2)}, u32[]{:S(2)}) collective-permute-start(f32[8,128]{1,0:T(8,128)S(1)} %select_add_fusion), channel_id=1, source_target_pairs={{0,1},{1,0},{2,3},{3,2},{4,5},{5,4},{6,7},{7,6},{8,9},{9,8},{10,11... | collective-permute-start | bytes 12296 | tf_op jit(solution)/shard_map/ppermute | solution.py:187
  360.0 1.6 collective-permute-done.36
  361.5 2.3 collective-permute-start.37
  363.8 2.2 collective-permute-done.37
  367.2 2.5 collective-permute-start.39
  369.7 1.6 collective-permute-done.39
  371.3 3.6 collective-permute-done.40
  375.5 2.8 apply_update.1
  (137 shorter events, 37.5 us)
Async XLA Ops:
  7.2 135.3 %all-gather.2.cloned.1.call-start = ((), (), s32[]{:S(2)}) async-start(), calls=%async_computation | async-start | bytes 3784704 | tf_op jit(solution)/shard_map/all_gather | solution.py:1374
  9.1 23.1 %copy-start.13 = (bf16[1,448,128]{2,1,0:T(8,128)(2,1)S(1)}, bf16[1,448,128]{2,1,0:T(8,128)(2,1)}, u32[]{:S(2)}) copy-start(bf16[1,448,128]{2,1,0:T(8,128)(2,1)} %get-tuple-element.108) | copy-start | bytes 344068
  9.2 7.7 %collective-permute-start = (bf16[1,448,128]{2,1,0:T(8,128)(2,1)}, bf16[1,448,128]{2,1,0:T(8,128)(2,1)S(1)}, u32[]{:S(2)}, u32[]{:S(2)}) collective-permute-start(bf16[1,448,128]{2,1,0:T(8,128)(2,1)} %get-tuple-element.103), channel_id=1, source_target_pairs={{0,16},{4,20},{8,24},{12,28},{1,17},{5,21},{9,25},{13,29},{2,18},{... | collective-permute-start | bytes 344072 | tf_op jit(solution)/shard_map/ppermute | solution.py:1354
  14.2 30.7 %copy-start.9 = (bf16[4,196,768]{2,0,1:T(4,128)(2,1)S(1)}, bf16[4,196,768]{2,0,1:T(4,128)(2,1)}, u32[]{:S(2)}) copy-start(bf16[4,196,768]{2,0,1:T(4,128)(2,1)} %param.17) | copy-start | bytes 3612676
  17.8 7.4 %collective-permute-start.1 = (bf16[1,448,128]{2,1,0:T(8,128)(2,1)S(1)}, bf16[1,448,128]{2,1,0:T(8,128)(2,1)S(1)}, u32[]{:S(2)}, u32[]{:S(2)}) collective-permute-start(bf16[1,448,128]{2,1,0:T(8,128)(2,1)S(1)} %broadcast_select_fusion), channel_id=1, source_target_pairs={{0,1},{1,0},{2,3},{3,2},{4,5},{5,4},{6,7},{7,6},{8,9},{9,8},{10,11... | collective-permute-start | bytes 344072 | tf_op jit(solution)/shard_map/ppermute | solution.py:194
  19.4 11.1 %collective-permute-start.2 = (bf16[1,448,128]{2,1,0:T(8,128)(2,1)S(1)}, bf16[1,448,128]{2,1,0:T(8,128)(2,1)S(1)}, u32[]{:S(2)}, u32[]{:S(2)}) collective-permute-start(bf16[1,448,128]{2,1,0:T(8,128)(2,1)S(1)} %broadcast_select_fusion), channel_id=1, source_target_pairs={{0,2},{1,3},{2,0},{3,1},{4,6},{5,7},{6,4},{7,5},{8,10},{9,11},{10,... | collective-permute-start | bytes 344072 | tf_op jit(solution)/shard_map/ppermute | solution.py:194
  22.0 8.6 %collective-permute-start.3 = (bf16[1,448,128]{2,1,0:T(8,128)(2,1)S(1)}, bf16[1,448,128]{2,1,0:T(8,128)(2,1)S(1)}, u32[]{:S(2)}, u32[]{:S(2)}) collective-permute-start(bf16[1,448,128]{2,1,0:T(8,128)(2,1)S(1)} %broadcast_select_fusion), channel_id=1, source_target_pairs={{0,3},{1,2},{2,1},{3,0},{4,7},{5,6},{6,5},{7,4},{8,11},{9,10},{10,... | collective-permute-start | bytes 344072 | tf_op jit(solution)/shard_map/ppermute | solution.py:194
  22.2 10.0 %collective-permute-start.7 = (bf16[1,448,128]{2,1,0:T(8,128)(2,1)}, bf16[1,448,128]{2,1,0:T(8,128)(2,1)S(1)}, u32[]{:S(2)}, u32[]{:S(2)}) collective-permute-start(bf16[1,448,128]{2,1,0:T(8,128)(2,1)} %get-tuple-element.108), channel_id=1, source_target_pairs={{0,24},{4,28},{8,16},{12,20},{16,8},{20,12},{24,0},{28,4},{1,25},{... | collective-permute-start | bytes 344072 | tf_op jit(solution)/shard_map/ppermute | solution.py:1356
  24.6 7.6 %collective-permute-start.8 = (bf16[1,448,128]{2,1,0:T(8,128)(2,1)}, bf16[1,448,128]{2,1,0:T(8,128)(2,1)S(1)}, u32[]{:S(2)}, u32[]{:S(2)}) collective-permute-start(bf16[1,448,128]{2,1,0:T(8,128)(2,1)} %get-tuple-element.108), channel_id=1, source_target_pairs={{0,16},{4,20},{8,24},{12,28},{16,0},{20,4},{24,8},{28,12},{1,17},{... | collective-permute-start | bytes 344072 | tf_op jit(solution)/shard_map/ppermute | solution.py:1356
  25.2 7.0 %collective-permute-start.9 = (bf16[1,448,128]{2,1,0:T(8,128)(2,1)}, bf16[1,448,128]{2,1,0:T(8,128)(2,1)S(1)}, u32[]{:S(2)}, u32[]{:S(2)}) collective-permute-start(bf16[1,448,128]{2,1,0:T(8,128)(2,1)} %get-tuple-element.108), channel_id=1, source_target_pairs={{0,8},{4,12},{8,0},{12,4},{16,24},{20,28},{24,16},{28,20},{1,9},{5... | collective-permute-start | bytes 344072 | tf_op jit(solution)/shard_map/ppermute | solution.py:1356
  30.6 15.4 %copy-start.6 = (bf16[4,448,128]{2,1,0:T(8,128)(2,1)}, bf16[4,448,128]{2,1,0:T(8,128)(2,1)S(1)}, u32[]{:S(2)}) copy-start(bf16[4,448,128]{2,1,0:T(8,128)(2,1)S(1)} %pad_maximum_fusion.refs_0_) | copy-start | bytes 1376260
  30.6 14.2 %collective-permute-start.4 = (bf16[4,448,128]{2,1,0:T(8,128)(2,1)S(1)}, bf16[4,448,128]{2,1,0:T(8,128)(2,1)}, u32[]{:S(2)}, u32[]{:S(2)}) collective-permute-start(bf16[4,448,128]{2,1,0:T(8,128)(2,1)S(1)} %pad_maximum_fusion.refs_0_), channel_id=1, source_target_pairs={{0,8},{4,12},{8,0},{12,4},{16,24},{20,28},{24,16},{28,20},{1,9},{5... | collective-permute-start | bytes 1376264 | tf_op jit(solution)/shard_map/ppermute | solution.py:189
  32.3 5.5 %collective-permute-start.10 = (bf16[1,448,128]{2,1,0:T(8,128)(2,1)S(1)}, bf16[1,448,128]{2,1,0:T(8,128)(2,1)S(1)}, u32[]{:S(2)}, u32[]{:S(2)}) collective-permute-start(bf16[1,448,128]{2,1,0:T(8,128)(2,1)S(1)} %get-tuple-element.218), channel_id=1, source_target_pairs={{0,1},{1,0},{2,3},{3,2},{4,5},{5,4},{6,7},{7,6},{8,9},{9,8},{10,11... | collective-permute-start | bytes 344072 | tf_op jit(solution)/shard_map/ppermute | solution.py:194
  34.1 10.0 %collective-permute-start.11 = (bf16[1,448,128]{2,1,0:T(8,128)(2,1)S(1)}, bf16[1,448,128]{2,1,0:T(8,128)(2,1)S(1)}, u32[]{:S(2)}, u32[]{:S(2)}) collective-permute-start(bf16[1,448,128]{2,1,0:T(8,128)(2,1)S(1)} %get-tuple-element.218), channel_id=1, source_target_pairs={{0,2},{1,3},{2,0},{3,1},{4,6},{5,7},{6,4},{7,5},{8,10},{9,11},{10,... | collective-permute-start | bytes 344072 | tf_op jit(solution)/shard_map/ppermute | solution.py:194
  35.6 8.5 %collective-permute-start.12 = (bf16[1,448,128]{2,1,0:T(8,128)(2,1)S(1)}, bf16[1,448,128]{2,1,0:T(8,128)(2,1)S(1)}, u32[]{:S(2)}, u32[]{:S(2)}) collective-permute-start(bf16[1,448,128]{2,1,0:T(8,128)(2,1)S(1)} %get-tuple-element.218), channel_id=1, source_target_pairs={{0,3},{1,2},{2,1},{3,0},{4,7},{5,6},{6,5},{7,4},{8,11},{9,10},{10,... | collective-permute-start | bytes 344072 | tf_op jit(solution)/shard_map/ppermute | solution.py:194
  44.2 4.8 %collective-permute-start.13 = (bf16[4,448,128]{2,1,0:T(8,128)(2,1)S(1)}, bf16[4,448,128]{2,1,0:T(8,128)(2,1)S(1)}, u32[]{:S(2)}, u32[]{:S(2)}) collective-permute-start(bf16[4,448,128]{2,1,0:T(8,128)(2,1)S(1)} %pad_maximum_fusion.1.refs_0_), channel_id=1, source_target_pairs={{0,4},{4,0},{8,12},{12,8},{16,20},{20,16},{24,28},{28,24},{1,5},{5... | collective-permute-start | bytes 1376264 | tf_op jit(solution)/shard_map/ppermute | solution.py:189
  44.3 9.0 %collective-permute-start.5 = (bf16[4,448,128]{2,1,0:T(8,128)(2,1)S(1)}, bf16[4,448,128]{2,1,0:T(8,128)(2,1)}, u32[]{:S(2)}, u32[]{:S(2)}) collective-permute-start(bf16[4,448,128]{2,1,0:T(8,128)(2,1)S(1)} %pad_maximum_fusion.refs_0_), channel_id=1, source_target_pairs={{0,4},{4,0},{8,12},{12,8},{16,20},{20,16},{24,28},{28,24},{1,5},{5... | collective-permute-start | bytes 1376264 | tf_op jit(solution)/shard_map/ppermute | solution.py:189
  44.8 8.5 %collective-permute-start.6 = (bf16[4,448,128]{2,1,0:T(8,128)(2,1)}, bf16[4,448,128]{2,1,0:T(8,128)(2,1)}, u32[]{:S(2)}, u32[]{:S(2)}) collective-permute-start(bf16[4,448,128]{2,1,0:T(8,128)(2,1)} %collective-permute-done.4.refs_1_), channel_id=1, source_target_pairs={{0,4},{4,0},{8,12},{12,8},{16,20},{20,16},{24,28},{28,24},{1,5},{5... | collective-permute-start | bytes 1376264 | tf_op jit(solution)/shard_map/ppermute | solution.py:189
  46.1 37.6 %collective-permute-start.14 = (bf16[3,448,128]{2,1,0:T(8,128)(2,1)S(1)}, bf16[3,448,128]{2,1,0:T(8,128)(2,1)S(1)}, u32[]{:S(2)}, u32[]{:S(2)}) collective-permute-start(bf16[3,448,128]{2,1,0:T(8,128)(2,1)S(1)} %pad_maximum_fusion.2), channel_id=1, source_target_pairs={{0,1},{1,0},{2,3},{3,2},{4,5},{5,4},{6,7},{7,6},{8,9},{9,8},{10,11... | collective-permute-start | bytes 1032200 | tf_op jit(solution)/shard_map/ppermute | solution.py:194
  48.0 35.6 %collective-permute-start.15 = (bf16[3,448,128]{2,1,0:T(8,128)(2,1)S(1)}, bf16[3,448,128]{2,1,0:T(8,128)(2,1)S(1)}, u32[]{:S(2)}, u32[]{:S(2)}) collective-permute-start(bf16[3,448,128]{2,1,0:T(8,128)(2,1)S(1)} %pad_maximum_fusion.2), channel_id=1, source_target_pairs={{0,2},{1,3},{2,0},{3,1},{4,6},{5,7},{6,4},{7,5},{8,10},{9,11},{10,... | collective-permute-start | bytes 1032200 | tf_op jit(solution)/shard_map/ppermute | solution.py:194
  49.0 34.6 %collective-permute-start.16 = (bf16[3,448,128]{2,1,0:T(8,128)(2,1)S(1)}, bf16[3,448,128]{2,1,0:T(8,128)(2,1)S(1)}, u32[]{:S(2)}, u32[]{:S(2)}) collective-permute-start(bf16[3,448,128]{2,1,0:T(8,128)(2,1)S(1)} %pad_maximum_fusion.2), channel_id=1, source_target_pairs={{0,3},{1,2},{2,1},{3,0},{4,7},{5,6},{6,5},{7,4},{8,11},{9,10},{10,... | collective-permute-start | bytes 1032200 | tf_op jit(solution)/shard_map/ppermute | solution.py:194
  83.8 27.0 %collective-permute-start.17 = (bf16[12,448,128]{2,1,0:T(8,128)(2,1)S(1)}, bf16[12,448,128]{2,1,0:T(8,128)(2,1)S(1)}, u32[]{:S(2)}, u32[]{:S(2)}) collective-permute-start(bf16[12,448,128]{2,1,0:T(8,128)(2,1)S(1)} %constant_dynamic-update-slice_fusion.refs_3_.refs_2_), channel_id=1, source_target_pairs={{0,4},{4,0},{8,12},{12,8},{16,20},{20,16},{24,28},{28,24},{1,5},{5... | collective-permute-start | bytes 4128776 | tf_op jit(solution)/shard_map/ppermute | solution.py:189
  159.8 31.6 %collective-permute-start.18 = (bf16[16,448,128]{2,1,0:T(8,128)(2,1)}, bf16[16,448,128]{2,1,0:T(8,128)(2,1)S(1)}, u32[]{:S(2)}, u32[]{:S(2)}) collective-permute-start(bf16[16,448,128]{2,1,0:T(8,128)(2,1)} %get-tuple-element.147.refs_18_), channel_id=1, source_target_pairs={{0,4},{4,0},{8,12},{12,8},{16,20},{20,16},{24,28},{28,24},{1,5},{5... | collective-permute-start | bytes 5505032 | tf_op jit(solution)/shard_map/ppermute | solution.py:189
  190.9 25.6 %collective-permute-start.20 = (bf16[16,448,128]{2,1,0:T(8,128)(2,1)}, bf16[16,448,128]{2,1,0:T(8,128)(2,1)}, u32[]{:S(2)}, u32[]{:S(2)}) collective-permute-start(bf16[16,448,128]{2,1,0:T(8,128)(2,1)} %get-tuple-element.161.refs_8_), channel_id=1, source_target_pairs={{0,4},{4,0},{8,12},{12,8},{16,20},{20,16},{24,28},{28,24},{1,5},{5... | collective-permute-start | bytes 5505032 | tf_op jit(solution)/shard_map/ppermute | solution.py:189
  195.5 25.5 %collective-permute-start.19 = (bf16[8,448,128]{2,1,0:T(8,128)(2,1)}, bf16[8,448,128]{2,1,0:T(8,128)(2,1)}, u32[]{:S(2)}, u32[]{:S(2)}) collective-permute-start(bf16[8,448,128]{2,1,0:T(8,128)(2,1)} %get-tuple-element.203.refs_7_), channel_id=1, source_target_pairs={{0,16},{4,20},{8,24},{12,28},{16,0},{20,4},{24,8},{28,12},{1,17},{... | collective-permute-start | bytes 2752520 | tf_op jit(solution)/shard_map/ppermute | solution.py:189
  220.0 27.4 %collective-permute-start.22 = (bf16[8,448,128]{2,1,0:T(8,128)(2,1)}, bf16[8,448,128]{2,1,0:T(8,128)(2,1)}, u32[]{:S(2)}, u32[]{:S(2)}) collective-permute-start(bf16[8,448,128]{2,1,0:T(8,128)(2,1)} %get-tuple-element.201.refs_9_), channel_id=1, source_target_pairs={{0,1},{1,0},{2,3},{3,2},{4,5},{5,4},{6,7},{7,6},{8,9},{9,8},{10,11... | collective-permute-start | bytes 2752520 | tf_op jit(solution)/shard_map/ppermute | solution.py:187
  223.4 27.2 %collective-permute-start.21 = (bf16[4,448,128]{2,1,0:T(8,128)(2,1)}, bf16[4,448,128]{2,1,0:T(8,128)(2,1)}, u32[]{:S(2)}, u32[]{:S(2)}) collective-permute-start(bf16[4,448,128]{2,1,0:T(8,128)(2,1)} %get-tuple-element.207.refs_8_), channel_id=1, source_target_pairs={{0,8},{4,12},{8,0},{12,4},{16,24},{20,28},{24,16},{28,20},{1,9},{5... | collective-permute-start | bytes 1376264 | tf_op jit(solution)/shard_map/ppermute | solution.py:189
  248.8 28.3 %collective-permute-start.24 = (bf16[4,448,128]{2,1,0:T(8,128)(2,1)S(1)}, bf16[4,448,128]{2,1,0:T(8,128)(2,1)S(1)}, u32[]{:S(2)}, u32[]{:S(2)}) collective-permute-start(bf16[4,448,128]{2,1,0:T(8,128)(2,1)S(1)} %get-tuple-element.205.refs_9_), channel_id=1, source_target_pairs={{0,2},{1,3},{2,0},{3,1},{4,6},{5,7},{6,4},{7,5},{8,10},{9,11},{10,... | collective-permute-start | bytes 1376264 | tf_op jit(solution)/shard_map/ppermute | solution.py:187
  252.4 23.6 %copy-start.12 = (bf16[2,448,128]{2,1,0:T(8,128)(2,1)S(1)}, bf16[2,448,128]{2,1,0:T(8,128)(2,1)}, u32[]{:S(2)}) copy-start(bf16[2,448,128]{2,1,0:T(8,128)(2,1)} %get-tuple-element.211.refs_8_) | copy-start | bytes 688132
  276.1 6.5 %collective-permute-start.23 = (bf16[2,448,128]{2,1,0:T(8,128)(2,1)S(1)}, bf16[2,448,128]{2,1,0:T(8,128)(2,1)S(1)}, u32[]{:S(2)}, u32[]{:S(2)}) collective-permute-start(bf16[2,448,128]{2,1,0:T(8,128)(2,1)S(1)} %copy-done.12), channel_id=1, source_target_pairs={{0,1},{1,0},{2,3},{3,2},{4,5},{5,4},{6,7},{7,6},{8,9},{9,8},{10,11... | collective-permute-start | bytes 688136 | tf_op jit(solution)/shard_map/ppermute | solution.py:187
  283.2 18.9 %copy-start.11 = (bf16[2,448,128]{2,1,0:T(8,128)(2,1)S(1)}, bf16[2,448,128]{2,1,0:T(8,128)(2,1)}, u32[]{:S(2)}) copy-start(bf16[2,448,128]{2,1,0:T(8,128)(2,1)} %get-tuple-element.209.refs_19_) | copy-start | bytes 688132
  302.0 2.7 collective-permute-start.25
  302.1 9.1 %collective-permute-start.32 = (bf16[2,448,128]{2,1,0:T(8,128)(2,1)S(1)}, bf16[2,448,128]{2,1,0:T(8,128)(2,1)S(1)}, u32[]{:S(2)}, u32[]{:S(2)}) collective-permute-start(bf16[2,448,128]{2,1,0:T(8,128)(2,1)S(1)} %copy-done.11), channel_id=1, source_target_pairs={{0,16},{4,20},{8,24},{12,28},{16,0},{20,4},{24,8},{28,12},{1,17},{... | collective-permute-start | bytes 688136 | tf_op jit(solution)/shard_map/ppermute | solution.py:189
  304.7 24.4 %copy-start.2 = (f32[4,896,128]{2,1,0:T(8,128)S(1)}, f32[4,896,128]{2,1,0:T(8,128)}, u32[]{:S(2)}) copy-start(f32[4,896,128]{2,1,0:T(8,128)} %get-tuple-element.183) | copy-start | bytes 5505028
  306.5 11.6 %collective-permute-start.26 = (bf16[896,128]{1,0:T(8,128)(2,1)S(1)}, bf16[896,128]{1,0:T(8,128)(2,1)S(1)}, u32[]{:S(2)}, u32[]{:S(2)}) collective-permute-start(bf16[896,128]{1,0:T(8,128)(2,1)S(1)} %get-tuple-element.212), channel_id=1, source_target_pairs={{0,1},{1,0},{2,3},{3,2},{4,5},{5,4},{6,7},{7,6},{8,9},{9,8},{10,11... | collective-permute-start | bytes 688136 | tf_op jit(solution)/shard_map/ppermute | solution.py:194
  307.4 21.7 %collective-permute-start.27 = (bf16[896,128]{1,0:T(8,128)(2,1)S(1)}, bf16[896,128]{1,0:T(8,128)(2,1)S(1)}, u32[]{:S(2)}, u32[]{:S(2)}) collective-permute-start(bf16[896,128]{1,0:T(8,128)(2,1)S(1)} %get-tuple-element.214), channel_id=1, source_target_pairs={{0,2},{1,3},{2,0},{3,1},{4,6},{5,7},{6,4},{7,5},{8,10},{9,11},{10,... | collective-permute-start | bytes 688136 | tf_op jit(solution)/shard_map/ppermute | solution.py:194
  308.6 20.5 %collective-permute-start.28 = (bf16[896,128]{1,0:T(8,128)(2,1)S(1)}, bf16[896,128]{1,0:T(8,128)(2,1)S(1)}, u32[]{:S(2)}, u32[]{:S(2)}) collective-permute-start(bf16[896,128]{1,0:T(8,128)(2,1)S(1)} %get-tuple-element.213), channel_id=1, source_target_pairs={{0,3},{1,2},{2,1},{3,0},{4,7},{5,6},{6,5},{7,4},{8,11},{9,10},{10,... | collective-permute-start | bytes 688136 | tf_op jit(solution)/shard_map/ppermute | solution.py:194
  310.9 24.5 %collective-permute-start.35 = (bf16[1,448,128]{2,1,0:T(8,128)(2,1)S(1)}, bf16[1,448,128]{2,1,0:T(8,128)(2,1)S(1)}, u32[]{:S(2)}, u32[]{:S(2)}) collective-permute-start(bf16[1,448,128]{2,1,0:T(8,128)(2,1)S(1)} %copy-done.14), channel_id=1, source_target_pairs={{0,2},{1,3},{2,0},{3,1},{4,6},{5,7},{6,4},{7,5},{8,10},{9,11},{10,... | collective-permute-start | bytes 344072 | tf_op jit(solution)/shard_map/ppermute | solution.py:187
  329.3 9.1 %collective-permute-start.29 = (bf16[896,128]{1,0:T(8,128)(2,1)S(1)}, bf16[896,128]{1,0:T(8,128)(2,1)S(1)}, u32[]{:S(2)}, u32[]{:S(2)}) collective-permute-start(bf16[896,128]{1,0:T(8,128)(2,1)S(1)} %fusion.12), channel_id=1, source_target_pairs={{8,0},{12,4},{9,1},{13,5},{10,2},{14,6},{11,3},{15,7}} | collective-permute-start | bytes 688136 | tf_op jit(solution)/shard_map/ppermute | solution.py:1449
  330.6 10.4 %collective-permute-start.30 = (bf16[896,128]{1,0:T(8,128)(2,1)S(1)}, bf16[896,128]{1,0:T(8,128)(2,1)S(1)}, u32[]{:S(2)}, u32[]{:S(2)}) collective-permute-start(bf16[896,128]{1,0:T(8,128)(2,1)S(1)} %fusion.12), channel_id=1, source_target_pairs={{16,0},{20,4},{17,1},{21,5},{18,2},{22,6},{19,3},{23,7}} | collective-permute-start | bytes 688136 | tf_op jit(solution)/shard_map/ppermute | solution.py:1449
  331.9 9.1 %collective-permute-start.31 = (bf16[896,128]{1,0:T(8,128)(2,1)S(1)}, bf16[896,128]{1,0:T(8,128)(2,1)S(1)}, u32[]{:S(2)}, u32[]{:S(2)}) collective-permute-start(bf16[896,128]{1,0:T(8,128)(2,1)S(1)} %fusion.12), channel_id=1, source_target_pairs={{24,0},{28,4},{25,1},{29,5},{26,2},{30,6},{27,3},{31,7}} | collective-permute-start | bytes 688136 | tf_op jit(solution)/shard_map/ppermute | solution.py:1449
  333.2 5.2 %collective-permute-start.33 = (bf16[1,448,128]{2,1,0:T(8,128)(2,1)S(1)}, bf16[1,448,128]{2,1,0:T(8,128)(2,1)S(1)}, u32[]{:S(2)}, u32[]{:S(2)}) collective-permute-start(bf16[1,448,128]{2,1,0:T(8,128)(2,1)S(1)} %fusion.8), channel_id=1, source_target_pairs={{0,8},{4,12},{8,0},{12,4},{16,24},{20,28},{24,16},{28,20},{1,9},{5... | collective-permute-start | bytes 344072 | tf_op jit(solution)/shard_map/ppermute | solution.py:189
  341.9 4.8 %collective-permute-start.34 = (f32[448,128]{1,0:T(8,128)S(1)}, f32[448,128]{1,0:T(8,128)S(1)}, u32[]{:S(2)}, u32[]{:S(2)}) collective-permute-start(f32[448,128]{1,0:T(8,128)S(1)} %get-tuple-element.199), channel_id=1, source_target_pairs={{0,8},{4,12},{1,9},{5,13},{2,10},{6,14},{3,11},{7,15}} | collective-permute-start | bytes 688136 | tf_op jit(solution)/shard_map/ppermute | solution.py:1451
  352.6 9.0 %collective-permute-start.36 = (f32[8,128]{1,0:T(8,128)S(1)}, f32[8,128]{1,0:T(8,128)S(1)}, u32[]{:S(2)}, u32[]{:S(2)}) collective-permute-start(f32[8,128]{1,0:T(8,128)S(1)} %select_add_fusion), channel_id=1, source_target_pairs={{0,1},{1,0},{2,3},{3,2},{4,5},{5,4},{6,7},{7,6},{8,9},{9,8},{10,11... | collective-permute-start | bytes 12296 | tf_op jit(solution)/shard_map/ppermute | solution.py:187
  361.5 4.5 %collective-permute-start.37 = (f32[8,128]{1,0:T(8,128)S(1)}, f32[8,128]{1,0:T(8,128)S(1)}, u32[]{:S(2)}, u32[]{:S(2)}) collective-permute-start(f32[8,128]{1,0:T(8,128)S(1)} %add.148), channel_id=1, source_target_pairs={{0,2},{1,3},{2,0},{3,1},{4,6},{5,7},{6,4},{7,5},{8,10},{9,11},{10,... | collective-permute-start | bytes 12296 | tf_op jit(solution)/shard_map/ppermute | solution.py:187
  366.1 1.2 collective-permute-start.38
  367.2 4.1 %collective-permute-start.39 = (f32[8,128]{1,0:T(8,128)S(1)}, f32[8,128]{1,0:T(8,128)S(1)}, u32[]{:S(2)}, u32[]{:S(2)}) collective-permute-start(f32[8,128]{1,0:T(8,128)S(1)} %add.150), channel_id=1, source_target_pairs={{0,8},{4,12},{8,0},{12,4},{16,24},{20,28},{24,16},{28,20},{1,9},{5... | collective-permute-start | bytes 12296 | tf_op jit(solution)/shard_map/ppermute | solution.py:189
  371.3 3.6 collective-permute-start.40
  (18 other events, 51.4 us)
Sparse Core Ops, SparseCore 0:
  49.1 72.1 all-gather.1

commit v5 on v4

--- a/solution.py
+++ b/solution.py
@@ -1392,7 +1392,7 @@
     z_order = list(range(z_bits - 1, -1, -1))
     near_far = list(range(z_bits))
     class_order = [core, top, second] + inner + near_far
-    feed_order = [core] + near_far + [top, second] + inner
+    feed_order = [core] + near_far + inner + [top, second]
     class_rels, feed_rels = slots_of(class_order), slots_of(feed_order)
     tail = padded_rows - rows + 8
 
@@ -1437,20 +1437,24 @@
         (pre_sum, post_sum, g_wo, g_svec, g_head_w), (late_rels, rows, quarter_rows), padded_rows,
         [chain.send for chain in chains],
     )
-    for chain in chains:
-        while not chain.done:
-            chain.step(send)
+    while not class_chain.done:
+        class_chain.step(send)
+    while len(feed_chain.order) > 1:
+        feed_chain.step(send)
+    head_part = feed_chain.send[0].astype(f32) + lax.ppermute(
+        feed_chain.keep[0].astype(bf16), "dp", [(i, i + n_quarter) for i in range(n_quarter)]
+    ).astype(f32)
+    feed_chain.step()
     late_chain = Chain(keep, send, [core] + inner, z_bits, True)
     while not late_chain.done:
         late_chain.step()
     part = late_chain.total
-    send = part.astype(bf16)
+    (send,) = tied(tied((part.astype(bf16),), head_part), feed_chain.total)
     for a in (1, 2, 3):
         got = lax.ppermute(send, "dp", [(i + a * n_quarter, i) for i in range(n_quarter)])
         part = part + got.astype(f32)
-    head_part = lax.ppermute(feed_chain.total, "dp", [(i, i + n_quarter) for i in range(n_quarter)])
     first = quarter_id == 0
-    grad_stem = jnp.where(first, part[:padded_rows], head_part)
+    grad_stem = jnp.where(first, part[:padded_rows], jnp.where(quarter_id == 1, head_part, 0.0))
     grad_self = jnp.where(first, part[padded_rows:], feed_chain.total)
 
     gradients, new_first, new_second, update, sums = adam(

time: 390 us -> 388 us (level)
    ppermute x12, waiting for transfers between devices: 30.2 us -> 24 us  [exchange_z(): return lax.ppermute(value, 'fsdp', [(i, i ^ k) for i in range(n)])]
    ppermute x3, waiting for transfers between devices: 2.53 us -> 6.83 us  [on_device(): lax.ppermute(send, 'dp', [(i + a * n_quarter, i) for i in range(n_quarter)])]
  transfers between devices with their start and end apart: 42 -> 42, of which waited for: 16 -> 16; matrix products, arithmetic and copies ran while one was open for 4% -> 5% of each run, Pallas kernels for 49% -> 49%
where the time goes in v5:
time: 388 us; the launch traced here: 383 us
  Pallas kernels  235 us (61%)
  waiting for transfers between devices  54.2 us (14%)
  starting transfers between devices  53.9 us (14%)
  other arithmetic  19.4 us (5%)
  between operations  15.4 us (4%)
  local copies, waits for them, and re-layouts  5.45 us (1%)
    pallas_call x9, Pallas kernels, call(): pl.pallas_call(wrapped, in_specs=specs, compiler_params=params(), **kw)  187 us
    ppermute x12, waiting for transfers between devices, exchange_z(): return lax.ppermute(value, 'fsdp', [(i, i ^ k) for i in range(n)])  24 us
    ppermute x12, starting transfers between devices, exchange_z(): return lax.ppermute(value, 'fsdp', [(i, i ^ k) for i in range(n)])  17.9 us
    pallas_call x1, Pallas kernels, class_step(): pl.pallas_call(functools.partial(class_step_kernel, ns, nl, valid, unpack...  17.4 us
    ppermute x6, starting transfers between devices, exchange(): return lax.ppermute(value, 'fsdp', [(i, i ^ 1 << bit) for i in range(n)])  13.6 us
    ppermute x15, waiting for transfers between devices, exchange(): lax.ppermute(value, 'dp', [(i, i ^ 1 << bit - z_bits) for i in range(n)])  13.6 us
    add x6, other arithmetic, step(): kept = self.keep[:half].astype(f32) + got[:half].astype(f32)  12.6 us
    ppermute x6, waiting for transfers between devices, exchange(): return lax.ppermute(value, 'fsdp', [(i, i ^ 1 << bit) for i in range(n)])  9.43 us
  transfers between devices with their start and end apart: 42, of which 16 were waited for; matrix products, arithmetic and copies ran while one was open for 5% of the time, Pallas kernels for 49%

profile of v5, /device:TPU:0, one launch (start us, length us, event | category | flops | bytes accessed | tf_op | source)
XLA Modules:
  0.0 383.2 jit_solution(253252727572064962)
XLA Ops:
  7.2 1.9 round_shards.1
  9.2 5.0 %collective-permute-start = (bf16[1,448,128]{2,1,0:T(8,128)(2,1)}, bf16[1,448,128]{2,1,0:T(8,128)(2,1)S(1)}, u32[]{:S(2)}, u32[]{:S(2)}) collective-permute-start(bf16[1,448,128]{2,1,0:T(8,128)(2,1)} %get-tuple-element.104), channel_id=1, source_target_pairs={{0,16},{4,20},{8,24},{12,28},{1,17},{5,21},{9,25},{13,29},{2,18},{... | collective-permute-start | bytes 344072 | tf_op jit(solution)/shard_map/ppermute | solution.py:1354
  14.2 2.4 weight_sums.1
  17.8 1.6 collective-permute-start.1
  19.4 2.6 collective-permute-start.2
  22.2 2.4 collective-permute-start.7
  25.7 4.8 %collective-permute-done.2 = bf16[1,448,128]{2,1,0:T(8,128)(2,1)S(1)} collective-permute-done((bf16[1,448,128]{2,1,0:T(8,128)(2,1)S(1)}, bf16[1,448,128]{2,1,0:T(8,128)(2,1)S(1)}, u32[]{:S(2)}, u32[]{:S(2)}) %collective-permute-start.2) | collective-permute-done | bytes 114720 | tf_op jit(solution)/shard_map/ppermute | solution.py:194
  32.3 1.9 collective-permute-start.10
  37.8 6.3 %collective-permute-done.11 = bf16[1,448,128]{2,1,0:T(8,128)(2,1)S(1)} collective-permute-done((bf16[1,448,128]{2,1,0:T(8,128)(2,1)S(1)}, bf16[1,448,128]{2,1,0:T(8,128)(2,1)S(1)}, u32[]{:S(2)}, u32[]{:S(2)}) %collective-permute-start.11) | collective-permute-done | bytes 114720 | tf_op jit(solution)/shard_map/ppermute | solution.py:194
  46.1 1.9 collective-permute-start.14
  49.0 1.7 collective-permute-start.16
  50.7 2.6 unpack_low.1
  53.3 4.9 %unpack_stem.1 = (bf16[768,384]{1,0:T(8,128)(2,1)}, f32[8,384]{1,0:T(8,128)}, f32[208,384]{1,0:T(8,128)}, f32[576,384]{1,0:T(8,128)}, bf16[384,1024]{1,0:T(8,128)(2,1)}, /*index=5*/f32[1,1024]{1,0:T(1,128)}) custom-call(s32[1]{0:T(128)S(6)} %and.15.me_ref, f32[576,208]{1,0:T(8,128)} %constant.47.clone.resize_ref, bf16[4,448,128]{2,1,0:T(8,128)(2,1)} %copy-done.6, ...), custom_call_target="tpu_custom_call" | custom-call | tf_op jit(solution)/shard_map/unpack_stem/pallas_call | solution.py:272
  58.2 8.9 %embed.1 = (f32[4,208,384]{2,1,0:T(8,128)}, f32[2,576,384]{2,1,0:T(8,128)}, bf16[4,208,1152]{2,1,0:T(8,128)(2,1)}, bf16[2,576,1152]{2,1,0:T(8,128)(2,1)}) custom-call(bf16[4,196,768]{2,1,0:T(8,128)(2,1)} %copy.25.refs_0_.refs_1_, bf16[2,576,768]{2,1,0:T(8,128)(2,1)} %refs_2_.1, bf16[768,384]{1,0:T(8,128)(2,1)} %get-tuple-element.106.refs_2_, ...), custom_call_target="tpu_custom_call" | custom-call | flops 12000000000 | bytes 20000000 | tf_op jit(solution)/shard_map/embed/pallas_call | solution.py:177
  67.2 16.5 %attend.2 = (bf16[4,208,384]{2,1,0:T(8,128)(2,1)}, f32[4,8,208]{2,1,0:T(8,128)}) custom-call(bf16[4,208,1152]{2,1,0:T(8,128)(2,1)} %get-tuple-element.114.refs_0_, f32[384,8]{1,0:T(8,128)} %get-tuple-element.117.refs_1_.refs_3_, f32[384,8]{1,0:T(8,128)} %get-tuple-element.118.refs_2_.refs_4_), custom_call_target="tpu_custom_call" | custom-call | flops 20000000000 | bytes 10000000 | tf_op jit(solution)/shard_map/attend/pallas_call | solution.py:177
  85.0 25.9 %attend.3 = (bf16[2,576,384]{2,1,0:T(8,128)(2,1)}, f32[2,8,576]{2,1,0:T(8,128)}) custom-call(bf16[2,576,1152]{2,1,0:T(8,128)(2,1)} %get-tuple-element.120.refs_0_, f32[384,8]{1,0:T(8,128)} %get-tuple-element.117.refs_1_.refs_3_, f32[384,8]{1,0:T(8,128)} %get-tuple-element.118.refs_2_.refs_4_, bf16[12,448,128]{2,1,0:T(8,128)(2,1)} %copy-done.3, ...), custom_call_target="tpu_custom_call" | custom-call | flops 30000001024 | bytes 10000000 | tf_op jit(solution)/shard_map/attend/pallas_call | solution.py:177
  112.1 4.3 %unpack_feed.1 = (bf16[384,384]{1,0:T(8,128)(2,1)}, bf16[384,1536]{1,0:T(8,128)(2,1)}, bf16[1536,384]{1,0:T(8,128)(2,1)}, f32[16,384]{1,0:T(8,128)}, f32[1,1536]{1,0:T(1,128)}) custom-call(s32[1]{0:T(128)S(6)} %and.14.me_ref.refs_0_, bf16[4,448,128]{2,1,0:T(8,128)(2,1)} %copy-done, bf16[4,448,128]{2,1,0:T(8,128)(2,1)} %copy-done.7, ...), custom_call_target="tpu_custom_call" | custom-call | tf_op jit(solution)/shard_map/unpack_feed/pallas_call | solution.py:355
  116.4 26.1 %feed.1 = (bf16[4,208,384]{2,1,0:T(8,128)(2,1)}, bf16[2,576,384]{2,1,0:T(8,128)(2,1)}, f32[4,208,384]{2,1,0:T(8,128)}, f32[2,576,384]{2,1,0:T(8,128)}, bf16[4,20...) custom-call(f32[4,208,384]{2,1,0:T(8,128)} %get-tuple-element.112.re, ...), custom_call_target="tpu_custom_call" | custom-call | flops 20000000000 | bytes 30000000 | tf_op jit(solution)/shard_map/feed/pallas_call | solution.py:177
  142.5 17.4 %class_step.1 = (f32[4,208,384]{2,1,0:T(8,128)}, f32[2,576,384]{2,1,0:T(8,128)}, f32[8,384]{1,0:T(8,128)}, f32[384,1024]{1,0:T(8,128)}, f32[1,1024]{1,0:T(1,128)...) custom-call(s32[1]{0:T(128)} %bitcast.me_ref, s32[1]{0:T(128)} %constant.43.clone.1.from_ref, ...), custom_call_target="tpu_custom_call" | custom-call | flops 24999999488 | bytes 40000000 | tf_op jit(solution)/shard_map/class_step/pallas_call | solution.py:752
  159.9 24.5 %feed_back.1 = (f32[4,208,384]{2,1,0:T(8,128)}, f32[2,576,384]{2,1,0:T(8,128)}, bf16[4,208,384]{2,1,0:T(8,128)(2,1)}, bf16[2,576,384]{2,1,0:T(8,128)(2,1)}, f32[...) custom-call(f32[4,208,384]{2,1,0:T(8,128)} %get-tuple-element.136.refs, ...), custom_call_target="tpu_custom_call" | custom-call | flops 35000000512 | bytes 30000000 | tf_op jit(solution)/shard_map/feed_back/pallas_call | solution.py:177
  184.4 6.6 %pack_feed.1 = (bf16[16,448,128]{2,1,0:T(8,128)(2,1)}, bf16[16,448,128]{2,1,0:T(8,128)(2,1)}) custom-call(s32[1]{0:T(128)} %bitcast.me_ref, f32[384,384]{1,0:T(8,128)} %get-tuple-element.155.wo.refs_15_, f32[384,1536]{1,0:T(8,128)} %get-tuple-element.156.w1, f32[1536,384]{1,0:T(8,128)} %get-tuple-element.157.w2, f32[16,384]{1,0:T(8,128)} %get-tuple-element.158.vec, ...), custom_call_target="tpu_custom_call" | custom-call | tf_op jit(solution)/shard_map/pack_feed/pallas_call | solution.py:1149
  192.7 2.8 convert_add_fusion.1
  196.4 20.1 %attend_back.3 = (bf16[4,208,1152]{2,1,0:T(8,128)(2,1)}, f32[8,384]{1,0:T(8,128)}, f32[8,384]{1,0:T(8,128)}) custom-call(bf16[4,208,1152]{2,1,0:T(8,128)(2,1)} %get-tuple-element.114.refs_0_, bf16[4,208,384]{2,1,0:T(8,128)(2,1)} %get-tuple-element.149.refs_1_, f32[4,8,208]{2,1,0:T(8,128)} %get-tuple-element.150.refs_2_, ...), custom_call_target="tpu_custom_call" | custom-call | flops 24999999488 | bytes 10000000 | tf_op jit(solution)/shard_map/attend_back/pallas_call | solution.py:177
  216.6 3.4 convert_add_fusion
  221.1 2.4 slice_add_fusion.2
  224.3 23.1 %attend_back.4 = (bf16[1,576,1152]{2,1,0:T(8,128)(2,1)}, f32[8,384]{1,0:T(8,128)}, f32[8,384]{1,0:T(8,128)}) custom-call(bf16[2,576,1152]{2,1,0:T(8,128)(2,1)} %get-tuple-element.120.refs_0_, bf16[2,576,384]{2,1,0:T(8,128)(2,1)} %get-tuple-element.166.refs_1_, f32[2,8,576]{2,1,0:T(8,128)} %get-tuple-element.167.refs_2_, ...), custom_call_target="tpu_custom_call" | custom-call | flops 24999999488 | bytes 10000000 | tf_op jit(solution)/shard_map/attend_back/pallas_call | solution.py:177
  248.8 1.8 collective-permute-start.24
  250.6 1.8 slice_add_fusion.6
  252.4 23.5 %attend_back.5 = (bf16[1,576,1152]{2,1,0:T(8,128)(2,1)}, f32[8,384]{1,0:T(8,128)}, f32[8,384]{1,0:T(8,128)}) custom-call(bf16[2,576,1152]{2,1,0:T(8,128)(2,1)} %get-tuple-element.120.refs_0_, bf16[2,576,384]{2,1,0:T(8,128)(2,1)} %get-tuple-element.166.refs_1_, f32[2,8,576]{2,1,0:T(8,128)} %get-tuple-element.167.refs_2_, ...), custom_call_target="tpu_custom_call" | custom-call | flops 24999999488 | bytes 10000000 | tf_op jit(solution)/shard_map/attend_back/pallas_call | solution.py:177
  278.5 4.1 %collective-permute-done.23 = bf16[2,448,128]{2,1,0:T(8,128)(2,1)S(1)} collective-permute-done((bf16[2,448,128]{2,1,0:T(8,128)(2,1)S(1)}, bf16[2,448,128]{2,1,0:T(8,128)(2,1)S(1)}, u32[]{:S(2)}, u32[]{:S(2)}) %collective-permute-start.23) | collective-permute-done | bytes 229408 | tf_op jit(solution)/shard_map/ppermute | solution.py:187
  283.2 18.8 %embed_back.1 = (f32[4,896,128]{2,1,0:T(8,128)}, bf16[4,896,128]{2,1,0:T(8,128)(2,1)}) custom-call(s32[1]{0:T(128)S(6)} %and.14.me_ref.refs_0_, bf16[4,196,768]{2,1,0:T(8,128)(2,1)} %copy.25.refs_0_.refs_1_, bf16[2,576,768]{2,1,0:T(8,128)(2,1)} %refs_2_.1, f32[196,576]{1,0:T(8,128)} %constant.48.clone.refs_3_, ...), custom_call_target="tpu_custom_call" | custom-call | flops 20000000000 | bytes 30000000 | tf_op jit(solution)/shard_map/embed_back/pallas_call | solution.py:177
  304.9 5.2 %collective-permute-done.29 = bf16[2,448,128]{2,1,0:T(8,128)(2,1)S(1)} collective-permute-done((bf16[2,448,128]{2,1,0:T(8,128)(2,1)S(1)}, bf16[2,448,128]{2,1,0:T(8,128)(2,1)S(1)}, u32[]{:S(2)}, u32[]{:S(2)}) %collective-permute-start.29) | collective-permute-done | bytes 229408 | tf_op jit(solution)/shard_map/ppermute | solution.py:189
  312.3 1.6 add_convert_fusion.2
  314.1 2.0 collective-permute-start.27
  316.1 2.3 collective-permute-start.28
  318.5 3.1 collective-permute-start.30
  321.7 3.5 collective-permute-done.26
  325.1 8.3 %collective-permute-done.27 = bf16[896,128]{1,0:T(8,128)(2,1)S(1)} collective-permute-done((bf16[896,128]{1,0:T(8,128)(2,1)S(1)}, bf16[896,128]{1,0:T(8,128)(2,1)S(1)}, u32[]{:S(2)}, u32[]{:S(2)}) %collective-permute-start.27) | collective-permute-done | bytes 229408 | tf_op jit(solution)/shard_map/ppermute | solution.py:194
  338.4 3.1 collective-permute-done.32
  341.5 3.8 collective-permute-done.33
  346.3 4.4 %adam.1 = (f32[3,55552]{1,0:T(4,128)}, f32[3,55552]{1,0:T(4,128)}, f32[3,55552]{1,0:T(4,128)}, f32[3,55552]{1,0:T(4,128)}, f32[8,128]{1,0:T(8,128)}) custom-call(s32[1]{0:T(128)} %bitcast.me_ref, s32[1]{0:T(128)S(6)} %copy.29.step_ref, s32[8,128]{1,0:T(8,128)} %constant.46.clone.bounds, f32[3,55552]{1,0:T(4,128)} %master.7, f32[3,55552]{1,0:T(4,128)} %first.1, ...), custom_call_target="tpu_custom_call" | custom-call | tf_op jit(solution)/shard_map/adam/pallas_call | solution.py:1235
  351.5 6.8 %collective-permute-start.36 = (f32[8,128]{1,0:T(8,128)S(1)}, f32[8,128]{1,0:T(8,128)S(1)}, u32[]{:S(2)}, u32[]{:S(2)}) collective-permute-start(f32[8,128]{1,0:T(8,128)S(1)} %select_add_fusion), channel_id=1, source_target_pairs={{0,1},{1,0},{2,3},{3,2},{4,5},{5,4},{6,7},{7,6},{8,9},{9,8},{10,11... | collective-permute-start | bytes 12296 | tf_op jit(solution)/shard_map/ppermute | solution.py:187
  358.2 1.6 collective-permute-done.36
  359.8 1.7 collective-permute-start.37
  361.5 2.8 collective-permute-done.37
  365.5 3.6 collective-permute-done.39
  369.1 3.6 collective-permute-done.40
  373.3 2.8 apply_update.1
  (137 shorter events, 35.5 us)
Async XLA Ops:
  7.2 135.3 %all-gather.2.cloned.1.call-start = ((), (), s32[]{:S(2)}) async-start(), calls=%async_computation | async-start | bytes 3784704 | tf_op jit(solution)/shard_map/all_gather | solution.py:1374
  9.2 23.1 %copy-start.13 = (bf16[1,448,128]{2,1,0:T(8,128)(2,1)S(1)}, bf16[1,448,128]{2,1,0:T(8,128)(2,1)}, u32[]{:S(2)}) copy-start(bf16[1,448,128]{2,1,0:T(8,128)(2,1)} %get-tuple-element.109) | copy-start | bytes 344068
  9.2 7.7 %collective-permute-start = (bf16[1,448,128]{2,1,0:T(8,128)(2,1)}, bf16[1,448,128]{2,1,0:T(8,128)(2,1)S(1)}, u32[]{:S(2)}, u32[]{:S(2)}) collective-permute-start(bf16[1,448,128]{2,1,0:T(8,128)(2,1)} %get-tuple-element.104), channel_id=1, source_target_pairs={{0,16},{4,20},{8,24},{12,28},{1,17},{5,21},{9,25},{13,29},{2,18},{... | collective-permute-start | bytes 344072 | tf_op jit(solution)/shard_map/ppermute | solution.py:1354
  14.2 30.7 %copy-start.9 = (bf16[4,196,768]{2,0,1:T(4,128)(2,1)S(1)}, bf16[4,196,768]{2,0,1:T(4,128)(2,1)}, u32[]{:S(2)}) copy-start(bf16[4,196,768]{2,0,1:T(4,128)(2,1)} %param.17) | copy-start | bytes 3612676
  17.8 7.4 %collective-permute-start.1 = (bf16[1,448,128]{2,1,0:T(8,128)(2,1)S(1)}, bf16[1,448,128]{2,1,0:T(8,128)(2,1)S(1)}, u32[]{:S(2)}, u32[]{:S(2)}) collective-permute-start(bf16[1,448,128]{2,1,0:T(8,128)(2,1)S(1)} %broadcast_select_fusion), channel_id=1, source_target_pairs={{0,1},{1,0},{2,3},{3,2},{4,5},{5,4},{6,7},{7,6},{8,9},{9,8},{10,11... | collective-permute-start | bytes 344072 | tf_op jit(solution)/shard_map/ppermute | solution.py:194
  19.4 11.2 %collective-permute-start.2 = (bf16[1,448,128]{2,1,0:T(8,128)(2,1)S(1)}, bf16[1,448,128]{2,1,0:T(8,128)(2,1)S(1)}, u32[]{:S(2)}, u32[]{:S(2)}) collective-permute-start(bf16[1,448,128]{2,1,0:T(8,128)(2,1)S(1)} %broadcast_select_fusion), channel_id=1, source_target_pairs={{0,2},{1,3},{2,0},{3,1},{4,6},{5,7},{6,4},{7,5},{8,10},{9,11},{10,... | collective-permute-start | bytes 344072 | tf_op jit(solution)/shard_map/ppermute | solution.py:194
  22.0 8.6 %collective-permute-start.3 = (bf16[1,448,128]{2,1,0:T(8,128)(2,1)S(1)}, bf16[1,448,128]{2,1,0:T(8,128)(2,1)S(1)}, u32[]{:S(2)}, u32[]{:S(2)}) collective-permute-start(bf16[1,448,128]{2,1,0:T(8,128)(2,1)S(1)} %broadcast_select_fusion), channel_id=1, source_target_pairs={{0,3},{1,2},{2,1},{3,0},{4,7},{5,6},{6,5},{7,4},{8,11},{9,10},{10,... | collective-permute-start | bytes 344072 | tf_op jit(solution)/shard_map/ppermute | solution.py:194
  22.2 10.0 %collective-permute-start.7 = (bf16[1,448,128]{2,1,0:T(8,128)(2,1)}, bf16[1,448,128]{2,1,0:T(8,128)(2,1)S(1)}, u32[]{:S(2)}, u32[]{:S(2)}) collective-permute-start(bf16[1,448,128]{2,1,0:T(8,128)(2,1)} %get-tuple-element.109), channel_id=1, source_target_pairs={{0,24},{4,28},{8,16},{12,20},{16,8},{20,12},{24,0},{28,4},{1,25},{... | collective-permute-start | bytes 344072 | tf_op jit(solution)/shard_map/ppermute | solution.py:1356
  24.6 7.6 %collective-permute-start.8 = (bf16[1,448,128]{2,1,0:T(8,128)(2,1)}, bf16[1,448,128]{2,1,0:T(8,128)(2,1)S(1)}, u32[]{:S(2)}, u32[]{:S(2)}) collective-permute-start(bf16[1,448,128]{2,1,0:T(8,128)(2,1)} %get-tuple-element.109), channel_id=1, source_target_pairs={{0,16},{4,20},{8,24},{12,28},{16,0},{20,4},{24,8},{28,12},{1,17},{... | collective-permute-start | bytes 344072 | tf_op jit(solution)/shard_map/ppermute | solution.py:1356
  25.2 7.0 %collective-permute-start.9 = (bf16[1,448,128]{2,1,0:T(8,128)(2,1)}, bf16[1,448,128]{2,1,0:T(8,128)(2,1)S(1)}, u32[]{:S(2)}, u32[]{:S(2)}) collective-permute-start(bf16[1,448,128]{2,1,0:T(8,128)(2,1)} %get-tuple-element.109), channel_id=1, source_target_pairs={{0,8},{4,12},{8,0},{12,4},{16,24},{20,28},{24,16},{28,20},{1,9},{5... | collective-permute-start | bytes 344072 | tf_op jit(solution)/shard_map/ppermute | solution.py:1356
  30.6 14.2 %collective-permute-start.4 = (bf16[4,448,128]{2,1,0:T(8,128)(2,1)S(1)}, bf16[4,448,128]{2,1,0:T(8,128)(2,1)}, u32[]{:S(2)}, u32[]{:S(2)}) collective-permute-start(bf16[4,448,128]{2,1,0:T(8,128)(2,1)S(1)} %pad_maximum_fusion.refs_0_), channel_id=1, source_target_pairs={{0,8},{4,12},{8,0},{12,4},{16,24},{20,28},{24,16},{28,20},{1,9},{5... | collective-permute-start | bytes 1376264 | tf_op jit(solution)/shard_map/ppermute | solution.py:189
  32.3 5.5 %collective-permute-start.10 = (bf16[1,448,128]{2,1,0:T(8,128)(2,1)S(1)}, bf16[1,448,128]{2,1,0:T(8,128)(2,1)S(1)}, u32[]{:S(2)}, u32[]{:S(2)}) collective-permute-start(bf16[1,448,128]{2,1,0:T(8,128)(2,1)S(1)} %get-tuple-element.222), channel_id=1, source_target_pairs={{0,1},{1,0},{2,3},{3,2},{4,5},{5,4},{6,7},{7,6},{8,9},{9,8},{10,11... | collective-permute-start | bytes 344072 | tf_op jit(solution)/shard_map/ppermute | solution.py:194
  34.1 10.0 %collective-permute-start.11 = (bf16[1,448,128]{2,1,0:T(8,128)(2,1)S(1)}, bf16[1,448,128]{2,1,0:T(8,128)(2,1)S(1)}, u32[]{:S(2)}, u32[]{:S(2)}) collective-permute-start(bf16[1,448,128]{2,1,0:T(8,128)(2,1)S(1)} %get-tuple-element.222), channel_id=1, source_target_pairs={{0,2},{1,3},{2,0},{3,1},{4,6},{5,7},{6,4},{7,5},{8,10},{9,11},{10,... | collective-permute-start | bytes 344072 | tf_op jit(solution)/shard_map/ppermute | solution.py:194
  35.6 8.5 %collective-permute-start.12 = (bf16[1,448,128]{2,1,0:T(8,128)(2,1)S(1)}, bf16[1,448,128]{2,1,0:T(8,128)(2,1)S(1)}, u32[]{:S(2)}, u32[]{:S(2)}) collective-permute-start(bf16[1,448,128]{2,1,0:T(8,128)(2,1)S(1)} %get-tuple-element.222), channel_id=1, source_target_pairs={{0,3},{1,2},{2,1},{3,0},{4,7},{5,6},{6,5},{7,4},{8,11},{9,10},{10,... | collective-permute-start | bytes 344072 | tf_op jit(solution)/shard_map/ppermute | solution.py:194
  44.2 4.8 %collective-permute-start.13 = (bf16[4,448,128]{2,1,0:T(8,128)(2,1)S(1)}, bf16[4,448,128]{2,1,0:T(8,128)(2,1)S(1)}, u32[]{:S(2)}, u32[]{:S(2)}) collective-permute-start(bf16[4,448,128]{2,1,0:T(8,128)(2,1)S(1)} %pad_maximum_fusion.1.refs_0_), channel_id=1, source_target_pairs={{0,4},{4,0},{8,12},{12,8},{16,20},{20,16},{24,28},{28,24},{1,5},{5... | collective-permute-start | bytes 1376264 | tf_op jit(solution)/shard_map/ppermute | solution.py:189
  44.3 9.0 %collective-permute-start.5 = (bf16[4,448,128]{2,1,0:T(8,128)(2,1)S(1)}, bf16[4,448,128]{2,1,0:T(8,128)(2,1)}, u32[]{:S(2)}, u32[]{:S(2)}) collective-permute-start(bf16[4,448,128]{2,1,0:T(8,128)(2,1)S(1)} %pad_maximum_fusion.refs_0_), channel_id=1, source_target_pairs={{0,4},{4,0},{8,12},{12,8},{16,20},{20,16},{24,28},{28,24},{1,5},{5... | collective-permute-start | bytes 1376264 | tf_op jit(solution)/shard_map/ppermute | solution.py:189
  44.8 8.5 %collective-permute-start.6 = (bf16[4,448,128]{2,1,0:T(8,128)(2,1)}, bf16[4,448,128]{2,1,0:T(8,128)(2,1)}, u32[]{:S(2)}, u32[]{:S(2)}) collective-permute-start(bf16[4,448,128]{2,1,0:T(8,128)(2,1)} %collective-permute-done.4.refs_1_), channel_id=1, source_target_pairs={{0,4},{4,0},{8,12},{12,8},{16,20},{20,16},{24,28},{28,24},{1,5},{5... | collective-permute-start | bytes 1376264 | tf_op jit(solution)/shard_map/ppermute | solution.py:189
  46.1 37.6 %collective-permute-start.14 = (bf16[3,448,128]{2,1,0:T(8,128)(2,1)S(1)}, bf16[3,448,128]{2,1,0:T(8,128)(2,1)S(1)}, u32[]{:S(2)}, u32[]{:S(2)}) collective-permute-start(bf16[3,448,128]{2,1,0:T(8,128)(2,1)S(1)} %pad_maximum_fusion.2), channel_id=1, source_target_pairs={{0,1},{1,0},{2,3},{3,2},{4,5},{5,4},{6,7},{7,6},{8,9},{9,8},{10,11... | collective-permute-start | bytes 1032200 | tf_op jit(solution)/shard_map/ppermute | solution.py:194
  48.0 35.7 %collective-permute-start.15 = (bf16[3,448,128]{2,1,0:T(8,128)(2,1)S(1)}, bf16[3,448,128]{2,1,0:T(8,128)(2,1)S(1)}, u32[]{:S(2)}, u32[]{:S(2)}) collective-permute-start(bf16[3,448,128]{2,1,0:T(8,128)(2,1)S(1)} %pad_maximum_fusion.2), channel_id=1, source_target_pairs={{0,2},{1,3},{2,0},{3,1},{4,6},{5,7},{6,4},{7,5},{8,10},{9,11},{10,... | collective-permute-start | bytes 1032200 | tf_op jit(solution)/shard_map/ppermute | solution.py:194
  49.0 34.6 %collective-permute-start.16 = (bf16[3,448,128]{2,1,0:T(8,128)(2,1)S(1)}, bf16[3,448,128]{2,1,0:T(8,128)(2,1)S(1)}, u32[]{:S(2)}, u32[]{:S(2)}) collective-permute-start(bf16[3,448,128]{2,1,0:T(8,128)(2,1)S(1)} %pad_maximum_fusion.2), channel_id=1, source_target_pairs={{0,3},{1,2},{2,1},{3,0},{4,7},{5,6},{6,5},{7,4},{8,11},{9,10},{10,... | collective-permute-start | bytes 1032200 | tf_op jit(solution)/shard_map/ppermute | solution.py:194
  83.9 27.0 %collective-permute-start.17 = (bf16[12,448,128]{2,1,0:T(8,128)(2,1)S(1)}, bf16[12,448,128]{2,1,0:T(8,128)(2,1)S(1)}, u32[]{:S(2)}, u32[]{:S(2)}) collective-permute-start(bf16[12,448,128]{2,1,0:T(8,128)(2,1)S(1)} %constant_dynamic-update-slice_fusion.refs_3_.refs_2_), channel_id=1, source_target_pairs={{0,4},{4,0},{8,12},{12,8},{16,20},{20,16},{24,28},{28,24},{1,5},{5... | collective-permute-start | bytes 4128776 | tf_op jit(solution)/shard_map/ppermute | solution.py:189
  159.9 31.6 %collective-permute-start.18 = (bf16[16,448,128]{2,1,0:T(8,128)(2,1)}, bf16[16,448,128]{2,1,0:T(8,128)(2,1)S(1)}, u32[]{:S(2)}, u32[]{:S(2)}) collective-permute-start(bf16[16,448,128]{2,1,0:T(8,128)(2,1)} %get-tuple-element.148.refs_18_), channel_id=1, source_target_pairs={{0,4},{4,0},{8,12},{12,8},{16,20},{20,16},{24,28},{28,24},{1,5},{5... | collective-permute-start | bytes 5505032 | tf_op jit(solution)/shard_map/ppermute | solution.py:189
  191.0 25.6 %collective-permute-start.20 = (bf16[16,448,128]{2,1,0:T(8,128)(2,1)}, bf16[16,448,128]{2,1,0:T(8,128)(2,1)}, u32[]{:S(2)}, u32[]{:S(2)}) collective-permute-start(bf16[16,448,128]{2,1,0:T(8,128)(2,1)} %get-tuple-element.162.refs_8_), channel_id=1, source_target_pairs={{0,4},{4,0},{8,12},{12,8},{16,20},{20,16},{24,28},{28,24},{1,5},{5... | collective-permute-start | bytes 5505032 | tf_op jit(solution)/shard_map/ppermute | solution.py:189
  195.5 25.6 %collective-permute-start.19 = (bf16[8,448,128]{2,1,0:T(8,128)(2,1)}, bf16[8,448,128]{2,1,0:T(8,128)(2,1)}, u32[]{:S(2)}, u32[]{:S(2)}) collective-permute-start(bf16[8,448,128]{2,1,0:T(8,128)(2,1)} %get-tuple-element.203.refs_7_), channel_id=1, source_target_pairs={{0,16},{4,20},{8,24},{12,28},{16,0},{20,4},{24,8},{28,12},{1,17},{... | collective-permute-start | bytes 2752520 | tf_op jit(solution)/shard_map/ppermute | solution.py:189
  220.0 27.4 %collective-permute-start.22 = (bf16[8,448,128]{2,1,0:T(8,128)(2,1)}, bf16[8,448,128]{2,1,0:T(8,128)(2,1)}, u32[]{:S(2)}, u32[]{:S(2)}) collective-permute-start(bf16[8,448,128]{2,1,0:T(8,128)(2,1)} %get-tuple-element.201.refs_9_), channel_id=1, source_target_pairs={{0,1},{1,0},{2,3},{3,2},{4,5},{5,4},{6,7},{7,6},{8,9},{9,8},{10,11... | collective-permute-start | bytes 2752520 | tf_op jit(solution)/shard_map/ppermute | solution.py:187
  223.4 27.1 %collective-permute-start.21 = (bf16[4,448,128]{2,1,0:T(8,128)(2,1)}, bf16[4,448,128]{2,1,0:T(8,128)(2,1)}, u32[]{:S(2)}, u32[]{:S(2)}) collective-permute-start(bf16[4,448,128]{2,1,0:T(8,128)(2,1)} %get-tuple-element.207.refs_8_), channel_id=1, source_target_pairs={{0,8},{4,12},{8,0},{12,4},{16,24},{20,28},{24,16},{28,20},{1,9},{5... | collective-permute-start | bytes 1376264 | tf_op jit(solution)/shard_map/ppermute | solution.py:189
  248.8 28.2 %collective-permute-start.24 = (bf16[4,448,128]{2,1,0:T(8,128)(2,1)S(1)}, bf16[4,448,128]{2,1,0:T(8,128)(2,1)S(1)}, u32[]{:S(2)}, u32[]{:S(2)}) collective-permute-start(bf16[4,448,128]{2,1,0:T(8,128)(2,1)S(1)} %get-tuple-element.205.refs_9_), channel_id=1, source_target_pairs={{0,2},{1,3},{2,0},{3,1},{4,6},{5,7},{6,4},{7,5},{8,10},{9,11},{10,... | collective-permute-start | bytes 1376264 | tf_op jit(solution)/shard_map/ppermute | solution.py:187
  252.4 23.5 %copy-start.12 = (bf16[2,448,128]{2,1,0:T(8,128)(2,1)S(1)}, bf16[2,448,128]{2,1,0:T(8,128)(2,1)}, u32[]{:S(2)}) copy-start(bf16[2,448,128]{2,1,0:T(8,128)(2,1)} %get-tuple-element.211.refs_8_) | copy-start | bytes 688132
  276.0 6.5 %collective-permute-start.23 = (bf16[2,448,128]{2,1,0:T(8,128)(2,1)S(1)}, bf16[2,448,128]{2,1,0:T(8,128)(2,1)S(1)}, u32[]{:S(2)}, u32[]{:S(2)}) collective-permute-start(bf16[2,448,128]{2,1,0:T(8,128)(2,1)S(1)} %copy-done.12), channel_id=1, source_target_pairs={{0,1},{1,0},{2,3},{3,2},{4,5},{5,4},{6,7},{7,6},{8,9},{9,8},{10,11... | collective-permute-start | bytes 688136 | tf_op jit(solution)/shard_map/ppermute | solution.py:187
  283.2 18.9 %copy-start.11 = (bf16[2,448,128]{2,1,0:T(8,128)(2,1)S(1)}, bf16[2,448,128]{2,1,0:T(8,128)(2,1)}, u32[]{:S(2)}) copy-start(bf16[2,448,128]{2,1,0:T(8,128)(2,1)} %get-tuple-element.209.refs_19_) | copy-start | bytes 688132
  283.2 20.5 %copy-start.14 = (bf16[1,448,128]{2,1,0:T(8,128)(2,1)S(1)}, bf16[1,448,128]{2,1,0:T(8,128)(2,1)}, u32[]{:S(2)}) copy-start(bf16[1,448,128]{2,1,0:T(8,128)(2,1)} %fusion.9.refs_18_) | copy-start | bytes 344068
  302.0 10.3 %collective-permute-start.25 = (bf16[4,896,128]{2,1,0:T(8,128)(2,1)}, bf16[4,896,128]{2,1,0:T(8,128)(2,1)S(1)}, u32[]{:S(2)}, u32[]{:S(2)}) collective-permute-start(bf16[4,896,128]{2,1,0:T(8,128)(2,1)} %get-tuple-element.185), channel_id=1, source_target_pairs={{0,4},{4,0},{8,12},{12,8},{16,20},{20,16},{24,28},{28,24},{1,5},{5... | collective-permute-start | bytes 2752520 | tf_op jit(solution)/shard_map/ppermute | solution.py:189
  302.1 8.0 %collective-permute-start.29 = (bf16[2,448,128]{2,1,0:T(8,128)(2,1)S(1)}, bf16[2,448,128]{2,1,0:T(8,128)(2,1)S(1)}, u32[]{:S(2)}, u32[]{:S(2)}) collective-permute-start(bf16[2,448,128]{2,1,0:T(8,128)(2,1)S(1)} %copy-done.11), channel_id=1, source_target_pairs={{0,16},{4,20},{8,24},{12,28},{16,0},{20,4},{24,8},{28,12},{1,17},{... | collective-permute-start | bytes 688136 | tf_op jit(solution)/shard_map/ppermute | solution.py:189
  303.7 8.6 %collective-permute-start.35 = (bf16[1,448,128]{2,1,0:T(8,128)(2,1)S(1)}, bf16[1,448,128]{2,1,0:T(8,128)(2,1)S(1)}, u32[]{:S(2)}, u32[]{:S(2)}) collective-permute-start(bf16[1,448,128]{2,1,0:T(8,128)(2,1)S(1)} %copy-done.14), channel_id=1, source_target_pairs={{0,2},{1,3},{2,0},{3,1},{4,6},{5,7},{6,4},{7,5},{8,10},{9,11},{10,... | collective-permute-start | bytes 344072 | tf_op jit(solution)/shard_map/ppermute | solution.py:187
  310.1 8.3 %collective-permute-start.31 = (bf16[1,448,128]{2,1,0:T(8,128)(2,1)S(1)}, bf16[1,448,128]{2,1,0:T(8,128)(2,1)S(1)}, u32[]{:S(2)}, u32[]{:S(2)}) collective-permute-start(bf16[1,448,128]{2,1,0:T(8,128)(2,1)S(1)} %fusion.8), channel_id=1, source_target_pairs={{0,8},{4,12},{8,0},{12,4},{16,24},{20,28},{24,16},{28,20},{1,9},{5... | collective-permute-start | bytes 344072 | tf_op jit(solution)/shard_map/ppermute | solution.py:189
  312.3 21.1 %copy-start.2 = (f32[4,896,128]{2,1,0:T(8,128)S(1)}, f32[4,896,128]{2,1,0:T(8,128)}, u32[]{:S(2)}) copy-start(f32[4,896,128]{2,1,0:T(8,128)} %get-tuple-element.184) | copy-start | bytes 5505028
  314.0 11.1 %collective-permute-start.26 = (bf16[896,128]{1,0:T(8,128)(2,1)S(1)}, bf16[896,128]{1,0:T(8,128)(2,1)S(1)}, u32[]{:S(2)}, u32[]{:S(2)}) collective-permute-start(bf16[896,128]{1,0:T(8,128)(2,1)S(1)} %get-tuple-element.214), channel_id=1, source_target_pairs={{0,1},{1,0},{2,3},{3,2},{4,5},{5,4},{6,7},{7,6},{8,9},{9,8},{10,11... | collective-permute-start | bytes 688136 | tf_op jit(solution)/shard_map/ppermute | solution.py:194
  314.1 19.3 %collective-permute-start.27 = (bf16[896,128]{1,0:T(8,128)(2,1)S(1)}, bf16[896,128]{1,0:T(8,128)(2,1)S(1)}, u32[]{:S(2)}, u32[]{:S(2)}) collective-permute-start(bf16[896,128]{1,0:T(8,128)(2,1)S(1)} %get-tuple-element.216), channel_id=1, source_target_pairs={{0,2},{1,3},{2,0},{3,1},{4,6},{5,7},{6,4},{7,5},{8,10},{9,11},{10,... | collective-permute-start | bytes 688136 | tf_op jit(solution)/shard_map/ppermute | solution.py:194
  316.1 17.3 %collective-permute-start.28 = (bf16[896,128]{1,0:T(8,128)(2,1)S(1)}, bf16[896,128]{1,0:T(8,128)(2,1)S(1)}, u32[]{:S(2)}, u32[]{:S(2)}) collective-permute-start(bf16[896,128]{1,0:T(8,128)(2,1)S(1)} %get-tuple-element.215), channel_id=1, source_target_pairs={{0,3},{1,2},{2,1},{3,0},{4,7},{5,6},{6,5},{7,4},{8,11},{9,10},{10,... | collective-permute-start | bytes 688136 | tf_op jit(solution)/shard_map/ppermute | solution.py:194
  318.5 27.0 %collective-permute-start.30 = (bf16[448,128]{1,0:T(8,128)(2,1)S(1)}, bf16[448,128]{1,0:T(8,128)(2,1)S(1)}, u32[]{:S(2)}, u32[]{:S(2)}) collective-permute-start(bf16[448,128]{1,0:T(8,128)(2,1)S(1)} %get-tuple-element.212), channel_id=1, source_target_pairs={{0,8},{4,12},{1,9},{5,13},{2,10},{6,14},{3,11},{7,15}} | collective-permute-start | bytes 344072 | tf_op jit(solution)/shard_map/ppermute | solution.py:1444
  333.6 7.9 %collective-permute-start.32 = (bf16[896,128]{1,0:T(8,128)(2,1)S(1)}, bf16[896,128]{1,0:T(8,128)(2,1)S(1)}, u32[]{:S(2)}, u32[]{:S(2)}) collective-permute-start(bf16[896,128]{1,0:T(8,128)(2,1)S(1)} %fusion.12), channel_id=1, source_target_pairs={{8,0},{12,4},{9,1},{13,5},{10,2},{14,6},{11,3},{15,7}} | collective-permute-start | bytes 688136 | tf_op jit(solution)/shard_map/ppermute | solution.py:1454
  334.9 10.4 %collective-permute-start.33 = (bf16[896,128]{1,0:T(8,128)(2,1)S(1)}, bf16[896,128]{1,0:T(8,128)(2,1)S(1)}, u32[]{:S(2)}, u32[]{:S(2)}) collective-permute-start(bf16[896,128]{1,0:T(8,128)(2,1)S(1)} %fusion.12), channel_id=1, source_target_pairs={{16,0},{20,4},{17,1},{21,5},{18,2},{22,6},{19,3},{23,7}} | collective-permute-start | bytes 688136 | tf_op jit(solution)/shard_map/ppermute | solution.py:1454
  336.2 9.1 %collective-permute-start.34 = (bf16[896,128]{1,0:T(8,128)(2,1)S(1)}, bf16[896,128]{1,0:T(8,128)(2,1)S(1)}, u32[]{:S(2)}, u32[]{:S(2)}) collective-permute-start(bf16[896,128]{1,0:T(8,128)(2,1)S(1)} %fusion.12), channel_id=1, source_target_pairs={{24,0},{28,4},{25,1},{29,5},{26,2},{30,6},{27,3},{31,7}} | collective-permute-start | bytes 688136 | tf_op jit(solution)/shard_map/ppermute | solution.py:1454
  351.5 8.3 %collective-permute-start.36 = (f32[8,128]{1,0:T(8,128)S(1)}, f32[8,128]{1,0:T(8,128)S(1)}, u32[]{:S(2)}, u32[]{:S(2)}) collective-permute-start(f32[8,128]{1,0:T(8,128)S(1)} %select_add_fusion), channel_id=1, source_target_pairs={{0,1},{1,0},{2,3},{3,2},{4,5},{5,4},{6,7},{7,6},{8,9},{9,8},{10,11... | collective-permute-start | bytes 12296 | tf_op jit(solution)/shard_map/ppermute | solution.py:187
  359.8 4.5 %collective-permute-start.37 = (f32[8,128]{1,0:T(8,128)S(1)}, f32[8,128]{1,0:T(8,128)S(1)}, u32[]{:S(2)}, u32[]{:S(2)}) collective-permute-start(f32[8,128]{1,0:T(8,128)S(1)} %add.152), channel_id=1, source_target_pairs={{0,2},{1,3},{2,0},{3,1},{4,6},{5,7},{6,4},{7,5},{8,10},{9,11},{10,... | collective-permute-start | bytes 12296 | tf_op jit(solution)/shard_map/ppermute | solution.py:187
  364.3 1.2 collective-permute-start.38
  365.5 3.6 collective-permute-start.39
  369.1 3.6 collective-permute-start.40
  (18 other events, 61.1 us)
Sparse Core Ops, SparseCore 0:
  49.1 72.0 all-gather.1
